TPU v7x, 512 devices: a whole 4x8x8 slice. The times are simulated.
512 devices in a mesh: dp: 32 (over x, z_hi, core), expert: 16 (over y, z_lo).
Axes of the slice: x: 4, y: 8, z: 8 (z_hi: 4, z_lo: 2; z = z_hi * 2 + z_lo), core: 2. Of those that a mesh axis runs over, the one named last changes fastest.
Arguments:
- tokens: bfloat16 [65536, 3584], P(('dp', 'expert')), may hold values from -6 to 6
- grad_out: bfloat16 [65536, 3584], P(('dp', 'expert')), may hold values from -24 to 24
- routing: int32 [65536, 1], P(('dp', 'expert')), may hold values from 0 to 31; in each aligned block of 128 rows (0 to 127, 128 to 255, ...) at most 6 rows name the same one
- route_weight: float32 [65536, 1], P(('dp', 'expert')), may hold values from 0.1 to 1
- gate_weight: bfloat16 [3584, 8192], P('dp', 'expert'), may hold values from -0.09375 to 0.09375
- up_weight: bfloat16 [3584, 8192], P('dp', 'expert'), may hold values from -0.09375 to 0.09375
- down_weight: bfloat16 [3584, 8192], P('dp', 'expert'), may hold values from -0.1875 to 0.1875
Outputs:
- token_grad: bfloat16 [65536, 3584], P(('dp', 'expert'))
- route_grad: float32 [65536, 1], P(('dp', 'expert'))
- down_grad: bfloat16 [3584, 8192], P('dp', 'expert')
Inputs may be any that keep to these rules, and one draw needn't show every extreme that they name: `routing`: ids under 8 name this group's experts, the others experts elsewhere. In the tokens of one device no id appears more than 6 times, and some id appears exactly 6 times.
All inputs are finite; a program needn't handle non-finite values.
Results may differ from a plain program's by a relative error of at most 0.024.
Values may be sent and summed in bfloat16 or wider, within the bound.
No kernel may reach another device: no remote copies, remote signals or barrier semaphores. Data moves between devices by JAX's collectives and lax.ppermute only.
A program may use at most 64 MiB of HBM per device.

v0:
```python
import jax
import jax.numpy as jnp
from jax import lax
from jax.sharding import PartitionSpec as P


def silu_parts(pre_gate):
    sigmoid_val = jax.nn.sigmoid(pre_gate)
    return (pre_gate * sigmoid_val, sigmoid_val * (1.0 + pre_gate * (1.0 - sigmoid_val)))


def per_device(tokens, grad_out, routing, route_weight, gate_weight, up_weight, down_weight):
    groups = lax.axis_size("expert")
    experts = groups // 2
    token_count = tokens.shape[0]
    model_width = tokens.shape[1]
    capacity = 3 * token_count // (8 * experts)
    chosen_ids = routing[:, 0]
    expert_ids = lax.broadcasted_iota(jnp.int32, (token_count, experts), 1)
    member = (chosen_ids[:, None] == expert_ids).astype(jnp.int32)
    ranking = jnp.cumsum(member, axis=0) - 1
    slot_index = jnp.sum(member * (expert_ids * capacity + ranking), axis=1)
    slot_index = jnp.where(chosen_ids < experts, slot_index, experts * capacity)
    slot_table = jnp.full((experts * capacity,), token_count, jnp.int32)
    slot_table = slot_table.at[slot_index].set(
        jnp.arange(token_count, dtype=jnp.int32), mode="drop"
    )
    x_send = jnp.take(tokens, slot_table, axis=0, mode="fill", fill_value=0).reshape(
        experts, capacity, model_width
    )
    g_send = jnp.take(grad_out, slot_table, axis=0, mode="fill", fill_value=0).reshape(
        experts, capacity, model_width
    )
    p_send = jnp.take(route_weight[:, 0], slot_table, axis=0, mode="fill", fill_value=0.0).reshape(
        experts, capacity
    )
    x_send = jnp.repeat(x_send, 2, axis=0)
    g_send = jnp.repeat(g_send, 2, axis=0)
    p_send = jnp.repeat(p_send, 2, axis=0)
    gate_full, up_full, down_full = (
        lax.all_gather(gate_weight, "dp", axis=0, tiled=True),
        lax.all_gather(up_weight, "dp", axis=0, tiled=True),
        lax.all_gather(down_weight, "dp", axis=0, tiled=True),
    )
    x_recv, g_recv, p_recv = (
        lax.all_to_all(x_send, "expert", split_axis=0, concat_axis=0, tiled=True),
        lax.all_to_all(g_send, "expert", split_axis=0, concat_axis=0, tiled=True),
        lax.all_to_all(
            p_send.astype(jnp.bfloat16), "expert", split_axis=0, concat_axis=0, tiled=True
        ).astype(p_send.dtype),
    )
    x_rows = x_recv.reshape(groups * capacity, model_width)
    g_rows = g_recv.reshape(groups * capacity, model_width)
    p_rows = p_recv.reshape(groups * capacity, 1)
    pre_gate = jnp.dot(x_rows, gate_full, preferred_element_type=jnp.float32)
    pre_up = jnp.dot(x_rows, up_full, preferred_element_type=jnp.float32)
    activated, derivative = silu_parts(pre_gate)
    hidden = (activated * pre_up).astype(jnp.bfloat16)
    hidden_grad = jnp.dot(g_rows, down_full, preferred_element_type=jnp.float32)
    part_route = jnp.sum(hidden.astype(jnp.float32) * hidden_grad, axis=1)
    scaled_grad = p_rows * hidden_grad
    d_gate_pre = (scaled_grad * pre_up * derivative).astype(jnp.bfloat16)
    d_up_pre = (scaled_grad * activated).astype(jnp.bfloat16)
    contract = (((1,), (1,)), ((), ()))
    part_tokens = lax.dot_general(
        d_gate_pre, gate_full, contract, preferred_element_type=jnp.float32
    )
    part_tokens = part_tokens + lax.dot_general(
        d_up_pre, up_full, contract, preferred_element_type=jnp.float32
    )
    part_tokens = part_tokens.astype(jnp.bfloat16)
    scaled = (p_rows * g_rows.astype(jnp.float32)).astype(jnp.bfloat16)
    grad_back, route_back = (
        lax.all_to_all(
            part_tokens.reshape(groups, capacity, model_width),
            "expert",
            split_axis=0,
            concat_axis=0,
            tiled=True,
        ),
        lax.all_to_all(
            part_route.reshape(groups, capacity).astype(jnp.bfloat16),
            "expert",
            split_axis=0,
            concat_axis=0,
            tiled=True,
        ).astype(jnp.float32),
    )
    pair_grad = jnp.sum(
        grad_back.reshape(experts, 2, capacity, model_width).astype(jnp.float32), axis=1
    )
    pair_grad = pair_grad.astype(jnp.bfloat16).reshape(experts * capacity, model_width)
    pair_route = jnp.sum(route_back.reshape(experts, 2, capacity), axis=1).reshape(
        experts * capacity
    )
    token_grad = jnp.take(pair_grad, slot_index, axis=0, mode="fill", fill_value=0)
    route_grad = jnp.take(pair_route, slot_index, axis=0, mode="fill", fill_value=0.0)[:, None]
    down_grad = lax.psum_scatter(
        lax.dot_general(
            scaled, hidden, (((0,), (0,)), ((), ())), preferred_element_type=jnp.float32
        ).astype(jnp.bfloat16),
        "dp",
        scatter_dimension=0,
        tiled=True,
    )
    return (token_grad, route_grad, down_grad)


def solution(mesh):
    placed = (
        P(("dp", "expert"), None),
        P(("dp", "expert"), None),
        P(("dp", "expert"), None),
        P(("dp", "expert"), None),
        P("dp", "expert"),
        P("dp", "expert"),
        P("dp", "expert"),
    )
    return jax.shard_map(
        per_device,
        mesh=mesh,
        in_specs=placed,
        out_specs=(P(("dp", "expert"), None), P(("dp", "expert"), None), P("dp", "expert")),
        check_vma=False,
    )
```

profile of v0, /device:TPU:6, one launch (start us, length us, event | category | flops | bytes accessed | tf_op | source)
XLA Modules:
  0.0 335.3 jit_solution(2613005690085777946)
XLA Ops:
  7.2 0.0 copy-start
  7.2 0.0 copy-start.2
  7.2 0.0 all-gather.8.cloned.1.call-start
  7.2 0.7 all-gather.8.cloned.1.call-update
  7.9 0.0 all-gather.6.cloned.1.call-start
  8.0 0.7 all-gather.6.cloned.1.call-update
  8.7 0.0 all-gather.4.cloned.1.call-start
  8.7 0.7 all-gather.4.cloned.1.call-update
  9.4 0.7 fusion.7
  10.2 0.2 reduce_window_sum.11
  10.3 0.8 select_reduce_fusion
  11.2 0.7 fusion.13
  11.8 1.0 scatter_custom_fusion
  12.8 1.4 gather_fusion
  14.3 0.1 convert_element_type.82
  14.4 0.6 copy.10
  15.0 9.0 %all-to-all-start = ((bf16[16,1,6]{2,1,0:T(2,128)(2,1)}), bf16[16,1,6]{2,1,0:T(2,128)(2,1)S(1)}, u32[]{:S(2)}, u32[]{:S(2)}) async-start(bf16[16,1,6]{2,1,0:T(2,128)(2,1)} %copy.10), calls=%async_computation | async-start | bytes 16384 | tf_op jit(solution)/shard_map/all_to_all | solution.py:48
  24.0 0.0 copy-done
  24.0 0.8 gather_fusion.3
  24.8 0.0 copy-done.2
  24.8 0.8 gather_fusion.4
  25.6 0.1 broadcast_select_fusion.2
  25.7 0.1 reshape.102
  25.8 6.6 %all-to-all-done = bf16[16,1,6]{2,1,0:T(2,128)(2,1)S(1)} async-done(((bf16[16,1,6]{2,1,0:T(2,128)(2,1)}), bf16[16,1,6]{2,1,0:T(2,128)(2,1)S(1)}, u32[]{:S(2)}, u32[]{:S(2)}) %all-to-all-start) | async-done | bytes 224 | tf_op jit(solution)/shard_map/all_to_all | solution.py:48
  32.4 1.0 broadcast_in_dim.58
  33.4 3.6 %all-to-all-start.2 = ((bf16[16,6,3584]{2,1,0:T(8,128)(2,1)}), bf16[16,6,3584]{2,1,0:T(8,128)(2,1)S(1)}, u32[]{:S(2)}, u32[]{:S(2)}) async-start(bf16[16,6,3584]{2,1,0:T(8,128)(2,1)} %bitcast.7), calls=%async_computation.2 | async-start | bytes 1835008 | tf_op jit(solution)/shard_map/all_to_all | solution.py:46
  37.1 0.1 reshape.99
  37.2 24.8 %all-to-all-done.2 = bf16[16,6,3584]{2,1,0:T(8,128)(2,1)S(1)} async-done(((bf16[16,6,3584]{2,1,0:T(8,128)(2,1)}), bf16[16,6,3584]{2,1,0:T(8,128)(2,1)S(1)}, u32[]{:S(2)}, u32[]{:S(2)}) %all-to-all-start.2) | async-done | bytes 688160 | tf_op jit(solution)/shard_map/all_to_all | solution.py:46
  62.0 1.0 broadcast_in_dim.57
  63.0 4.3 %all-to-all-start.1 = ((bf16[16,6,3584]{2,1,0:T(8,128)(2,1)}), bf16[16,6,3584]{2,1,0:T(8,128)(2,1)}, u32[]{:S(2)}, u32[]{:S(2)}) async-start(bf16[16,6,3584]{2,1,0:T(8,128)(2,1)} %bitcast.6), calls=%async_computation.1 | async-start | bytes 1835008 | tf_op jit(solution)/shard_map/all_to_all | solution.py:47
  67.3 0.0 reduce-scatter.2.cloned.1.call-start
  67.4 0.1 reshape.109
  67.5 0.2 reshape.104
  67.7 22.9 %all-to-all-done.1 = bf16[16,6,3584]{2,1,0:T(8,128)(2,1)} async-done(((bf16[16,6,3584]{2,1,0:T(8,128)(2,1)}), bf16[16,6,3584]{2,1,0:T(8,128)(2,1)}, u32[]{:S(2)}, u32[]{:S(2)}) %all-to-all-start.1) | async-done | bytes 688160 | tf_op jit(solution)/shard_map/all_to_all | solution.py:47
  90.7 1.4 reshape.101
  92.0 0.0 all-gather.8.cloned.1.call-done
  92.1 2.7 fusion.15
  94.8 59.9 %all-gather.6.cloned.1.call-done = bf16[3584,512]{1,0:T(8,128)(2,1)} async-done(((bf16[112,512]{1,0:T(8,128)(2,1)}), bf16[3584,512]{1,0:T(8,128)(2,1)}) %all-gather.6.cloned.1.call-update) | async-done | bytes 3670032 | tf_op jit(solution)/shard_map/all_gather | solution.py:42
  154.7 2.8 fusion.14
  157.5 62.5 %all-gather.4.cloned.1.call-done = bf16[3584,512]{1,0:T(8,128)(2,1)} async-done(((bf16[112,512]{1,0:T(8,128)(2,1)}), bf16[3584,512]{1,0:T(8,128)(2,1)}) %all-gather.4.cloned.1.call-update) | async-done | bytes 3670032 | tf_op jit(solution)/shard_map/all_gather | solution.py:43
  220.0 2.9 multiply_reduce_fusion
  222.8 3.2 convolution_convert_fusion
  226.0 0.0 reduce-scatter.2.cloned.1.call-update
  226.0 0.7 convert_element_type.100
  226.7 6.8 %all-to-all-start.4 = ((bf16[16,1,6]{2,1,0:T(2,128)(2,1)}), bf16[16,1,6]{2,1,0:T(2,128)(2,1)S(1)}, u32[]{:S(2)}, u32[]{:S(2)}) async-start(bf16[16,1,6]{2,1,0:T(2,128)(2,1)} %convert_element_type.100), calls=%async_computation.4 | async-start | bytes 16384 | tf_op jit(solution)/shard_map/all_to_all | solution.py:81
  233.6 0.0 copy-start.1
  233.6 3.4 %fusion.3 = f32[96,3584]{1,0:T(8,128)S(1)} fusion(bf16[3584,512]{1,0:T(8,128)(2,1)} %all-gather.8.cloned.1.call-done, f32[96,512]{1,0:T(8,128)S(1)} %fusion.15, f32[96,512]{1,0:T(8,128)S(1)} %fusion.14, f32[96,512]{1,0:T(8,128)S(1)} %get-tuple-element.12, f32[96]{0:T(128)S(1)} %reshape.109), kind=kOutput, calls=%fused_computation.21 | convolution fusion | flops 352862208 | bytes 5636480 | tf_op jit(solution)/shard_map/dot_general | solution.py:65
  237.0 0.0 copy-done.1
  237.0 1.2 fusion
  238.3 1.2 reshape.105
  239.5 2.6 all-to-all-done.4
  242.1 5.5 %all-to-all-start.3 = ((bf16[16,6,3584]{2,1,0:T(8,128)(2,1)}), bf16[16,6,3584]{2,1,0:T(8,128)(2,1)S(1)}, u32[]{:S(2)}, u32[]{:S(2)}) async-start(bf16[16,6,3584]{2,1,0:T(8,128)(2,1)} %reshape.105), calls=%async_computation.3 | async-start | bytes 1835008 | tf_op jit(solution)/shard_map/all_to_all | solution.py:74
  247.6 0.1 reshape.108
  247.7 1.2 gather_fusion.2
  249.0 0.5 bitcast_select_fusion
  249.5 23.6 %all-to-all-done.3 = bf16[16,6,3584]{2,1,0:T(8,128)(2,1)S(1)} async-done(((bf16[16,6,3584]{2,1,0:T(8,128)(2,1)}), bf16[16,6,3584]{2,1,0:T(8,128)(2,1)S(1)}, u32[]{:S(2)}, u32[]{:S(2)}) %all-to-all-start.3) | async-done | bytes 688160 | tf_op jit(solution)/shard_map/all_to_all | solution.py:74
  273.1 0.2 bitcast_reduce_fusion
  273.3 0.1 reshape.107
  273.4 1.1 gather_fusion.1
  274.5 1.1 broadcast_select_fusion
  275.6 53.2 %reduce-scatter.2.cloned.1.call-done = bf16[112,512]{1,0:T(8,128)(2,1)} async-done(((bf16[3584,512]{1,0:T(8,128)(2,1)}), bf16[112,512]{1,0:T(8,128)(2,1)}) %reduce-scatter.2.cloned.1.call-update) | async-done | bytes 114704 | tf_op jit(solution)/shard_map/reduce_scatter | solution.py:98
  (10 shorter events, 0.1 us)
Async XLA Ops:
  7.2 16.9 %copy-start = (bf16[128,3584]{1,0:T(8,128)(2,1)S(1)}, bf16[128,3584]{1,0:T(8,128)(2,1)}, u32[]{:S(2)}) copy-start(bf16[128,3584]{1,0:T(8,128)(2,1)} %param.10) | copy-start | bytes 2752516
  7.2 17.6 %copy-start.2 = (bf16[128,3584]{1,0:T(8,128)(2,1)S(1)}, bf16[128,3584]{1,0:T(8,128)(2,1)}, u32[]{:S(2)}) copy-start(bf16[128,3584]{1,0:T(8,128)(2,1)} %param.9) | copy-start | bytes 2752516
  7.2 84.9 %all-gather.8.cloned.1.call-start = ((), (), s32[]{:S(2)}) async-start(), calls=%async_computation.8 | async-start | bytes 3784704 | tf_op jit(solution)/shard_map/all_gather | solution.py:41
  7.9 146.8 %all-gather.6.cloned.1.call-start = ((), (), s32[]{:S(2)}) async-start(), calls=%async_computation.7 | async-start | bytes 3784704 | tf_op jit(solution)/shard_map/all_gather | solution.py:42
  8.7 211.3 %all-gather.4.cloned.1.call-start = ((), (), s32[]{:S(2)}) async-start(), calls=%async_computation.6 | async-start | bytes 3784704 | tf_op jit(solution)/shard_map/all_gather | solution.py:43
  15.0 17.4 %all-to-all-start = ((bf16[16,1,6]{2,1,0:T(2,128)(2,1)}), bf16[16,1,6]{2,1,0:T(2,128)(2,1)S(1)}, u32[]{:S(2)}, u32[]{:S(2)}) async-start(bf16[16,1,6]{2,1,0:T(2,128)(2,1)} %copy.10), calls=%async_computation | async-start | bytes 16384 | tf_op jit(solution)/shard_map/all_to_all | solution.py:48
  33.4 28.6 %all-to-all-start.2 = ((bf16[16,6,3584]{2,1,0:T(8,128)(2,1)}), bf16[16,6,3584]{2,1,0:T(8,128)(2,1)S(1)}, u32[]{:S(2)}, u32[]{:S(2)}) async-start(bf16[16,6,3584]{2,1,0:T(8,128)(2,1)} %bitcast.7), calls=%async_computation.2 | async-start | bytes 1835008 | tf_op jit(solution)/shard_map/all_to_all | solution.py:46
  63.0 27.7 %all-to-all-start.1 = ((bf16[16,6,3584]{2,1,0:T(8,128)(2,1)}), bf16[16,6,3584]{2,1,0:T(8,128)(2,1)}, u32[]{:S(2)}, u32[]{:S(2)}) async-start(bf16[16,6,3584]{2,1,0:T(8,128)(2,1)} %bitcast.6), calls=%async_computation.1 | async-start | bytes 1835008 | tf_op jit(solution)/shard_map/all_to_all | solution.py:47
  67.3 261.4 %reduce-scatter.2.cloned.1.call-start = ((), (), s32[]{:S(2)}) async-start(), calls=%async_computation.9 | async-start | bytes 3784704 | tf_op jit(solution)/shard_map/reduce_scatter | solution.py:98
  226.7 15.3 %all-to-all-start.4 = ((bf16[16,1,6]{2,1,0:T(2,128)(2,1)}), bf16[16,1,6]{2,1,0:T(2,128)(2,1)S(1)}, u32[]{:S(2)}, u32[]{:S(2)}) async-start(bf16[16,1,6]{2,1,0:T(2,128)(2,1)} %convert_element_type.100), calls=%async_computation.4 | async-start | bytes 16384 | tf_op jit(solution)/shard_map/all_to_all | solution.py:81
  233.6 3.4 %copy-start.1 = (bf16[3584,512]{1,0:T(8,128)(2,1)S(1)}, bf16[3584,512]{1,0:T(8,128)(2,1)}, u32[]{:S(2)}) copy-start(bf16[3584,512]{1,0:T(8,128)(2,1)} %all-gather.6.cloned.1.call-done) | copy-start | bytes 11010052
  242.1 31.0 %all-to-all-start.3 = ((bf16[16,6,3584]{2,1,0:T(8,128)(2,1)}), bf16[16,6,3584]{2,1,0:T(8,128)(2,1)S(1)}, u32[]{:S(2)}, u32[]{:S(2)}) async-start(bf16[16,6,3584]{2,1,0:T(8,128)(2,1)} %reshape.105), calls=%async_computation.3 | async-start | bytes 1835008 | tf_op jit(solution)/shard_map/all_to_all | solution.py:74
Sparse Core Ops, SparseCore 0:
  11.1 73.8 all-gather.7
  88.1 66.5 all-gather.5
  157.9 62.0 all-gather.3
  226.2 102.5 reduce-scatter.1
where the time goes:
time: 337 us; the launch traced here: 335 us
  waiting for transfers between devices  258 us (77%)
  starting transfers between devices  29.5 us (9%)
  matrix products  16.2 us (5%)
  between operations  14 us (4%)
  local copies, waits for them, and re-layouts  12.9 us (4%)
  other arithmetic  4.36 us (1%)
    all_gather x1, waiting for transfers between devices, per_device(): lax.all_gather(down_weight, 'dp', axis=0, tiled=True)  62.5 us
    all_gather x1, waiting for transfers between devices, per_device(): lax.all_gather(up_weight, 'dp', axis=0, tiled=True)  59.9 us
    reduce_scatter x1, waiting for transfers between devices, per_device(): lax.psum_scatter(lax.dot_general(scaled, hidden, (((0,), (0,)), ((), ()))...  53.2 us
    all_to_all x1, waiting for transfers between devices, per_device(): lax.all_to_all(x_send, 'expert', split_axis=0, concat_axis=0, tiled=True)  24.8 us
    all_to_all x1, waiting for transfers between devices, per_device(): lax.all_to_all(part_tokens.reshape(groups, capacity, model_width), 'exper...  23.6 us
    all_to_all x1, waiting for transfers between devices, per_device(): lax.all_to_all(g_send, 'expert', split_axis=0, concat_axis=0, tiled=True)  22.9 us
    all_to_all x1, starting transfers between devices, per_device(): lax.all_to_all(p_send.astype(jnp.bfloat16), 'expert', split_axis=0, conca...  9.01 us
    all_to_all x1, starting transfers between devices, per_device(): lax.all_to_all(part_route.reshape(groups, capacity).astype(jnp.bfloat16),...  6.85 us
  transfers between devices with their start and end apart: 9, of which 8 were waited for; matrix products, arithmetic and copies ran while one was open for 8% of the time, Pallas kernels for 0%

commit v1 on v0

v1 whole, which is shorter than its diff:
```python
import jax
import jax.numpy as jnp
from jax import lax
from jax.experimental import pallas as pl
from jax.experimental.pallas import tpu as pltpu
from jax.sharding import Mesh, PartitionSpec as P

BF = jnp.bfloat16
F32 = jnp.float32
AXES = ("x", "zh", "c", "y", "zl")
TOK = 128
D = 3584
EXPERTS = 8
HALF = 512
QUART = 256
SHARD = 112
BLOCK = 2 * SHARD
XROWS = 4 * BLOCK
SLOTS = 16
ROWS = EXPERTS * SLOTS
BACK = EXPERTS * 8


def expert_rank(ids):
    lanes = lax.broadcasted_iota(jnp.int32, (TOK, TOK), 1)
    subs = lax.broadcasted_iota(jnp.int32, (TOK, TOK), 0)
    member = jnp.where((ids == lanes) & (lanes < EXPERTS), 1.0, 0.0)
    earlier = jnp.where(lanes < subs, 1.0, 0.0)
    counts = jnp.dot(earlier.astype(BF), member.astype(BF), preferred_element_type=F32)
    rank = jnp.sum(member * counts, axis=1, keepdims=True).astype(jnp.int32)
    return rank, lanes


def dispatch_kernel(ids_ref, p_ref, x_ref, g_ref, out_ref):
    ids = ids_ref[...]
    rank, lanes = expert_rank(ids)
    slot = jnp.where(ids < EXPERTS, ids * SLOTS + rank, -SLOTS)
    sel_x = jnp.where(slot == lanes, 1.0, 0.0).astype(BF)
    sel_g = jnp.where(slot + 8 == lanes, 1.0, 0.0).astype(BF)
    scaled = (p_ref[...] * g_ref[...].astype(F32)).astype(BF)
    first = (((0,), (0,)), ((), ()))
    rows = lax.dot_general(sel_x, x_ref[...], first, preferred_element_type=F32)
    rows = rows + lax.dot_general(sel_g, scaled, first, preferred_element_type=F32)
    out_ref[...] = rows.astype(BF)


def dispatch(ids, weight, tokens, grads):
    chunk = D // 4
    whole = pl.BlockSpec((TOK, 1), lambda i: (0, 0))
    part = pl.BlockSpec((TOK, chunk), lambda i: (0, i))
    return pl.pallas_call(
        dispatch_kernel,
        grid=(4,),
        in_specs=[whole, whole, part, part],
        out_specs=pl.BlockSpec((ROWS, chunk), lambda i: (0, i)),
        out_shape=jax.ShapeDtypeStruct((ROWS, D), BF),
        cost_estimate=pl.CostEstimate(flops=4 * TOK * ROWS * D, bytes_accessed=6 * TOK * D, transcendentals=0),
        name="dispatch",
    )(ids, weight, tokens, grads)


def finish_kernel(ids_ref, p_ref, rows_ref, head_ref, tok_ref, route_ref):
    ids = ids_ref[...]
    rank, lanes = expert_rank(ids)
    valid = ids < EXPERTS
    slot = jnp.where(valid, ids * 8 + rank, -8)
    cols = lax.broadcasted_iota(jnp.int32, (TOK, BACK), 1)
    sel = jnp.where(slot == cols, 1.0, 0.0).astype(BF)
    tok_ref[...] = jnp.dot(sel, rows_ref[...], preferred_element_type=F32).astype(BF)

    @pl.when(pl.program_id(0) == 0)
    def _():
        pick = jnp.where(jnp.where(valid, ids * 8 + 6, -8) == cols, 1.0, 0.0).astype(BF)
        values = jnp.dot(pick, head_ref[...], preferred_element_type=F32)
        total = jnp.sum(jnp.where(lanes == rank, values, 0.0), axis=1, keepdims=True)
        route_ref[...] = total / p_ref[...]


def finish(ids, weight, rows):
    chunk = D // 4
    whole = pl.BlockSpec((TOK, 1), lambda i: (0, 0))
    return pl.pallas_call(
        finish_kernel,
        grid=(4,),
        in_specs=[
            whole,
            whole,
            pl.BlockSpec((BACK, chunk), lambda i: (0, i)),
            pl.BlockSpec((BACK, TOK), lambda i: (0, 0)),
        ],
        out_specs=[pl.BlockSpec((TOK, chunk), lambda i: (0, i)), whole],
        out_shape=[jax.ShapeDtypeStruct((TOK, D), BF), jax.ShapeDtypeStruct((TOK, 1), F32)],
        cost_estimate=pl.CostEstimate(flops=2 * TOK * BACK * D, bytes_accessed=4 * TOK * D, transcendentals=0),
        name="finish",
    )(ids, weight, rows, rows)


def expert_kernel(pieces, *refs):
    row_refs = refs[:4]
    weight_refs = refs[4:4 + len(pieces)]
    keep_ref, send_ref, far_ref, plus_ref, minus_ref, own_ref = refs[4 + len(pieces):10 + len(pieces)]
    rows, weights, sem_rows, sem_weights = refs[10 + len(pieces):]
    xi, zi, ci = lax.axis_index("x"), lax.axis_index("zh"), lax.axis_index("c")
    copies = []
    for i, ref in enumerate(row_refs):
        copies.append(pltpu.make_async_copy(ref, rows.at[pl.ds(i * ROWS, ROWS)], sem_rows.at[i]))
    count = 0
    for ref, listed in zip(weight_refs, pieces):
        for at, (dx, dz, which) in enumerate(listed):
            block = lax.rem(xi + dx, 4) * 4 + lax.rem(zi + dz, 4)
            core = ci if which == 0 else 1 - ci
            start = pl.multiple_of(block * BLOCK + core * SHARD, 16)
            copies.append(pltpu.make_async_copy(
                ref.at[pl.ds(at * SHARD, SHARD)], weights.at[pl.ds(start, SHARD)], sem_weights.at[count]
            ))
            count += 1
    for copy in copies:
        copy.start()
    for copy in copies:
        copy.wait()
    pre = jnp.dot(rows[...], weights[...], preferred_element_type=F32)
    pre = pre.reshape(4 * EXPERTS, SLOTS, 3 * QUART)
    tall = 4 * BACK
    gate = pre[:, :8, :QUART].reshape(tall, QUART)
    up = pre[:, :8, QUART:2 * QUART].reshape(tall, QUART)
    grad = pre[:, 8:, 2 * QUART:].reshape(tall, QUART)
    sig = jax.nn.sigmoid(gate)
    act = gate * sig
    slope = sig * (1.0 + gate * (1.0 - sig))
    hidden = (act * up).astype(BF).astype(F32)
    route = jnp.sum(hidden * grad, axis=1, keepdims=True).reshape(4 * EXPERTS, 8, 1)
    spread = jnp.concatenate([jnp.zeros((4 * EXPERTS, 8, QUART), F32), hidden.reshape(4 * EXPERTS, 8, QUART)], axis=1)
    spread = spread.reshape(4 * ROWS, QUART).astype(BF)
    for ref, shift in ((far_ref, 2), (plus_ref, 1), (minus_ref, 3), (own_ref, 0)):
        start = pl.multiple_of(lax.rem(xi + shift, 4) * XROWS, 128)
        ref[...] = lax.dot_general(
            rows[:, pl.ds(start, XROWS)], spread, (((0,), (0,)), ((), ())), preferred_element_type=F32
        ).astype(BF)
    d_pre = jnp.concatenate([(grad * up * slope).astype(BF), (grad * act).astype(BF)], axis=1)
    lanes = lax.broadcasted_iota(jnp.int32, (4 * EXPERTS, 8, 128), 2)
    subs = lax.broadcasted_iota(jnp.int32, (4 * EXPERTS, 8, 128), 1)
    line = jnp.sum(jnp.where(lanes == subs, route, 0.0), axis=1, keepdims=True)
    extra = jnp.where(subs == 6, line, 0.0).reshape(tall, 128)
    chunk = D // 4
    for i in range(4):
        part = lax.dot_general(
            d_pre, weights[i * chunk:(i + 1) * chunk, :2 * QUART], (((1,), (1,)), ((), ())),
            preferred_element_type=F32,
        )
        if i == 0:
            part = jnp.concatenate([part[:, :128] + extra, part[:, 128:]], axis=1)
        part = part.astype(BF)
        keep_ref[:, i * chunk:(i + 1) * chunk] = part[:2 * BACK]
        send_ref[:, i * chunk:(i + 1) * chunk] = part[2 * BACK:]


def expert_compute(rows, blocks, pieces):
    anywhere = pl.BlockSpec(memory_space=pl.ANY)
    vmem = pl.BlockSpec(memory_space=pltpu.VMEM)
    count = sum(len(p) for p in pieces)
    big = jax.ShapeDtypeStruct((2 * BACK, D), BF)
    down = jax.ShapeDtypeStruct((XROWS, QUART), BF)
    return pl.pallas_call(
        lambda *refs: expert_kernel(pieces, *refs),
        in_specs=[anywhere] * (4 + len(blocks)),
        out_specs=[vmem] * 6,
        out_shape=[big, big, down, down, down, down],
        scratch_shapes=[
            pltpu.VMEM((4 * ROWS, D), BF),
            pltpu.VMEM((D, 3 * QUART), BF),
            pltpu.SemaphoreType.DMA((4,)),
            pltpu.SemaphoreType.DMA((count,)),
        ],
        compiler_params=pltpu.CompilerParams(vmem_limit_bytes=48 * 1024 * 1024),
        cost_estimate=pl.CostEstimate(flops=6 * 10**9, bytes_accessed=14 * 10**6, transcendentals=65536),
        name="experts",
    )(*rows, *blocks)


def hop(a, axis, shift):
    n = lax.axis_size(axis)
    return lax.ppermute(a, axis, [(i, (i + shift) % n) for i in range(n)])


def both_ways(a, axis):
    return hop(a, axis, 1), hop(a, axis, -1)


def ring_gather(a, axis):
    n = a.shape[0] // 2
    before, after = both_ways(a, axis)
    return before, after, hop(before[:n], axis, 1), hop(after[n:], axis, -1)


def ring_scatter(far, plus, minus, own, axis):
    n = far.shape[0] // 2
    low = hop(far[:n], axis, 1)
    high = hop(far[n:], axis, -1)
    plus = jnp.concatenate([(plus[:n].astype(F32) + low.astype(F32)).astype(BF), plus[n:]], axis=0)
    minus = jnp.concatenate([minus[:n], (minus[n:].astype(F32) + high.astype(F32)).astype(BF)], axis=0)
    total = hop(plus, axis, 1).astype(F32) + hop(minus, axis, -1).astype(F32) + own.astype(F32)
    return total.astype(BF)


def per_device(tokens, grad_out, routing, route_weight, gate_weight, up_weight, down_weight):
    zi, ci = lax.axis_index("zh"), lax.axis_index("c")

    def columns(which):
        return jnp.concatenate([
            lax.dynamic_slice(w, (0, which * QUART), (SHARD, QUART)) for w in (gate_weight, up_weight, down_weight)
        ], axis=1)

    own = jnp.concatenate([columns(ci), hop(columns(1 - ci), "c", 1)], axis=0)

    sent = dispatch(routing, route_weight, tokens, grad_out).reshape(EXPERTS, SLOTS, D)
    rows_own = lax.all_to_all(sent, "y", split_axis=0, concat_axis=0, tiled=True).reshape(ROWS, D)
    rows_zl = hop(rows_own, "zl", 1)
    rows_c = hop(rows_own, "c", 1)
    rows_czl = hop(rows_zl, "c", 1)

    pair = lambda dx, dz: [(dx, dz, 0), (dx, dz, 1)]
    blocks, pieces = [], []

    def add_x(block, listed):
        before, after, low, high = ring_gather(block, "x")
        half = len(listed) // 2
        blocks.extend([block, before, after, low, high])
        pieces.append(listed)
        pieces.append([((dx + 3) % 4, dz, w) for dx, dz, w in listed])
        pieces.append([((dx + 1) % 4, dz, w) for dx, dz, w in listed])
        pieces.append([((dx + 2) % 4, dz, w) for dx, dz, w in listed[:half]])
        pieces.append([((dx + 2) % 4, dz, w) for dx, dz, w in listed[half:]])

    z_before, z_after, z_low, z_high = ring_gather(own, "zh")
    add_x(own, pair(0, 0))
    add_x(jnp.concatenate([z_before, z_after], axis=0), pair(0, 3) + pair(0, 1))
    add_x(jnp.concatenate([z_low, z_high], axis=0), pair(0, 2))

    keep, send, far, plus, minus, mine = expert_compute([rows_own, rows_zl, rows_c, rows_czl], blocks, pieces)

    got = hop(send, "c", 1)
    to_zl = (keep[BACK:].astype(F32) + got[BACK:].astype(F32)).astype(BF)
    from_zl = hop(to_zl, "zl", 1)
    back = (keep[:BACK].astype(F32) + got[:BACK].astype(F32) + from_zl.astype(F32)).astype(BF)
    back = lax.all_to_all(back.reshape(EXPERTS, 8, D), "y", split_axis=0, concat_axis=0, tiled=True)
    token_grad, route_grad = finish(routing, route_weight, back.reshape(BACK, D))

    summed = ring_scatter(far, plus, minus, mine, "x")
    quarter = lambda shift: lax.dynamic_slice(summed, (lax.rem(zi + shift, 4) * BLOCK, 0), (BLOCK, QUART))
    summed = ring_scatter(quarter(2), quarter(1), quarter(3), quarter(0), "zh")
    stay = lax.dynamic_slice(summed, (ci * SHARD, 0), (SHARD, QUART))
    cross = hop(lax.dynamic_slice(summed, ((1 - ci) * SHARD, 0), (SHARD, QUART)), "c", 1)
    down_grad = jnp.where(ci == 0, jnp.concatenate([stay, cross], axis=1), jnp.concatenate([cross, stay], axis=1))
    return token_grad, route_grad, down_grad


def solution(mesh):
    inner = Mesh(mesh.devices.reshape(4, 4, 2, 8, 2), AXES)
    rows = P(AXES, None)
    weights = P(("x", "zh", "c"), ("y", "zl"))
    return jax.shard_map(
        per_device,
        mesh=inner,
        in_specs=(rows, rows, rows, rows, weights, weights, weights),
        out_specs=(rows, rows, weights),
        check_vma=False,
    )
```

time: 337 us -> 222 us (0.66)
  waiting for transfers between devices: 258 us -> 68.1 us
  starting transfers between devices: 29.5 us -> 117 us
  Pallas kernels: 0 us -> 22.7 us
  matrix products: 16.2 us -> 0 us
  between operations: 14 us -> 1.38 us
  local copies, waits for them, and re-layouts: 12.9 us -> 7.48 us
    all_gather x3 -> x0, waiting for transfers between devices: 122 us -> none  [the longest x1 62.5 us: per_device(): lax.all_gather(down_weight, 'dp', axis=0, tiled=True)]
    ppermute x0 -> x31, starting transfers between devices: none -> 107 us  [hop(): return lax.ppermute(a, axis, [(i, (i + shift) % n) for i in range(n)])]
    all_to_all x5 -> x2, waiting for transfers between devices: 80.6 us -> 8.72 us  [the longest x1 8.71 us: per_device(): lax.all_to_all(sent, 'y', split_axis=0, concat_axis=0, tiled=True)]
    ppermute x0 -> x31, waiting for transfers between devices: none -> 59.4 us  [hop(): return lax.ppermute(a, axis, [(i, (i + shift) % n) for i in range(n)])]
    reduce_scatter x1 -> x0, waiting for transfers between devices: 53.2 us -> none  [per_device(): lax.psum_scatter(lax.dot_general(scaled, hidden, (((0,), (0,)), ((), ()))...]
    pallas_call x0 -> x3, Pallas kernels: none -> 22.7 us  [the longest x1 13 us: expert_compute(): pl.pallas_call(lambda *refs: expert_kernel(pieces, *refs), in_specs=[anyw...]
    all_to_all x5 -> x2, starting transfers between devices: 29.3 us -> 10.7 us  [the longest x1 7.23 us: per_device(): lax.all_to_all(sent, 'y', split_axis=0, concat_axis=0, tiled=True)]
    dot_general x6 -> x0, matrix products: 16.2 us -> none  [the longest x1 3.43 us: per_device(): lax.dot_general(d_gate_pre, gate_full, contract, preferred_element_type=j...]
  transfers between devices with their start and end apart: 9 -> 33, of which waited for: 8 -> 15; matrix products, arithmetic and copies ran while one was open for 8% -> 1% of each run, Pallas kernels for 0% -> 0%
where the time goes in v1:
time: 222 us; the launch traced here: 220 us
  starting transfers between devices  117 us (53%)
  waiting for transfers between devices  68.1 us (31%)
  Pallas kernels  22.7 us (10%)
  local copies, waits for them, and re-layouts  7.48 us (3%)
  other arithmetic  2.96 us (1%)
    ppermute x31, starting transfers between devices, hop(): return lax.ppermute(a, axis, [(i, (i + shift) % n) for i in range(n)])  107 us
    ppermute x31, waiting for transfers between devices, hop(): return lax.ppermute(a, axis, [(i, (i + shift) % n) for i in range(n)])  59.4 us
    pallas_call x1, Pallas kernels, expert_compute(): pl.pallas_call(lambda *refs: expert_kernel(pieces, *refs), in_specs=[anyw...  13 us
    all_to_all x1, waiting for transfers between devices, per_device(): lax.all_to_all(sent, 'y', split_axis=0, concat_axis=0, tiled=True)  8.71 us
    all_to_all x1, starting transfers between devices, per_device(): lax.all_to_all(sent, 'y', split_axis=0, concat_axis=0, tiled=True)  7.23 us
    unnamed x29, local copies, waits for them, and re-layouts  7.17 us
    pallas_call x1, Pallas kernels, dispatch(): pl.pallas_call(dispatch_kernel, grid=(4,), in_specs=[whole, whole, part,...  5.09 us
    pallas_call x1, Pallas kernels, finish(): pl.pallas_call(finish_kernel, grid=(4,), in_specs=[whole, whole, pl.Block...  4.62 us
  transfers between devices with their start and end apart: 33, of which 15 were waited for; matrix products, arithmetic and copies ran while one was open for 1% of the time, Pallas kernels for 0%

profile of v1, /device:TPU:6, one launch (start us, length us, event | category | flops | bytes accessed | tf_op | source)
XLA Modules:
  0.0 220.0 jit_solution(12618858645355788486)
XLA Ops:
  0.6 1.4 copy.12.ids_ref
  2.0 0.7 copy.13.p_ref
  2.8 5.1 %dispatch.1 = bf16[128,3584]{1,0:T(8,128)(2,1)} custom-call(s32[128,1]{1,0:T(8,128)} %copy.12.ids_ref, f32[128,1]{1,0:T(8,128)} %copy.13.p_ref, bf16[128,3584]{1,0:T(8,128)(2,1)} %x_ref.1, bf16[128,3584]{1,0:T(8,128)(2,1)} %g_ref.1), custom_call_target="tpu_custom_call" | custom-call | flops 234881024 | bytes 2752512 | tf_op jit(solution)/shard_map/dispatch/pallas_call | solution.py:51
  7.9 7.2 %all-to-all-start = ((bf16[8,16,3584]{2,1,0:T(8,128)(2,1)}), bf16[8,16,3584]{2,1,0:T(8,128)(2,1)S(1)}, u32[]{:S(2)}, u32[]{:S(2)}) async-start(bf16[8,16,3584]{2,1,0:T(8,128)(2,1)} %bitcast.7), calls=%async_computation | async-start | bytes 1835008 | tf_op jit(solution)/shard_map/all_to_all | solution.py:216
  15.2 0.9 copy-done.5
  16.0 0.1 copy-done.6
  16.1 1.9 collective-permute-start.3
  18.0 1.4 collective-permute-done.3
  19.4 6.1 %collective-permute-start.8 = (bf16[224,768]{1,0:T(8,128)(2,1)S(1)}, bf16[224,768]{1,0:T(8,128)(2,1)S(1)}, u32[]{:S(2)}, u32[]{:S(2)}) collective-permute-start(bf16[224,768]{1,0:T(8,128)(2,1)S(1)} %pad_maximum_fusion.2.refs_4_), channel_id=1, source_target_pairs={{0,32},{32,64},{64,96},{96,0},{1,33},{33,65},{65,97},{97,1},{2,34}... | collective-permute-start | bytes 1032200 | tf_op jit(solution)/shard_map/ppermute | solution.py:182
  25.5 6.8 %collective-permute-start.9 = (bf16[224,768]{1,0:T(8,128)(2,1)S(1)}, bf16[224,768]{1,0:T(8,128)(2,1)S(1)}, u32[]{:S(2)}, u32[]{:S(2)}) collective-permute-start(bf16[224,768]{1,0:T(8,128)(2,1)S(1)} %pad_maximum_fusion.2.refs_4_), channel_id=1, source_target_pairs={{0,96},{32,0},{64,32},{96,64},{1,97},{33,1},{65,33},{97,65},{2,98}... | collective-permute-start | bytes 1032200 | tf_op jit(solution)/shard_map/ppermute | solution.py:182
  32.3 8.7 %all-to-all-done = bf16[8,16,3584]{2,1,0:T(8,128)(2,1)S(1)} async-done(((bf16[8,16,3584]{2,1,0:T(8,128)(2,1)}), bf16[8,16,3584]{2,1,0:T(8,128)(2,1)S(1)}, u32[]{:S(2)}, u32[]{:S(2)}) %all-to-all-start) | async-done | bytes 917536 | tf_op jit(solution)/shard_map/all_to_all | solution.py:216
  41.0 4.3 %collective-permute-start = (bf16[128,3584]{1,0:T(8,128)(2,1)S(1)}, bf16[128,3584]{1,0:T(8,128)(2,1)S(1)}, u32[]{:S(2)}, u32[]{:S(2)}) collective-permute-start(bf16[128,3584]{1,0:T(8,128)(2,1)S(1)} %bitcast.8), channel_id=1, source_target_pairs={{0,1},{1,0},{2,3},{3,2},{4,5},{5,4},{6,7},{7,6},{8,9},{9,8},{10,11... | collective-permute-start | bytes 2752520 | tf_op jit(solution)/shard_map/ppermute | solution.py:182
  45.3 2.4 %collective-permute-start.4 = (bf16[224,768]{1,0:T(8,128)(2,1)S(1)}, bf16[224,768]{1,0:T(8,128)(2,1)S(1)}, u32[]{:S(2)}, u32[]{:S(2)}) collective-permute-start(bf16[224,768]{1,0:T(8,128)(2,1)S(1)} %pad_maximum_fusion.2.refs_4_), channel_id=1, source_target_pairs={{0,128},{128,256},{256,384},{384,0},{1,129},{129,257},{257,385},{3... | collective-permute-start | bytes 1032200 | tf_op jit(solution)/shard_map/ppermute | solution.py:182
  47.7 3.4 %collective-permute-start.5 = (bf16[224,768]{1,0:T(8,128)(2,1)S(1)}, bf16[224,768]{1,0:T(8,128)(2,1)S(1)}, u32[]{:S(2)}, u32[]{:S(2)}) collective-permute-start(bf16[224,768]{1,0:T(8,128)(2,1)S(1)} %pad_maximum_fusion.2.refs_4_), channel_id=1, source_target_pairs={{0,384},{128,0},{256,128},{384,256},{1,385},{129,1},{257,129},{385... | collective-permute-start | bytes 1032200 | tf_op jit(solution)/shard_map/ppermute | solution.py:182
  51.2 6.1 %collective-permute-start.14 = (bf16[112,768]{1,0:T(8,128)(2,1)S(1)}, bf16[112,768]{1,0:T(8,128)(2,1)S(1)}, u32[]{:S(2)}, u32[]{:S(2)}) collective-permute-start(bf16[112,768]{1,0:T(8,128)(2,1)S(1)} %slice.100), channel_id=1, source_target_pairs={{0,32},{32,64},{64,96},{96,0},{1,33},{33,65},{65,97},{97,1},{2,34}... | collective-permute-start | bytes 516104 | tf_op jit(solution)/shard_map/ppermute | solution.py:182
  57.3 5.9 %collective-permute-start.15 = (bf16[112,768]{1,0:T(8,128)(2,1)S(1)}, bf16[112,768]{1,0:T(8,128)(2,1)S(1)}, u32[]{:S(2)}, u32[]{:S(2)}) collective-permute-start(bf16[112,768]{1,0:T(8,128)(2,1)S(1)} %slice.101), channel_id=1, source_target_pairs={{0,96},{32,0},{64,32},{96,64},{1,97},{33,1},{65,33},{97,65},{2,98}... | collective-permute-start | bytes 516104 | tf_op jit(solution)/shard_map/ppermute | solution.py:182
  63.3 17.8 %collective-permute-done.14 = bf16[112,768]{1,0:T(8,128)(2,1)S(1)} collective-permute-done((bf16[112,768]{1,0:T(8,128)(2,1)S(1)}, bf16[112,768]{1,0:T(8,128)(2,1)S(1)}, u32[]{:S(2)}, u32[]{:S(2)}) %collective-permute-start.14) | collective-permute-done | bytes 172064 | tf_op jit(solution)/shard_map/ppermute | solution.py:182
  81.0 2.4 %collective-permute-start.10 = (bf16[448,768]{1,0:T(8,128)(2,1)S(1)}, bf16[448,768]{1,0:T(8,128)(2,1)S(1)}, u32[]{:S(2)}, u32[]{:S(2)}) collective-permute-start(bf16[448,768]{1,0:T(8,128)(2,1)S(1)} %constant_dynamic-update-slice_fusion.refs_9_), channel_id=1, source_target_pairs={{0,128},{128,256},{256,384},{384,0},{1,129},{129,257},{257,385},{3... | collective-permute-start | bytes 2064392 | tf_op jit(solution)/shard_map/ppermute | solution.py:182
  83.4 3.5 %collective-permute-start.11 = (bf16[448,768]{1,0:T(8,128)(2,1)S(1)}, bf16[448,768]{1,0:T(8,128)(2,1)S(1)}, u32[]{:S(2)}, u32[]{:S(2)}) collective-permute-start(bf16[448,768]{1,0:T(8,128)(2,1)S(1)} %constant_dynamic-update-slice_fusion.refs_9_), channel_id=1, source_target_pairs={{0,384},{128,0},{256,128},{384,256},{1,385},{129,1},{257,129},{385... | collective-permute-start | bytes 2064392 | tf_op jit(solution)/shard_map/ppermute | solution.py:182
  86.9 3.6 %collective-permute-start.16 = (bf16[224,768]{1,0:T(8,128)(2,1)S(1)}, bf16[224,768]{1,0:T(8,128)(2,1)S(1)}, u32[]{:S(2)}, u32[]{:S(2)}) collective-permute-start(bf16[224,768]{1,0:T(8,128)(2,1)S(1)} %constant_dynamic-update-slice_fusion.2.refs_14_), channel_id=1, source_target_pairs={{0,128},{128,256},{256,384},{384,0},{1,129},{129,257},{257,385},{3... | collective-permute-start | bytes 1032200 | tf_op jit(solution)/shard_map/ppermute | solution.py:182
  90.6 1.9 collective-permute-start.1
  92.5 2.4 %collective-permute-start.2 = (bf16[128,3584]{1,0:T(8,128)(2,1)S(1)}, bf16[128,3584]{1,0:T(8,128)(2,1)S(1)}, u32[]{:S(2)}, u32[]{:S(2)}) collective-permute-start(bf16[128,3584]{1,0:T(8,128)(2,1)S(1)} %collective-permute-done.refs_1_), channel_id=1, source_target_pairs={{0,16},{16,0},{1,17},{17,1},{2,18},{18,2},{3,19},{19,3},{4,20},{20... | collective-permute-start | bytes 2752520 | tf_op jit(solution)/shard_map/ppermute | solution.py:182
  94.9 11.9 %collective-permute-done.16.refs_15_ = bf16[224,768]{1,0:T(8,128)(2,1)S(1)} collective-permute-done((bf16[224,768]{1,0:T(8,128)(2,1)S(1)}, bf16[224,768]{1,0:T(8,128)(2,1)S(1)}, u32[]{:S(2)}, u32[]{:S(2)}) %collective-permute-start.16) | collective-permute-done | bytes 344096 | tf_op jit(solution)/shard_map/ppermute | solution.py:182
  106.8 2.7 %collective-permute-start.17 = (bf16[224,768]{1,0:T(8,128)(2,1)S(1)}, bf16[224,768]{1,0:T(8,128)(2,1)S(1)}, u32[]{:S(2)}, u32[]{:S(2)}) collective-permute-start(bf16[224,768]{1,0:T(8,128)(2,1)S(1)} %constant_dynamic-update-slice_fusion.2.refs_14_), channel_id=1, source_target_pairs={{0,384},{128,0},{256,128},{384,256},{1,385},{129,1},{257,129},{385... | collective-permute-start | bytes 1032200 | tf_op jit(solution)/shard_map/ppermute | solution.py:182
  109.6 4.3 %collective-permute-start.6 = (bf16[112,768]{1,0:T(8,128)(2,1)S(1)}, bf16[112,768]{1,0:T(8,128)(2,1)S(1)}, u32[]{:S(2)}, u32[]{:S(2)}) collective-permute-start(bf16[112,768]{1,0:T(8,128)(2,1)S(1)} %slice.96), channel_id=1, source_target_pairs={{0,128},{128,256},{256,384},{384,0},{1,129},{129,257},{257,385},{3... | collective-permute-start | bytes 516104 | tf_op jit(solution)/shard_map/ppermute | solution.py:182
  113.9 1.9 collective-permute-start.7
  116.0 0.9 collective-permute-done.6.refs_7_
  116.9 5.5 %collective-permute-start.18 = (bf16[112,768]{1,0:T(8,128)(2,1)S(1)}, bf16[112,768]{1,0:T(8,128)(2,1)S(1)}, u32[]{:S(2)}, u32[]{:S(2)}) collective-permute-start(bf16[112,768]{1,0:T(8,128)(2,1)S(1)} %slice.102), channel_id=1, source_target_pairs={{0,128},{128,256},{256,384},{384,0},{1,129},{129,257},{257,385},{3... | collective-permute-start | bytes 516104 | tf_op jit(solution)/shard_map/ppermute | solution.py:182
  122.5 1.9 collective-permute-start.12
  124.4 3.9 %collective-permute-start.13 = (bf16[224,768]{1,0:T(8,128)(2,1)S(1)}, bf16[224,768]{1,0:T(8,128)(2,1)S(1)}, u32[]{:S(2)}, u32[]{:S(2)}) collective-permute-start(bf16[224,768]{1,0:T(8,128)(2,1)S(1)} %slice.99), channel_id=1, source_target_pairs={{0,384},{128,0},{256,128},{384,256},{1,385},{129,1},{257,129},{385... | collective-permute-start | bytes 1032200 | tf_op jit(solution)/shard_map/ppermute | solution.py:182
  128.3 1.9 collective-permute-start.19
  130.3 8.6 %collective-permute-done.19.refs_18_ = bf16[112,768]{1,0:T(8,128)(2,1)S(1)} collective-permute-done((bf16[112,768]{1,0:T(8,128)(2,1)S(1)}, bf16[112,768]{1,0:T(8,128)(2,1)S(1)}, u32[]{:S(2)}, u32[]{:S(2)}) %collective-permute-start.19) | collective-permute-done | bytes 172064 | tf_op jit(solution)/shard_map/ppermute | solution.py:182
  138.9 0.9 copy-done.10
  139.8 0.9 copy-done.11
  140.7 13.0 %experts.1 = (bf16[128,3584]{1,0:T(8,128)(2,1)}, bf16[128,3584]{1,0:T(8,128)(2,1)}, bf16[896,256]{1,0:T(8,128)(2,1)S(1)}, bf16[896,256]{1,0:T(8,128)(2,1)S(1)}, ...) custom-call(bf16[128,3584]{1,0:T(8,128)(2,1)} %bitcast.10, bf16[128,3584]{1,0:T(8,128)(2,1)} %copy-done.9, ...), custom_call_target="tpu_custom_call" | custom-call | flops 6000000000 | bytes 14000000 | tf_op jit(solution)/shard_map/experts/pallas_call | solution.py:163
  153.8 1.9 collective-permute-start.22
  155.7 1.9 collective-permute-start.20
  157.7 3.9 %collective-permute-start.24 = (bf16[448,256]{1,0:T(8,128)(2,1)S(1)}, bf16[448,256]{1,0:T(8,128)(2,1)S(1)}, u32[]{:S(2)}, u32[]{:S(2)}) collective-permute-start(bf16[448,256]{1,0:T(8,128)(2,1)S(1)} %get-tuple-element.29), channel_id=1, source_target_pairs={{0,384},{128,0},{256,128},{384,256},{1,385},{129,1},{257,129},{385... | collective-permute-start | bytes 688136 | tf_op jit(solution)/shard_map/ppermute | solution.py:182
  161.7 0.1 add_convert_fusion.4
  161.8 3.3 %collective-permute-start.23 = (bf16[896,256]{1,0:T(8,128)(2,1)S(1)}, bf16[896,256]{1,0:T(8,128)(2,1)S(1)}, u32[]{:S(2)}, u32[]{:S(2)}) collective-permute-start(bf16[896,256]{1,0:T(8,128)(2,1)S(1)} %pad_maximum_fusion), channel_id=1, source_target_pairs={{0,128},{128,256},{256,384},{384,0},{1,129},{129,257},{257,385},{3... | collective-permute-start | bytes 1376264 | tf_op jit(solution)/shard_map/ppermute | solution.py:182
  165.0 3.7 %collective-permute-done.24 = bf16[448,256]{1,0:T(8,128)(2,1)S(1)} collective-permute-done((bf16[448,256]{1,0:T(8,128)(2,1)S(1)}, bf16[448,256]{1,0:T(8,128)(2,1)S(1)}, u32[]{:S(2)}, u32[]{:S(2)}) %collective-permute-start.24) | collective-permute-done | bytes 229408 | tf_op jit(solution)/shard_map/ppermute | solution.py:182
  168.8 0.1 add_convert_fusion.3
  168.9 2.7 %collective-permute-start.25 = (bf16[896,256]{1,0:T(8,128)(2,1)S(1)}, bf16[896,256]{1,0:T(8,128)(2,1)S(1)}, u32[]{:S(2)}, u32[]{:S(2)}) collective-permute-start(bf16[896,256]{1,0:T(8,128)(2,1)S(1)} %pad_maximum_fusion.1), channel_id=1, source_target_pairs={{0,384},{128,0},{256,128},{384,256},{1,385},{129,1},{257,129},{385... | collective-permute-start | bytes 1376264 | tf_op jit(solution)/shard_map/ppermute | solution.py:182
  171.6 0.9 add_convert_fusion.2
  172.5 1.9 collective-permute-start.21
  174.4 2.0 collective-permute-done.23
  176.4 7.7 %collective-permute-done.25 = bf16[896,256]{1,0:T(8,128)(2,1)S(1)} collective-permute-done((bf16[896,256]{1,0:T(8,128)(2,1)S(1)}, bf16[896,256]{1,0:T(8,128)(2,1)S(1)}, u32[]{:S(2)}, u32[]{:S(2)}) %collective-permute-start.25) | collective-permute-done | bytes 458784 | tf_op jit(solution)/shard_map/ppermute | solution.py:182
  184.1 0.2 add_convert_fusion
  184.3 1.9 collective-permute-start.26
  186.3 6.0 %collective-permute-start.28 = (bf16[112,256]{1,0:T(8,128)(2,1)S(1)}, bf16[112,256]{1,0:T(8,128)(2,1)S(1)}, u32[]{:S(2)}, u32[]{:S(2)}) collective-permute-start(bf16[112,256]{1,0:T(8,128)(2,1)S(1)} %get-tuple-element.26), channel_id=1, source_target_pairs={{0,96},{32,0},{64,32},{96,64},{1,97},{33,1},{65,33},{97,65},{2,98}... | collective-permute-start | bytes 172040 | tf_op jit(solution)/shard_map/ppermute | solution.py:182
  192.3 0.2 collective-permute-done.26
  192.5 1.6 collective-permute-done.28
  194.1 0.9 fusion
  195.1 3.5 %all-to-all-start.1 = ((bf16[8,8,3584]{2,1,0:T(8,128)(2,1)}), bf16[8,8,3584]{2,1,0:T(8,128)(2,1)S(1)}, u32[]{:S(2)}, u32[]{:S(2)}) async-start(bf16[8,8,3584]{2,1,0:T(8,128)(2,1)} %fusion), calls=%async_computation.1 | async-start | bytes 917504 | tf_op jit(solution)/shard_map/all_to_all | solution.py:245
  198.6 2.7 %collective-permute-start.27 = (bf16[224,256]{1,0:T(8,128)(2,1)S(1)}, bf16[224,256]{1,0:T(8,128)(2,1)S(1)}, u32[]{:S(2)}, u32[]{:S(2)}) collective-permute-start(bf16[224,256]{1,0:T(8,128)(2,1)S(1)} %pad_maximum_fusion.4), channel_id=1, source_target_pairs={{0,32},{32,64},{64,96},{96,0},{1,33},{33,65},{65,97},{97,1},{2,34}... | collective-permute-start | bytes 344072 | tf_op jit(solution)/shard_map/ppermute | solution.py:182
  201.3 5.6 %collective-permute-start.29 = (bf16[224,256]{1,0:T(8,128)(2,1)S(1)}, bf16[224,256]{1,0:T(8,128)(2,1)S(1)}, u32[]{:S(2)}, u32[]{:S(2)}) collective-permute-start(bf16[224,256]{1,0:T(8,128)(2,1)S(1)} %pad_maximum_fusion.5), channel_id=1, source_target_pairs={{0,96},{32,0},{64,32},{96,64},{1,97},{33,1},{65,33},{97,65},{2,98}... | collective-permute-start | bytes 344072 | tf_op jit(solution)/shard_map/ppermute | solution.py:182
  206.9 0.8 collective-permute-done.27
  207.7 1.5 collective-permute-done.29
  209.3 1.9 collective-permute-start.30
  211.3 1.2 collective-permute-done.30
  212.5 0.7 maximum_select_fusion
  213.1 0.8 copy-done
  213.9 4.6 %finish.1 = (bf16[128,3584]{1,0:T(8,128)(2,1)}, f32[128,1]{1,0:T(8,128)}) custom-call(s32[128,1]{1,0:T(8,128)} %copy.12.ids_ref, f32[128,1]{1,0:T(8,128)} %copy.13.p_ref, bf16[64,3584]{1,0:T(8,128)(2,1)} %bitcast.5, bf16[64,3584]{1,0:T(8,128)(2,1)} %bitcast.6), custom_call_target="tpu_custom_call" | custom-call | flops 58720256 | bytes 1835008 | tf_op jit(solution)/shard_map/finish/pallas_call | solution.py:82
  218.5 1.4 copy.14
  (65 shorter events, 0.7 us)
Async XLA Ops:
  0.6 1.4 copy-start.8
  7.9 7.2 %copy-start.7 = (bf16[112,512]{1,0:T(8,128)(2,1)S(1)}, bf16[112,512]{1,0:T(8,128)(2,1)}, u32[]{:S(2)}) copy-start(bf16[112,512]{1,0:T(8,128)(2,1)} %param.11) | copy-start | bytes 344068
  7.9 33.2 %all-to-all-start = ((bf16[8,16,3584]{2,1,0:T(8,128)(2,1)}), bf16[8,16,3584]{2,1,0:T(8,128)(2,1)S(1)}, u32[]{:S(2)}, u32[]{:S(2)}) async-start(bf16[8,16,3584]{2,1,0:T(8,128)(2,1)} %bitcast.7), calls=%async_computation | async-start | bytes 1835008 | tf_op jit(solution)/shard_map/all_to_all | solution.py:216
  15.1 0.9 copy-start.5
  15.1 0.9 copy-start.6
  16.1 3.3 %collective-permute-start.3 = (bf16[112,768]{1,0:T(8,128)(2,1)S(1)}, bf16[112,768]{1,0:T(8,128)(2,1)S(1)}, u32[]{:S(2)}, u32[]{:S(2)}) collective-permute-start(bf16[112,768]{1,0:T(8,128)(2,1)S(1)} %pad_maximum_fusion.3), channel_id=1, source_target_pairs={{0,16},{16,0},{1,17},{17,1},{2,18},{18,2},{3,19},{19,3},{4,20},{20... | collective-permute-start | bytes 516104 | tf_op jit(solution)/shard_map/ppermute | solution.py:182
  19.4 31.7 %collective-permute-start.8 = (bf16[224,768]{1,0:T(8,128)(2,1)S(1)}, bf16[224,768]{1,0:T(8,128)(2,1)S(1)}, u32[]{:S(2)}, u32[]{:S(2)}) collective-permute-start(bf16[224,768]{1,0:T(8,128)(2,1)S(1)} %pad_maximum_fusion.2.refs_4_), channel_id=1, source_target_pairs={{0,32},{32,64},{64,96},{96,0},{1,33},{33,65},{65,97},{97,1},{2,34}... | collective-permute-start | bytes 1032200 | tf_op jit(solution)/shard_map/ppermute | solution.py:182
  25.5 31.8 %collective-permute-start.9 = (bf16[224,768]{1,0:T(8,128)(2,1)S(1)}, bf16[224,768]{1,0:T(8,128)(2,1)S(1)}, u32[]{:S(2)}, u32[]{:S(2)}) collective-permute-start(bf16[224,768]{1,0:T(8,128)(2,1)S(1)} %pad_maximum_fusion.2.refs_4_), channel_id=1, source_target_pairs={{0,96},{32,0},{64,32},{96,64},{1,97},{33,1},{65,33},{97,65},{2,98}... | collective-permute-start | bytes 1032200 | tf_op jit(solution)/shard_map/ppermute | solution.py:182
  41.0 49.5 %copy-start.1 = (bf16[8,16,3584]{2,1,0:T(8,128)(2,1)}, bf16[8,16,3584]{2,1,0:T(8,128)(2,1)S(1)}, u32[]{:S(2)}) copy-start(bf16[8,16,3584]{2,1,0:T(8,128)(2,1)S(1)} %all-to-all-done) | copy-start | bytes 2752516
  41.0 51.5 %collective-permute-start = (bf16[128,3584]{1,0:T(8,128)(2,1)S(1)}, bf16[128,3584]{1,0:T(8,128)(2,1)S(1)}, u32[]{:S(2)}, u32[]{:S(2)}) collective-permute-start(bf16[128,3584]{1,0:T(8,128)(2,1)S(1)} %bitcast.8), channel_id=1, source_target_pairs={{0,1},{1,0},{2,3},{3,2},{4,5},{5,4},{6,7},{7,6},{8,9},{9,8},{10,11... | collective-permute-start | bytes 2752520 | tf_op jit(solution)/shard_map/ppermute | solution.py:182
  45.3 41.6 %collective-permute-start.4 = (bf16[224,768]{1,0:T(8,128)(2,1)S(1)}, bf16[224,768]{1,0:T(8,128)(2,1)S(1)}, u32[]{:S(2)}, u32[]{:S(2)}) collective-permute-start(bf16[224,768]{1,0:T(8,128)(2,1)S(1)} %pad_maximum_fusion.2.refs_4_), channel_id=1, source_target_pairs={{0,128},{128,256},{256,384},{384,0},{1,129},{129,257},{257,385},{3... | collective-permute-start | bytes 1032200 | tf_op jit(solution)/shard_map/ppermute | solution.py:182
  47.7 42.8 %collective-permute-start.5 = (bf16[224,768]{1,0:T(8,128)(2,1)S(1)}, bf16[224,768]{1,0:T(8,128)(2,1)S(1)}, u32[]{:S(2)}, u32[]{:S(2)}) collective-permute-start(bf16[224,768]{1,0:T(8,128)(2,1)S(1)} %pad_maximum_fusion.2.refs_4_), channel_id=1, source_target_pairs={{0,384},{128,0},{256,128},{384,256},{1,385},{129,1},{257,129},{385... | collective-permute-start | bytes 1032200 | tf_op jit(solution)/shard_map/ppermute | solution.py:182
  51.2 29.8 %collective-permute-start.14 = (bf16[112,768]{1,0:T(8,128)(2,1)S(1)}, bf16[112,768]{1,0:T(8,128)(2,1)S(1)}, u32[]{:S(2)}, u32[]{:S(2)}) collective-permute-start(bf16[112,768]{1,0:T(8,128)(2,1)S(1)} %slice.100), channel_id=1, source_target_pairs={{0,32},{32,64},{64,96},{96,0},{1,33},{33,65},{65,97},{97,1},{2,34}... | collective-permute-start | bytes 516104 | tf_op jit(solution)/shard_map/ppermute | solution.py:182
  57.3 26.1 %collective-permute-start.15 = (bf16[112,768]{1,0:T(8,128)(2,1)S(1)}, bf16[112,768]{1,0:T(8,128)(2,1)S(1)}, u32[]{:S(2)}, u32[]{:S(2)}) collective-permute-start(bf16[112,768]{1,0:T(8,128)(2,1)S(1)} %slice.101), channel_id=1, source_target_pairs={{0,96},{32,0},{64,32},{96,64},{1,97},{33,1},{65,33},{97,65},{2,98}... | collective-permute-start | bytes 516104 | tf_op jit(solution)/shard_map/ppermute | solution.py:182
  81.0 28.5 %collective-permute-start.10 = (bf16[448,768]{1,0:T(8,128)(2,1)S(1)}, bf16[448,768]{1,0:T(8,128)(2,1)S(1)}, u32[]{:S(2)}, u32[]{:S(2)}) collective-permute-start(bf16[448,768]{1,0:T(8,128)(2,1)S(1)} %constant_dynamic-update-slice_fusion.refs_9_), channel_id=1, source_target_pairs={{0,128},{128,256},{256,384},{384,0},{1,129},{129,257},{257,385},{3... | collective-permute-start | bytes 2064392 | tf_op jit(solution)/shard_map/ppermute | solution.py:182
  83.4 30.5 %collective-permute-start.11 = (bf16[448,768]{1,0:T(8,128)(2,1)S(1)}, bf16[448,768]{1,0:T(8,128)(2,1)S(1)}, u32[]{:S(2)}, u32[]{:S(2)}) collective-permute-start(bf16[448,768]{1,0:T(8,128)(2,1)S(1)} %constant_dynamic-update-slice_fusion.refs_9_), channel_id=1, source_target_pairs={{0,384},{128,0},{256,128},{384,256},{1,385},{129,1},{257,129},{385... | collective-permute-start | bytes 2064392 | tf_op jit(solution)/shard_map/ppermute | solution.py:182
  86.9 19.9 %collective-permute-start.16 = (bf16[224,768]{1,0:T(8,128)(2,1)S(1)}, bf16[224,768]{1,0:T(8,128)(2,1)S(1)}, u32[]{:S(2)}, u32[]{:S(2)}) collective-permute-start(bf16[224,768]{1,0:T(8,128)(2,1)S(1)} %constant_dynamic-update-slice_fusion.2.refs_14_), channel_id=1, source_target_pairs={{0,128},{128,256},{256,384},{384,0},{1,129},{129,257},{257,385},{3... | collective-permute-start | bytes 1032200 | tf_op jit(solution)/shard_map/ppermute | solution.py:182
  90.6 48.3 %collective-permute-start.1 = (bf16[128,3584]{1,0:T(8,128)(2,1)S(1)}, bf16[128,3584]{1,0:T(8,128)(2,1)S(1)}, u32[]{:S(2)}, u32[]{:S(2)}) collective-permute-start(bf16[128,3584]{1,0:T(8,128)(2,1)S(1)} %bitcast.9), channel_id=1, source_target_pairs={{0,16},{16,0},{1,17},{17,1},{2,18},{18,2},{3,19},{19,3},{4,20},{20... | collective-permute-start | bytes 2752520 | tf_op jit(solution)/shard_map/ppermute | solution.py:182
  92.5 23.5 %copy-start.9 = (bf16[128,3584]{1,0:T(8,128)(2,1)}, bf16[128,3584]{1,0:T(8,128)(2,1)S(1)}, u32[]{:S(2)}) copy-start(bf16[128,3584]{1,0:T(8,128)(2,1)S(1)} %collective-permute-done.refs_1_) | copy-start | bytes 2752516
  92.5 46.4 %collective-permute-start.2 = (bf16[128,3584]{1,0:T(8,128)(2,1)S(1)}, bf16[128,3584]{1,0:T(8,128)(2,1)S(1)}, u32[]{:S(2)}, u32[]{:S(2)}) collective-permute-start(bf16[128,3584]{1,0:T(8,128)(2,1)S(1)} %collective-permute-done.refs_1_), channel_id=1, source_target_pairs={{0,16},{16,0},{1,17},{17,1},{2,18},{18,2},{3,19},{19,3},{4,20},{20... | collective-permute-start | bytes 2752520 | tf_op jit(solution)/shard_map/ppermute | solution.py:182
  106.8 17.6 %collective-permute-start.17 = (bf16[224,768]{1,0:T(8,128)(2,1)S(1)}, bf16[224,768]{1,0:T(8,128)(2,1)S(1)}, u32[]{:S(2)}, u32[]{:S(2)}) collective-permute-start(bf16[224,768]{1,0:T(8,128)(2,1)S(1)} %constant_dynamic-update-slice_fusion.2.refs_14_), channel_id=1, source_target_pairs={{0,384},{128,0},{256,128},{384,256},{1,385},{129,1},{257,129},{385... | collective-permute-start | bytes 1032200 | tf_op jit(solution)/shard_map/ppermute | solution.py:182
  109.6 6.4 %copy-start.3 = (bf16[448,768]{1,0:T(8,128)(2,1)}, bf16[448,768]{1,0:T(8,128)(2,1)S(1)}, u32[]{:S(2)}) copy-start(bf16[448,768]{1,0:T(8,128)(2,1)S(1)} %collective-permute-done.10.refs_10_) | copy-start | bytes 2064388
  109.6 7.3 %collective-permute-start.6 = (bf16[112,768]{1,0:T(8,128)(2,1)S(1)}, bf16[112,768]{1,0:T(8,128)(2,1)S(1)}, u32[]{:S(2)}, u32[]{:S(2)}) collective-permute-start(bf16[112,768]{1,0:T(8,128)(2,1)S(1)} %slice.96), channel_id=1, source_target_pairs={{0,128},{128,256},{256,384},{384,0},{1,129},{129,257},{257,385},{3... | collective-permute-start | bytes 516104 | tf_op jit(solution)/shard_map/ppermute | solution.py:182
  113.9 2.0 copy-start.4
  113.9 8.5 %collective-permute-start.7 = (bf16[112,768]{1,0:T(8,128)(2,1)S(1)}, bf16[112,768]{1,0:T(8,128)(2,1)S(1)}, u32[]{:S(2)}, u32[]{:S(2)}) collective-permute-start(bf16[112,768]{1,0:T(8,128)(2,1)S(1)} %slice.97), channel_id=1, source_target_pairs={{0,384},{128,0},{256,128},{384,256},{1,385},{129,1},{257,129},{385... | collective-permute-start | bytes 516104 | tf_op jit(solution)/shard_map/ppermute | solution.py:182
  116.9 11.4 %collective-permute-start.18 = (bf16[112,768]{1,0:T(8,128)(2,1)S(1)}, bf16[112,768]{1,0:T(8,128)(2,1)S(1)}, u32[]{:S(2)}, u32[]{:S(2)}) collective-permute-start(bf16[112,768]{1,0:T(8,128)(2,1)S(1)} %slice.102), channel_id=1, source_target_pairs={{0,128},{128,256},{256,384},{384,0},{1,129},{129,257},{257,385},{3... | collective-permute-start | bytes 516104 | tf_op jit(solution)/shard_map/ppermute | solution.py:182
  122.5 16.4 %collective-permute-start.12 = (bf16[224,768]{1,0:T(8,128)(2,1)S(1)}, bf16[224,768]{1,0:T(8,128)(2,1)S(1)}, u32[]{:S(2)}, u32[]{:S(2)}) collective-permute-start(bf16[224,768]{1,0:T(8,128)(2,1)S(1)} %slice.98), channel_id=1, source_target_pairs={{0,128},{128,256},{256,384},{384,0},{1,129},{129,257},{257,385},{3... | collective-permute-start | bytes 1032200 | tf_op jit(solution)/shard_map/ppermute | solution.py:182
  124.4 14.5 %collective-permute-start.13 = (bf16[224,768]{1,0:T(8,128)(2,1)S(1)}, bf16[224,768]{1,0:T(8,128)(2,1)S(1)}, u32[]{:S(2)}, u32[]{:S(2)}) collective-permute-start(bf16[224,768]{1,0:T(8,128)(2,1)S(1)} %slice.99), channel_id=1, source_target_pairs={{0,384},{128,0},{256,128},{384,256},{1,385},{129,1},{257,129},{385... | collective-permute-start | bytes 1032200 | tf_op jit(solution)/shard_map/ppermute | solution.py:182
  128.3 10.5 %collective-permute-start.19 = (bf16[112,768]{1,0:T(8,128)(2,1)S(1)}, bf16[112,768]{1,0:T(8,128)(2,1)S(1)}, u32[]{:S(2)}, u32[]{:S(2)}) collective-permute-start(bf16[112,768]{1,0:T(8,128)(2,1)S(1)} %slice.103), channel_id=1, source_target_pairs={{0,384},{128,0},{256,128},{384,256},{1,385},{129,1},{257,129},{385... | collective-permute-start | bytes 516104 | tf_op jit(solution)/shard_map/ppermute | solution.py:182
  138.9 0.9 copy-start.10
  139.8 0.9 copy-start.11
  153.8 7.9 %collective-permute-start.22 = (bf16[448,256]{1,0:T(8,128)(2,1)S(1)}, bf16[448,256]{1,0:T(8,128)(2,1)S(1)}, u32[]{:S(2)}, u32[]{:S(2)}) collective-permute-start(bf16[448,256]{1,0:T(8,128)(2,1)S(1)} %get-tuple-element.28), channel_id=1, source_target_pairs={{0,128},{128,256},{256,384},{384,0},{1,129},{129,257},{257,385},{3... | collective-permute-start | bytes 688136 | tf_op jit(solution)/shard_map/ppermute | solution.py:182
  155.7 15.9 %collective-permute-start.20 = (bf16[128,3584]{1,0:T(8,128)(2,1)}, bf16[128,3584]{1,0:T(8,128)(2,1)S(1)}, u32[]{:S(2)}, u32[]{:S(2)}) collective-permute-start(bf16[128,3584]{1,0:T(8,128)(2,1)} %get-tuple-element.12), channel_id=1, source_target_pairs={{0,16},{16,0},{1,17},{17,1},{2,18},{18,2},{3,19},{19,3},{4,20},{20... | collective-permute-start | bytes 2752520 | tf_op jit(solution)/shard_map/ppermute | solution.py:182
  157.7 11.1 %collective-permute-start.24 = (bf16[448,256]{1,0:T(8,128)(2,1)S(1)}, bf16[448,256]{1,0:T(8,128)(2,1)S(1)}, u32[]{:S(2)}, u32[]{:S(2)}) collective-permute-start(bf16[448,256]{1,0:T(8,128)(2,1)S(1)} %get-tuple-element.29), channel_id=1, source_target_pairs={{0,384},{128,0},{256,128},{384,256},{1,385},{129,1},{257,129},{385... | collective-permute-start | bytes 688136 | tf_op jit(solution)/shard_map/ppermute | solution.py:182
  161.8 9.8 %copy-start.2 = (bf16[128,3584]{1,0:T(8,128)(2,1)S(1)}, bf16[128,3584]{1,0:T(8,128)(2,1)}, u32[]{:S(2)}) copy-start(bf16[128,3584]{1,0:T(8,128)(2,1)} %get-tuple-element.11) | copy-start | bytes 2752516
  161.8 14.6 %collective-permute-start.23 = (bf16[896,256]{1,0:T(8,128)(2,1)S(1)}, bf16[896,256]{1,0:T(8,128)(2,1)S(1)}, u32[]{:S(2)}, u32[]{:S(2)}) collective-permute-start(bf16[896,256]{1,0:T(8,128)(2,1)S(1)} %pad_maximum_fusion), channel_id=1, source_target_pairs={{0,128},{128,256},{256,384},{384,0},{1,129},{129,257},{257,385},{3... | collective-permute-start | bytes 1376264 | tf_op jit(solution)/shard_map/ppermute | solution.py:182
  168.9 15.2 %collective-permute-start.25 = (bf16[896,256]{1,0:T(8,128)(2,1)S(1)}, bf16[896,256]{1,0:T(8,128)(2,1)S(1)}, u32[]{:S(2)}, u32[]{:S(2)}) collective-permute-start(bf16[896,256]{1,0:T(8,128)(2,1)S(1)} %pad_maximum_fusion.1), channel_id=1, source_target_pairs={{0,384},{128,0},{256,128},{384,256},{1,385},{129,1},{257,129},{385... | collective-permute-start | bytes 1376264 | tf_op jit(solution)/shard_map/ppermute | solution.py:182
  172.5 21.7 %collective-permute-start.21 = (bf16[64,3584]{1,0:T(8,128)(2,1)}, bf16[64,3584]{1,0:T(8,128)(2,1)S(1)}, u32[]{:S(2)}, u32[]{:S(2)}) collective-permute-start(bf16[64,3584]{1,0:T(8,128)(2,1)} %add_convert_fusion.2), channel_id=1, source_target_pairs={{0,1},{1,0},{2,3},{3,2},{4,5},{5,4},{6,7},{7,6},{8,9},{9,8},{10,11... | collective-permute-start | bytes 1376264 | tf_op jit(solution)/shard_map/ppermute | solution.py:182
  184.3 8.2 %collective-permute-start.26 = (bf16[112,256]{1,0:T(8,128)(2,1)S(1)}, bf16[112,256]{1,0:T(8,128)(2,1)S(1)}, u32[]{:S(2)}, u32[]{:S(2)}) collective-permute-start(bf16[112,256]{1,0:T(8,128)(2,1)S(1)} %get-tuple-element.24), channel_id=1, source_target_pairs={{0,32},{32,64},{64,96},{96,0},{1,33},{33,65},{65,97},{97,1},{2,34}... | collective-permute-start | bytes 172040 | tf_op jit(solution)/shard_map/ppermute | solution.py:182
  186.3 7.8 %collective-permute-start.28 = (bf16[112,256]{1,0:T(8,128)(2,1)S(1)}, bf16[112,256]{1,0:T(8,128)(2,1)S(1)}, u32[]{:S(2)}, u32[]{:S(2)}) collective-permute-start(bf16[112,256]{1,0:T(8,128)(2,1)S(1)} %get-tuple-element.26), channel_id=1, source_target_pairs={{0,96},{32,0},{64,32},{96,64},{1,97},{33,1},{65,33},{97,65},{2,98}... | collective-permute-start | bytes 172040 | tf_op jit(solution)/shard_map/ppermute | solution.py:182
  195.1 18.1 %all-to-all-start.1 = ((bf16[8,8,3584]{2,1,0:T(8,128)(2,1)}), bf16[8,8,3584]{2,1,0:T(8,128)(2,1)S(1)}, u32[]{:S(2)}, u32[]{:S(2)}) async-start(bf16[8,8,3584]{2,1,0:T(8,128)(2,1)} %fusion), calls=%async_computation.1 | async-start | bytes 917504 | tf_op jit(solution)/shard_map/all_to_all | solution.py:245
  198.6 9.1 %collective-permute-start.27 = (bf16[224,256]{1,0:T(8,128)(2,1)S(1)}, bf16[224,256]{1,0:T(8,128)(2,1)S(1)}, u32[]{:S(2)}, u32[]{:S(2)}) collective-permute-start(bf16[224,256]{1,0:T(8,128)(2,1)S(1)} %pad_maximum_fusion.4), channel_id=1, source_target_pairs={{0,32},{32,64},{64,96},{96,0},{1,33},{33,65},{65,97},{97,1},{2,34}... | collective-permute-start | bytes 344072 | tf_op jit(solution)/shard_map/ppermute | solution.py:182
  201.3 8.0 %collective-permute-start.29 = (bf16[224,256]{1,0:T(8,128)(2,1)S(1)}, bf16[224,256]{1,0:T(8,128)(2,1)S(1)}, u32[]{:S(2)}, u32[]{:S(2)}) collective-permute-start(bf16[224,256]{1,0:T(8,128)(2,1)S(1)} %pad_maximum_fusion.5), channel_id=1, source_target_pairs={{0,96},{32,0},{64,32},{96,64},{1,97},{33,1},{65,33},{97,65},{2,98}... | collective-permute-start | bytes 344072 | tf_op jit(solution)/shard_map/ppermute | solution.py:182
  209.3 3.1 %collective-permute-start.30 = (bf16[112,256]{1,0:T(8,128)(2,1)S(1)}, bf16[112,256]{1,0:T(8,128)(2,1)S(1)}, u32[]{:S(2)}, u32[]{:S(2)}) collective-permute-start(bf16[112,256]{1,0:T(8,128)(2,1)S(1)} %get-tuple-element.31), channel_id=1, source_target_pairs={{0,16},{16,0},{1,17},{17,1},{2,18},{18,2},{3,19},{19,3},{4,20},{20... | collective-permute-start | bytes 172040 | tf_op jit(solution)/shard_map/ppermute | solution.py:182
  213.1 0.8 copy-start

commit v2 on v1

--- a/solution.py
+++ b/solution.py
@@ -19,6 +19,7 @@
 SLOTS = 16
 ROWS = EXPERTS * SLOTS
 BACK = EXPERTS * 8
+VMEM_LIMIT = 28 * 1024 * 1024
 
 
 def expert_rank(ids):
@@ -90,9 +91,26 @@
         ],
         out_specs=[pl.BlockSpec((TOK, chunk), lambda i: (0, i)), whole],
         out_shape=[jax.ShapeDtypeStruct((TOK, D), BF), jax.ShapeDtypeStruct((TOK, 1), F32)],
-        cost_estimate=pl.CostEstimate(flops=2 * TOK * BACK * D, bytes_accessed=4 * TOK * D, transcendentals=0),
+        cost_estimate=pl.CostEstimate(flops=10**7, bytes_accessed=10**4, transcendentals=0),
         name="finish",
     )(ids, weight, rows, rows)
+
+
+def weight_copies(weight_refs, pieces, weights, sems, width):
+    xi, zi, ci = lax.axis_index("x"), lax.axis_index("zh"), lax.axis_index("c")
+    copies = []
+    for ref, listed in zip(weight_refs, pieces):
+        for at, (dx, dz, which) in enumerate(listed):
+            x = lax.rem(xi + jnp.where(ci == 0, dx, 4 - dx), 4)
+            z = lax.rem(zi + jnp.where(ci == 0, dz, 4 - dz), 4)
+            core = ci if which == 0 else 1 - ci
+            start = pl.multiple_of((x * 4 + z) * BLOCK + core * SHARD, 16)
+            copies.append(pltpu.make_async_copy(
+                ref.at[pl.ds(at * SHARD, SHARD), pl.ds(0, width)],
+                weights.at[pl.ds(start, SHARD), pl.ds(0, width)],
+                sems.at[len(copies)],
+            ))
+    return copies
 
 
 def expert_kernel(pieces, *refs):
@@ -100,20 +118,11 @@
     weight_refs = refs[4:4 + len(pieces)]
     keep_ref, send_ref, far_ref, plus_ref, minus_ref, own_ref = refs[4 + len(pieces):10 + len(pieces)]
     rows, weights, sem_rows, sem_weights = refs[10 + len(pieces):]
-    xi, zi, ci = lax.axis_index("x"), lax.axis_index("zh"), lax.axis_index("c")
-    copies = []
-    for i, ref in enumerate(row_refs):
-        copies.append(pltpu.make_async_copy(ref, rows.at[pl.ds(i * ROWS, ROWS)], sem_rows.at[i]))
-    count = 0
-    for ref, listed in zip(weight_refs, pieces):
-        for at, (dx, dz, which) in enumerate(listed):
-            block = lax.rem(xi + dx, 4) * 4 + lax.rem(zi + dz, 4)
-            core = ci if which == 0 else 1 - ci
-            start = pl.multiple_of(block * BLOCK + core * SHARD, 16)
-            copies.append(pltpu.make_async_copy(
-                ref.at[pl.ds(at * SHARD, SHARD)], weights.at[pl.ds(start, SHARD)], sem_weights.at[count]
-            ))
-            count += 1
+    xi, ci = lax.axis_index("x"), lax.axis_index("c")
+    copies = [
+        pltpu.make_async_copy(ref, rows.at[pl.ds(i * ROWS, ROWS)], sem_rows.at[i]) for i, ref in enumerate(row_refs)
+    ]
+    copies += weight_copies(weight_refs, pieces, weights, sem_weights, 3 * QUART)
     for copy in copies:
         copy.start()
     for copy in copies:
@@ -132,7 +141,8 @@
     spread = jnp.concatenate([jnp.zeros((4 * EXPERTS, 8, QUART), F32), hidden.reshape(4 * EXPERTS, 8, QUART)], axis=1)
     spread = spread.reshape(4 * ROWS, QUART).astype(BF)
     for ref, shift in ((far_ref, 2), (plus_ref, 1), (minus_ref, 3), (own_ref, 0)):
-        start = pl.multiple_of(lax.rem(xi + shift, 4) * XROWS, 128)
+        around = jnp.where(ci == 0, shift, 4 - shift)
+        start = pl.multiple_of(lax.rem(xi + around, 4) * XROWS, 128)
         ref[...] = lax.dot_general(
             rows[:, pl.ds(start, XROWS)], spread, (((0,), (0,)), ((), ())), preferred_element_type=F32
         ).astype(BF)
@@ -171,7 +181,7 @@
             pltpu.SemaphoreType.DMA((4,)),
             pltpu.SemaphoreType.DMA((count,)),
         ],
-        compiler_params=pltpu.CompilerParams(vmem_limit_bytes=48 * 1024 * 1024),
+        compiler_params=pltpu.CompilerParams(vmem_limit_bytes=VMEM_LIMIT),
         cost_estimate=pl.CostEstimate(flops=6 * 10**9, bytes_accessed=14 * 10**6, transcendentals=65536),
         name="experts",
     )(*rows, *blocks)
@@ -182,24 +192,29 @@
     return lax.ppermute(a, axis, [(i, (i + shift) % n) for i in range(n)])
 
 
-def both_ways(a, axis):
-    return hop(a, axis, 1), hop(a, axis, -1)
+def turn(a, axis, shift):
+    n = lax.axis_size(axis)
+    pairs = []
+    for i in range(n):
+        pairs.append((2 * i, 2 * ((i + shift) % n)))
+        pairs.append((2 * i + 1, 2 * ((i - shift) % n) + 1))
+    return lax.ppermute(a, (axis, "c"), pairs)
 
 
 def ring_gather(a, axis):
-    n = a.shape[0] // 2
-    before, after = both_ways(a, axis)
-    return before, after, hop(before[:n], axis, 1), hop(after[n:], axis, -1)
+    before, after = turn(a, axis, 1), turn(a, axis, -1)
+    return before, after, turn(before, axis, 1)
 
 
 def ring_scatter(far, plus, minus, own, axis):
-    n = far.shape[0] // 2
-    low = hop(far[:n], axis, 1)
-    high = hop(far[n:], axis, -1)
-    plus = jnp.concatenate([(plus[:n].astype(F32) + low.astype(F32)).astype(BF), plus[n:]], axis=0)
-    minus = jnp.concatenate([minus[:n], (minus[n:].astype(F32) + high.astype(F32)).astype(BF)], axis=0)
-    total = hop(plus, axis, 1).astype(F32) + hop(minus, axis, -1).astype(F32) + own.astype(F32)
-    return total.astype(BF)
+    last = turn(minus, axis, -1)
+    passed = turn(far, axis, 1)
+    total = turn((plus.astype(F32) + passed.astype(F32)).astype(BF), axis, 1)
+    return (total.astype(F32) + last.astype(F32) + own.astype(F32)).astype(BF)
+
+
+def after(a, *others):
+    return lax.optimization_barrier((a,) + others)[0]
 
 
 def per_device(tokens, grad_out, routing, route_weight, gate_weight, up_weight, down_weight):
@@ -210,31 +225,28 @@
             lax.dynamic_slice(w, (0, which * QUART), (SHARD, QUART)) for w in (gate_weight, up_weight, down_weight)
         ], axis=1)
 
-    own = jnp.concatenate([columns(ci), hop(columns(1 - ci), "c", 1)], axis=0)
-
-    sent = dispatch(routing, route_weight, tokens, grad_out).reshape(EXPERTS, SLOTS, D)
-    rows_own = lax.all_to_all(sent, "y", split_axis=0, concat_axis=0, tiled=True).reshape(ROWS, D)
+    sent = dispatch(routing, route_weight, tokens, grad_out)
+    own = jnp.concatenate([columns(ci), hop(after(columns(1 - ci), sent), "c", 1)], axis=0)
+
+    pair = lambda dx, dz: [(dx, dz, 0), (dx, dz, 1)]
+    z_before, z_after = turn(own, "zh", 1), turn(own, "zh", -1)
+    x_before, x_after = turn(own, "x", 1), turn(own, "x", -1)
+    z_far = turn(after(z_before, x_before), "zh", 1)
+    x_far = turn(x_before, "x", 1)
+    rest = jnp.concatenate([z_before, z_after, z_far], axis=0)
+    r_before, r_after, r_far = ring_gather(after(rest, x_far, x_after), "x")
+    across = pair(0, 3) + pair(0, 1) + pair(0, 2)
+    moved = lambda dx: [(dx, dz, w) for _, dz, w in across]
+    blocks = [own, x_before, x_after, x_far, rest, r_before, r_after, r_far]
+    pieces = [pair(0, 0), pair(3, 0), pair(1, 0), pair(2, 0), across, moved(3), moved(1), moved(2)]
+
+    rows_own = lax.all_to_all(
+        sent.reshape(EXPERTS, SLOTS, D), "y", split_axis=0, concat_axis=0, tiled=True
+    ).reshape(ROWS, D)
+    rows_own = after(rows_own, rest)
     rows_zl = hop(rows_own, "zl", 1)
     rows_c = hop(rows_own, "c", 1)
     rows_czl = hop(rows_zl, "c", 1)
-
-    pair = lambda dx, dz: [(dx, dz, 0), (dx, dz, 1)]
-    blocks, pieces = [], []
-
-    def add_x(block, listed):
-        before, after, low, high = ring_gather(block, "x")
-        half = len(listed) // 2
-        blocks.extend([block, before, after, low, high])
-        pieces.append(listed)
-        pieces.append([((dx + 3) % 4, dz, w) for dx, dz, w in listed])
-        pieces.append([((dx + 1) % 4, dz, w) for dx, dz, w in listed])
-        pieces.append([((dx + 2) % 4, dz, w) for dx, dz, w in listed[:half]])
-        pieces.append([((dx + 2) % 4, dz, w) for dx, dz, w in listed[half:]])
-
-    z_before, z_after, z_low, z_high = ring_gather(own, "zh")
-    add_x(own, pair(0, 0))
-    add_x(jnp.concatenate([z_before, z_after], axis=0), pair(0, 3) + pair(0, 1))
-    add_x(jnp.concatenate([z_low, z_high], axis=0), pair(0, 2))
 
     keep, send, far, plus, minus, mine = expert_compute([rows_own, rows_zl, rows_c, rows_czl], blocks, pieces)
 
@@ -246,7 +258,11 @@
     token_grad, route_grad = finish(routing, route_weight, back.reshape(BACK, D))
 
     summed = ring_scatter(far, plus, minus, mine, "x")
-    quarter = lambda shift: lax.dynamic_slice(summed, (lax.rem(zi + shift, 4) * BLOCK, 0), (BLOCK, QUART))
+
+    def quarter(shift):
+        at = lax.rem(zi + jnp.where(ci == 0, shift, 4 - shift), 4)
+        return lax.dynamic_slice(summed, (at * BLOCK, 0), (BLOCK, QUART))
+
     summed = ring_scatter(quarter(2), quarter(1), quarter(3), quarter(0), "zh")
     stay = lax.dynamic_slice(summed, (ci * SHARD, 0), (SHARD, QUART))
     cross = hop(lax.dynamic_slice(summed, ((1 - ci) * SHARD, 0), (SHARD, QUART)), "c", 1)

time: 222 us -> 195 us (0.88)
  the two profiles are of different devices: /device:TPU:6 before, /device:TPU:1 now
where the time goes in v2:
time: 195 us; the launch traced here: 193 us
  starting transfers between devices  109 us (56%)
  waiting for transfers between devices  44.6 us (23%)
  Pallas kernels  22.9 us (12%)
  local copies, waits for them, and re-layouts  11 us (6%)
  other arithmetic  5.01 us (3%)
    ppermute x15, starting transfers between devices, turn(): return lax.ppermute(a, (axis, 'c'), pairs)  61.3 us
    ppermute x15, waiting for transfers between devices, turn(): return lax.ppermute(a, (axis, 'c'), pairs)  42.6 us
    ppermute x7, starting transfers between devices, hop(): return lax.ppermute(a, axis, [(i, (i + shift) % n) for i in range(n)])  32.8 us
    pallas_call x1, Pallas kernels, expert_compute(): pl.pallas_call(lambda *refs: expert_kernel(pieces, *refs), in_specs=[anyw...  13.2 us
    unnamed x31, local copies, waits for them, and re-layouts  10.9 us
    all_to_all x1, starting transfers between devices, per_device(): lax.all_to_all(sent.reshape(EXPERTS, SLOTS, D), 'y', split_axis=0, concat...  7.78 us
    all_to_all x1, starting transfers between devices, per_device(): lax.all_to_all(back.reshape(EXPERTS, 8, D), 'y', split_axis=0, concat_axi...  6.88 us
    pallas_call x1, Pallas kernels, dispatch(): pl.pallas_call(dispatch_kernel, grid=(4,), in_specs=[whole, whole, part,...  5.08 us
  transfers between devices with their start and end apart: 24, of which 11 were waited for; matrix products, arithmetic and copies ran while one was open for 3% of the time, Pallas kernels for 0%

profile of v2, /device:TPU:1, one launch (start us, length us, event | category | flops | bytes accessed | tf_op | source)
XLA Modules:
  0.0 193.4 jit_solution(5824127225249769194)
XLA Ops:
  0.6 1.4 copy.12.ids_ref
  2.0 0.7 copy.13.p_ref
  2.8 5.1 %dispatch.1 = bf16[128,3584]{1,0:T(8,128)(2,1)} custom-call(s32[128,1]{1,0:T(8,128)} %copy.12.ids_ref, f32[128,1]{1,0:T(8,128)} %copy.13.p_ref, bf16[128,3584]{1,0:T(8,128)(2,1)} %x_ref.1, bf16[128,3584]{1,0:T(8,128)(2,1)} %g_ref.1), custom_call_target="tpu_custom_call" | custom-call | flops 234881024 | bytes 2752512 | tf_op jit(solution)/shard_map/dispatch/pallas_call | solution.py:52
  7.9 7.8 %all-to-all-start = ((bf16[8,16,3584]{2,1,0:T(8,128)(2,1)}), bf16[8,16,3584]{2,1,0:T(8,128)(2,1)S(1)}, u32[]{:S(2)}, u32[]{:S(2)}) async-start(bf16[8,16,3584]{2,1,0:T(8,128)(2,1)} %bitcast.10), calls=%async_computation | async-start | bytes 1835008 | tf_op jit(solution)/shard_map/all_to_all | solution.py:243
  15.7 0.0 copy-start.9
  15.7 0.0 copy-start.10
  15.7 0.9 copy-done.9
  16.6 0.1 copy-done.10
  16.7 4.7 %collective-permute-start = (bf16[112,768]{1,0:T(8,128)(2,1)S(1)}, bf16[112,768]{1,0:T(8,128)(2,1)S(1)}, u32[]{:S(2)}, u32[]{:S(2)}) collective-permute-start(bf16[112,768]{1,0:T(8,128)(2,1)S(1)} %pad_maximum_fusion.1), channel_id=1, source_target_pairs={{0,16},{16,0},{1,17},{17,1},{2,18},{18,2},{3,19},{19,3},{4,20},{20... | collective-permute-start | bytes 516104 | tf_op jit(solution)/shard_map/ppermute | solution.py:192
  21.4 1.0 collective-permute-done
  22.4 8.8 %collective-permute-start.1 = (bf16[224,768]{1,0:T(8,128)(2,1)S(1)}, bf16[224,768]{1,0:T(8,128)(2,1)S(1)}, u32[]{:S(2)}, u32[]{:S(2)}) collective-permute-start(bf16[224,768]{1,0:T(8,128)(2,1)S(1)} %pad_maximum_fusion.refs_4_), channel_id=1, source_target_pairs={{0,32},{16,112},{32,64},{48,16},{64,96},{80,48},{96,0},{112,80},{1... | collective-permute-start | bytes 1032200 | tf_op jit(solution)/shard_map/ppermute | solution.py:201
  31.2 4.4 %collective-permute-start.3 = (bf16[224,768]{1,0:T(8,128)(2,1)S(1)}, bf16[224,768]{1,0:T(8,128)(2,1)S(1)}, u32[]{:S(2)}, u32[]{:S(2)}) collective-permute-start(bf16[224,768]{1,0:T(8,128)(2,1)S(1)} %pad_maximum_fusion.refs_4_), channel_id=1, source_target_pairs={{0,128},{16,400},{128,256},{144,16},{256,384},{272,144},{384,0},{4... | collective-permute-start | bytes 1032200 | tf_op jit(solution)/shard_map/ppermute | solution.py:201
  35.6 1.9 collective-permute-start.2
  37.6 5.3 %collective-permute-done.1 = bf16[224,768]{1,0:T(8,128)(2,1)S(1)} collective-permute-done((bf16[224,768]{1,0:T(8,128)(2,1)S(1)}, bf16[224,768]{1,0:T(8,128)(2,1)S(1)}, u32[]{:S(2)}, u32[]{:S(2)}) %collective-permute-start.1) | collective-permute-done | bytes 344096 | tf_op jit(solution)/shard_map/ppermute | solution.py:201
  42.9 0.0 collective-permute-done.3.refs_5_
  42.9 6.4 %collective-permute-start.4 = (bf16[224,768]{1,0:T(8,128)(2,1)S(1)}, bf16[224,768]{1,0:T(8,128)(2,1)S(1)}, u32[]{:S(2)}, u32[]{:S(2)}) collective-permute-start(bf16[224,768]{1,0:T(8,128)(2,1)S(1)} %collective-permute-done.1), channel_id=1, source_target_pairs={{0,32},{16,112},{32,64},{48,16},{64,96},{80,48},{96,0},{112,80},{1... | collective-permute-start | bytes 1032200 | tf_op jit(solution)/shard_map/ppermute | solution.py:201
  49.2 3.1 %collective-permute-start.8 = (bf16[224,768]{1,0:T(8,128)(2,1)S(1)}, bf16[224,768]{1,0:T(8,128)(2,1)S(1)}, u32[]{:S(2)}, u32[]{:S(2)}) collective-permute-start(bf16[224,768]{1,0:T(8,128)(2,1)S(1)} %pad_maximum_fusion.refs_4_), channel_id=1, source_target_pairs={{0,384},{16,144},{128,0},{144,272},{256,128},{272,400},{384,256},{... | collective-permute-start | bytes 1032200 | tf_op jit(solution)/shard_map/ppermute | solution.py:201
  52.4 4.9 %collective-permute-start.9 = (bf16[224,768]{1,0:T(8,128)(2,1)S(1)}, bf16[224,768]{1,0:T(8,128)(2,1)S(1)}, u32[]{:S(2)}, u32[]{:S(2)}) collective-permute-start(bf16[224,768]{1,0:T(8,128)(2,1)S(1)} %collective-permute-done.3.refs_5_), channel_id=1, source_target_pairs={{0,128},{16,400},{128,256},{144,16},{256,384},{272,144},{384,0},{4... | collective-permute-start | bytes 1032200 | tf_op jit(solution)/shard_map/ppermute | solution.py:201
  57.4 3.1 %collective-permute-done.8.refs_6_ = bf16[224,768]{1,0:T(8,128)(2,1)S(1)} collective-permute-done((bf16[224,768]{1,0:T(8,128)(2,1)S(1)}, bf16[224,768]{1,0:T(8,128)(2,1)S(1)}, u32[]{:S(2)}, u32[]{:S(2)}) %collective-permute-start.8) | collective-permute-done | bytes 344096 | tf_op jit(solution)/shard_map/ppermute | solution.py:201
  60.5 0.7 copy-done.2
  61.2 0.5 collective-permute-done.9.refs_7_
  61.8 0.7 copy-done.4
  62.5 5.0 %collective-permute-start.10 = (bf16[672,768]{1,0:T(8,128)(2,1)S(1)}, bf16[672,768]{1,0:T(8,128)(2,1)}, u32[]{:S(2)}, u32[]{:S(2)}) collective-permute-start(bf16[672,768]{1,0:T(8,128)(2,1)S(1)} %constant_dynamic-update-slice_fusion.refs_8_), channel_id=1, source_target_pairs={{0,128},{16,400},{128,256},{144,16},{256,384},{272,144},{384,0},{4... | collective-permute-start | bytes 3096584 | tf_op jit(solution)/shard_map/ppermute | solution.py:201
  67.5 1.9 collective-permute-start.5
  69.4 1.9 collective-permute-start.11
  71.4 1.0 copy-done
  72.4 10.9 %collective-permute-done.10.refs_9_ = bf16[672,768]{1,0:T(8,128)(2,1)} collective-permute-done((bf16[672,768]{1,0:T(8,128)(2,1)S(1)}, bf16[672,768]{1,0:T(8,128)(2,1)}, u32[]{:S(2)}, u32[]{:S(2)}) %collective-permute-start.10) | collective-permute-done | bytes 1032224 | tf_op jit(solution)/shard_map/ppermute | solution.py:201
  83.3 5.3 %collective-permute-start.12 = (bf16[672,768]{1,0:T(8,128)(2,1)}, bf16[672,768]{1,0:T(8,128)(2,1)S(1)}, u32[]{:S(2)}, u32[]{:S(2)}) collective-permute-start(bf16[672,768]{1,0:T(8,128)(2,1)} %collective-permute-done.10.refs_9_), channel_id=1, source_target_pairs={{0,128},{16,400},{128,256},{144,16},{256,384},{272,144},{384,0},{4... | collective-permute-start | bytes 3096584 | tf_op jit(solution)/shard_map/ppermute | solution.py:201
  88.6 5.2 %collective-permute-start.6 = (bf16[128,3584]{1,0:T(8,128)(2,1)S(1)}, bf16[128,3584]{1,0:T(8,128)(2,1)S(1)}, u32[]{:S(2)}, u32[]{:S(2)}) collective-permute-start(bf16[128,3584]{1,0:T(8,128)(2,1)S(1)} %bitcast.6), channel_id=1, source_target_pairs={{0,16},{16,0},{1,17},{17,1},{2,18},{18,2},{3,19},{19,3},{4,20},{20... | collective-permute-start | bytes 2752520 | tf_op jit(solution)/shard_map/ppermute | solution.py:192
  93.8 0.0 collective-permute-done.5.refs_1_
  93.8 1.9 collective-permute-start.7
  95.8 0.0 collective-permute-done.11.refs_10_
  95.8 0.1 collective-permute-done.6.refs_2_
  95.9 5.4 %collective-permute-done.12.refs_11_ = bf16[672,768]{1,0:T(8,128)(2,1)S(1)} collective-permute-done((bf16[672,768]{1,0:T(8,128)(2,1)}, bf16[672,768]{1,0:T(8,128)(2,1)S(1)}, u32[]{:S(2)}, u32[]{:S(2)}) %collective-permute-start.12) | collective-permute-done | bytes 1032224 | tf_op jit(solution)/shard_map/ppermute | solution.py:201
  101.3 0.0 collective-permute-done.7.refs_3_
  101.3 1.2 copy-done.1
  102.5 1.0 copy-done.3
  103.5 1.0 copy-done.5
  104.5 13.2 %experts.1 = (bf16[128,3584]{1,0:T(8,128)(2,1)S(1)}, bf16[128,3584]{1,0:T(8,128)(2,1)S(1)}, bf16[896,256]{1,0:T(8,128)(2,1)S(1)}, bf16[896,256]{1,0:T(8,128)(2,1...) custom-call(bf16[128,3584]{1,0:T(8,128)(2,1)S(1)} %bitcast.7, ...), custom_call_target="tpu_custom_call" | custom-call | flops 6000000000 | bytes 14000000 | tf_op jit(solution)/shard_map/experts/pallas_call | solution.py:173
  117.7 8.5 %collective-permute-start.13 = (bf16[128,3584]{1,0:T(8,128)(2,1)S(1)}, bf16[128,3584]{1,0:T(8,128)(2,1)S(1)}, u32[]{:S(2)}, u32[]{:S(2)}) collective-permute-start(bf16[128,3584]{1,0:T(8,128)(2,1)S(1)} %get-tuple-element.20), channel_id=1, source_target_pairs={{0,16},{16,0},{1,17},{17,1},{2,18},{18,2},{3,19},{19,3},{4,20},{20... | collective-permute-start | bytes 2752520 | tf_op jit(solution)/shard_map/ppermute | solution.py:192
  126.2 2.4 %collective-permute-start.15 = (bf16[896,256]{1,0:T(8,128)(2,1)S(1)}, bf16[896,256]{1,0:T(8,128)(2,1)S(1)}, u32[]{:S(2)}, u32[]{:S(2)}) collective-permute-start(bf16[896,256]{1,0:T(8,128)(2,1)S(1)} %get-tuple-element.24), channel_id=1, source_target_pairs={{0,128},{16,400},{128,256},{144,16},{256,384},{272,144},{384,0},{4... | collective-permute-start | bytes 1376264 | tf_op jit(solution)/shard_map/ppermute | solution.py:201
  128.6 2.9 %collective-permute-start.17 = (bf16[896,256]{1,0:T(8,128)(2,1)S(1)}, bf16[896,256]{1,0:T(8,128)(2,1)}, u32[]{:S(2)}, u32[]{:S(2)}) collective-permute-start(bf16[896,256]{1,0:T(8,128)(2,1)S(1)} %get-tuple-element.25), channel_id=1, source_target_pairs={{0,384},{16,144},{128,0},{144,272},{256,128},{272,400},{384,256},{... | collective-permute-start | bytes 1376264 | tf_op jit(solution)/shard_map/ppermute | solution.py:201
  131.5 6.8 %collective-permute-done.15 = bf16[896,256]{1,0:T(8,128)(2,1)S(1)} collective-permute-done((bf16[896,256]{1,0:T(8,128)(2,1)S(1)}, bf16[896,256]{1,0:T(8,128)(2,1)S(1)}, u32[]{:S(2)}, u32[]{:S(2)}) %collective-permute-start.15) | collective-permute-done | bytes 458784 | tf_op jit(solution)/shard_map/ppermute | solution.py:201
  138.3 0.9 add_convert_fusion.1
  139.2 1.9 collective-permute-start.16
  141.1 0.0 collective-permute-done.13
  141.1 0.0 copy-start.7
  141.1 1.0 add_convert_fusion.3
  142.1 1.9 collective-permute-start.14
  144.1 0.0 collective-permute-done.17
  144.1 4.9 %collective-permute-done.16 = bf16[896,256]{1,0:T(8,128)(2,1)} collective-permute-done((bf16[896,256]{1,0:T(8,128)(2,1)}, bf16[896,256]{1,0:T(8,128)(2,1)}, u32[]{:S(2)}, u32[]{:S(2)}) %collective-permute-start.16) | collective-permute-done | bytes 458784 | tf_op jit(solution)/shard_map/ppermute | solution.py:201
  149.0 1.4 add_convert_fusion
  150.4 2.8 %collective-permute-start.18 = (bf16[224,256]{1,0:T(8,128)(2,1)S(1)}, bf16[224,256]{1,0:T(8,128)(2,1)S(1)}, u32[]{:S(2)}, u32[]{:S(2)}) collective-permute-start(bf16[224,256]{1,0:T(8,128)(2,1)S(1)} %get-tuple-element.30), channel_id=1, source_target_pairs={{0,32},{16,112},{32,64},{48,16},{64,96},{80,48},{96,0},{112,80},{1... | collective-permute-start | bytes 344072 | tf_op jit(solution)/shard_map/ppermute | solution.py:201
  153.3 7.6 %collective-permute-start.20 = (bf16[224,256]{1,0:T(8,128)(2,1)S(1)}, bf16[224,256]{1,0:T(8,128)(2,1)S(1)}, u32[]{:S(2)}, u32[]{:S(2)}) collective-permute-start(bf16[224,256]{1,0:T(8,128)(2,1)S(1)} %get-tuple-element.31), channel_id=1, source_target_pairs={{0,96},{16,48},{32,0},{48,80},{64,32},{80,112},{96,64},{112,16},{1... | collective-permute-start | bytes 344072 | tf_op jit(solution)/shard_map/ppermute | solution.py:201
  160.9 0.9 fusion
  161.8 6.9 %all-to-all-start.1 = ((bf16[8,8,3584]{2,1,0:T(8,128)(2,1)}), bf16[8,8,3584]{2,1,0:T(8,128)(2,1)S(1)}, u32[]{:S(2)}, u32[]{:S(2)}) async-start(bf16[8,8,3584]{2,1,0:T(8,128)(2,1)} %fusion), calls=%async_computation.1 | async-start | bytes 917504 | tf_op jit(solution)/shard_map/all_to_all | solution.py:257
  168.8 1.9 collective-permute-start.19
  170.7 5.7 %collective-permute-done.19 = bf16[224,256]{1,0:T(8,128)(2,1)S(1)} collective-permute-done((bf16[224,256]{1,0:T(8,128)(2,1)S(1)}, bf16[224,256]{1,0:T(8,128)(2,1)S(1)}, u32[]{:S(2)}, u32[]{:S(2)}) %collective-permute-start.19) | collective-permute-done | bytes 114720 | tf_op jit(solution)/shard_map/ppermute | solution.py:201
  176.5 8.6 %collective-permute-start.21 = (bf16[112,256]{1,0:T(8,128)(2,1)S(1)}, bf16[112,256]{1,0:T(8,128)(2,1)S(1)}, u32[]{:S(2)}, u32[]{:S(2)}) collective-permute-start(bf16[112,256]{1,0:T(8,128)(2,1)S(1)} %get-tuple-element.33), channel_id=1, source_target_pairs={{0,16},{16,0},{1,17},{17,1},{2,18},{18,2},{3,19},{19,3},{4,20},{20... | collective-permute-start | bytes 172040 | tf_op jit(solution)/shard_map/ppermute | solution.py:192
  185.1 0.9 collective-permute-done.21
  186.0 0.7 maximum_select_fusion
  186.6 0.8 copy-done.6
  187.4 4.6 %finish.1 = (bf16[128,3584]{1,0:T(8,128)(2,1)}, f32[128,1]{1,0:T(8,128)}) custom-call(s32[128,1]{1,0:T(8,128)} %copy.12.ids_ref, f32[128,1]{1,0:T(8,128)} %copy.13.p_ref, bf16[64,3584]{1,0:T(8,128)(2,1)} %bitcast.8, bf16[64,3584]{1,0:T(8,128)(2,1)} %bitcast.9), custom_call_target="tpu_custom_call" | custom-call | flops 10000000 | bytes 10000 | tf_op jit(solution)/shard_map/finish/pallas_call | solution.py:83
  192.0 1.4 copy.14
  (32 shorter events, 0.3 us)
Async XLA Ops:
  0.6 1.4 copy-start.12
  7.9 7.8 %copy-start.11 = (bf16[112,512]{1,0:T(8,128)(2,1)S(1)}, bf16[112,512]{1,0:T(8,128)(2,1)}, u32[]{:S(2)}) copy-start(bf16[112,512]{1,0:T(8,128)(2,1)} %param.11) | copy-start | bytes 344068
  7.9 59.6 %all-to-all-start = ((bf16[8,16,3584]{2,1,0:T(8,128)(2,1)}), bf16[8,16,3584]{2,1,0:T(8,128)(2,1)S(1)}, u32[]{:S(2)}, u32[]{:S(2)}) async-start(bf16[8,16,3584]{2,1,0:T(8,128)(2,1)} %bitcast.10), calls=%async_computation | async-start | bytes 1835008 | tf_op jit(solution)/shard_map/all_to_all | solution.py:243
  15.7 0.9 copy-start.9
  15.7 0.9 copy-start.10
  16.7 5.7 %collective-permute-start = (bf16[112,768]{1,0:T(8,128)(2,1)S(1)}, bf16[112,768]{1,0:T(8,128)(2,1)S(1)}, u32[]{:S(2)}, u32[]{:S(2)}) collective-permute-start(bf16[112,768]{1,0:T(8,128)(2,1)S(1)} %pad_maximum_fusion.1), channel_id=1, source_target_pairs={{0,16},{16,0},{1,17},{17,1},{2,18},{18,2},{3,19},{19,3},{4,20},{20... | collective-permute-start | bytes 516104 | tf_op jit(solution)/shard_map/ppermute | solution.py:192
  22.4 20.4 %collective-permute-start.1 = (bf16[224,768]{1,0:T(8,128)(2,1)S(1)}, bf16[224,768]{1,0:T(8,128)(2,1)S(1)}, u32[]{:S(2)}, u32[]{:S(2)}) collective-permute-start(bf16[224,768]{1,0:T(8,128)(2,1)S(1)} %pad_maximum_fusion.refs_4_), channel_id=1, source_target_pairs={{0,32},{16,112},{32,64},{48,16},{64,96},{80,48},{96,0},{112,80},{1... | collective-permute-start | bytes 1032200 | tf_op jit(solution)/shard_map/ppermute | solution.py:201
  31.2 11.6 %collective-permute-start.3 = (bf16[224,768]{1,0:T(8,128)(2,1)S(1)}, bf16[224,768]{1,0:T(8,128)(2,1)S(1)}, u32[]{:S(2)}, u32[]{:S(2)}) collective-permute-start(bf16[224,768]{1,0:T(8,128)(2,1)S(1)} %pad_maximum_fusion.refs_4_), channel_id=1, source_target_pairs={{0,128},{16,400},{128,256},{144,16},{256,384},{272,144},{384,0},{4... | collective-permute-start | bytes 1032200 | tf_op jit(solution)/shard_map/ppermute | solution.py:201
  35.6 21.7 %collective-permute-start.2 = (bf16[224,768]{1,0:T(8,128)(2,1)S(1)}, bf16[224,768]{1,0:T(8,128)(2,1)S(1)}, u32[]{:S(2)}, u32[]{:S(2)}) collective-permute-start(bf16[224,768]{1,0:T(8,128)(2,1)S(1)} %pad_maximum_fusion.refs_4_), channel_id=1, source_target_pairs={{0,96},{16,48},{32,0},{48,80},{64,32},{80,112},{96,64},{112,16},{1... | collective-permute-start | bytes 1032200 | tf_op jit(solution)/shard_map/ppermute | solution.py:201
  42.9 14.5 %collective-permute-start.4 = (bf16[224,768]{1,0:T(8,128)(2,1)S(1)}, bf16[224,768]{1,0:T(8,128)(2,1)S(1)}, u32[]{:S(2)}, u32[]{:S(2)}) collective-permute-start(bf16[224,768]{1,0:T(8,128)(2,1)S(1)} %collective-permute-done.1), channel_id=1, source_target_pairs={{0,32},{16,112},{32,64},{48,16},{64,96},{80,48},{96,0},{112,80},{1... | collective-permute-start | bytes 1032200 | tf_op jit(solution)/shard_map/ppermute | solution.py:201
  49.2 11.3 %collective-permute-start.8 = (bf16[224,768]{1,0:T(8,128)(2,1)S(1)}, bf16[224,768]{1,0:T(8,128)(2,1)S(1)}, u32[]{:S(2)}, u32[]{:S(2)}) collective-permute-start(bf16[224,768]{1,0:T(8,128)(2,1)S(1)} %pad_maximum_fusion.refs_4_), channel_id=1, source_target_pairs={{0,384},{16,144},{128,0},{144,272},{256,128},{272,400},{384,256},{... | collective-permute-start | bytes 1032200 | tf_op jit(solution)/shard_map/ppermute | solution.py:201
  52.4 9.4 %collective-permute-start.9 = (bf16[224,768]{1,0:T(8,128)(2,1)S(1)}, bf16[224,768]{1,0:T(8,128)(2,1)S(1)}, u32[]{:S(2)}, u32[]{:S(2)}) collective-permute-start(bf16[224,768]{1,0:T(8,128)(2,1)S(1)} %collective-permute-done.3.refs_5_), channel_id=1, source_target_pairs={{0,128},{16,400},{128,256},{144,16},{256,384},{272,144},{384,0},{4... | collective-permute-start | bytes 1032200 | tf_op jit(solution)/shard_map/ppermute | solution.py:201
  60.5 0.7 copy-start.2
  61.8 0.7 copy-start.4
  62.5 20.8 %collective-permute-start.10 = (bf16[672,768]{1,0:T(8,128)(2,1)S(1)}, bf16[672,768]{1,0:T(8,128)(2,1)}, u32[]{:S(2)}, u32[]{:S(2)}) collective-permute-start(bf16[672,768]{1,0:T(8,128)(2,1)S(1)} %constant_dynamic-update-slice_fusion.refs_8_), channel_id=1, source_target_pairs={{0,128},{16,400},{128,256},{144,16},{256,384},{272,144},{384,0},{4... | collective-permute-start | bytes 3096584 | tf_op jit(solution)/shard_map/ppermute | solution.py:201
  67.5 26.3 %collective-permute-start.5 = (bf16[128,3584]{1,0:T(8,128)(2,1)S(1)}, bf16[128,3584]{1,0:T(8,128)(2,1)S(1)}, u32[]{:S(2)}, u32[]{:S(2)}) collective-permute-start(bf16[128,3584]{1,0:T(8,128)(2,1)S(1)} %bitcast.5), channel_id=1, source_target_pairs={{0,1},{1,0},{2,3},{3,2},{4,5},{5,4},{6,7},{7,6},{8,9},{9,8},{10,11... | collective-permute-start | bytes 2752520 | tf_op jit(solution)/shard_map/ppermute | solution.py:192
  69.4 26.3 %collective-permute-start.11 = (bf16[672,768]{1,0:T(8,128)(2,1)S(1)}, bf16[672,768]{1,0:T(8,128)(2,1)S(1)}, u32[]{:S(2)}, u32[]{:S(2)}) collective-permute-start(bf16[672,768]{1,0:T(8,128)(2,1)S(1)} %constant_dynamic-update-slice_fusion.refs_8_), channel_id=1, source_target_pairs={{0,384},{16,144},{128,0},{144,272},{256,128},{272,400},{384,256},{... | collective-permute-start | bytes 3096584 | tf_op jit(solution)/shard_map/ppermute | solution.py:201
  71.4 1.0 copy-start
  83.3 18.0 %collective-permute-start.12 = (bf16[672,768]{1,0:T(8,128)(2,1)}, bf16[672,768]{1,0:T(8,128)(2,1)S(1)}, u32[]{:S(2)}, u32[]{:S(2)}) collective-permute-start(bf16[672,768]{1,0:T(8,128)(2,1)} %collective-permute-done.10.refs_9_), channel_id=1, source_target_pairs={{0,128},{16,400},{128,256},{144,16},{256,384},{272,144},{384,0},{4... | collective-permute-start | bytes 3096584 | tf_op jit(solution)/shard_map/ppermute | solution.py:201
  88.6 7.3 %collective-permute-start.6 = (bf16[128,3584]{1,0:T(8,128)(2,1)S(1)}, bf16[128,3584]{1,0:T(8,128)(2,1)S(1)}, u32[]{:S(2)}, u32[]{:S(2)}) collective-permute-start(bf16[128,3584]{1,0:T(8,128)(2,1)S(1)} %bitcast.6), channel_id=1, source_target_pairs={{0,16},{16,0},{1,17},{17,1},{2,18},{18,2},{3,19},{19,3},{4,20},{20... | collective-permute-start | bytes 2752520 | tf_op jit(solution)/shard_map/ppermute | solution.py:192
  93.8 7.4 %collective-permute-start.7 = (bf16[128,3584]{1,0:T(8,128)(2,1)S(1)}, bf16[128,3584]{1,0:T(8,128)(2,1)S(1)}, u32[]{:S(2)}, u32[]{:S(2)}) collective-permute-start(bf16[128,3584]{1,0:T(8,128)(2,1)S(1)} %collective-permute-done.5.refs_1_), channel_id=1, source_target_pairs={{0,16},{16,0},{1,17},{17,1},{2,18},{18,2},{3,19},{19,3},{4,20},{20... | collective-permute-start | bytes 2752520 | tf_op jit(solution)/shard_map/ppermute | solution.py:192
  101.3 1.2 copy-start.1
  102.5 1.0 copy-start.3
  103.5 1.0 copy-start.5
  117.7 23.4 %collective-permute-start.13 = (bf16[128,3584]{1,0:T(8,128)(2,1)S(1)}, bf16[128,3584]{1,0:T(8,128)(2,1)S(1)}, u32[]{:S(2)}, u32[]{:S(2)}) collective-permute-start(bf16[128,3584]{1,0:T(8,128)(2,1)S(1)} %get-tuple-element.20), channel_id=1, source_target_pairs={{0,16},{16,0},{1,17},{17,1},{2,18},{18,2},{3,19},{19,3},{4,20},{20... | collective-permute-start | bytes 2752520 | tf_op jit(solution)/shard_map/ppermute | solution.py:192
  126.2 12.1 %collective-permute-start.15 = (bf16[896,256]{1,0:T(8,128)(2,1)S(1)}, bf16[896,256]{1,0:T(8,128)(2,1)S(1)}, u32[]{:S(2)}, u32[]{:S(2)}) collective-permute-start(bf16[896,256]{1,0:T(8,128)(2,1)S(1)} %get-tuple-element.24), channel_id=1, source_target_pairs={{0,128},{16,400},{128,256},{144,16},{256,384},{272,144},{384,0},{4... | collective-permute-start | bytes 1376264 | tf_op jit(solution)/shard_map/ppermute | solution.py:201
  128.6 15.5 %collective-permute-start.17 = (bf16[896,256]{1,0:T(8,128)(2,1)S(1)}, bf16[896,256]{1,0:T(8,128)(2,1)}, u32[]{:S(2)}, u32[]{:S(2)}) collective-permute-start(bf16[896,256]{1,0:T(8,128)(2,1)S(1)} %get-tuple-element.25), channel_id=1, source_target_pairs={{0,384},{16,144},{128,0},{144,272},{256,128},{272,400},{384,256},{... | collective-permute-start | bytes 1376264 | tf_op jit(solution)/shard_map/ppermute | solution.py:201
  139.2 9.8 %collective-permute-start.16 = (bf16[896,256]{1,0:T(8,128)(2,1)}, bf16[896,256]{1,0:T(8,128)(2,1)}, u32[]{:S(2)}, u32[]{:S(2)}) collective-permute-start(bf16[896,256]{1,0:T(8,128)(2,1)} %add_convert_fusion.1), channel_id=1, source_target_pairs={{0,128},{16,400},{128,256},{144,16},{256,384},{272,144},{384,0},{4... | collective-permute-start | bytes 1376264 | tf_op jit(solution)/shard_map/ppermute | solution.py:201
  141.1 7.9 %copy-start.7 = (bf16[128,3584]{1,0:T(8,128)(2,1)}, bf16[128,3584]{1,0:T(8,128)(2,1)S(1)}, u32[]{:S(2)}) copy-start(bf16[128,3584]{1,0:T(8,128)(2,1)S(1)} %collective-permute-done.13) | copy-start | bytes 2752516
  142.1 18.8 %collective-permute-start.14 = (bf16[64,3584]{1,0:T(8,128)(2,1)}, bf16[64,3584]{1,0:T(8,128)(2,1)S(1)}, u32[]{:S(2)}, u32[]{:S(2)}) collective-permute-start(bf16[64,3584]{1,0:T(8,128)(2,1)} %add_convert_fusion.3), channel_id=1, source_target_pairs={{0,1},{1,0},{2,3},{3,2},{4,5},{5,4},{6,7},{7,6},{8,9},{9,8},{10,11... | collective-permute-start | bytes 1376264 | tf_op jit(solution)/shard_map/ppermute | solution.py:192
  149.0 11.9 %copy-start.8 = (bf16[128,3584]{1,0:T(8,128)(2,1)S(1)}, bf16[128,3584]{1,0:T(8,128)(2,1)}, u32[]{:S(2)}) copy-start(bf16[128,3584]{1,0:T(8,128)(2,1)} %copy-done.7) | copy-start | bytes 2752516
  150.4 18.3 %collective-permute-start.18 = (bf16[224,256]{1,0:T(8,128)(2,1)S(1)}, bf16[224,256]{1,0:T(8,128)(2,1)S(1)}, u32[]{:S(2)}, u32[]{:S(2)}) collective-permute-start(bf16[224,256]{1,0:T(8,128)(2,1)S(1)} %get-tuple-element.30), channel_id=1, source_target_pairs={{0,32},{16,112},{32,64},{48,16},{64,96},{80,48},{96,0},{112,80},{1... | collective-permute-start | bytes 344072 | tf_op jit(solution)/shard_map/ppermute | solution.py:201
  153.3 17.4 %collective-permute-start.20 = (bf16[224,256]{1,0:T(8,128)(2,1)S(1)}, bf16[224,256]{1,0:T(8,128)(2,1)S(1)}, u32[]{:S(2)}, u32[]{:S(2)}) collective-permute-start(bf16[224,256]{1,0:T(8,128)(2,1)S(1)} %get-tuple-element.31), channel_id=1, source_target_pairs={{0,96},{16,48},{32,0},{48,80},{64,32},{80,112},{96,64},{112,16},{1... | collective-permute-start | bytes 344072 | tf_op jit(solution)/shard_map/ppermute | solution.py:201
  161.8 24.8 %all-to-all-start.1 = ((bf16[8,8,3584]{2,1,0:T(8,128)(2,1)}), bf16[8,8,3584]{2,1,0:T(8,128)(2,1)S(1)}, u32[]{:S(2)}, u32[]{:S(2)}) async-start(bf16[8,8,3584]{2,1,0:T(8,128)(2,1)} %fusion), calls=%async_computation.1 | async-start | bytes 917504 | tf_op jit(solution)/shard_map/all_to_all | solution.py:257
  168.8 7.6 %collective-permute-start.19 = (bf16[224,256]{1,0:T(8,128)(2,1)S(1)}, bf16[224,256]{1,0:T(8,128)(2,1)S(1)}, u32[]{:S(2)}, u32[]{:S(2)}) collective-permute-start(bf16[224,256]{1,0:T(8,128)(2,1)S(1)} %add_convert_fusion.5), channel_id=1, source_target_pairs={{0,32},{16,112},{32,64},{48,16},{64,96},{80,48},{96,0},{112,80},{1... | collective-permute-start | bytes 344072 | tf_op jit(solution)/shard_map/ppermute | solution.py:201
  176.5 9.5 %collective-permute-start.21 = (bf16[112,256]{1,0:T(8,128)(2,1)S(1)}, bf16[112,256]{1,0:T(8,128)(2,1)S(1)}, u32[]{:S(2)}, u32[]{:S(2)}) collective-permute-start(bf16[112,256]{1,0:T(8,128)(2,1)S(1)} %get-tuple-element.33), channel_id=1, source_target_pairs={{0,16},{16,0},{1,17},{17,1},{2,18},{18,2},{3,19},{19,3},{4,20},{20... | collective-permute-start | bytes 172040 | tf_op jit(solution)/shard_map/ppermute | solution.py:192
  186.6 0.8 copy-start.6

commit v3 on v1

v3 whole, which is shorter than its diff:
```python
import jax
import jax.numpy as jnp
from jax import lax
from jax.experimental import pallas as pl
from jax.experimental.pallas import tpu as pltpu
from jax.sharding import Mesh, PartitionSpec as P

BF = jnp.bfloat16
F32 = jnp.float32
I32 = jnp.int32
AXES = ("x", "zh", "c", "y", "zl")
TOK = 128
D = 3584
EXPERTS = 8
CAP = 6
QUART = 256
SHARD = 112
BLOCK = 2 * SHARD
XROWS = 4 * BLOCK
PEERS = 16
CHUNK = D // 4
SLAB = 48
GROUP = 8 * SLAB
ROWS = PEERS * CAP
PIECE = 512
WIDE = D + 128
VMEM_LIMIT = 28 * 1024 * 1024
VMEM = pl.BlockSpec(memory_space=pltpu.VMEM)


def iota(shape, dim):
    return lax.broadcasted_iota(I32, shape, dim)


def sixth(i):
    return (i * 43) >> 8


def regroup():
    a, i = iota((8, SLAB, GROUP), 0), iota((8, SLAB, GROUP), 1)
    b = sixth(i)
    hit = iota((8, SLAB, GROUP), 2) == b * SLAB + a * CAP + (i - CAP * b)
    return jnp.where(hit, 1.0, 0.0).reshape(GROUP, GROUP).astype(BF)


def token_ranks(ids):
    member = jnp.where(ids == iota((EXPERTS, TOK), 0), 1.0, 0.0)
    earlier = jnp.where(iota((TOK, TOK), 0) < iota((TOK, TOK), 1), 1.0, 0.0)
    counts = jnp.dot(member.astype(BF), earlier.astype(BF), preferred_element_type=F32)
    return jnp.sum(member * counts, axis=0, keepdims=True).astype(I32)


def to_column(row):
    diagonal = iota((TOK, TOK), 0) == iota((TOK, TOK), 1)
    return jnp.sum(jnp.where(diagonal, row, 0.0), axis=1, keepdims=True)


def dispatch_kernel(ids_ref, p_ref, x_ref, g_ref, out_ref):
    ids = ids_ref[...]
    slot = jnp.where(ids < EXPERTS, ids * CAP + token_ranks(ids), -1)
    i = iota((EXPERTS, 24, TOK), 1)
    which = sixth(i)
    mine = slot == iota((EXPERTS, 24, TOK), 0) * CAP + (i - CAP * which)
    sel = jnp.concatenate([
        jnp.where(mine & (which == j), 1.0, 0.0).reshape(EXPERTS * 24, TOK) for j in range(4)
    ], axis=1).astype(BF)
    scaled = (to_column(p_ref[...]) * g_ref[...].astype(F32)).astype(BF)
    halves = []
    for h in range(2):
        stack = []
        for q in (2 * h, 2 * h + 1):
            stack += [x_ref[:, q * CHUNK:(q + 1) * CHUNK], scaled[:, q * CHUNK:(q + 1) * CHUNK]]
        rows = jnp.dot(sel, jnp.concatenate(stack, axis=0), preferred_element_type=F32)
        halves.append(rows.reshape(EXPERTS, 24, CHUNK))
    rows = jnp.concatenate(halves, axis=1).astype(BF)
    for e in range(EXPERTS):
        out_ref[2 * e] = rows[e]
        out_ref[2 * e + 1] = rows[e]


def dispatch(ids, weight, tokens, grads):
    return pl.pallas_call(
        dispatch_kernel,
        in_specs=[VMEM] * 4,
        out_specs=VMEM,
        out_shape=jax.ShapeDtypeStruct((PEERS, SLAB, CHUNK), BF),
        compiler_params=pltpu.CompilerParams(vmem_limit_bytes=VMEM_LIMIT),
        cost_estimate=pl.CostEstimate(flops=4 * 10**8, bytes_accessed=4 * 10**6, transcendentals=0),
        name="dispatch",
    )(ids, weight, tokens, grads)


def combine_kernel(keep_ref, got_ref, out_ref):
    total = keep_ref[...].astype(F32) + got_ref[...].astype(F32)
    total = jnp.concatenate([total, jnp.zeros((ROWS, 8 * PIECE - WIDE), F32)], axis=1).astype(BF)
    order = regroup()
    for half in range(2):
        rows = total[half * SLAB:(half + 1) * SLAB]
        stack = jnp.concatenate([rows[:, q * PIECE:(q + 1) * PIECE] for q in range(8)], axis=0)
        moved = jnp.dot(order, stack, preferred_element_type=F32).astype(BF)
        out_ref[half * 8:(half + 1) * 8] = moved.reshape(8, SLAB, PIECE)


def combine(keep, got):
    return pl.pallas_call(
        combine_kernel,
        in_specs=[VMEM] * 2,
        out_specs=VMEM,
        out_shape=jax.ShapeDtypeStruct((PEERS, SLAB, PIECE), BF),
        compiler_params=pltpu.CompilerParams(vmem_limit_bytes=VMEM_LIMIT),
        cost_estimate=pl.CostEstimate(flops=3 * 10**8, bytes_accessed=2 * 10**6, transcendentals=0),
        name="combine",
    )(keep, got)


def finish_kernel(ids_ref, p_ref, rows_ref, tok_ref, route_ref):
    ids = ids_ref[...]
    base = jnp.where(ids < EXPERTS, ids * (2 * SLAB) + token_ranks(ids), -2 * D)
    base = to_column(base.astype(F32)).astype(I32)
    offset = iota((TOK, PEERS * SLAB), 1) - base
    for q in range(8):
        sel = jnp.where((offset == q * CAP) | (offset == q * CAP + SLAB), 1.0, 0.0).astype(BF)
        if q < 7:
            got = jnp.dot(sel, rows_ref[...], preferred_element_type=F32)
            tok_ref[:, q * PIECE:(q + 1) * PIECE] = got.astype(BF)
        else:
            route = jnp.dot(sel, rows_ref[:, :TOK], preferred_element_type=F32)[:, :1]
            diagonal = iota((TOK, TOK), 0) == iota((TOK, TOK), 1)
            route_ref[...] = jnp.sum(jnp.where(diagonal, route, 0.0), axis=0, keepdims=True) / p_ref[...]


def finish(ids, weight, rows):
    return pl.pallas_call(
        finish_kernel,
        in_specs=[VMEM] * 3,
        out_specs=[VMEM] * 2,
        out_shape=[jax.ShapeDtypeStruct((TOK, D), BF), jax.ShapeDtypeStruct((1, TOK), F32)],
        compiler_params=pltpu.CompilerParams(vmem_limit_bytes=VMEM_LIMIT),
        cost_estimate=pl.CostEstimate(flops=7 * 10**8, bytes_accessed=2 * 10**6, transcendentals=0),
        name="finish",
    )(ids, weight, rows)


def expert_kernel(pieces, *refs):
    row_refs = refs[:2]
    weight_refs = refs[2:2 + len(pieces)]
    keep_ref, send_ref, far_ref, plus_ref, minus_ref, own_ref = refs[2 + len(pieces):8 + len(pieces)]
    raw, x_rows, g_rows, weights, sem_rows, sem_weights = refs[8 + len(pieces):]
    xi, zi, ci = lax.axis_index("x"), lax.axis_index("zh"), lax.axis_index("c")
    row_copies = [pltpu.make_async_copy(ref, raw.at[i], sem_rows.at[i]) for i, ref in enumerate(row_refs)]
    weight_copies = []
    for ref, listed in zip(weight_refs, pieces):
        for at, (dx, dz, which) in enumerate(listed):
            block = lax.rem(xi + dx, 4) * 4 + lax.rem(zi + dz, 4)
            core = ci if which == 0 else 1 - ci
            start = pl.multiple_of(block * BLOCK + core * SHARD, 16)
            weight_copies.append(pltpu.make_async_copy(
                ref.at[pl.ds(at * SHARD, SHARD)],
                weights.at[pl.ds(start, SHARD)],
                sem_weights.at[len(weight_copies)],
            ))
    for copy in row_copies + weight_copies:
        copy.start()
    order = regroup()
    for i, copy in enumerate(row_copies):
        copy.wait()
        for half in range(2):
            part = raw[i, half * 8:(half + 1) * 8].reshape(GROUP, CHUNK)
            moved = jnp.dot(order, part, preferred_element_type=F32).astype(BF)
            at = (2 * i + half) * SLAB
            for q in range(4):
                columns = pl.ds(q * CHUNK, CHUNK)
                x_rows[at:at + SLAB, columns] = moved[2 * q * SLAB:(2 * q + 1) * SLAB]
                g_rows[at:at + SLAB, columns] = moved[(2 * q + 1) * SLAB:(2 * q + 2) * SLAB]
    for copy in weight_copies:
        copy.wait()
    pre = jnp.dot(x_rows[...], weights[:, :2 * QUART], preferred_element_type=F32)
    grad = jnp.dot(g_rows[...], weights[:, 2 * QUART:], preferred_element_type=F32)
    gate, up = pre[:, :QUART], pre[:, QUART:]
    sig = jax.nn.sigmoid(gate)
    act = gate * sig
    slope = sig * (1.0 + gate * (1.0 - sig))
    hidden = (act * up).astype(BF)
    route = jnp.sum(hidden.astype(F32) * grad, axis=1, keepdims=True)
    for ref, shift in ((far_ref, 2), (plus_ref, 1), (minus_ref, 3), (own_ref, 0)):
        start = pl.multiple_of(lax.rem(xi + shift, 4) * XROWS, 128)
        ref[...] = lax.dot_general(
            g_rows[:, pl.ds(start, XROWS)], hidden, (((0,), (0,)), ((), ())), preferred_element_type=F32
        ).astype(BF)
    d_pre = jnp.concatenate([(grad * up * slope).astype(BF), (grad * act).astype(BF)], axis=1)
    for i in range(4):
        part = lax.dot_general(
            d_pre, weights[i * CHUNK:(i + 1) * CHUNK, :2 * QUART], (((1,), (1,)), ((), ())),
            preferred_element_type=F32,
        ).astype(BF)
        keep_ref[:, i * CHUNK:(i + 1) * CHUNK] = part[:ROWS]
        send_ref[:, i * CHUNK:(i + 1) * CHUNK] = part[ROWS:]
    line = jnp.where(iota((2 * ROWS, 128), 1) == 0, route, 0.0).astype(BF)
    keep_ref[:, D:] = line[:ROWS]
    send_ref[:, D:] = line[ROWS:]


def expert_compute(rows, blocks, pieces):
    anywhere = pl.BlockSpec(memory_space=pl.ANY)
    count = sum(len(p) for p in pieces)
    back = jax.ShapeDtypeStruct((ROWS, WIDE), BF)
    down = jax.ShapeDtypeStruct((XROWS, QUART), BF)
    return pl.pallas_call(
        lambda *refs: expert_kernel(pieces, *refs),
        in_specs=[anywhere] * (2 + len(blocks)),
        out_specs=[VMEM] * 6,
        out_shape=[back, back, down, down, down, down],
        scratch_shapes=[
            pltpu.VMEM((2, PEERS, SLAB, CHUNK), BF),
            pltpu.VMEM((2 * ROWS, D), BF),
            pltpu.VMEM((2 * ROWS, D), BF),
            pltpu.VMEM((D, 3 * QUART), BF),
            pltpu.SemaphoreType.DMA((2,)),
            pltpu.SemaphoreType.DMA((count,)),
        ],
        compiler_params=pltpu.CompilerParams(vmem_limit_bytes=VMEM_LIMIT),
        cost_estimate=pl.CostEstimate(flops=4 * 10**9, bytes_accessed=12 * 10**6, transcendentals=49152),
        name="experts",
    )(*rows, *blocks)


def relay_kernel(plus_ref, minus_ref, low_ref, high_ref, _, plus_out, minus_out):
    half = XROWS // 2
    plus_out[:half] = add(plus_ref[:half], low_ref[...])
    plus_out[half:] = plus_ref[half:]
    minus_out[:half] = minus_ref[:half]
    minus_out[half:] = add(minus_ref[half:], high_ref[...])


def relay(plus, minus, low, high, message):
    down = jax.ShapeDtypeStruct((XROWS, QUART), BF)
    return pl.pallas_call(
        relay_kernel,
        in_specs=[VMEM] * 4 + [pl.BlockSpec(memory_space=pl.ANY)],
        out_specs=[VMEM] * 2,
        out_shape=[down, down],
        compiler_params=pltpu.CompilerParams(vmem_limit_bytes=VMEM_LIMIT),
        cost_estimate=pl.CostEstimate(flops=10**6, bytes_accessed=3 * 10**6, transcendentals=0),
        name="relay",
    )(plus, minus, low, high, message)


def hop(a, axis, shift):
    n = lax.axis_size(axis)
    return lax.ppermute(a, axis, [(i, (i + shift) % n) for i in range(n)])


def tie(*arrays):
    return lax.optimization_barrier(arrays)


def add(*terms):
    return sum(a.astype(F32) for a in terms).astype(BF)


def exchange(a, axes):
    return lax.all_to_all(a, axes, split_axis=0, concat_axis=0, tiled=True)


def per_device(tokens, grad_out, routing, route_weight, gate_weight, up_weight, down_weight):
    ci = lax.axis_index("c")
    ids, share = routing.reshape(1, TOK), route_weight.reshape(1, TOK)

    def columns(which):
        return jnp.concatenate([
            lax.dynamic_slice(w, (0, which * QUART), (SHARD, QUART)) for w in (gate_weight, up_weight, down_weight)
        ], axis=1)

    theirs = hop(columns(1 - ci), "c", 1)
    sent = dispatch(ids, share, tokens, grad_out)
    mine, sent = tie(columns(ci), sent)
    own = jnp.concatenate([mine, theirs], axis=0)

    z_before, z_after = hop(own, "zh", 1), hop(own, "zh", -1)
    x_before, x_after = hop(own, "x", 1), hop(own, "x", -1)
    z_before, z_after, x_before, x_after = tie(z_before, z_after, x_before, x_after)
    z_low, z_high = hop(z_before[:SHARD], "zh", 1), hop(z_after[SHARD:], "zh", -1)
    x_low, x_high = hop(x_before[:SHARD], "x", 1), hop(x_after[SHARD:], "x", -1)
    rest = jnp.concatenate([z_before, z_after, z_low, z_high], axis=0)
    r_before, r_after = hop(rest, "x", 1), hop(rest, "x", -1)
    half = 3 * SHARD
    r_low, r_high = hop(r_before[:half], "x", 1), hop(r_after[half:], "x", -1)

    across = [(0, 3, 0), (0, 3, 1), (0, 1, 0), (0, 1, 1), (0, 2, 0), (0, 2, 1)]
    moved = lambda dx, listed: [(dx, dz, w) for _, dz, w in listed]
    pair = [(0, 0, 0), (0, 0, 1)]
    blocks = [own, x_before, x_after, x_low, x_high, rest, r_before, r_after, r_low, r_high]
    pieces = [
        pair, moved(3, pair), moved(1, pair), moved(2, pair[:1]), moved(2, pair[1:]),
        across, moved(3, across), moved(1, across), moved(2, across[:3]), moved(2, across[3:]),
    ]

    rows = exchange(sent, ("y", "zl"))
    keep, send, far, plus, minus, mine = expert_compute([rows, hop(rows, "c", 1)], blocks, pieces)

    far, got = tie(far, hop(send, "c", 1))
    low, high = hop(far[:XROWS // 2], "x", 1), hop(far[XROWS // 2:], "x", -1)
    message = combine(keep, got)
    back = exchange(message, ("y", "zl"))
    token_grad, route_grad = finish(ids, share, back.reshape(PEERS * SLAB, PIECE))

    plus, minus = relay(plus, minus, low, high, message)
    summed = add(hop(plus, "x", 1), hop(minus, "x", -1), mine)
    summed = exchange(summed.reshape(8, SHARD, QUART), ("zh", "c")).reshape(4, 2, SHARD, QUART)
    summed = jnp.sum(summed.astype(F32), axis=0).astype(BF)
    down_grad = jnp.concatenate([summed[0], summed[1]], axis=1)
    return token_grad, route_grad.reshape(TOK, 1), down_grad


def solution(mesh):
    inner = Mesh(mesh.devices.reshape(4, 4, 2, 8, 2), AXES)
    rows = P(AXES, None)
    weights = P(("x", "zh", "c"), ("y", "zl"))
    return jax.shard_map(
        per_device,
        mesh=inner,
        in_specs=(rows, rows, rows, rows, weights, weights, weights),
        out_specs=(rows, rows, weights),
        check_vma=False,
    )
```

time: 222 us -> 211 us (0.950)
  starting transfers between devices: 117 us -> 87.9 us
  waiting for transfers between devices: 68.1 us -> 89.9 us
  Pallas kernels: 22.7 us -> 16.8 us
  local copies, waits for them, and re-layouts: 7.48 us -> 12.4 us
    ppermute x31 -> x19, starting transfers between devices: 107 us -> 69.1 us  [hop(): return lax.ppermute(a, axis, [(i, (i + shift) % n) for i in range(n)])]
    ppermute x31 -> x19, waiting for transfers between devices: 59.4 us -> 75.1 us  [hop(): return lax.ppermute(a, axis, [(i, (i + shift) % n) for i in range(n)])]
    all_to_all x2 -> x3, starting transfers between devices: 10.7 us -> 18.8 us  [exchange(): return lax.all_to_all(a, axes, split_axis=0, concat_axis=0, tiled=True)]
    all_to_all x2 -> x3, waiting for transfers between devices: 8.72 us -> 14.9 us  [exchange(): return lax.all_to_all(a, axes, split_axis=0, concat_axis=0, tiled=True)]
    pallas_call x2 -> x4, Pallas kernels: 9.71 us -> 5.44 us  [the longest x1 2.02 us: finish(): pl.pallas_call(finish_kernel, in_specs=[VMEM] * 3, out_specs=[VMEM] * 2,...]
    unnamed x29 -> x28, local copies, waits for them, and re-layouts: 7.17 us -> 7.89 us
  transfers between devices with their start and end apart: 33 -> 22, of which waited for: 15 -> 14; matrix products, arithmetic and copies ran while one was open for 1% -> 3% of each run, Pallas kernels for 0% -> 1%
where the time goes in v3:
time: 211 us; the launch traced here: 210 us
  waiting for transfers between devices  89.9 us (43%)
  starting transfers between devices  87.9 us (42%)
  Pallas kernels  16.8 us (8%)
  local copies, waits for them, and re-layouts  12.4 us (6%)
    ppermute x19, waiting for transfers between devices, hop(): return lax.ppermute(a, axis, [(i, (i + shift) % n) for i in range(n)])  75.1 us
    ppermute x19, starting transfers between devices, hop(): return lax.ppermute(a, axis, [(i, (i + shift) % n) for i in range(n)])  69.1 us
    all_to_all x3, starting transfers between devices, exchange(): return lax.all_to_all(a, axes, split_axis=0, concat_axis=0, tiled=True)  18.8 us
    all_to_all x3, waiting for transfers between devices, exchange(): return lax.all_to_all(a, axes, split_axis=0, concat_axis=0, tiled=True)  14.9 us
    pallas_call x1, Pallas kernels, expert_compute(): pl.pallas_call(lambda *refs: expert_kernel(pieces, *refs), in_specs=[anyw...  11.3 us
    unnamed x28, local copies, waits for them, and re-layouts  7.89 us
  transfers between devices with their start and end apart: 22, of which 14 were waited for; matrix products, arithmetic and copies ran while one was open for 3% of the time, Pallas kernels for 1%

profile of v3, /device:TPU:6, one launch (start us, length us, event | category | flops | bytes accessed | tf_op | source)
XLA Modules:
  0.0 209.8 jit_solution(3680594410261781088)
XLA Ops:
  0.6 0.9 constant_dynamic-slice_fusion.2
  1.6 0.9 constant_dynamic-slice_fusion
  2.5 0.0 copy-start.1
  2.6 1.2 copy-done.1
  3.7 0.7 copy-done.8
  4.4 0.7 copy-done.10
  5.0 1.8 dispatch.1
  6.9 9.0 %all-to-all-start = ((bf16[16,48,896]{2,1,0:T(8,128)(2,1)}), bf16[16,48,896]{2,1,0:T(8,128)(2,1)S(1)}, u32[]{:S(2)}, u32[]{:S(2)}) async-start(bf16[16,48,896]{2,1,0:T(8,128)(2,1)} %dispatch.1), calls=%async_computation | async-start | bytes 2752512 | tf_op jit(solution)/shard_map/all_to_all | solution.py:262
  15.9 1.9 collective-permute-start.1
  17.9 1.4 collective-permute-done.1
  19.2 2.7 %collective-permute-start.5 = (bf16[224,768]{1,0:T(8,128)(2,1)S(1)}, bf16[224,768]{1,0:T(8,128)(2,1)}, u32[]{:S(2)}, u32[]{:S(2)}) collective-permute-start(bf16[224,768]{1,0:T(8,128)(2,1)S(1)} %constant_dynamic-update-slice_fusion.refs_2_), channel_id=1, source_target_pairs={{0,384},{128,0},{256,128},{384,256},{1,385},{129,1},{257,129},{385... | collective-permute-start | bytes 1032200 | tf_op jit(solution)/shard_map/ppermute | solution.py:250
  21.9 4.3 %collective-permute-start.4 = (bf16[224,768]{1,0:T(8,128)(2,1)S(1)}, bf16[224,768]{1,0:T(8,128)(2,1)}, u32[]{:S(2)}, u32[]{:S(2)}) collective-permute-start(bf16[224,768]{1,0:T(8,128)(2,1)S(1)} %constant_dynamic-update-slice_fusion.refs_2_), channel_id=1, source_target_pairs={{0,128},{128,256},{256,384},{384,0},{1,129},{129,257},{257,385},{3... | collective-permute-start | bytes 1032200 | tf_op jit(solution)/shard_map/ppermute | solution.py:250
  26.3 10.0 %collective-permute-start.3 = (bf16[224,768]{1,0:T(8,128)(2,1)S(1)}, bf16[224,768]{1,0:T(8,128)(2,1)S(1)}, u32[]{:S(2)}, u32[]{:S(2)}) collective-permute-start(bf16[224,768]{1,0:T(8,128)(2,1)S(1)} %constant_dynamic-update-slice_fusion.refs_2_), channel_id=1, source_target_pairs={{0,96},{32,0},{64,32},{96,64},{1,97},{33,1},{65,33},{97,65},{2,98}... | collective-permute-start | bytes 1032200 | tf_op jit(solution)/shard_map/ppermute | solution.py:250
  36.3 1.9 collective-permute-start.2
  38.3 0.0 copy-start.6
  38.3 0.7 copy-done.6
  39.0 0.0 collective-permute-done.5.refs_4_
  39.0 11.7 %collective-permute-done.3 = bf16[224,768]{1,0:T(8,128)(2,1)S(1)} collective-permute-done((bf16[224,768]{1,0:T(8,128)(2,1)S(1)}, bf16[224,768]{1,0:T(8,128)(2,1)S(1)}, u32[]{:S(2)}, u32[]{:S(2)}) %collective-permute-start.3) | collective-permute-done | bytes 344096 | tf_op jit(solution)/shard_map/ppermute | solution.py:250
  50.7 17.0 %collective-permute-done.2 = bf16[224,768]{1,0:T(8,128)(2,1)S(1)} collective-permute-done((bf16[224,768]{1,0:T(8,128)(2,1)S(1)}, bf16[224,768]{1,0:T(8,128)(2,1)S(1)}, u32[]{:S(2)}, u32[]{:S(2)}) %collective-permute-start.2) | collective-permute-done | bytes 344096 | tf_op jit(solution)/shard_map/ppermute | solution.py:250
  67.8 1.9 collective-permute-start.8
  69.7 0.8 constant_dynamic-update-slice_fusion.5
  70.5 6.0 %collective-permute-start.9 = (bf16[112,768]{1,0:T(8,128)(2,1)S(1)}, bf16[112,768]{1,0:T(8,128)(2,1)S(1)}, u32[]{:S(2)}, u32[]{:S(2)}) collective-permute-start(bf16[112,768]{1,0:T(8,128)(2,1)S(1)} %slice.33), channel_id=1, source_target_pairs={{0,96},{32,0},{64,32},{96,64},{1,97},{33,1},{65,33},{97,65},{2,98}... | collective-permute-start | bytes 516104 | tf_op jit(solution)/shard_map/ppermute | solution.py:250
  76.5 0.8 constant_dynamic-update-slice_fusion.4
  77.3 0.7 collective-permute-done.8
  78.0 0.7 constant_dynamic-update-slice_fusion.3
  78.6 1.6 collective-permute-done.9
  80.3 0.7 constant_dynamic-update-slice_fusion.2.refs_7_
  80.9 1.9 collective-permute-start.11
  82.9 5.1 %collective-permute-start.10 = (bf16[672,768]{1,0:T(8,128)(2,1)}, bf16[672,768]{1,0:T(8,128)(2,1)S(1)}, u32[]{:S(2)}, u32[]{:S(2)}) collective-permute-start(bf16[672,768]{1,0:T(8,128)(2,1)} %constant_dynamic-update-slice_fusion.2.refs_7_), channel_id=1, source_target_pairs={{0,128},{128,256},{256,384},{384,0},{1,129},{129,257},{257,385},{3... | collective-permute-start | bytes 3096584 | tf_op jit(solution)/shard_map/ppermute | solution.py:250
  88.0 0.0 copy-start.7
  88.0 2.1 collective-permute-start
  90.1 18.7 %collective-permute-done.11.refs_9_ = bf16[672,768]{1,0:T(8,128)(2,1)S(1)} collective-permute-done((bf16[672,768]{1,0:T(8,128)(2,1)}, bf16[672,768]{1,0:T(8,128)(2,1)S(1)}, u32[]{:S(2)}, u32[]{:S(2)}) %collective-permute-start.11) | collective-permute-done | bytes 1032224 | tf_op jit(solution)/shard_map/ppermute | solution.py:250
  108.9 1.9 collective-permute-start.13
  110.9 5.1 %collective-permute-start.12 = (bf16[336,768]{1,0:T(8,128)(2,1)S(1)}, bf16[336,768]{1,0:T(8,128)(2,1)S(1)}, u32[]{:S(2)}, u32[]{:S(2)}) collective-permute-start(bf16[336,768]{1,0:T(8,128)(2,1)S(1)} %slice.40), channel_id=1, source_target_pairs={{0,128},{128,256},{256,384},{384,0},{1,129},{129,257},{257,385},{3... | collective-permute-start | bytes 1548296 | tf_op jit(solution)/shard_map/ppermute | solution.py:250
  116.0 0.9 slice.30
  116.9 0.9 slice.31
  117.9 1.9 collective-permute-start.7
  119.8 5.1 %collective-permute-start.6 = (bf16[112,768]{1,0:T(8,128)(2,1)S(1)}, bf16[112,768]{1,0:T(8,128)(2,1)S(1)}, u32[]{:S(2)}, u32[]{:S(2)}) collective-permute-start(bf16[112,768]{1,0:T(8,128)(2,1)S(1)} %slice.30), channel_id=1, source_target_pairs={{0,128},{128,256},{256,384},{384,0},{1,129},{129,257},{257,385},{3... | collective-permute-start | bytes 516104 | tf_op jit(solution)/shard_map/ppermute | solution.py:250
  124.9 3.4 %collective-permute-done.7.refs_6_ = bf16[112,768]{1,0:T(8,128)(2,1)S(1)} collective-permute-done((bf16[112,768]{1,0:T(8,128)(2,1)S(1)}, bf16[112,768]{1,0:T(8,128)(2,1)S(1)}, u32[]{:S(2)}, u32[]{:S(2)}) %collective-permute-start.7) | collective-permute-done | bytes 172064 | tf_op jit(solution)/shard_map/ppermute | solution.py:250
  128.3 1.2 collective-permute-done.6.refs_5_
  129.6 0.0 collective-permute-done.13.refs_11_
  129.6 0.0 collective-permute-done.12.refs_10_
  129.6 1.2 copy-done.3
  130.8 1.2 copy-done.5
  132.0 11.3 %experts.1 = (bf16[96,3712]{1,0:T(8,128)(2,1)S(1)}, bf16[96,3712]{1,0:T(8,128)(2,1)S(1)}, bf16[896,256]{1,0:T(8,128)(2,1)S(1)}, bf16[896,256]{1,0:T(8,128)(2,1)S...) custom-call(bf16[16,48,896]{2,1,0:T(8,128)(2,1)S(1)} %all-to-all-done.refs_0_, ...), custom_call_target="tpu_custom_call" | custom-call | flops 4000000000 | bytes 12000000 | tf_op jit(solution)/shard_map/experts/pallas_call | solution.py:208
  143.4 1.9 collective-permute-start.14
  145.3 2.1 %collective-permute-done.14.got_ref = bf16[96,3712]{1,0:T(8,128)(2,1)S(1)} collective-permute-done((bf16[96,3712]{1,0:T(8,128)(2,1)S(1)}, bf16[96,3712]{1,0:T(8,128)(2,1)S(1)}, u32[]{:S(2)}, u32[]{:S(2)}) %collective-permute-start.14) | collective-permute-done | bytes 712736 | tf_op jit(solution)/shard_map/ppermute | solution.py:250
  147.4 1.5 combine.1._
  148.9 5.4 %all-to-all-start.1 = ((bf16[16,48,512]{2,1,0:T(8,128)(2,1)}), bf16[16,48,512]{2,1,0:T(8,128)(2,1)S(1)}, u32[]{:S(2)}, u32[]{:S(2)}) async-start(bf16[16,48,512]{2,1,0:T(8,128)(2,1)} %combine.1._), calls=%async_computation.1 | async-start | bytes 1572864 | tf_op jit(solution)/shard_map/all_to_all | solution.py:262
  154.4 1.9 collective-permute-start.16
  156.3 5.6 %collective-permute-start.15 = (bf16[448,256]{1,0:T(8,128)(2,1)S(1)}, bf16[448,256]{1,0:T(8,128)(2,1)S(1)}, u32[]{:S(2)}, u32[]{:S(2)}) collective-permute-start(bf16[448,256]{1,0:T(8,128)(2,1)S(1)} %get-tuple-element.40), channel_id=1, source_target_pairs={{0,128},{128,256},{256,384},{384,0},{1,129},{129,257},{257,385},{3... | collective-permute-start | bytes 688136 | tf_op jit(solution)/shard_map/ppermute | solution.py:250
  162.0 3.7 %collective-permute-done.16.high_ref = bf16[448,256]{1,0:T(8,128)(2,1)S(1)} collective-permute-done((bf16[448,256]{1,0:T(8,128)(2,1)S(1)}, bf16[448,256]{1,0:T(8,128)(2,1)S(1)}, u32[]{:S(2)}, u32[]{:S(2)}) %collective-permute-start.16) | collective-permute-done | bytes 229408 | tf_op jit(solution)/shard_map/ppermute | solution.py:250
  165.6 1.2 collective-permute-done.15.low_ref
  166.8 0.1 relay.1
  166.9 5.6 %collective-permute-start.17 = (bf16[896,256]{1,0:T(8,128)(2,1)S(1)}, bf16[896,256]{1,0:T(8,128)(2,1)S(1)}, u32[]{:S(2)}, u32[]{:S(2)}) collective-permute-start(bf16[896,256]{1,0:T(8,128)(2,1)S(1)} %get-tuple-element.36), channel_id=1, source_target_pairs={{0,128},{128,256},{256,384},{384,0},{1,129},{129,257},{257,385},{3... | collective-permute-start | bytes 1376264 | tf_op jit(solution)/shard_map/ppermute | solution.py:250
  172.6 1.9 collective-permute-start.18
  174.5 7.0 %collective-permute-done.17 = bf16[896,256]{1,0:T(8,128)(2,1)S(1)} collective-permute-done((bf16[896,256]{1,0:T(8,128)(2,1)S(1)}, bf16[896,256]{1,0:T(8,128)(2,1)S(1)}, u32[]{:S(2)}, u32[]{:S(2)}) %collective-permute-start.17) | collective-permute-done | bytes 458784 | tf_op jit(solution)/shard_map/ppermute | solution.py:250
  181.4 5.3 %collective-permute-done.18 = bf16[896,256]{1,0:T(8,128)(2,1)S(1)} collective-permute-done((bf16[896,256]{1,0:T(8,128)(2,1)S(1)}, bf16[896,256]{1,0:T(8,128)(2,1)S(1)}, u32[]{:S(2)}, u32[]{:S(2)}) %collective-permute-start.18) | collective-permute-done | bytes 458784 | tf_op jit(solution)/shard_map/ppermute | solution.py:250
  186.8 1.0 add_convert_fusion
  187.7 4.4 %all-to-all-start.2 = ((bf16[8,112,256]{2,1,0:T(8,128)(2,1)}), bf16[8,112,256]{2,1,0:T(8,128)(2,1)S(1)}, u32[]{:S(2)}, u32[]{:S(2)}) async-start(bf16[8,112,256]{2,1,0:T(8,128)(2,1)} %bitcast.4), calls=%async_computation.2 | async-start | bytes 917504 | tf_op jit(solution)/shard_map/all_to_all | solution.py:262
  192.1 2.0 finish.1
  194.2 14.8 %all-to-all-done.2 = bf16[8,112,256]{2,1,0:T(8,128)(2,1)S(1)} async-done(((bf16[8,112,256]{2,1,0:T(8,128)(2,1)}), bf16[8,112,256]{2,1,0:T(8,128)(2,1)S(1)}, u32[]{:S(2)}, u32[]{:S(2)}) %all-to-all-start.2) | async-done | bytes 458784 | tf_op jit(solution)/shard_map/all_to_all | solution.py:262
  209.0 0.1 reduce_sum.12
  209.1 0.7 pad_maximum_fusion.2
  (30 shorter events, 0.2 us)
Async XLA Ops:
  0.6 1.9 copy-start
  2.5 1.2 copy-start.1
  3.7 0.7 copy-start.8
  4.4 0.7 copy-start.10
  6.9 81.1 %all-to-all-start = ((bf16[16,48,896]{2,1,0:T(8,128)(2,1)}), bf16[16,48,896]{2,1,0:T(8,128)(2,1)S(1)}, u32[]{:S(2)}, u32[]{:S(2)}) async-start(bf16[16,48,896]{2,1,0:T(8,128)(2,1)} %dispatch.1), calls=%async_computation | async-start | bytes 2752512 | tf_op jit(solution)/shard_map/all_to_all | solution.py:262
  15.9 3.3 %collective-permute-start.1 = (bf16[112,768]{1,0:T(8,128)(2,1)S(1)}, bf16[112,768]{1,0:T(8,128)(2,1)S(1)}, u32[]{:S(2)}, u32[]{:S(2)}) collective-permute-start(bf16[112,768]{1,0:T(8,128)(2,1)S(1)} %pad_maximum_fusion.1), channel_id=1, source_target_pairs={{0,16},{16,0},{1,17},{17,1},{2,18},{18,2},{3,19},{19,3},{4,20},{20... | collective-permute-start | bytes 516104 | tf_op jit(solution)/shard_map/ppermute | solution.py:250
  19.2 19.8 %collective-permute-start.5 = (bf16[224,768]{1,0:T(8,128)(2,1)S(1)}, bf16[224,768]{1,0:T(8,128)(2,1)}, u32[]{:S(2)}, u32[]{:S(2)}) collective-permute-start(bf16[224,768]{1,0:T(8,128)(2,1)S(1)} %constant_dynamic-update-slice_fusion.refs_2_), channel_id=1, source_target_pairs={{0,384},{128,0},{256,128},{384,256},{1,385},{129,1},{257,129},{385... | collective-permute-start | bytes 1032200 | tf_op jit(solution)/shard_map/ppermute | solution.py:250
  21.9 17.0 %collective-permute-start.4 = (bf16[224,768]{1,0:T(8,128)(2,1)S(1)}, bf16[224,768]{1,0:T(8,128)(2,1)}, u32[]{:S(2)}, u32[]{:S(2)}) collective-permute-start(bf16[224,768]{1,0:T(8,128)(2,1)S(1)} %constant_dynamic-update-slice_fusion.refs_2_), channel_id=1, source_target_pairs={{0,128},{128,256},{256,384},{384,0},{1,129},{129,257},{257,385},{3... | collective-permute-start | bytes 1032200 | tf_op jit(solution)/shard_map/ppermute | solution.py:250
  26.3 24.4 %collective-permute-start.3 = (bf16[224,768]{1,0:T(8,128)(2,1)S(1)}, bf16[224,768]{1,0:T(8,128)(2,1)S(1)}, u32[]{:S(2)}, u32[]{:S(2)}) collective-permute-start(bf16[224,768]{1,0:T(8,128)(2,1)S(1)} %constant_dynamic-update-slice_fusion.refs_2_), channel_id=1, source_target_pairs={{0,96},{32,0},{64,32},{96,64},{1,97},{33,1},{65,33},{97,65},{2,98}... | collective-permute-start | bytes 1032200 | tf_op jit(solution)/shard_map/ppermute | solution.py:250
  36.3 31.4 %collective-permute-start.2 = (bf16[224,768]{1,0:T(8,128)(2,1)S(1)}, bf16[224,768]{1,0:T(8,128)(2,1)S(1)}, u32[]{:S(2)}, u32[]{:S(2)}) collective-permute-start(bf16[224,768]{1,0:T(8,128)(2,1)S(1)} %constant_dynamic-update-slice_fusion.refs_2_), channel_id=1, source_target_pairs={{0,32},{32,64},{64,96},{96,0},{1,33},{33,65},{65,97},{97,1},{2,34}... | collective-permute-start | bytes 1032200 | tf_op jit(solution)/shard_map/ppermute | solution.py:250
  38.3 0.7 copy-start.6
  67.8 10.2 %collective-permute-start.8 = (bf16[112,768]{1,0:T(8,128)(2,1)S(1)}, bf16[112,768]{1,0:T(8,128)(2,1)S(1)}, u32[]{:S(2)}, u32[]{:S(2)}) collective-permute-start(bf16[112,768]{1,0:T(8,128)(2,1)S(1)} %slice.32), channel_id=1, source_target_pairs={{0,32},{32,64},{64,96},{96,0},{1,33},{33,65},{65,97},{97,1},{2,34}... | collective-permute-start | bytes 516104 | tf_op jit(solution)/shard_map/ppermute | solution.py:250
  70.5 9.8 %collective-permute-start.9 = (bf16[112,768]{1,0:T(8,128)(2,1)S(1)}, bf16[112,768]{1,0:T(8,128)(2,1)S(1)}, u32[]{:S(2)}, u32[]{:S(2)}) collective-permute-start(bf16[112,768]{1,0:T(8,128)(2,1)S(1)} %slice.33), channel_id=1, source_target_pairs={{0,96},{32,0},{64,32},{96,64},{1,97},{33,1},{65,33},{97,65},{2,98}... | collective-permute-start | bytes 516104 | tf_op jit(solution)/shard_map/ppermute | solution.py:250
  80.9 27.9 %collective-permute-start.11 = (bf16[672,768]{1,0:T(8,128)(2,1)}, bf16[672,768]{1,0:T(8,128)(2,1)S(1)}, u32[]{:S(2)}, u32[]{:S(2)}) collective-permute-start(bf16[672,768]{1,0:T(8,128)(2,1)} %constant_dynamic-update-slice_fusion.2.refs_7_), channel_id=1, source_target_pairs={{0,384},{128,0},{256,128},{384,256},{1,385},{129,1},{257,129},{385... | collective-permute-start | bytes 3096584 | tf_op jit(solution)/shard_map/ppermute | solution.py:250
  82.9 27.9 %collective-permute-start.10 = (bf16[672,768]{1,0:T(8,128)(2,1)}, bf16[672,768]{1,0:T(8,128)(2,1)S(1)}, u32[]{:S(2)}, u32[]{:S(2)}) collective-permute-start(bf16[672,768]{1,0:T(8,128)(2,1)} %constant_dynamic-update-slice_fusion.2.refs_7_), channel_id=1, source_target_pairs={{0,128},{128,256},{256,384},{384,0},{1,129},{129,257},{257,385},{3... | collective-permute-start | bytes 3096584 | tf_op jit(solution)/shard_map/ppermute | solution.py:250
  88.0 41.6 %copy-start.7 = (bf16[224,768]{1,0:T(8,128)(2,1)S(1)}, bf16[224,768]{1,0:T(8,128)(2,1)}, u32[]{:S(2)}) copy-start(bf16[224,768]{1,0:T(8,128)(2,1)} %copy-done.6) | copy-start | bytes 1032196
  88.0 41.6 %collective-permute-start = (bf16[16,48,896]{2,1,0:T(8,128)(2,1)S(1)}, bf16[16,48,896]{2,1,0:T(8,128)(2,1)S(1)}, u32[]{:S(2)}, u32[]{:S(2)}) collective-permute-start(bf16[16,48,896]{2,1,0:T(8,128)(2,1)S(1)} %all-to-all-done.refs_0_), channel_id=1, source_target_pairs={{0,16},{16,0},{1,17},{17,1},{2,18},{18,2},{3,19},{19,3},{4,20},{20... | collective-permute-start | bytes 4128776 | tf_op jit(solution)/shard_map/ppermute | solution.py:250
  108.8 9.0 %copy-start.2 = (bf16[672,768]{1,0:T(8,128)(2,1)}, bf16[672,768]{1,0:T(8,128)(2,1)S(1)}, u32[]{:S(2)}) copy-start(bf16[672,768]{1,0:T(8,128)(2,1)S(1)} %collective-permute-done.11.refs_9_) | copy-start | bytes 3096580
  108.9 20.7 %collective-permute-start.13 = (bf16[336,768]{1,0:T(8,128)(2,1)S(1)}, bf16[336,768]{1,0:T(8,128)(2,1)S(1)}, u32[]{:S(2)}, u32[]{:S(2)}) collective-permute-start(bf16[336,768]{1,0:T(8,128)(2,1)S(1)} %slice.41), channel_id=1, source_target_pairs={{0,384},{128,0},{256,128},{384,256},{1,385},{129,1},{257,129},{385... | collective-permute-start | bytes 1548296 | tf_op jit(solution)/shard_map/ppermute | solution.py:250
  110.8 18.8 %copy-start.4 = (bf16[672,768]{1,0:T(8,128)(2,1)}, bf16[672,768]{1,0:T(8,128)(2,1)S(1)}, u32[]{:S(2)}) copy-start(bf16[672,768]{1,0:T(8,128)(2,1)S(1)} %collective-permute-done.10.refs_8_) | copy-start | bytes 3096580
  110.9 18.7 %collective-permute-start.12 = (bf16[336,768]{1,0:T(8,128)(2,1)S(1)}, bf16[336,768]{1,0:T(8,128)(2,1)S(1)}, u32[]{:S(2)}, u32[]{:S(2)}) collective-permute-start(bf16[336,768]{1,0:T(8,128)(2,1)S(1)} %slice.40), channel_id=1, source_target_pairs={{0,128},{128,256},{256,384},{384,0},{1,129},{129,257},{257,385},{3... | collective-permute-start | bytes 1548296 | tf_op jit(solution)/shard_map/ppermute | solution.py:250
  117.9 10.4 %collective-permute-start.7 = (bf16[112,768]{1,0:T(8,128)(2,1)S(1)}, bf16[112,768]{1,0:T(8,128)(2,1)S(1)}, u32[]{:S(2)}, u32[]{:S(2)}) collective-permute-start(bf16[112,768]{1,0:T(8,128)(2,1)S(1)} %slice.31), channel_id=1, source_target_pairs={{0,384},{128,0},{256,128},{384,256},{1,385},{129,1},{257,129},{385... | collective-permute-start | bytes 516104 | tf_op jit(solution)/shard_map/ppermute | solution.py:250
  119.8 9.8 %collective-permute-start.6 = (bf16[112,768]{1,0:T(8,128)(2,1)S(1)}, bf16[112,768]{1,0:T(8,128)(2,1)S(1)}, u32[]{:S(2)}, u32[]{:S(2)}) collective-permute-start(bf16[112,768]{1,0:T(8,128)(2,1)S(1)} %slice.30), channel_id=1, source_target_pairs={{0,128},{128,256},{256,384},{384,0},{1,129},{129,257},{257,385},{3... | collective-permute-start | bytes 516104 | tf_op jit(solution)/shard_map/ppermute | solution.py:250
  129.6 1.2 copy-start.3
  130.8 1.2 copy-start.5
  143.4 4.1 %collective-permute-start.14 = (bf16[96,3712]{1,0:T(8,128)(2,1)S(1)}, bf16[96,3712]{1,0:T(8,128)(2,1)S(1)}, u32[]{:S(2)}, u32[]{:S(2)}) collective-permute-start(bf16[96,3712]{1,0:T(8,128)(2,1)S(1)} %get-tuple-element.29), channel_id=1, source_target_pairs={{0,16},{16,0},{1,17},{17,1},{2,18},{18,2},{3,19},{19,3},{4,20},{20... | collective-permute-start | bytes 2138120 | tf_op jit(solution)/shard_map/ppermute | solution.py:250
  148.9 38.8 %all-to-all-start.1 = ((bf16[16,48,512]{2,1,0:T(8,128)(2,1)}), bf16[16,48,512]{2,1,0:T(8,128)(2,1)S(1)}, u32[]{:S(2)}, u32[]{:S(2)}) async-start(bf16[16,48,512]{2,1,0:T(8,128)(2,1)} %combine.1._), calls=%async_computation.1 | async-start | bytes 1572864 | tf_op jit(solution)/shard_map/all_to_all | solution.py:262
  154.4 11.2 %collective-permute-start.16 = (bf16[448,256]{1,0:T(8,128)(2,1)S(1)}, bf16[448,256]{1,0:T(8,128)(2,1)S(1)}, u32[]{:S(2)}, u32[]{:S(2)}) collective-permute-start(bf16[448,256]{1,0:T(8,128)(2,1)S(1)} %get-tuple-element.39), channel_id=1, source_target_pairs={{0,384},{128,0},{256,128},{384,256},{1,385},{129,1},{257,129},{385... | collective-permute-start | bytes 688136 | tf_op jit(solution)/shard_map/ppermute | solution.py:250
  156.3 10.5 %collective-permute-start.15 = (bf16[448,256]{1,0:T(8,128)(2,1)S(1)}, bf16[448,256]{1,0:T(8,128)(2,1)S(1)}, u32[]{:S(2)}, u32[]{:S(2)}) collective-permute-start(bf16[448,256]{1,0:T(8,128)(2,1)S(1)} %get-tuple-element.40), channel_id=1, source_target_pairs={{0,128},{128,256},{256,384},{384,0},{1,129},{129,257},{257,385},{3... | collective-permute-start | bytes 688136 | tf_op jit(solution)/shard_map/ppermute | solution.py:250
  166.9 14.5 %collective-permute-start.17 = (bf16[896,256]{1,0:T(8,128)(2,1)S(1)}, bf16[896,256]{1,0:T(8,128)(2,1)S(1)}, u32[]{:S(2)}, u32[]{:S(2)}) collective-permute-start(bf16[896,256]{1,0:T(8,128)(2,1)S(1)} %get-tuple-element.36), channel_id=1, source_target_pairs={{0,128},{128,256},{256,384},{384,0},{1,129},{129,257},{257,385},{3... | collective-permute-start | bytes 1376264 | tf_op jit(solution)/shard_map/ppermute | solution.py:250
  172.6 14.2 %collective-permute-start.18 = (bf16[896,256]{1,0:T(8,128)(2,1)S(1)}, bf16[896,256]{1,0:T(8,128)(2,1)S(1)}, u32[]{:S(2)}, u32[]{:S(2)}) collective-permute-start(bf16[896,256]{1,0:T(8,128)(2,1)S(1)} %get-tuple-element.37), channel_id=1, source_target_pairs={{0,384},{128,0},{256,128},{384,256},{1,385},{129,1},{257,129},{385... | collective-permute-start | bytes 1376264 | tf_op jit(solution)/shard_map/ppermute | solution.py:250
  186.8 5.4 %copy-start.9 = (s32[128,1]{0,1:T(1,128)S(1)}, s32[128,1]{0,1:T(1,128)}, u32[]{:S(2)}) copy-start(s32[128,1]{0,1:T(1,128)} %param.9) | copy-start | bytes 1540
  186.8 5.4 %copy-start.11 = (f32[128,1]{0,1:T(1,128)S(1)}, f32[128,1]{0,1:T(1,128)}, u32[]{:S(2)}) copy-start(f32[128,1]{0,1:T(1,128)} %param.10) | copy-start | bytes 1540
  187.7 21.3 %all-to-all-start.2 = ((bf16[8,112,256]{2,1,0:T(8,128)(2,1)}), bf16[8,112,256]{2,1,0:T(8,128)(2,1)S(1)}, u32[]{:S(2)}, u32[]{:S(2)}) async-start(bf16[8,112,256]{2,1,0:T(8,128)(2,1)} %bitcast.4), calls=%async_computation.2 | async-start | bytes 917504 | tf_op jit(solution)/shard_map/all_to_all | solution.py:262

commit v4 on v3

--- a/solution.py
+++ b/solution.py
@@ -24,7 +24,8 @@
 ROWS = PEERS * CAP
 PIECE = 512
 WIDE = D + 128
-VMEM_LIMIT = 28 * 1024 * 1024
+VMEM_LIMIT = 16 * 1024 * 1024
+MOST_VMEM = 56 * 1024 * 1024
 VMEM = pl.BlockSpec(memory_space=pltpu.VMEM)
 
 
@@ -73,9 +74,7 @@
         rows = jnp.dot(sel, jnp.concatenate(stack, axis=0), preferred_element_type=F32)
         halves.append(rows.reshape(EXPERTS, 24, CHUNK))
     rows = jnp.concatenate(halves, axis=1).astype(BF)
-    for e in range(EXPERTS):
-        out_ref[2 * e] = rows[e]
-        out_ref[2 * e + 1] = rows[e]
+    out_ref[...] = rows
 
 
 def dispatch(ids, weight, tokens, grads):
@@ -83,7 +82,7 @@
         dispatch_kernel,
         in_specs=[VMEM] * 4,
         out_specs=VMEM,
-        out_shape=jax.ShapeDtypeStruct((PEERS, SLAB, CHUNK), BF),
+        out_shape=jax.ShapeDtypeStruct((EXPERTS, SLAB, CHUNK), BF),
         compiler_params=pltpu.CompilerParams(vmem_limit_bytes=VMEM_LIMIT),
         cost_estimate=pl.CostEstimate(flops=4 * 10**8, bytes_accessed=4 * 10**6, transcendentals=0),
         name="dispatch",
@@ -98,7 +97,7 @@
         rows = total[half * SLAB:(half + 1) * SLAB]
         stack = jnp.concatenate([rows[:, q * PIECE:(q + 1) * PIECE] for q in range(8)], axis=0)
         moved = jnp.dot(order, stack, preferred_element_type=F32).astype(BF)
-        out_ref[half * 8:(half + 1) * 8] = moved.reshape(8, SLAB, PIECE)
+        out_ref[:, half] = moved.reshape(EXPERTS, SLAB, PIECE)
 
 
 def combine(keep, got):
@@ -106,7 +105,7 @@
         combine_kernel,
         in_specs=[VMEM] * 2,
         out_specs=VMEM,
-        out_shape=jax.ShapeDtypeStruct((PEERS, SLAB, PIECE), BF),
+        out_shape=jax.ShapeDtypeStruct((EXPERTS, 2, SLAB, PIECE), BF),
         compiler_params=pltpu.CompilerParams(vmem_limit_bytes=VMEM_LIMIT),
         cost_estimate=pl.CostEstimate(flops=3 * 10**8, bytes_accessed=2 * 10**6, transcendentals=0),
         name="combine",
@@ -141,41 +140,84 @@
     )(ids, weight, rows)
 
 
-def expert_kernel(pieces, *refs):
-    row_refs = refs[:2]
+def unpack_kernel(*refs):
+    row_refs, x_ref, g_ref = refs[:4], refs[4], refs[5]
+    zl = lax.axis_index("zl")
+    order = regroup()
+    for i, ref in enumerate(row_refs):
+        moved = jnp.dot(order, ref[...].reshape(GROUP, CHUNK), preferred_element_type=F32).astype(BF)
+        group = 2 * (i // 2) + (zl if i % 2 == 0 else 1 - zl)
+        rows = pl.ds(pl.multiple_of(group * SLAB, SLAB), SLAB)
+        for q in range(4):
+            columns = pl.ds(q * CHUNK, CHUNK)
+            x_ref[rows, columns] = moved[2 * q * SLAB:(2 * q + 1) * SLAB]
+            g_ref[rows, columns] = moved[(2 * q + 1) * SLAB:(2 * q + 2) * SLAB]
+
+
+def unpack(*rows):
+    dense = jax.ShapeDtypeStruct((2 * ROWS, D), BF)
+    return pl.pallas_call(
+        unpack_kernel,
+        in_specs=[VMEM] * 4,
+        out_specs=[VMEM] * 2,
+        out_shape=[dense, dense],
+        compiler_params=pltpu.CompilerParams(vmem_limit_bytes=VMEM_LIMIT),
+        cost_estimate=pl.CostEstimate(flops=10**9, bytes_accessed=5 * 10**6, transcendentals=0),
+        name="unpack",
+    )(*rows)
+
+
+def stack_kernel(before_ref, after_ref, low_ref, high_ref, wide_ref, down_ref):
+    at = 0
+    for ref in (before_ref, after_ref, low_ref, high_ref):
+        n = ref.shape[0]
+        wide_ref[at:at + n] = ref[:, :2 * QUART]
+        down_ref[at:at + n] = ref[:, 2 * QUART:]
+        at += n
+
+
+def stack(*parts):
+    n = 6 * SHARD
+    return pl.pallas_call(
+        stack_kernel,
+        in_specs=[VMEM] * 4,
+        out_specs=[VMEM] * 2,
+        out_shape=[jax.ShapeDtypeStruct((n, 2 * QUART), BF), jax.ShapeDtypeStruct((n, QUART), BF)],
+        compiler_params=pltpu.CompilerParams(vmem_limit_bytes=VMEM_LIMIT),
+        cost_estimate=pl.CostEstimate(flops=10**6, bytes_accessed=2 * 10**6, transcendentals=0),
+        name="stack",
+    )(*parts)
+
+
+def hidden_kernel(pieces, *refs):
+    x_ref, g_ref = refs[:2]
     weight_refs = refs[2:2 + len(pieces)]
-    keep_ref, send_ref, far_ref, plus_ref, minus_ref, own_ref = refs[2 + len(pieces):8 + len(pieces)]
-    raw, x_rows, g_rows, weights, sem_rows, sem_weights = refs[8 + len(pieces):]
+    wide_ref, d_ref, line_ref, far_ref, plus_ref, minus_ref, own_ref, down, sems = refs[2 + len(pieces):]
     xi, zi, ci = lax.axis_index("x"), lax.axis_index("zh"), lax.axis_index("c")
-    row_copies = [pltpu.make_async_copy(ref, raw.at[i], sem_rows.at[i]) for i, ref in enumerate(row_refs)]
-    weight_copies = []
+    copies = []
+
+    def copy(source, target):
+        copies.append(pltpu.make_async_copy(source, target, sems.at[len(copies)]))
+
     for ref, listed in zip(weight_refs, pieces):
-        for at, (dx, dz, which) in enumerate(listed):
-            block = lax.rem(xi + dx, 4) * 4 + lax.rem(zi + dz, 4)
+        for at, (kind, dx, dz, which) in enumerate(listed):
+            x = dx if kind == "fixed" else lax.rem(xi + dx, 4)
             core = ci if which == 0 else 1 - ci
-            start = pl.multiple_of(block * BLOCK + core * SHARD, 16)
-            weight_copies.append(pltpu.make_async_copy(
-                ref.at[pl.ds(at * SHARD, SHARD)],
-                weights.at[pl.ds(start, SHARD)],
-                sem_weights.at[len(weight_copies)],
-            ))
-    for copy in row_copies + weight_copies:
-        copy.start()
-    order = regroup()
-    for i, copy in enumerate(row_copies):
-        copy.wait()
-        for half in range(2):
-            part = raw[i, half * 8:(half + 1) * 8].reshape(GROUP, CHUNK)
-            moved = jnp.dot(order, part, preferred_element_type=F32).astype(BF)
-            at = (2 * i + half) * SLAB
-            for q in range(4):
-                columns = pl.ds(q * CHUNK, CHUNK)
-                x_rows[at:at + SLAB, columns] = moved[2 * q * SLAB:(2 * q + 1) * SLAB]
-                g_rows[at:at + SLAB, columns] = moved[(2 * q + 1) * SLAB:(2 * q + 2) * SLAB]
-    for copy in weight_copies:
-        copy.wait()
-    pre = jnp.dot(x_rows[...], weights[:, :2 * QUART], preferred_element_type=F32)
-    grad = jnp.dot(g_rows[...], weights[:, 2 * QUART:], preferred_element_type=F32)
+            rows = pl.ds(pl.multiple_of((x * 4 + lax.rem(zi + dz, 4)) * BLOCK + core * SHARD, 16), SHARD)
+            source = ref.at[pl.ds(at * SHARD, SHARD)]
+            if ref.shape[1] == QUART:
+                copy(source, down.at[rows])
+            elif ref.shape[1] == 2 * QUART:
+                copy(source, wide_ref.at[rows])
+            else:
+                copy(source.at[:, pl.ds(0, 2 * QUART)], wide_ref.at[rows])
+                copy(source.at[:, pl.ds(2 * QUART, QUART)], down.at[rows])
+    for one in copies:
+        one.start()
+    for one in copies:
+        one.wait()
+    pre = jnp.dot(x_ref[...], wide_ref[...], preferred_element_type=F32)
+    grad = jnp.dot(g_ref[...], down[...], preferred_element_type=F32)
     gate, up = pre[:, :QUART], pre[:, QUART:]
     sig = jax.nn.sigmoid(gate)
     act = gate * sig
@@ -185,43 +227,55 @@
     for ref, shift in ((far_ref, 2), (plus_ref, 1), (minus_ref, 3), (own_ref, 0)):
         start = pl.multiple_of(lax.rem(xi + shift, 4) * XROWS, 128)
         ref[...] = lax.dot_general(
-            g_rows[:, pl.ds(start, XROWS)], hidden, (((0,), (0,)), ((), ())), preferred_element_type=F32
+            g_ref[:, pl.ds(start, XROWS)], hidden, (((0,), (0,)), ((), ())), preferred_element_type=F32
         ).astype(BF)
-    d_pre = jnp.concatenate([(grad * up * slope).astype(BF), (grad * act).astype(BF)], axis=1)
+    d_ref[...] = jnp.concatenate([(grad * up * slope).astype(BF), (grad * act).astype(BF)], axis=1)
+    line_ref[...] = jnp.where(iota((2 * ROWS, 128), 1) == 0, route, 0.0).astype(BF)
+
+
+def hidden_compute(x_rows, g_rows, blocks, pieces):
+    anywhere = pl.BlockSpec(memory_space=pl.ANY)
+    count = sum(len(p) * (2 if b.shape[1] == 3 * QUART else 1) for p, b in zip(pieces, blocks))
+    down = jax.ShapeDtypeStruct((XROWS, QUART), BF)
+    return pl.pallas_call(
+        lambda *refs: hidden_kernel(pieces, *refs),
+        in_specs=[VMEM] * 2 + [anywhere] * len(blocks),
+        out_specs=[VMEM] * 7,
+        out_shape=[
+            jax.ShapeDtypeStruct((D, 2 * QUART), BF),
+            jax.ShapeDtypeStruct((2 * ROWS, 2 * QUART), BF),
+            jax.ShapeDtypeStruct((2 * ROWS, 128), BF),
+            down, down, down, down,
+        ],
+        scratch_shapes=[pltpu.VMEM((D, QUART), BF), pltpu.SemaphoreType.DMA((count,))],
+        compiler_params=pltpu.CompilerParams(vmem_limit_bytes=MOST_VMEM),
+        cost_estimate=pl.CostEstimate(flops=2 * 10**9, bytes_accessed=12 * 10**6, transcendentals=49152),
+        name="hidden",
+    )(x_rows, g_rows, *blocks)
+
+
+def inputs_kernel(d_ref, line_ref, wide_ref, keep_ref, send_ref):
     for i in range(4):
         part = lax.dot_general(
-            d_pre, weights[i * CHUNK:(i + 1) * CHUNK, :2 * QUART], (((1,), (1,)), ((), ())),
-            preferred_element_type=F32,
+            d_ref[...], wide_ref[i * CHUNK:(i + 1) * CHUNK], (((1,), (1,)), ((), ())), preferred_element_type=F32
         ).astype(BF)
         keep_ref[:, i * CHUNK:(i + 1) * CHUNK] = part[:ROWS]
         send_ref[:, i * CHUNK:(i + 1) * CHUNK] = part[ROWS:]
-    line = jnp.where(iota((2 * ROWS, 128), 1) == 0, route, 0.0).astype(BF)
-    keep_ref[:, D:] = line[:ROWS]
-    send_ref[:, D:] = line[ROWS:]
-
-
-def expert_compute(rows, blocks, pieces):
-    anywhere = pl.BlockSpec(memory_space=pl.ANY)
-    count = sum(len(p) for p in pieces)
+    keep_ref[:, D:] = line_ref[:ROWS]
+    send_ref[:, D:] = line_ref[ROWS:]
+
+
+def inputs_compute(d_pre, line, wide):
     back = jax.ShapeDtypeStruct((ROWS, WIDE), BF)
-    down = jax.ShapeDtypeStruct((XROWS, QUART), BF)
-    return pl.pallas_call(
-        lambda *refs: expert_kernel(pieces, *refs),
-        in_specs=[anywhere] * (2 + len(blocks)),
-        out_specs=[VMEM] * 6,
-        out_shape=[back, back, down, down, down, down],
-        scratch_shapes=[
-            pltpu.VMEM((2, PEERS, SLAB, CHUNK), BF),
-            pltpu.VMEM((2 * ROWS, D), BF),
-            pltpu.VMEM((2 * ROWS, D), BF),
-            pltpu.VMEM((D, 3 * QUART), BF),
-            pltpu.SemaphoreType.DMA((2,)),
-            pltpu.SemaphoreType.DMA((count,)),
-        ],
-        compiler_params=pltpu.CompilerParams(vmem_limit_bytes=VMEM_LIMIT),
-        cost_estimate=pl.CostEstimate(flops=4 * 10**9, bytes_accessed=12 * 10**6, transcendentals=49152),
-        name="experts",
-    )(*rows, *blocks)
+    return pl.pallas_call(
+        inputs_kernel,
+        in_specs=[VMEM] * 3,
+        out_specs=[VMEM] * 2,
+        out_shape=[back, back],
+        compiler_params=pltpu.CompilerParams(vmem_limit_bytes=VMEM_LIMIT),
+        cost_estimate=pl.CostEstimate(flops=7 * 10**8, bytes_accessed=6 * 10**6, transcendentals=0),
+        name="inputs",
+    )(d_pre, line, wide)
 
 
 def relay_kernel(plus_ref, minus_ref, low_ref, high_ref, _, plus_out, minus_out):
@@ -273,34 +327,36 @@
 
     theirs = hop(columns(1 - ci), "c", 1)
     sent = dispatch(ids, share, tokens, grad_out)
-    mine, sent = tie(columns(ci), sent)
-    own = jnp.concatenate([mine, theirs], axis=0)
-
+    own = jnp.concatenate([columns(ci), theirs], axis=0)
+
+    own_all = lax.all_gather(own, "x", axis=0, tiled=True)
     z_before, z_after = hop(own, "zh", 1), hop(own, "zh", -1)
-    x_before, x_after = hop(own, "x", 1), hop(own, "x", -1)
-    z_before, z_after, x_before, x_after = tie(z_before, z_after, x_before, x_after)
     z_low, z_high = hop(z_before[:SHARD], "zh", 1), hop(z_after[SHARD:], "zh", -1)
-    x_low, x_high = hop(x_before[:SHARD], "x", 1), hop(x_after[SHARD:], "x", -1)
-    rest = jnp.concatenate([z_before, z_after, z_low, z_high], axis=0)
+    rest, rest_down = stack(z_before, z_after, z_low, z_high)
+    down_all = lax.all_gather(rest_down, "x", axis=0, tiled=True)
     r_before, r_after = hop(rest, "x", 1), hop(rest, "x", -1)
     half = 3 * SHARD
     r_low, r_high = hop(r_before[:half], "x", 1), hop(r_after[half:], "x", -1)
 
-    across = [(0, 3, 0), (0, 3, 1), (0, 1, 0), (0, 1, 1), (0, 2, 0), (0, 2, 1)]
-    moved = lambda dx, listed: [(dx, dz, w) for _, dz, w in listed]
-    pair = [(0, 0, 0), (0, 0, 1)]
-    blocks = [own, x_before, x_after, x_low, x_high, rest, r_before, r_after, r_low, r_high]
+    across = [(3, 0), (3, 1), (1, 0), (1, 1), (2, 0), (2, 1)]
+    listed = lambda kind, dx, shards: [(kind, dx, dz, w) for dz, w in shards]
+    blocks = [own_all, down_all, rest, r_before, r_after, r_low, r_high]
     pieces = [
-        pair, moved(3, pair), moved(1, pair), moved(2, pair[:1]), moved(2, pair[1:]),
-        across, moved(3, across), moved(1, across), moved(2, across[:3]), moved(2, across[3:]),
+        sum([listed("fixed", x, [(0, 0), (0, 1)]) for x in range(4)], []),
+        sum([listed("fixed", x, across) for x in range(4)], []),
+        listed("moved", 0, across), listed("moved", 3, across), listed("moved", 1, across),
+        listed("moved", 2, across[:3]), listed("moved", 2, across[3:]),
     ]
 
-    rows = exchange(sent, ("y", "zl"))
-    keep, send, far, plus, minus, mine = expert_compute([rows, hop(rows, "c", 1)], blocks, pieces)
-
-    far, got = tie(far, hop(send, "c", 1))
+    rows = exchange(sent, "y")
+    rows = tie(rows, rest)[0]
+    rows_zl = hop(rows, "zl", 1)
+    x_rows, g_rows = unpack(rows, rows_zl, hop(rows, "c", 1), hop(rows_zl, "c", 1))
+    wide, d_pre, line, far, plus, minus, mine = hidden_compute(x_rows, g_rows, blocks, pieces)
+    keep, send = inputs_compute(d_pre, line, wide)
+
     low, high = hop(far[:XROWS // 2], "x", 1), hop(far[XROWS // 2:], "x", -1)
-    message = combine(keep, got)
+    message = combine(keep, hop(send, "c", 1)).reshape(PEERS, SLAB, PIECE)
     back = exchange(message, ("y", "zl"))
     token_grad, route_grad = finish(ids, share, back.reshape(PEERS * SLAB, PIECE))
 

time: 211 us -> 221 us (1.047)
  blocking collectives: 0 us -> 19.4 us
  between operations: 1.02 us -> 14.5 us
  starting transfers between devices: 87.9 us -> 74.9 us
  waiting for transfers between devices: 89.9 us -> 83.9 us
  local copies, waits for them, and re-layouts: 12.4 us -> 8.18 us
    all_to_all x0 -> x1, blocking collectives: none -> 19.4 us  [exchange(): return lax.all_to_all(a, axes, split_axis=0, concat_axis=0, tiled=True)]
    ppermute x19 -> x17, waiting for transfers between devices: 75.1 us -> 62 us  [hop(): return lax.ppermute(a, axis, [(i, (i + shift) % n) for i in range(n)])]
    ppermute x19 -> x17, starting transfers between devices: 69.1 us -> 60.6 us  [hop(): return lax.ppermute(a, axis, [(i, (i + shift) % n) for i in range(n)])]
    all_to_all x3 -> x2, waiting for transfers between devices: 14.9 us -> 21.9 us  [exchange(): return lax.all_to_all(a, axes, split_axis=0, concat_axis=0, tiled=True)]
    all_to_all x3 -> x2, starting transfers between devices: 18.8 us -> 14.2 us  [exchange(): return lax.all_to_all(a, axes, split_axis=0, concat_axis=0, tiled=True)]
    unnamed x28 -> x36, local copies, waits for them, and re-layouts: 7.89 us -> 6.16 us
    pallas_call x1 -> x4, Pallas kernels: 11.3 us -> 12.3 us  [the longest x1 8.51 us: hidden_compute(): pl.pallas_call(lambda *refs: hidden_kernel(pieces, *refs), in_specs=[VMEM...]
  transfers between devices with their start and end apart: 22 -> 21, of which waited for: 14 -> 13; matrix products, arithmetic and copies ran while one was open for 3% -> 0% of each run, Pallas kernels for 1% -> 3%
where the time goes in v4:
time: 221 us; the launch traced here: 220 us
  waiting for transfers between devices  83.9 us (38%)
  starting transfers between devices  74.9 us (34%)
  blocking collectives  19.4 us (9%)
  Pallas kernels  17.5 us (8%)
  between operations  14.5 us (7%)
  local copies, waits for them, and re-layouts  8.18 us (4%)
    ppermute x17, waiting for transfers between devices, hop(): return lax.ppermute(a, axis, [(i, (i + shift) % n) for i in range(n)])  62 us
    ppermute x17, starting transfers between devices, hop(): return lax.ppermute(a, axis, [(i, (i + shift) % n) for i in range(n)])  60.6 us
    all_to_all x2, waiting for transfers between devices, exchange(): return lax.all_to_all(a, axes, split_axis=0, concat_axis=0, tiled=True)  21.9 us
    all_to_all x1, blocking collectives, exchange(): return lax.all_to_all(a, axes, split_axis=0, concat_axis=0, tiled=True)  19.4 us
    all_to_all x2, starting transfers between devices, exchange(): return lax.all_to_all(a, axes, split_axis=0, concat_axis=0, tiled=True)  14.2 us
    pallas_call x1, Pallas kernels, hidden_compute(): pl.pallas_call(lambda *refs: hidden_kernel(pieces, *refs), in_specs=[VMEM...  8.51 us
    unnamed x36, local copies, waits for them, and re-layouts  6.16 us
  transfers between devices with their start and end apart: 21, of which 13 were waited for; matrix products, arithmetic and copies ran while one was open for 0% of the time, Pallas kernels for 3%

profile of v4, /device:TPU:6, one launch (start us, length us, event | category | flops | bytes accessed | tf_op | source)
XLA Modules:
  0.0 220.0 jit_solution(11731783173726106712)
XLA Ops:
  7.2 0.0 copy-start.11
  7.2 0.0 all-gather.3.cloned.1.call-start
  7.3 1.0 constant_dynamic-slice_fusion.5
  8.2 0.9 constant_dynamic-slice_fusion.3
  9.2 1.9 collective-permute-start
  11.1 1.4 collective-permute-done
  12.5 0.7 pad_maximum_fusion
  13.2 0.0 all-gather.3.cloned.1.call-update
  13.3 1.6 dispatch.1
  14.9 7.1 %all-to-all-start = ((bf16[8,48,896]{2,1,0:T(8,128)(2,1)}), bf16[8,48,896]{2,1,0:T(8,128)(2,1)S(1)}, u32[]{:S(2)}, u32[]{:S(2)}) async-start(bf16[8,48,896]{2,1,0:T(8,128)(2,1)} %dispatch.1), calls=%async_computation | async-start | bytes 1376256 | tf_op jit(solution)/shard_map/all_to_all | solution.py:316
  22.0 0.0 all-gather.5.cloned.1.call-start
  22.0 10.9 %collective-permute-start.2 = (bf16[224,768]{1,0:T(8,128)(2,1)S(1)}, bf16[224,768]{1,0:T(8,128)(2,1)S(1)}, u32[]{:S(2)}, u32[]{:S(2)}) collective-permute-start(bf16[224,768]{1,0:T(8,128)(2,1)S(1)} %copy-done.14), channel_id=1, source_target_pairs={{0,96},{32,0},{64,32},{96,64},{1,97},{33,1},{65,33},{97,65},{2,98}... | collective-permute-start | bytes 1032200 | tf_op jit(solution)/shard_map/ppermute | solution.py:304
  33.0 1.9 collective-permute-start.1
  34.9 12.8 %collective-permute-done.2.after_ref = bf16[224,768]{1,0:T(8,128)(2,1)S(1)} collective-permute-done((bf16[224,768]{1,0:T(8,128)(2,1)S(1)}, bf16[224,768]{1,0:T(8,128)(2,1)S(1)}, u32[]{:S(2)}, u32[]{:S(2)}) %collective-permute-start.2) | collective-permute-done | bytes 344096 | tf_op jit(solution)/shard_map/ppermute | solution.py:304
  47.7 6.5 %collective-permute-start.4 = (bf16[112,768]{1,0:T(8,128)(2,1)S(1)}, bf16[112,768]{1,0:T(8,128)(2,1)S(1)}, u32[]{:S(2)}, u32[]{:S(2)}) collective-permute-start(bf16[112,768]{1,0:T(8,128)(2,1)S(1)} %slice.33), channel_id=1, source_target_pairs={{0,96},{32,0},{64,32},{96,64},{1,97},{33,1},{65,33},{97,65},{2,98}... | collective-permute-start | bytes 516104 | tf_op jit(solution)/shard_map/ppermute | solution.py:304
  54.2 0.0 collective-permute-done.1.before_ref
  54.3 1.9 collective-permute-start.3
  56.2 3.0 %collective-permute-done.4.high_ref = bf16[112,768]{1,0:T(8,128)(2,1)S(1)} collective-permute-done((bf16[112,768]{1,0:T(8,128)(2,1)S(1)}, bf16[112,768]{1,0:T(8,128)(2,1)S(1)}, u32[]{:S(2)}, u32[]{:S(2)}) %collective-permute-start.4) | collective-permute-done | bytes 172064 | tf_op jit(solution)/shard_map/ppermute | solution.py:304
  59.2 7.7 %collective-permute-done.3.low_ref = bf16[112,768]{1,0:T(8,128)(2,1)S(1)} collective-permute-done((bf16[112,768]{1,0:T(8,128)(2,1)S(1)}, bf16[112,768]{1,0:T(8,128)(2,1)S(1)}, u32[]{:S(2)}, u32[]{:S(2)}) %collective-permute-start.3) | collective-permute-done | bytes 172064 | tf_op jit(solution)/shard_map/ppermute | solution.py:304
  67.0 0.8 stack.1
  67.8 0.0 all-gather.5.cloned.1.call-update
  67.8 0.0 all-to-all-done.refs_0_
  67.8 1.9 collective-permute-start.5
  69.7 2.7 %collective-permute-start.9 = (bf16[672,512]{1,0:T(8,128)(2,1)S(1)}, bf16[672,512]{1,0:T(8,128)(2,1)S(1)}, u32[]{:S(2)}, u32[]{:S(2)}) collective-permute-start(bf16[672,512]{1,0:T(8,128)(2,1)S(1)} %get-tuple-element.21.refs_4_), channel_id=1, source_target_pairs={{0,384},{128,0},{256,128},{384,256},{1,385},{129,1},{257,129},{385... | collective-permute-start | bytes 2064392 | tf_op jit(solution)/shard_map/ppermute | solution.py:304
  72.5 4.3 %collective-permute-start.8 = (bf16[672,512]{1,0:T(8,128)(2,1)S(1)}, bf16[672,512]{1,0:T(8,128)(2,1)S(1)}, u32[]{:S(2)}, u32[]{:S(2)}) collective-permute-start(bf16[672,512]{1,0:T(8,128)(2,1)S(1)} %get-tuple-element.21.refs_4_), channel_id=1, source_target_pairs={{0,128},{128,256},{256,384},{384,0},{1,129},{129,257},{257,385},{3... | collective-permute-start | bytes 2064392 | tf_op jit(solution)/shard_map/ppermute | solution.py:304
  76.8 1.9 collective-permute-start.6
  78.7 6.4 %collective-permute-done.5.refs_1_ = bf16[8,48,896]{2,1,0:T(8,128)(2,1)S(1)} collective-permute-done((bf16[8,48,896]{2,1,0:T(8,128)(2,1)S(1)}, bf16[8,48,896]{2,1,0:T(8,128)(2,1)S(1)}, u32[]{:S(2)}, u32[]{:S(2)}) %collective-permute-start.5) | collective-permute-done | bytes 688160 | tf_op jit(solution)/shard_map/ppermute | solution.py:304
  85.1 1.9 collective-permute-start.7
  87.0 12.7 %collective-permute-done.9.refs_6_ = bf16[672,512]{1,0:T(8,128)(2,1)S(1)} collective-permute-done((bf16[672,512]{1,0:T(8,128)(2,1)S(1)}, bf16[672,512]{1,0:T(8,128)(2,1)S(1)}, u32[]{:S(2)}, u32[]{:S(2)}) %collective-permute-start.9) | collective-permute-done | bytes 688160 | tf_op jit(solution)/shard_map/ppermute | solution.py:304
  99.8 1.9 collective-permute-start.11
  101.7 0.3 collective-permute-done.8.refs_5_
  102.0 5.6 %collective-permute-start.10 = (bf16[336,512]{1,0:T(8,128)(2,1)S(1)}, bf16[336,512]{1,0:T(8,128)(2,1)}, u32[]{:S(2)}, u32[]{:S(2)}) collective-permute-start(bf16[336,512]{1,0:T(8,128)(2,1)S(1)} %slice.34), channel_id=1, source_target_pairs={{0,128},{128,256},{256,384},{384,0},{1,129},{129,257},{257,385},{3... | collective-permute-start | bytes 1032200 | tf_op jit(solution)/shard_map/ppermute | solution.py:304
  107.6 0.0 collective-permute-done.6.refs_2_
  107.6 0.0 collective-permute-done.7.refs_3_
  107.6 1.7 unpack.1
  109.3 1.1 copy-done.1
  110.5 1.2 copy-done.2
  111.6 0.0 collective-permute-done.11.refs_8_
  111.6 0.7 collective-permute-done.10.refs_7_
  112.3 0.1 copy-done.17
  112.4 8.5 %hidden.1 = (bf16[3584,512]{1,0:T(8,128)(2,1)}, bf16[192,512]{1,0:T(8,128)(2,1)}, bf16[192,128]{1,0:T(8,128)(2,1)}, bf16[896,256]{1,0:T(8,128)(2,1)}, bf16[896,2...) custom-call(bf16[192,3584]{1,0:T(8,128)(2,1)} %copy-done.1, bf16[192,3584]{1,0:T(8,128)(2,1)} %copy-done.2, ...), custom_call_target="tpu_custom_call" | custom-call | flops 2000000000 | bytes 12000000 | tf_op jit(solution)/shard_map/hidden/pallas_call | solution.py:240
  120.9 2.0 copy-done
  122.9 0.9 copy-done.8
  123.8 0.8 copy-done.9
  124.6 1.3 inputs.1
  126.0 1.9 collective-permute-start.12
  128.0 2.1 collective-permute-start.14
  130.0 5.6 %collective-permute-start.13 = (bf16[448,256]{1,0:T(8,128)(2,1)S(1)}, bf16[448,256]{1,0:T(8,128)(2,1)S(1)}, u32[]{:S(2)}, u32[]{:S(2)}) collective-permute-start(bf16[448,256]{1,0:T(8,128)(2,1)S(1)} %get-tuple-element.40), channel_id=1, source_target_pairs={{0,128},{128,256},{256,384},{384,0},{1,129},{129,257},{257,385},{3... | collective-permute-start | bytes 688136 | tf_op jit(solution)/shard_map/ppermute | solution.py:304
  135.7 0.0 collective-permute-done.12.got_ref
  135.7 1.5 combine.1
  137.2 2.8 %collective-permute-done.14.high_ref = bf16[448,256]{1,0:T(8,128)(2,1)S(1)} collective-permute-done((bf16[448,256]{1,0:T(8,128)(2,1)S(1)}, bf16[448,256]{1,0:T(8,128)(2,1)S(1)}, u32[]{:S(2)}, u32[]{:S(2)}) %collective-permute-start.14) | collective-permute-done | bytes 229408 | tf_op jit(solution)/shard_map/ppermute | solution.py:304
  140.0 1.2 collective-permute-done.13.low_ref
  141.2 0.1 relay.1
  141.3 5.6 %collective-permute-start.15 = (bf16[896,256]{1,0:T(8,128)(2,1)S(1)}, bf16[896,256]{1,0:T(8,128)(2,1)S(1)}, u32[]{:S(2)}, u32[]{:S(2)}) collective-permute-start(bf16[896,256]{1,0:T(8,128)(2,1)S(1)} %get-tuple-element.36), channel_id=1, source_target_pairs={{0,128},{128,256},{256,384},{384,0},{1,129},{129,257},{257,385},{3... | collective-permute-start | bytes 1376264 | tf_op jit(solution)/shard_map/ppermute | solution.py:304
  146.9 1.9 collective-permute-start.16
  148.9 7.7 %collective-permute-done.15 = bf16[896,256]{1,0:T(8,128)(2,1)S(1)} collective-permute-done((bf16[896,256]{1,0:T(8,128)(2,1)S(1)}, bf16[896,256]{1,0:T(8,128)(2,1)S(1)}, u32[]{:S(2)}, u32[]{:S(2)}) %collective-permute-start.15) | collective-permute-done | bytes 458784 | tf_op jit(solution)/shard_map/ppermute | solution.py:304
  156.6 5.3 %collective-permute-done.16 = bf16[896,256]{1,0:T(8,128)(2,1)S(1)} collective-permute-done((bf16[896,256]{1,0:T(8,128)(2,1)S(1)}, bf16[896,256]{1,0:T(8,128)(2,1)S(1)}, u32[]{:S(2)}, u32[]{:S(2)}) %collective-permute-start.16) | collective-permute-done | bytes 458784 | tf_op jit(solution)/shard_map/ppermute | solution.py:304
  161.9 0.2 add_convert_fusion
  162.1 19.4 %all_to_all.15 = bf16[8,112,256]{2,1,0:T(8,128)(2,1)S(1)} all-to-all(bf16[8,112,256]{2,1,0:T(8,128)(2,1)S(1)} %bitcast.16), channel_id=1, replica_groups=mesh['x'=4,'zh'=4,'c'=2,'y'=8,'zl'=2] {'zh','c'}, dimensions={0} | all-to-all | bytes 917504 | tf_op jit(solution)/shard_map/all_to_all | solution.py:316
  181.4 7.1 %all-to-all-start.1 = ((bf16[16,48,512]{2,1,0:T(8,128)(2,1)}), bf16[16,48,512]{2,1,0:T(8,128)(2,1)S(1)}, u32[]{:S(2)}, u32[]{:S(2)}) async-start(bf16[16,48,512]{2,1,0:T(8,128)(2,1)} %bitcast.2._), calls=%async_computation.1 | async-start | bytes 1572864 | tf_op jit(solution)/shard_map/all_to_all | solution.py:316
  188.6 0.1 reduce_sum.12
  188.7 0.7 pad_maximum_fusion.2
  189.3 21.9 %all-to-all-done.1 = bf16[16,48,512]{2,1,0:T(8,128)(2,1)S(1)} async-done(((bf16[16,48,512]{2,1,0:T(8,128)(2,1)}), bf16[16,48,512]{2,1,0:T(8,128)(2,1)S(1)}, u32[]{:S(2)}, u32[]{:S(2)}) %all-to-all-start.1) | async-done | bytes 786464 | tf_op jit(solution)/shard_map/all_to_all | solution.py:316
  211.2 2.0 finish.1
  (38 shorter events, 0.2 us)
Async XLA Ops:
  7.2 6.1 %copy-start.11 = (f32[128,1]{0,1:T(1,128)S(1)}, f32[128,1]{0,1:T(1,128)}, u32[]{:S(2)}) copy-start(f32[128,1]{0,1:T(1,128)} %param.10) | copy-start | bytes 1540
  7.2 6.1 %copy-start.10 = (s32[128,1]{0,1:T(1,128)S(1)}, s32[128,1]{0,1:T(1,128)}, u32[]{:S(2)}) copy-start(s32[128,1]{0,1:T(1,128)} %param.9) | copy-start | bytes 1540
  7.2 6.1 %copy-start.4 = (bf16[128,3584]{1,0:T(8,128)(2,1)S(1)}, bf16[128,3584]{1,0:T(8,128)(2,1)}, u32[]{:S(2)}) copy-start(bf16[128,3584]{1,0:T(8,128)(2,1)} %g_ref.1) | copy-start | bytes 2752516
  7.2 6.1 %copy-start.3 = (bf16[128,3584]{1,0:T(8,128)(2,1)S(1)}, bf16[128,3584]{1,0:T(8,128)(2,1)}, u32[]{:S(2)}) copy-start(bf16[128,3584]{1,0:T(8,128)(2,1)} %x_ref.1) | copy-start | bytes 2752516
  7.2 105.1 %all-gather.3.cloned.1.call-start = ((), (), s32[]{:S(2)}) async-start(), calls=%async_computation.3 | async-start | bytes 1720320 | tf_op jit(solution)/shard_map/all_gather | solution.py:332
  9.2 3.3 %collective-permute-start = (bf16[112,768]{1,0:T(8,128)(2,1)S(1)}, bf16[112,768]{1,0:T(8,128)(2,1)S(1)}, u32[]{:S(2)}, u32[]{:S(2)}) collective-permute-start(bf16[112,768]{1,0:T(8,128)(2,1)S(1)} %pad_maximum_fusion.1), channel_id=1, source_target_pairs={{0,16},{16,0},{1,17},{17,1},{2,18},{18,2},{3,19},{19,3},{4,20},{20... | collective-permute-start | bytes 516104 | tf_op jit(solution)/shard_map/ppermute | solution.py:304
  13.3 8.7 %copy-start.14 = (bf16[224,768]{1,0:T(8,128)(2,1)S(1)}, bf16[224,768]{1,0:T(8,128)(2,1)}, u32[]{:S(2)}) copy-start(bf16[224,768]{1,0:T(8,128)(2,1)} %pad_maximum_fusion) | copy-start | bytes 1032196
  14.9 52.9 %all-to-all-start = ((bf16[8,48,896]{2,1,0:T(8,128)(2,1)}), bf16[8,48,896]{2,1,0:T(8,128)(2,1)S(1)}, u32[]{:S(2)}, u32[]{:S(2)}) async-start(bf16[8,48,896]{2,1,0:T(8,128)(2,1)} %dispatch.1), calls=%async_computation | async-start | bytes 1376256 | tf_op jit(solution)/shard_map/all_to_all | solution.py:316
  22.0 90.3 %all-gather.5.cloned.1.call-start = ((), (), s32[]{:S(2)}) async-start(), calls=%async_computation.4 | async-start | bytes 1720320 | tf_op jit(solution)/shard_map/all_gather | solution.py:336
  22.0 25.7 %collective-permute-start.2 = (bf16[224,768]{1,0:T(8,128)(2,1)S(1)}, bf16[224,768]{1,0:T(8,128)(2,1)S(1)}, u32[]{:S(2)}, u32[]{:S(2)}) collective-permute-start(bf16[224,768]{1,0:T(8,128)(2,1)S(1)} %copy-done.14), channel_id=1, source_target_pairs={{0,96},{32,0},{64,32},{96,64},{1,97},{33,1},{65,33},{97,65},{2,98}... | collective-permute-start | bytes 1032200 | tf_op jit(solution)/shard_map/ppermute | solution.py:304
  33.0 21.3 %collective-permute-start.1 = (bf16[224,768]{1,0:T(8,128)(2,1)S(1)}, bf16[224,768]{1,0:T(8,128)(2,1)S(1)}, u32[]{:S(2)}, u32[]{:S(2)}) collective-permute-start(bf16[224,768]{1,0:T(8,128)(2,1)S(1)} %copy-done.14), channel_id=1, source_target_pairs={{0,32},{32,64},{64,96},{96,0},{1,33},{33,65},{65,97},{97,1},{2,34}... | collective-permute-start | bytes 1032200 | tf_op jit(solution)/shard_map/ppermute | solution.py:304
  47.7 11.5 %collective-permute-start.4 = (bf16[112,768]{1,0:T(8,128)(2,1)S(1)}, bf16[112,768]{1,0:T(8,128)(2,1)S(1)}, u32[]{:S(2)}, u32[]{:S(2)}) collective-permute-start(bf16[112,768]{1,0:T(8,128)(2,1)S(1)} %slice.33), channel_id=1, source_target_pairs={{0,96},{32,0},{64,32},{96,64},{1,97},{33,1},{65,33},{97,65},{2,98}... | collective-permute-start | bytes 516104 | tf_op jit(solution)/shard_map/ppermute | solution.py:304
  54.3 12.7 %collective-permute-start.3 = (bf16[112,768]{1,0:T(8,128)(2,1)S(1)}, bf16[112,768]{1,0:T(8,128)(2,1)S(1)}, u32[]{:S(2)}, u32[]{:S(2)}) collective-permute-start(bf16[112,768]{1,0:T(8,128)(2,1)S(1)} %slice.32), channel_id=1, source_target_pairs={{0,32},{32,64},{64,96},{96,0},{1,33},{33,65},{65,97},{97,1},{2,34}... | collective-permute-start | bytes 516104 | tf_op jit(solution)/shard_map/ppermute | solution.py:304
  67.8 41.5 %copy-start.5 = (bf16[672,512]{1,0:T(8,128)(2,1)}, bf16[672,512]{1,0:T(8,128)(2,1)S(1)}, u32[]{:S(2)}) copy-start(bf16[672,512]{1,0:T(8,128)(2,1)S(1)} %get-tuple-element.21.refs_4_) | copy-start | bytes 2064388
  67.8 17.3 %collective-permute-start.5 = (bf16[8,48,896]{2,1,0:T(8,128)(2,1)S(1)}, bf16[8,48,896]{2,1,0:T(8,128)(2,1)S(1)}, u32[]{:S(2)}, u32[]{:S(2)}) collective-permute-start(bf16[8,48,896]{2,1,0:T(8,128)(2,1)S(1)} %all-to-all-done.refs_0_), channel_id=1, source_target_pairs={{0,1},{1,0},{2,3},{3,2},{4,5},{5,4},{6,7},{7,6},{8,9},{9,8},{10,11... | collective-permute-start | bytes 2064392 | tf_op jit(solution)/shard_map/ppermute | solution.py:304
  69.7 30.0 %collective-permute-start.9 = (bf16[672,512]{1,0:T(8,128)(2,1)S(1)}, bf16[672,512]{1,0:T(8,128)(2,1)S(1)}, u32[]{:S(2)}, u32[]{:S(2)}) collective-permute-start(bf16[672,512]{1,0:T(8,128)(2,1)S(1)} %get-tuple-element.21.refs_4_), channel_id=1, source_target_pairs={{0,384},{128,0},{256,128},{384,256},{1,385},{129,1},{257,129},{385... | collective-permute-start | bytes 2064392 | tf_op jit(solution)/shard_map/ppermute | solution.py:304
  72.5 29.5 %collective-permute-start.8 = (bf16[672,512]{1,0:T(8,128)(2,1)S(1)}, bf16[672,512]{1,0:T(8,128)(2,1)S(1)}, u32[]{:S(2)}, u32[]{:S(2)}) collective-permute-start(bf16[672,512]{1,0:T(8,128)(2,1)S(1)} %get-tuple-element.21.refs_4_), channel_id=1, source_target_pairs={{0,128},{128,256},{256,384},{384,0},{1,129},{129,257},{257,385},{3... | collective-permute-start | bytes 2064392 | tf_op jit(solution)/shard_map/ppermute | solution.py:304
  76.8 30.8 %collective-permute-start.6 = (bf16[8,48,896]{2,1,0:T(8,128)(2,1)S(1)}, bf16[8,48,896]{2,1,0:T(8,128)(2,1)S(1)}, u32[]{:S(2)}, u32[]{:S(2)}) collective-permute-start(bf16[8,48,896]{2,1,0:T(8,128)(2,1)S(1)} %all-to-all-done.refs_0_), channel_id=1, source_target_pairs={{0,16},{16,0},{1,17},{17,1},{2,18},{18,2},{3,19},{19,3},{4,20},{20... | collective-permute-start | bytes 2064392 | tf_op jit(solution)/shard_map/ppermute | solution.py:304
  85.1 22.5 %collective-permute-start.7 = (bf16[8,48,896]{2,1,0:T(8,128)(2,1)S(1)}, bf16[8,48,896]{2,1,0:T(8,128)(2,1)S(1)}, u32[]{:S(2)}, u32[]{:S(2)}) collective-permute-start(bf16[8,48,896]{2,1,0:T(8,128)(2,1)S(1)} %collective-permute-done.5.refs_1_), channel_id=1, source_target_pairs={{0,16},{16,0},{1,17},{17,1},{2,18},{18,2},{3,19},{19,3},{4,20},{20... | collective-permute-start | bytes 2064392 | tf_op jit(solution)/shard_map/ppermute | solution.py:304
  99.7 9.6 %copy-start.12 = (bf16[672,512]{1,0:T(8,128)(2,1)}, bf16[672,512]{1,0:T(8,128)(2,1)S(1)}, u32[]{:S(2)}) copy-start(bf16[672,512]{1,0:T(8,128)(2,1)S(1)} %collective-permute-done.9.refs_6_) | copy-start | bytes 2064388
  99.8 11.9 %collective-permute-start.11 = (bf16[336,512]{1,0:T(8,128)(2,1)S(1)}, bf16[336,512]{1,0:T(8,128)(2,1)S(1)}, u32[]{:S(2)}, u32[]{:S(2)}) collective-permute-start(bf16[336,512]{1,0:T(8,128)(2,1)S(1)} %slice.35), channel_id=1, source_target_pairs={{0,384},{128,0},{256,128},{384,256},{1,385},{129,1},{257,129},{385... | collective-permute-start | bytes 1032200 | tf_op jit(solution)/shard_map/ppermute | solution.py:304
  102.0 7.3 %copy-start.13 = (bf16[672,512]{1,0:T(8,128)(2,1)}, bf16[672,512]{1,0:T(8,128)(2,1)S(1)}, u32[]{:S(2)}) copy-start(bf16[672,512]{1,0:T(8,128)(2,1)S(1)} %collective-permute-done.8.refs_5_) | copy-start | bytes 2064388
  102.0 10.3 %collective-permute-start.10 = (bf16[336,512]{1,0:T(8,128)(2,1)S(1)}, bf16[336,512]{1,0:T(8,128)(2,1)}, u32[]{:S(2)}, u32[]{:S(2)}) collective-permute-start(bf16[336,512]{1,0:T(8,128)(2,1)S(1)} %slice.34), channel_id=1, source_target_pairs={{0,128},{128,256},{256,384},{384,0},{1,129},{129,257},{257,385},{3... | collective-permute-start | bytes 1032200 | tf_op jit(solution)/shard_map/ppermute | solution.py:304
  109.3 1.1 copy-start.1
  110.5 1.2 copy-start.2
  111.6 0.7 copy-start.17
  120.9 2.0 copy-start
  122.9 0.9 copy-start.8
  123.8 0.8 copy-start.9
  124.6 3.3 %copy-start.16 = (bf16[896,256]{1,0:T(8,128)(2,1)S(1)}, bf16[896,256]{1,0:T(8,128)(2,1)}, u32[]{:S(2)}) copy-start(bf16[896,256]{1,0:T(8,128)(2,1)} %get-tuple-element.35) | copy-start | bytes 1376260
  126.0 9.7 %collective-permute-start.12 = (bf16[96,3712]{1,0:T(8,128)(2,1)S(1)}, bf16[96,3712]{1,0:T(8,128)(2,1)S(1)}, u32[]{:S(2)}, u32[]{:S(2)}) collective-permute-start(bf16[96,3712]{1,0:T(8,128)(2,1)S(1)} %get-tuple-element.30), channel_id=1, source_target_pairs={{0,16},{16,0},{1,17},{17,1},{2,18},{18,2},{3,19},{19,3},{4,20},{20... | collective-permute-start | bytes 2138120 | tf_op jit(solution)/shard_map/ppermute | solution.py:304
  127.9 13.3 %copy-start.6 = (bf16[896,256]{1,0:T(8,128)(2,1)S(1)}, bf16[896,256]{1,0:T(8,128)(2,1)}, u32[]{:S(2)}) copy-start(bf16[896,256]{1,0:T(8,128)(2,1)} %get-tuple-element.33.plus_ref) | copy-start | bytes 1376260
  127.9 13.3 %copy-start.7 = (bf16[896,256]{1,0:T(8,128)(2,1)S(1)}, bf16[896,256]{1,0:T(8,128)(2,1)}, u32[]{:S(2)}) copy-start(bf16[896,256]{1,0:T(8,128)(2,1)} %get-tuple-element.34.minus_ref) | copy-start | bytes 1376260
  128.0 12.0 %collective-permute-start.14 = (bf16[448,256]{1,0:T(8,128)(2,1)S(1)}, bf16[448,256]{1,0:T(8,128)(2,1)S(1)}, u32[]{:S(2)}, u32[]{:S(2)}) collective-permute-start(bf16[448,256]{1,0:T(8,128)(2,1)S(1)} %get-tuple-element.39), channel_id=1, source_target_pairs={{0,384},{128,0},{256,128},{384,256},{1,385},{129,1},{257,129},{385... | collective-permute-start | bytes 688136 | tf_op jit(solution)/shard_map/ppermute | solution.py:304
  130.0 11.2 %collective-permute-start.13 = (bf16[448,256]{1,0:T(8,128)(2,1)S(1)}, bf16[448,256]{1,0:T(8,128)(2,1)S(1)}, u32[]{:S(2)}, u32[]{:S(2)}) collective-permute-start(bf16[448,256]{1,0:T(8,128)(2,1)S(1)} %get-tuple-element.40), channel_id=1, source_target_pairs={{0,128},{128,256},{256,384},{384,0},{1,129},{129,257},{257,385},{3... | collective-permute-start | bytes 688136 | tf_op jit(solution)/shard_map/ppermute | solution.py:304
  137.2 24.7 %copy-start.15 = (bf16[896,256]{1,0:T(8,128)(2,1)S(1)}, bf16[896,256]{1,0:T(8,128)(2,1)}, u32[]{:S(2)}) copy-start(bf16[896,256]{1,0:T(8,128)(2,1)} %get-tuple-element.38) | copy-start | bytes 1376260
  141.3 15.2 %collective-permute-start.15 = (bf16[896,256]{1,0:T(8,128)(2,1)S(1)}, bf16[896,256]{1,0:T(8,128)(2,1)S(1)}, u32[]{:S(2)}, u32[]{:S(2)}) collective-permute-start(bf16[896,256]{1,0:T(8,128)(2,1)S(1)} %get-tuple-element.36), channel_id=1, source_target_pairs={{0,128},{128,256},{256,384},{384,0},{1,129},{129,257},{257,385},{3... | collective-permute-start | bytes 1376264 | tf_op jit(solution)/shard_map/ppermute | solution.py:304
  146.9 15.0 %collective-permute-start.16 = (bf16[896,256]{1,0:T(8,128)(2,1)S(1)}, bf16[896,256]{1,0:T(8,128)(2,1)S(1)}, u32[]{:S(2)}, u32[]{:S(2)}) collective-permute-start(bf16[896,256]{1,0:T(8,128)(2,1)S(1)} %get-tuple-element.37), channel_id=1, source_target_pairs={{0,384},{128,0},{256,128},{384,256},{1,385},{129,1},{257,129},{385... | collective-permute-start | bytes 1376264 | tf_op jit(solution)/shard_map/ppermute | solution.py:304
  181.4 29.7 %all-to-all-start.1 = ((bf16[16,48,512]{2,1,0:T(8,128)(2,1)}), bf16[16,48,512]{2,1,0:T(8,128)(2,1)S(1)}, u32[]{:S(2)}, u32[]{:S(2)}) async-start(bf16[16,48,512]{2,1,0:T(8,128)(2,1)} %bitcast.2._), calls=%async_computation.1 | async-start | bytes 1572864 | tf_op jit(solution)/shard_map/all_to_all | solution.py:316
Sparse Core Ops, SparseCore 0:
  13.4 34.2 all-gather.2
  67.9 34.0 all-gather.4

commit v5 on v4

--- a/solution.py
+++ b/solution.py
@@ -25,7 +25,8 @@
 PIECE = 512
 WIDE = D + 128
 VMEM_LIMIT = 16 * 1024 * 1024
-MOST_VMEM = 56 * 1024 * 1024
+MOST_VMEM = 44 * 1024 * 1024
+INPUTS_VMEM = 24 * 1024 * 1024
 VMEM = pl.BlockSpec(memory_space=pltpu.VMEM)
 
 
@@ -167,75 +168,38 @@
     )(*rows)
 
 
-def stack_kernel(before_ref, after_ref, low_ref, high_ref, wide_ref, down_ref):
-    at = 0
-    for ref in (before_ref, after_ref, low_ref, high_ref):
-        n = ref.shape[0]
-        wide_ref[at:at + n] = ref[:, :2 * QUART]
-        down_ref[at:at + n] = ref[:, 2 * QUART:]
-        at += n
-
-
-def stack(*parts):
-    n = 6 * SHARD
-    return pl.pallas_call(
-        stack_kernel,
-        in_specs=[VMEM] * 4,
-        out_specs=[VMEM] * 2,
-        out_shape=[jax.ShapeDtypeStruct((n, 2 * QUART), BF), jax.ShapeDtypeStruct((n, QUART), BF)],
-        compiler_params=pltpu.CompilerParams(vmem_limit_bytes=VMEM_LIMIT),
-        cost_estimate=pl.CostEstimate(flops=10**6, bytes_accessed=2 * 10**6, transcendentals=0),
-        name="stack",
-    )(*parts)
-
-
 def hidden_kernel(pieces, *refs):
     x_ref, g_ref = refs[:2]
     weight_refs = refs[2:2 + len(pieces)]
-    wide_ref, d_ref, line_ref, far_ref, plus_ref, minus_ref, own_ref, down, sems = refs[2 + len(pieces):]
+    wide_ref, pre_ref, hidden_ref, far_ref, plus_ref, minus_ref, own_ref, sems = refs[2 + len(pieces):]
     xi, zi, ci = lax.axis_index("x"), lax.axis_index("zh"), lax.axis_index("c")
     copies = []
-
-    def copy(source, target):
-        copies.append(pltpu.make_async_copy(source, target, sems.at[len(copies)]))
-
     for ref, listed in zip(weight_refs, pieces):
-        for at, (kind, dx, dz, which) in enumerate(listed):
-            x = dx if kind == "fixed" else lax.rem(xi + dx, 4)
+        for at, (dx, dz, which) in enumerate(listed):
+            block = lax.rem(xi + dx, 4) * 4 + lax.rem(zi + dz, 4)
             core = ci if which == 0 else 1 - ci
-            rows = pl.ds(pl.multiple_of((x * 4 + lax.rem(zi + dz, 4)) * BLOCK + core * SHARD, 16), SHARD)
-            source = ref.at[pl.ds(at * SHARD, SHARD)]
-            if ref.shape[1] == QUART:
-                copy(source, down.at[rows])
-            elif ref.shape[1] == 2 * QUART:
-                copy(source, wide_ref.at[rows])
-            else:
-                copy(source.at[:, pl.ds(0, 2 * QUART)], wide_ref.at[rows])
-                copy(source.at[:, pl.ds(2 * QUART, QUART)], down.at[rows])
-    for one in copies:
-        one.start()
-    for one in copies:
-        one.wait()
+            start = pl.multiple_of(block * BLOCK + core * SHARD, 16)
+            copies.append(pltpu.make_async_copy(
+                ref.at[pl.ds(at * SHARD, SHARD)], wide_ref.at[pl.ds(start, SHARD)], sems.at[len(copies)]
+            ))
+    for copy in copies:
+        copy.start()
+    for copy in copies:
+        copy.wait()
     pre = jnp.dot(x_ref[...], wide_ref[...], preferred_element_type=F32)
-    grad = jnp.dot(g_ref[...], down[...], preferred_element_type=F32)
+    pre_ref[...] = pre
     gate, up = pre[:, :QUART], pre[:, QUART:]
-    sig = jax.nn.sigmoid(gate)
-    act = gate * sig
-    slope = sig * (1.0 + gate * (1.0 - sig))
-    hidden = (act * up).astype(BF)
-    route = jnp.sum(hidden.astype(F32) * grad, axis=1, keepdims=True)
+    hidden = (gate * jax.nn.sigmoid(gate) * up).astype(BF)
+    hidden_ref[...] = hidden
     for ref, shift in ((far_ref, 2), (plus_ref, 1), (minus_ref, 3), (own_ref, 0)):
         start = pl.multiple_of(lax.rem(xi + shift, 4) * XROWS, 128)
         ref[...] = lax.dot_general(
             g_ref[:, pl.ds(start, XROWS)], hidden, (((0,), (0,)), ((), ())), preferred_element_type=F32
         ).astype(BF)
-    d_ref[...] = jnp.concatenate([(grad * up * slope).astype(BF), (grad * act).astype(BF)], axis=1)
-    line_ref[...] = jnp.where(iota((2 * ROWS, 128), 1) == 0, route, 0.0).astype(BF)
 
 
 def hidden_compute(x_rows, g_rows, blocks, pieces):
     anywhere = pl.BlockSpec(memory_space=pl.ANY)
-    count = sum(len(p) * (2 if b.shape[1] == 3 * QUART else 1) for p, b in zip(pieces, blocks))
     down = jax.ShapeDtypeStruct((XROWS, QUART), BF)
     return pl.pallas_call(
         lambda *refs: hidden_kernel(pieces, *refs),
@@ -243,42 +207,55 @@
         out_specs=[VMEM] * 7,
         out_shape=[
             jax.ShapeDtypeStruct((D, 2 * QUART), BF),
-            jax.ShapeDtypeStruct((2 * ROWS, 2 * QUART), BF),
-            jax.ShapeDtypeStruct((2 * ROWS, 128), BF),
+            jax.ShapeDtypeStruct((2 * ROWS, 2 * QUART), F32),
+            jax.ShapeDtypeStruct((2 * ROWS, QUART), BF),
             down, down, down, down,
         ],
-        scratch_shapes=[pltpu.VMEM((D, QUART), BF), pltpu.SemaphoreType.DMA((count,))],
+        scratch_shapes=[pltpu.SemaphoreType.DMA((sum(len(p) for p in pieces),))],
         compiler_params=pltpu.CompilerParams(vmem_limit_bytes=MOST_VMEM),
-        cost_estimate=pl.CostEstimate(flops=2 * 10**9, bytes_accessed=12 * 10**6, transcendentals=49152),
+        cost_estimate=pl.CostEstimate(flops=10**9, bytes_accessed=8 * 10**6, transcendentals=49152),
         name="hidden",
     )(x_rows, g_rows, *blocks)
 
 
-def inputs_kernel(d_ref, line_ref, wide_ref, keep_ref, send_ref):
+def inputs_kernel(g_ref, wide_ref, pre_ref, hidden_ref, down_ref, keep_ref, send_ref, down, sem):
+    columns = pl.ds(pl.multiple_of(lax.axis_index("c") * QUART, QUART), QUART)
+    copy = pltpu.make_async_copy(down_ref.at[:, columns], down, sem)
+    copy.start()
+    gate, up = pre_ref[:, :QUART], pre_ref[:, QUART:]
+    sig = jax.nn.sigmoid(gate)
+    act = gate * sig
+    slope = sig * (1.0 + gate * (1.0 - sig))
+    copy.wait()
+    grad = jnp.dot(g_ref[...], down[...], preferred_element_type=F32)
+    route = jnp.sum(hidden_ref[...].astype(F32) * grad, axis=1, keepdims=True)
+    d_pre = jnp.concatenate([(grad * up * slope).astype(BF), (grad * act).astype(BF)], axis=1)
     for i in range(4):
         part = lax.dot_general(
-            d_ref[...], wide_ref[i * CHUNK:(i + 1) * CHUNK], (((1,), (1,)), ((), ())), preferred_element_type=F32
+            d_pre, wide_ref[i * CHUNK:(i + 1) * CHUNK], (((1,), (1,)), ((), ())), preferred_element_type=F32
         ).astype(BF)
         keep_ref[:, i * CHUNK:(i + 1) * CHUNK] = part[:ROWS]
         send_ref[:, i * CHUNK:(i + 1) * CHUNK] = part[ROWS:]
-    keep_ref[:, D:] = line_ref[:ROWS]
-    send_ref[:, D:] = line_ref[ROWS:]
-
-
-def inputs_compute(d_pre, line, wide):
+    line = jnp.where(iota((2 * ROWS, 128), 1) == 0, route, 0.0).astype(BF)
+    keep_ref[:, D:] = line[:ROWS]
+    send_ref[:, D:] = line[ROWS:]
+
+
+def inputs_compute(g_rows, wide, pre, hidden, down_all):
     back = jax.ShapeDtypeStruct((ROWS, WIDE), BF)
     return pl.pallas_call(
         inputs_kernel,
-        in_specs=[VMEM] * 3,
+        in_specs=[VMEM] * 4 + [pl.BlockSpec(memory_space=pl.ANY)],
         out_specs=[VMEM] * 2,
         out_shape=[back, back],
-        compiler_params=pltpu.CompilerParams(vmem_limit_bytes=VMEM_LIMIT),
-        cost_estimate=pl.CostEstimate(flops=7 * 10**8, bytes_accessed=6 * 10**6, transcendentals=0),
+        scratch_shapes=[pltpu.VMEM((D, QUART), BF), pltpu.SemaphoreType.DMA(())],
+        compiler_params=pltpu.CompilerParams(vmem_limit_bytes=INPUTS_VMEM),
+        cost_estimate=pl.CostEstimate(flops=10**9, bytes_accessed=8 * 10**6, transcendentals=49152),
         name="inputs",
-    )(d_pre, line, wide)
-
-
-def relay_kernel(plus_ref, minus_ref, low_ref, high_ref, _, plus_out, minus_out):
+    )(g_rows, wide, pre, hidden, down_all)
+
+
+def relay_kernel(plus_ref, minus_ref, low_ref, high_ref, plus_out, minus_out):
     half = XROWS // 2
     plus_out[:half] = add(plus_ref[:half], low_ref[...])
     plus_out[half:] = plus_ref[half:]
@@ -286,17 +263,17 @@
     minus_out[half:] = add(minus_ref[half:], high_ref[...])
 
 
-def relay(plus, minus, low, high, message):
+def relay(plus, minus, low, high):
     down = jax.ShapeDtypeStruct((XROWS, QUART), BF)
     return pl.pallas_call(
         relay_kernel,
-        in_specs=[VMEM] * 4 + [pl.BlockSpec(memory_space=pl.ANY)],
+        in_specs=[VMEM] * 4,
         out_specs=[VMEM] * 2,
         out_shape=[down, down],
         compiler_params=pltpu.CompilerParams(vmem_limit_bytes=VMEM_LIMIT),
         cost_estimate=pl.CostEstimate(flops=10**6, bytes_accessed=3 * 10**6, transcendentals=0),
         name="relay",
-    )(plus, minus, low, high, message)
+    )(plus, minus, low, high)
 
 
 def hop(a, axis, shift):
@@ -317,54 +294,57 @@
 
 
 def per_device(tokens, grad_out, routing, route_weight, gate_weight, up_weight, down_weight):
-    ci = lax.axis_index("c")
+    zi, ci = lax.axis_index("zh"), lax.axis_index("c")
     ids, share = routing.reshape(1, TOK), route_weight.reshape(1, TOK)
 
     def columns(which):
         return jnp.concatenate([
-            lax.dynamic_slice(w, (0, which * QUART), (SHARD, QUART)) for w in (gate_weight, up_weight, down_weight)
+            lax.dynamic_slice(w, (0, which * QUART), (SHARD, QUART)) for w in (gate_weight, up_weight)
         ], axis=1)
 
+    down_all = lax.all_gather(down_weight, ("x", "zh", "c"), axis=0, tiled=True)
     theirs = hop(columns(1 - ci), "c", 1)
     sent = dispatch(ids, share, tokens, grad_out)
     own = jnp.concatenate([columns(ci), theirs], axis=0)
 
-    own_all = lax.all_gather(own, "x", axis=0, tiled=True)
     z_before, z_after = hop(own, "zh", 1), hop(own, "zh", -1)
     z_low, z_high = hop(z_before[:SHARD], "zh", 1), hop(z_after[SHARD:], "zh", -1)
-    rest, rest_down = stack(z_before, z_after, z_low, z_high)
-    down_all = lax.all_gather(rest_down, "x", axis=0, tiled=True)
-    r_before, r_after = hop(rest, "x", 1), hop(rest, "x", -1)
-    half = 3 * SHARD
-    r_low, r_high = hop(r_before[:half], "x", 1), hop(r_after[half:], "x", -1)
-
-    across = [(3, 0), (3, 1), (1, 0), (1, 1), (2, 0), (2, 1)]
-    listed = lambda kind, dx, shards: [(kind, dx, dz, w) for dz, w in shards]
-    blocks = [own_all, down_all, rest, r_before, r_after, r_low, r_high]
-    pieces = [
-        sum([listed("fixed", x, [(0, 0), (0, 1)]) for x in range(4)], []),
-        sum([listed("fixed", x, across) for x in range(4)], []),
-        listed("moved", 0, across), listed("moved", 3, across), listed("moved", 1, across),
-        listed("moved", 2, across[:3]), listed("moved", 2, across[3:]),
-    ]
-
-    rows = exchange(sent, "y")
-    rows = tie(rows, rest)[0]
+    line = jnp.concatenate([own, z_before, z_after, z_low, z_high], axis=0)
+    before, after = hop(line, "x", 1), hop(line, "x", -1)
+    half = 4 * SHARD
+    low, high = hop(before[:half], "x", 1), hop(after[half:], "x", -1)
+
+    across = [(0, 0), (0, 1), (3, 0), (3, 1), (1, 0), (1, 1), (2, 0), (2, 1)]
+    listed = lambda dx, shards: [(dx, dz, w) for dz, w in shards]
+    blocks = [line, before, after, low, high]
+    pieces = [listed(0, across), listed(3, across), listed(1, across), listed(2, across[:4]), listed(2, across[4:])]
+
+    rows = tie(exchange(sent, "y"), line)[0]
     rows_zl = hop(rows, "zl", 1)
     x_rows, g_rows = unpack(rows, rows_zl, hop(rows, "c", 1), hop(rows_zl, "c", 1))
-    wide, d_pre, line, far, plus, minus, mine = hidden_compute(x_rows, g_rows, blocks, pieces)
-    keep, send = inputs_compute(d_pre, line, wide)
+    wide, pre, hidden, far, plus, minus, mine = hidden_compute(x_rows, g_rows, blocks, pieces)
 
     low, high = hop(far[:XROWS // 2], "x", 1), hop(far[XROWS // 2:], "x", -1)
+    down_all, low, high = tie(down_all, low, high)
+    keep, send = inputs_compute(g_rows, wide, pre, hidden, down_all)
     message = combine(keep, hop(send, "c", 1)).reshape(PEERS, SLAB, PIECE)
     back = exchange(message, ("y", "zl"))
     token_grad, route_grad = finish(ids, share, back.reshape(PEERS * SLAB, PIECE))
 
-    plus, minus = relay(plus, minus, low, high, message)
+    plus, minus = relay(plus, minus, low, high)
     summed = add(hop(plus, "x", 1), hop(minus, "x", -1), mine)
-    summed = exchange(summed.reshape(8, SHARD, QUART), ("zh", "c")).reshape(4, 2, SHARD, QUART)
-    summed = jnp.sum(summed.astype(F32), axis=0).astype(BF)
-    down_grad = jnp.concatenate([summed[0], summed[1]], axis=1)
+
+    def quarter(shift):
+        return lax.dynamic_slice(summed, (lax.rem(zi + shift, 4) * BLOCK, 0), (BLOCK, QUART))
+
+    far, plus, minus, mine = quarter(2), quarter(1), quarter(3), quarter(0)
+    low, high = hop(far[:SHARD], "zh", 1), hop(far[SHARD:], "zh", -1)
+    plus = jnp.concatenate([add(plus[:SHARD], low), plus[SHARD:]], axis=0)
+    minus = jnp.concatenate([minus[:SHARD], add(minus[SHARD:], high)], axis=0)
+    summed = add(hop(plus, "zh", 1), hop(minus, "zh", -1), mine)
+    stay = lax.dynamic_slice(summed, (ci * SHARD, 0), (SHARD, QUART))
+    cross = hop(lax.dynamic_slice(summed, ((1 - ci) * SHARD, 0), (SHARD, QUART)), "c", 1)
+    down_grad = jnp.where(ci == 0, jnp.concatenate([stay, cross], axis=1), jnp.concatenate([cross, stay], axis=1))
     return token_grad, route_grad.reshape(TOK, 1), down_grad
 
 

time: 221 us -> 211 us (0.955)
  the two profiles are of different devices: /device:TPU:6 before, /device:TPU:103 now
where the time goes in v5:
time: 211 us; the launch traced here: 210 us
  starting transfers between devices  92.4 us (44%)
  waiting for transfers between devices  71.1 us (34%)
  Pallas kernels  19.8 us (9%)
  between operations  14.6 us (7%)
  local copies, waits for them, and re-layouts  10.5 us (5%)
    ppermute x22, starting transfers between devices, hop(): return lax.ppermute(a, axis, [(i, (i + shift) % n) for i in range(n)])  77.9 us
    ppermute x22, waiting for transfers between devices, hop(): return lax.ppermute(a, axis, [(i, (i + shift) % n) for i in range(n)])  70.4 us
    all_to_all x2, starting transfers between devices, exchange(): return lax.all_to_all(a, axes, split_axis=0, concat_axis=0, tiled=True)  14.4 us
    unnamed x36, local copies, waits for them, and re-layouts  10.3 us
    pallas_call x1, Pallas kernels, hidden_compute(): pl.pallas_call(lambda *refs: hidden_kernel(pieces, *refs), in_specs=[VMEM...  8.67 us
  transfers between devices with their start and end apart: 25, of which 13 were waited for; matrix products, arithmetic and copies ran while one was open for 1% of the time, Pallas kernels for 7%

profile of v5, /device:TPU:103, one launch (start us, length us, event | category | flops | bytes accessed | tf_op | source)
XLA Modules:
  0.0 210.4 jit_solution(7367465185527604988)
XLA Ops:
  7.2 0.0 all-gather.2.cloned.1.call-start
  7.2 0.7 all-gather.2.cloned.1.call-update
  7.9 1.2 copy-done.2
  9.1 1.2 copy-done.3
  10.3 0.7 copy-done.10
  10.9 0.7 copy-done.12
  11.6 1.6 dispatch.1
  13.1 6.6 %all-to-all-start = ((bf16[8,48,896]{2,1,0:T(8,128)(2,1)}), bf16[8,48,896]{2,1,0:T(8,128)(2,1)S(1)}, u32[]{:S(2)}, u32[]{:S(2)}) async-start(bf16[8,48,896]{2,1,0:T(8,128)(2,1)} %dispatch.1), calls=%async_computation | async-start | bytes 1376256 | tf_op jit(solution)/shard_map/all_to_all | solution.py:293
  19.8 3.1 %collective-permute-start = (bf16[112,512]{1,0:T(8,128)(2,1)S(1)}, bf16[112,512]{1,0:T(8,128)(2,1)S(1)}, u32[]{:S(2)}, u32[]{:S(2)}) collective-permute-start(bf16[112,512]{1,0:T(8,128)(2,1)S(1)} %pad_maximum_fusion.1), channel_id=1, source_target_pairs={{0,16},{16,0},{1,17},{17,1},{2,18},{18,2},{3,19},{19,3},{4,20},{20... | collective-permute-start | bytes 344072 | tf_op jit(solution)/shard_map/ppermute | solution.py:281
  23.0 0.9 collective-permute-done
  24.0 5.8 %collective-permute-start.1 = (bf16[224,512]{1,0:T(8,128)(2,1)S(1)}, bf16[224,512]{1,0:T(8,128)(2,1)S(1)}, u32[]{:S(2)}, u32[]{:S(2)}) collective-permute-start(bf16[224,512]{1,0:T(8,128)(2,1)S(1)} %pad_maximum_fusion), channel_id=1, source_target_pairs={{0,32},{32,64},{64,96},{96,0},{1,33},{33,65},{65,97},{97,1},{2,34}... | collective-permute-start | bytes 688136 | tf_op jit(solution)/shard_map/ppermute | solution.py:281
  29.8 5.9 %collective-permute-start.2 = (bf16[224,512]{1,0:T(8,128)(2,1)S(1)}, bf16[224,512]{1,0:T(8,128)(2,1)S(1)}, u32[]{:S(2)}, u32[]{:S(2)}) collective-permute-start(bf16[224,512]{1,0:T(8,128)(2,1)S(1)} %pad_maximum_fusion), channel_id=1, source_target_pairs={{0,96},{32,0},{64,32},{96,64},{1,97},{33,1},{65,33},{97,65},{2,98}... | collective-permute-start | bytes 688136 | tf_op jit(solution)/shard_map/ppermute | solution.py:281
  35.7 11.6 %collective-permute-done.1 = bf16[224,512]{1,0:T(8,128)(2,1)S(1)} collective-permute-done((bf16[224,512]{1,0:T(8,128)(2,1)S(1)}, bf16[224,512]{1,0:T(8,128)(2,1)S(1)}, u32[]{:S(2)}, u32[]{:S(2)}) %collective-permute-start.1) | collective-permute-done | bytes 229408 | tf_op jit(solution)/shard_map/ppermute | solution.py:281
  47.3 1.9 collective-permute-start.3
  49.2 0.0 collective-permute-done.2
  49.2 5.5 %collective-permute-start.4 = (bf16[112,512]{1,0:T(8,128)(2,1)S(1)}, bf16[112,512]{1,0:T(8,128)(2,1)S(1)}, u32[]{:S(2)}, u32[]{:S(2)}) collective-permute-start(bf16[112,512]{1,0:T(8,128)(2,1)S(1)} %slice.49), channel_id=1, source_target_pairs={{0,96},{32,0},{64,32},{96,64},{1,97},{33,1},{65,33},{97,65},{2,98}... | collective-permute-start | bytes 344072 | tf_op jit(solution)/shard_map/ppermute | solution.py:281
  54.8 3.3 %collective-permute-done.3 = bf16[112,512]{1,0:T(8,128)(2,1)S(1)} collective-permute-done((bf16[112,512]{1,0:T(8,128)(2,1)S(1)}, bf16[112,512]{1,0:T(8,128)(2,1)S(1)}, u32[]{:S(2)}, u32[]{:S(2)}) %collective-permute-start.3) | collective-permute-done | bytes 114720 | tf_op jit(solution)/shard_map/ppermute | solution.py:281
  58.1 0.0 collective-permute-done.4
  58.1 0.0 all-to-all-done.refs_0_
  58.1 4.2 %collective-permute-start.5 = (bf16[8,48,896]{2,1,0:T(8,128)(2,1)S(1)}, bf16[8,48,896]{2,1,0:T(8,128)(2,1)S(1)}, u32[]{:S(2)}, u32[]{:S(2)}) collective-permute-start(bf16[8,48,896]{2,1,0:T(8,128)(2,1)S(1)} %all-to-all-done.refs_0_), channel_id=1, source_target_pairs={{0,1},{1,0},{2,3},{3,2},{4,5},{5,4},{6,7},{7,6},{8,9},{9,8},{10,11... | collective-permute-start | bytes 2064392 | tf_op jit(solution)/shard_map/ppermute | solution.py:281
  62.3 1.9 collective-permute-start.8
  64.2 3.4 %collective-permute-start.9 = (bf16[896,512]{1,0:T(8,128)(2,1)S(1)}, bf16[896,512]{1,0:T(8,128)(2,1)S(1)}, u32[]{:S(2)}, u32[]{:S(2)}) collective-permute-start(bf16[896,512]{1,0:T(8,128)(2,1)S(1)} %constant_dynamic-update-slice_fusion.refs_2_), channel_id=1, source_target_pairs={{0,384},{128,0},{256,128},{384,256},{1,385},{129,1},{257,129},{385... | collective-permute-start | bytes 2752520 | tf_op jit(solution)/shard_map/ppermute | solution.py:281
  67.6 3.9 %collective-permute-start.6 = (bf16[8,48,896]{2,1,0:T(8,128)(2,1)S(1)}, bf16[8,48,896]{2,1,0:T(8,128)(2,1)S(1)}, u32[]{:S(2)}, u32[]{:S(2)}) collective-permute-start(bf16[8,48,896]{2,1,0:T(8,128)(2,1)S(1)} %all-to-all-done.refs_0_), channel_id=1, source_target_pairs={{0,16},{16,0},{1,17},{17,1},{2,18},{18,2},{3,19},{19,3},{4,20},{20... | collective-permute-start | bytes 2064392 | tf_op jit(solution)/shard_map/ppermute | solution.py:281
  71.5 20.2 %collective-permute-done.5.refs_1_ = bf16[8,48,896]{2,1,0:T(8,128)(2,1)S(1)} collective-permute-done((bf16[8,48,896]{2,1,0:T(8,128)(2,1)S(1)}, bf16[8,48,896]{2,1,0:T(8,128)(2,1)S(1)}, u32[]{:S(2)}, u32[]{:S(2)}) %collective-permute-start.5) | collective-permute-done | bytes 688160 | tf_op jit(solution)/shard_map/ppermute | solution.py:281
  91.8 2.9 %collective-permute-start.7 = (bf16[8,48,896]{2,1,0:T(8,128)(2,1)S(1)}, bf16[8,48,896]{2,1,0:T(8,128)(2,1)S(1)}, u32[]{:S(2)}, u32[]{:S(2)}) collective-permute-start(bf16[8,48,896]{2,1,0:T(8,128)(2,1)S(1)} %collective-permute-done.5.refs_1_), channel_id=1, source_target_pairs={{0,16},{16,0},{1,17},{17,1},{2,18},{18,2},{3,19},{19,3},{4,20},{20... | collective-permute-start | bytes 2064392 | tf_op jit(solution)/shard_map/ppermute | solution.py:281
  94.7 1.9 collective-permute-start.10
  96.7 3.4 %collective-permute-start.11 = (bf16[448,512]{1,0:T(8,128)(2,1)S(1)}, bf16[448,512]{1,0:T(8,128)(2,1)S(1)}, u32[]{:S(2)}, u32[]{:S(2)}) collective-permute-start(bf16[448,512]{1,0:T(8,128)(2,1)S(1)} %slice.51), channel_id=1, source_target_pairs={{0,384},{128,0},{256,128},{384,256},{1,385},{129,1},{257,129},{385... | collective-permute-start | bytes 1376264 | tf_op jit(solution)/shard_map/ppermute | solution.py:281
  100.1 1.7 unpack.1
  101.8 7.0 %collective-permute-done.10.refs_5_ = bf16[448,512]{1,0:T(8,128)(2,1)S(1)} collective-permute-done((bf16[448,512]{1,0:T(8,128)(2,1)S(1)}, bf16[448,512]{1,0:T(8,128)(2,1)S(1)}, u32[]{:S(2)}, u32[]{:S(2)}) %collective-permute-start.10) | collective-permute-done | bytes 458784 | tf_op jit(solution)/shard_map/ppermute | solution.py:281
  108.8 3.2 %collective-permute-done.11.refs_6_ = bf16[448,512]{1,0:T(8,128)(2,1)S(1)} collective-permute-done((bf16[448,512]{1,0:T(8,128)(2,1)S(1)}, bf16[448,512]{1,0:T(8,128)(2,1)S(1)}, u32[]{:S(2)}, u32[]{:S(2)}) %collective-permute-start.11) | collective-permute-done | bytes 458784 | tf_op jit(solution)/shard_map/ppermute | solution.py:281
  112.0 8.7 %hidden.1 = (bf16[3584,512]{1,0:T(8,128)(2,1)}, f32[192,512]{1,0:T(8,128)S(1)}, bf16[192,256]{1,0:T(8,128)(2,1)S(1)}, bf16[896,256]{1,0:T(8,128)(2,1)S(1)}, bf16...) custom-call(bf16[192,3584]{1,0:T(8,128)(2,1)S(1)} %get-tuple-element.24.refs_0_, ...), custom_call_target="tpu_custom_call" | custom-call | flops 1000000000 | bytes 8000000 | tf_op jit(solution)/shard_map/hidden/pallas_call | solution.py:204
  120.6 0.0 copy-start.6
  120.7 0.8 copy-done.4
  121.5 0.1 copy-done.6
  121.5 1.9 collective-permute-start.12
  123.4 3.4 %collective-permute-start.13 = (bf16[448,256]{1,0:T(8,128)(2,1)S(1)}, bf16[448,256]{1,0:T(8,128)(2,1)S(1)}, u32[]{:S(2)}, u32[]{:S(2)}) collective-permute-start(bf16[448,256]{1,0:T(8,128)(2,1)S(1)} %get-tuple-element.47), channel_id=1, source_target_pairs={{0,384},{128,0},{256,128},{384,256},{1,385},{129,1},{257,129},{385... | collective-permute-start | bytes 688136 | tf_op jit(solution)/shard_map/ppermute | solution.py:281
  126.8 2.9 %collective-permute-done.12.low_ref = bf16[448,256]{1,0:T(8,128)(2,1)S(1)} collective-permute-done((bf16[448,256]{1,0:T(8,128)(2,1)S(1)}, bf16[448,256]{1,0:T(8,128)(2,1)S(1)}, u32[]{:S(2)}, u32[]{:S(2)}) %collective-permute-start.12) | collective-permute-done | bytes 229408 | tf_op jit(solution)/shard_map/ppermute | solution.py:281
  129.7 2.6 %collective-permute-done.13.high_ref = bf16[448,256]{1,0:T(8,128)(2,1)S(1)} collective-permute-done((bf16[448,256]{1,0:T(8,128)(2,1)S(1)}, bf16[448,256]{1,0:T(8,128)(2,1)S(1)}, u32[]{:S(2)}, u32[]{:S(2)}) %collective-permute-start.13) | collective-permute-done | bytes 229408 | tf_op jit(solution)/shard_map/ppermute | solution.py:281
  132.4 0.7 copy-done.8
  133.1 2.0 copy-done
  135.1 2.0 copy-done.1
  137.1 1.0 copy-done.7
  138.1 3.5 %inputs.1 = (bf16[96,3712]{1,0:T(8,128)(2,1)S(1)}, bf16[96,3712]{1,0:T(8,128)(2,1)}) custom-call(bf16[192,3584]{1,0:T(8,128)(2,1)S(1)} %get-tuple-element.23.refs_1_.g_ref, bf16[3584,512]{1,0:T(8,128)(2,1)S(1)} %copy-done.1, f32[192,512]{1,0:T(8,128)S(1)} %copy-done.7, bf16[192,256]{1,0:T(8,128)(2,1)S(1)} %get-tuple-element.27.hidden_ref, ...), custom_call_target="tpu_custom_call" | custom-call | flops 1000000000 | bytes 8000000 | tf_op jit(solution)/shard_map/inputs/pallas_call | solution.py:246
  141.6 4.1 %collective-permute-start.14 = (bf16[96,3712]{1,0:T(8,128)(2,1)}, bf16[96,3712]{1,0:T(8,128)(2,1)S(1)}, u32[]{:S(2)}, u32[]{:S(2)}) collective-permute-start(bf16[96,3712]{1,0:T(8,128)(2,1)} %get-tuple-element.31), channel_id=1, source_target_pairs={{0,16},{16,0},{1,17},{17,1},{2,18},{18,2},{3,19},{19,3},{4,20},{20... | collective-permute-start | bytes 2138120 | tf_op jit(solution)/shard_map/ppermute | solution.py:281
  145.8 0.9 relay.1
  146.6 1.9 collective-permute-start.15
  148.6 3.4 %collective-permute-start.16 = (bf16[896,256]{1,0:T(8,128)(2,1)S(1)}, bf16[896,256]{1,0:T(8,128)(2,1)}, u32[]{:S(2)}, u32[]{:S(2)}) collective-permute-start(bf16[896,256]{1,0:T(8,128)(2,1)S(1)} %get-tuple-element.39), channel_id=1, source_target_pairs={{0,384},{128,0},{256,128},{384,256},{1,385},{129,1},{257,129},{385... | collective-permute-start | bytes 1376264 | tf_op jit(solution)/shard_map/ppermute | solution.py:281
  152.0 0.0 copy-start.11
  152.0 0.0 copy-start.13
  152.0 1.5 combine.1
  153.5 7.8 %all-to-all-start.1 = ((bf16[16,48,512]{2,1,0:T(8,128)(2,1)}), bf16[16,48,512]{2,1,0:T(8,128)(2,1)S(1)}, u32[]{:S(2)}, u32[]{:S(2)}) async-start(bf16[16,48,512]{2,1,0:T(8,128)(2,1)} %bitcast.2), calls=%async_computation.1 | async-start | bytes 1572864 | tf_op jit(solution)/shard_map/all_to_all | solution.py:293
  161.2 2.5 %collective-permute-done.16 = bf16[896,256]{1,0:T(8,128)(2,1)} collective-permute-done((bf16[896,256]{1,0:T(8,128)(2,1)S(1)}, bf16[896,256]{1,0:T(8,128)(2,1)}, u32[]{:S(2)}, u32[]{:S(2)}) %collective-permute-start.16) | collective-permute-done | bytes 458784 | tf_op jit(solution)/shard_map/ppermute | solution.py:281
  163.7 1.2 add_convert_fusion
  165.0 4.1 %collective-permute-start.17 = (bf16[112,256]{1,0:T(8,128)(2,1)S(1)}, bf16[112,256]{1,0:T(8,128)(2,1)S(1)}, u32[]{:S(2)}, u32[]{:S(2)}) collective-permute-start(bf16[112,256]{1,0:T(8,128)(2,1)S(1)} %get-tuple-element.43), channel_id=1, source_target_pairs={{0,32},{32,64},{64,96},{96,0},{1,33},{33,65},{65,97},{97,1},{2,34}... | collective-permute-start | bytes 172040 | tf_op jit(solution)/shard_map/ppermute | solution.py:281
  169.1 3.7 %collective-permute-start.19 = (bf16[112,256]{1,0:T(8,128)(2,1)S(1)}, bf16[112,256]{1,0:T(8,128)(2,1)S(1)}, u32[]{:S(2)}, u32[]{:S(2)}) collective-permute-start(bf16[112,256]{1,0:T(8,128)(2,1)S(1)} %get-tuple-element.45), channel_id=1, source_target_pairs={{0,96},{32,0},{64,32},{96,64},{1,97},{33,1},{65,33},{97,65},{2,98}... | collective-permute-start | bytes 172040 | tf_op jit(solution)/shard_map/ppermute | solution.py:281
  172.8 7.4 %collective-permute-done.19 = bf16[112,256]{1,0:T(8,128)(2,1)S(1)} collective-permute-done((bf16[112,256]{1,0:T(8,128)(2,1)S(1)}, bf16[112,256]{1,0:T(8,128)(2,1)S(1)}, u32[]{:S(2)}, u32[]{:S(2)}) %collective-permute-start.19) | collective-permute-done | bytes 57376 | tf_op jit(solution)/shard_map/ppermute | solution.py:281
  180.3 7.2 %collective-permute-start.18 = (bf16[224,256]{1,0:T(8,128)(2,1)S(1)}, bf16[224,256]{1,0:T(8,128)(2,1)S(1)}, u32[]{:S(2)}, u32[]{:S(2)}) collective-permute-start(bf16[224,256]{1,0:T(8,128)(2,1)S(1)} %pad_maximum_fusion.2), channel_id=1, source_target_pairs={{0,32},{32,64},{64,96},{96,0},{1,33},{33,65},{65,97},{97,1},{2,34}... | collective-permute-start | bytes 344072 | tf_op jit(solution)/shard_map/ppermute | solution.py:281
  187.5 1.9 collective-permute-start.20
  189.4 0.3 collective-permute-done.18
  189.7 7.6 %collective-permute-done.20 = bf16[224,256]{1,0:T(8,128)(2,1)S(1)} collective-permute-done((bf16[224,256]{1,0:T(8,128)(2,1)S(1)}, bf16[224,256]{1,0:T(8,128)(2,1)S(1)}, u32[]{:S(2)}, u32[]{:S(2)}) %collective-permute-start.20) | collective-permute-done | bytes 114720 | tf_op jit(solution)/shard_map/ppermute | solution.py:281
  197.4 2.6 %collective-permute-start.21 = (bf16[112,256]{1,0:T(8,128)(2,1)S(1)}, bf16[112,256]{1,0:T(8,128)(2,1)S(1)}, u32[]{:S(2)}, u32[]{:S(2)}) collective-permute-start(bf16[112,256]{1,0:T(8,128)(2,1)S(1)} %get-tuple-element.50), channel_id=1, source_target_pairs={{0,16},{16,0},{1,17},{17,1},{2,18},{18,2},{3,19},{19,3},{4,20},{20... | collective-permute-start | bytes 172040 | tf_op jit(solution)/shard_map/ppermute | solution.py:281
  199.9 0.9 collective-permute-done.21
  200.8 0.7 maximum_select_fusion
  201.5 2.0 finish.1
  (48 shorter events, 0.4 us)
Async XLA Ops:
  7.2 12.6 %copy-start.14 = (bf16[112,512]{1,0:T(8,128)(2,1)S(1)}, bf16[112,512]{1,0:T(8,128)(2,1)}, u32[]{:S(2)}) copy-start(bf16[112,512]{1,0:T(8,128)(2,1)} %param.12) | copy-start | bytes 344068
  7.2 125.9 %all-gather.2.cloned.1.call-start = ((), (), s32[]{:S(2)}) async-start(), calls=%async_computation.2 | async-start | bytes 3784704 | tf_op jit(solution)/shard_map/all_gather | solution.py:305
  7.9 1.2 copy-start.2
  9.1 1.2 copy-start.3
  10.3 0.7 copy-start.10
  10.9 0.7 copy-start.12
  11.6 8.2 %copy-start.15 = (bf16[112,512]{1,0:T(8,128)(2,1)S(1)}, bf16[112,512]{1,0:T(8,128)(2,1)}, u32[]{:S(2)}) copy-start(bf16[112,512]{1,0:T(8,128)(2,1)} %param.11) | copy-start | bytes 344068
  13.1 45.0 %all-to-all-start = ((bf16[8,48,896]{2,1,0:T(8,128)(2,1)}), bf16[8,48,896]{2,1,0:T(8,128)(2,1)S(1)}, u32[]{:S(2)}, u32[]{:S(2)}) async-start(bf16[8,48,896]{2,1,0:T(8,128)(2,1)} %dispatch.1), calls=%async_computation | async-start | bytes 1376256 | tf_op jit(solution)/shard_map/all_to_all | solution.py:293
  19.8 4.1 %collective-permute-start = (bf16[112,512]{1,0:T(8,128)(2,1)S(1)}, bf16[112,512]{1,0:T(8,128)(2,1)S(1)}, u32[]{:S(2)}, u32[]{:S(2)}) collective-permute-start(bf16[112,512]{1,0:T(8,128)(2,1)S(1)} %pad_maximum_fusion.1), channel_id=1, source_target_pairs={{0,16},{16,0},{1,17},{17,1},{2,18},{18,2},{3,19},{19,3},{4,20},{20... | collective-permute-start | bytes 344072 | tf_op jit(solution)/shard_map/ppermute | solution.py:281
  24.0 23.3 %collective-permute-start.1 = (bf16[224,512]{1,0:T(8,128)(2,1)S(1)}, bf16[224,512]{1,0:T(8,128)(2,1)S(1)}, u32[]{:S(2)}, u32[]{:S(2)}) collective-permute-start(bf16[224,512]{1,0:T(8,128)(2,1)S(1)} %pad_maximum_fusion), channel_id=1, source_target_pairs={{0,32},{32,64},{64,96},{96,0},{1,33},{33,65},{65,97},{97,1},{2,34}... | collective-permute-start | bytes 688136 | tf_op jit(solution)/shard_map/ppermute | solution.py:281
  29.8 19.4 %collective-permute-start.2 = (bf16[224,512]{1,0:T(8,128)(2,1)S(1)}, bf16[224,512]{1,0:T(8,128)(2,1)S(1)}, u32[]{:S(2)}, u32[]{:S(2)}) collective-permute-start(bf16[224,512]{1,0:T(8,128)(2,1)S(1)} %pad_maximum_fusion), channel_id=1, source_target_pairs={{0,96},{32,0},{64,32},{96,64},{1,97},{33,1},{65,33},{97,65},{2,98}... | collective-permute-start | bytes 688136 | tf_op jit(solution)/shard_map/ppermute | solution.py:281
  47.3 10.8 %collective-permute-start.3 = (bf16[112,512]{1,0:T(8,128)(2,1)S(1)}, bf16[112,512]{1,0:T(8,128)(2,1)S(1)}, u32[]{:S(2)}, u32[]{:S(2)}) collective-permute-start(bf16[112,512]{1,0:T(8,128)(2,1)S(1)} %slice.48), channel_id=1, source_target_pairs={{0,32},{32,64},{64,96},{96,0},{1,33},{33,65},{65,97},{97,1},{2,34}... | collective-permute-start | bytes 344072 | tf_op jit(solution)/shard_map/ppermute | solution.py:281
  49.2 8.9 %collective-permute-start.4 = (bf16[112,512]{1,0:T(8,128)(2,1)S(1)}, bf16[112,512]{1,0:T(8,128)(2,1)S(1)}, u32[]{:S(2)}, u32[]{:S(2)}) collective-permute-start(bf16[112,512]{1,0:T(8,128)(2,1)S(1)} %slice.49), channel_id=1, source_target_pairs={{0,96},{32,0},{64,32},{96,64},{1,97},{33,1},{65,33},{97,65},{2,98}... | collective-permute-start | bytes 344072 | tf_op jit(solution)/shard_map/ppermute | solution.py:281
  58.1 33.6 %collective-permute-start.5 = (bf16[8,48,896]{2,1,0:T(8,128)(2,1)S(1)}, bf16[8,48,896]{2,1,0:T(8,128)(2,1)S(1)}, u32[]{:S(2)}, u32[]{:S(2)}) collective-permute-start(bf16[8,48,896]{2,1,0:T(8,128)(2,1)S(1)} %all-to-all-done.refs_0_), channel_id=1, source_target_pairs={{0,1},{1,0},{2,3},{3,2},{4,5},{5,4},{6,7},{7,6},{8,9},{9,8},{10,11... | collective-permute-start | bytes 2064392 | tf_op jit(solution)/shard_map/ppermute | solution.py:281
  62.3 32.4 %collective-permute-start.8 = (bf16[896,512]{1,0:T(8,128)(2,1)S(1)}, bf16[896,512]{1,0:T(8,128)(2,1)S(1)}, u32[]{:S(2)}, u32[]{:S(2)}) collective-permute-start(bf16[896,512]{1,0:T(8,128)(2,1)S(1)} %constant_dynamic-update-slice_fusion.refs_2_), channel_id=1, source_target_pairs={{0,128},{128,256},{256,384},{384,0},{1,129},{129,257},{257,385},{3... | collective-permute-start | bytes 2752520 | tf_op jit(solution)/shard_map/ppermute | solution.py:281
  64.2 32.4 %collective-permute-start.9 = (bf16[896,512]{1,0:T(8,128)(2,1)S(1)}, bf16[896,512]{1,0:T(8,128)(2,1)S(1)}, u32[]{:S(2)}, u32[]{:S(2)}) collective-permute-start(bf16[896,512]{1,0:T(8,128)(2,1)S(1)} %constant_dynamic-update-slice_fusion.refs_2_), channel_id=1, source_target_pairs={{0,384},{128,0},{256,128},{384,256},{1,385},{129,1},{257,129},{385... | collective-permute-start | bytes 2752520 | tf_op jit(solution)/shard_map/ppermute | solution.py:281
  67.6 32.5 %collective-permute-start.6 = (bf16[8,48,896]{2,1,0:T(8,128)(2,1)S(1)}, bf16[8,48,896]{2,1,0:T(8,128)(2,1)S(1)}, u32[]{:S(2)}, u32[]{:S(2)}) collective-permute-start(bf16[8,48,896]{2,1,0:T(8,128)(2,1)S(1)} %all-to-all-done.refs_0_), channel_id=1, source_target_pairs={{0,16},{16,0},{1,17},{17,1},{2,18},{18,2},{3,19},{19,3},{4,20},{20... | collective-permute-start | bytes 2064392 | tf_op jit(solution)/shard_map/ppermute | solution.py:281
  91.8 8.3 %collective-permute-start.7 = (bf16[8,48,896]{2,1,0:T(8,128)(2,1)S(1)}, bf16[8,48,896]{2,1,0:T(8,128)(2,1)S(1)}, u32[]{:S(2)}, u32[]{:S(2)}) collective-permute-start(bf16[8,48,896]{2,1,0:T(8,128)(2,1)S(1)} %collective-permute-done.5.refs_1_), channel_id=1, source_target_pairs={{0,16},{16,0},{1,17},{17,1},{2,18},{18,2},{3,19},{19,3},{4,20},{20... | collective-permute-start | bytes 2064392 | tf_op jit(solution)/shard_map/ppermute | solution.py:281
  94.7 14.0 %collective-permute-start.10 = (bf16[448,512]{1,0:T(8,128)(2,1)S(1)}, bf16[448,512]{1,0:T(8,128)(2,1)S(1)}, u32[]{:S(2)}, u32[]{:S(2)}) collective-permute-start(bf16[448,512]{1,0:T(8,128)(2,1)S(1)} %slice.50), channel_id=1, source_target_pairs={{0,128},{128,256},{256,384},{384,0},{1,129},{129,257},{257,385},{3... | collective-permute-start | bytes 1376264 | tf_op jit(solution)/shard_map/ppermute | solution.py:281
  96.7 15.2 %collective-permute-start.11 = (bf16[448,512]{1,0:T(8,128)(2,1)S(1)}, bf16[448,512]{1,0:T(8,128)(2,1)S(1)}, u32[]{:S(2)}, u32[]{:S(2)}) collective-permute-start(bf16[448,512]{1,0:T(8,128)(2,1)S(1)} %slice.51), channel_id=1, source_target_pairs={{0,384},{128,0},{256,128},{384,256},{1,385},{129,1},{257,129},{385... | collective-permute-start | bytes 1376264 | tf_op jit(solution)/shard_map/ppermute | solution.py:281
  120.6 0.8 copy-start.4
  120.6 0.9 copy-start.6
  121.5 8.2 %collective-permute-start.12 = (bf16[448,256]{1,0:T(8,128)(2,1)S(1)}, bf16[448,256]{1,0:T(8,128)(2,1)S(1)}, u32[]{:S(2)}, u32[]{:S(2)}) collective-permute-start(bf16[448,256]{1,0:T(8,128)(2,1)S(1)} %get-tuple-element.48), channel_id=1, source_target_pairs={{0,128},{128,256},{256,384},{384,0},{1,129},{129,257},{257,385},{3... | collective-permute-start | bytes 688136 | tf_op jit(solution)/shard_map/ppermute | solution.py:281
  123.4 8.9 %collective-permute-start.13 = (bf16[448,256]{1,0:T(8,128)(2,1)S(1)}, bf16[448,256]{1,0:T(8,128)(2,1)S(1)}, u32[]{:S(2)}, u32[]{:S(2)}) collective-permute-start(bf16[448,256]{1,0:T(8,128)(2,1)S(1)} %get-tuple-element.47), channel_id=1, source_target_pairs={{0,384},{128,0},{256,128},{384,256},{1,385},{129,1},{257,129},{385... | collective-permute-start | bytes 688136 | tf_op jit(solution)/shard_map/ppermute | solution.py:281
  132.4 0.7 copy-start.8
  133.1 2.0 copy-start
  135.1 2.0 copy-start.1
  137.1 1.0 copy-start.7
  138.1 7.6 %copy-start.5 = (bf16[896,256]{1,0:T(8,128)(2,1)S(1)}, bf16[896,256]{1,0:T(8,128)(2,1)}, u32[]{:S(2)}) copy-start(bf16[896,256]{1,0:T(8,128)(2,1)} %copy-done.4) | copy-start | bytes 1376260
  138.1 7.6 %copy-start.9 = (bf16[448,256]{1,0:T(8,128)(2,1)S(1)}, bf16[448,256]{1,0:T(8,128)(2,1)}, u32[]{:S(2)}) copy-start(bf16[448,256]{1,0:T(8,128)(2,1)} %copy-done.8) | copy-start | bytes 688132
  141.6 10.3 %collective-permute-start.14 = (bf16[96,3712]{1,0:T(8,128)(2,1)}, bf16[96,3712]{1,0:T(8,128)(2,1)S(1)}, u32[]{:S(2)}, u32[]{:S(2)}) collective-permute-start(bf16[96,3712]{1,0:T(8,128)(2,1)} %get-tuple-element.31), channel_id=1, source_target_pairs={{0,16},{16,0},{1,17},{17,1},{2,18},{18,2},{3,19},{19,3},{4,20},{20... | collective-permute-start | bytes 2138120 | tf_op jit(solution)/shard_map/ppermute | solution.py:281
  146.6 14.6 %collective-permute-start.15 = (bf16[896,256]{1,0:T(8,128)(2,1)}, bf16[896,256]{1,0:T(8,128)(2,1)S(1)}, u32[]{:S(2)}, u32[]{:S(2)}) collective-permute-start(bf16[896,256]{1,0:T(8,128)(2,1)} %get-tuple-element.38), channel_id=1, source_target_pairs={{0,128},{128,256},{256,384},{384,0},{1,129},{129,257},{257,385},{3... | collective-permute-start | bytes 1376264 | tf_op jit(solution)/shard_map/ppermute | solution.py:281
  148.6 15.2 %collective-permute-start.16 = (bf16[896,256]{1,0:T(8,128)(2,1)S(1)}, bf16[896,256]{1,0:T(8,128)(2,1)}, u32[]{:S(2)}, u32[]{:S(2)}) collective-permute-start(bf16[896,256]{1,0:T(8,128)(2,1)S(1)} %get-tuple-element.39), channel_id=1, source_target_pairs={{0,384},{128,0},{256,128},{384,256},{1,385},{129,1},{257,129},{385... | collective-permute-start | bytes 1376264 | tf_op jit(solution)/shard_map/ppermute | solution.py:281
  152.0 49.5 %copy-start.11 = (s32[128,1]{0,1:T(1,128)S(1)}, s32[128,1]{0,1:T(1,128)}, u32[]{:S(2)}) copy-start(s32[128,1]{0,1:T(1,128)} %param.9) | copy-start | bytes 1540
  152.0 49.5 %copy-start.13 = (f32[128,1]{0,1:T(1,128)S(1)}, f32[128,1]{0,1:T(1,128)}, u32[]{:S(2)}) copy-start(f32[128,1]{0,1:T(1,128)} %param.10) | copy-start | bytes 1540
  153.5 48.0 %all-to-all-start.1 = ((bf16[16,48,512]{2,1,0:T(8,128)(2,1)}), bf16[16,48,512]{2,1,0:T(8,128)(2,1)S(1)}, u32[]{:S(2)}, u32[]{:S(2)}) async-start(bf16[16,48,512]{2,1,0:T(8,128)(2,1)} %bitcast.2), calls=%async_computation.1 | async-start | bytes 1572864 | tf_op jit(solution)/shard_map/all_to_all | solution.py:293
  165.0 7.9 %collective-permute-start.17 = (bf16[112,256]{1,0:T(8,128)(2,1)S(1)}, bf16[112,256]{1,0:T(8,128)(2,1)S(1)}, u32[]{:S(2)}, u32[]{:S(2)}) collective-permute-start(bf16[112,256]{1,0:T(8,128)(2,1)S(1)} %get-tuple-element.43), channel_id=1, source_target_pairs={{0,32},{32,64},{64,96},{96,0},{1,33},{33,65},{65,97},{97,1},{2,34}... | collective-permute-start | bytes 172040 | tf_op jit(solution)/shard_map/ppermute | solution.py:281
  169.1 11.1 %collective-permute-start.19 = (bf16[112,256]{1,0:T(8,128)(2,1)S(1)}, bf16[112,256]{1,0:T(8,128)(2,1)S(1)}, u32[]{:S(2)}, u32[]{:S(2)}) collective-permute-start(bf16[112,256]{1,0:T(8,128)(2,1)S(1)} %get-tuple-element.45), channel_id=1, source_target_pairs={{0,96},{32,0},{64,32},{96,64},{1,97},{33,1},{65,33},{97,65},{2,98}... | collective-permute-start | bytes 172040 | tf_op jit(solution)/shard_map/ppermute | solution.py:281
  180.3 9.4 %collective-permute-start.18 = (bf16[224,256]{1,0:T(8,128)(2,1)S(1)}, bf16[224,256]{1,0:T(8,128)(2,1)S(1)}, u32[]{:S(2)}, u32[]{:S(2)}) collective-permute-start(bf16[224,256]{1,0:T(8,128)(2,1)S(1)} %pad_maximum_fusion.2), channel_id=1, source_target_pairs={{0,32},{32,64},{64,96},{96,0},{1,33},{33,65},{65,97},{97,1},{2,34}... | collective-permute-start | bytes 344072 | tf_op jit(solution)/shard_map/ppermute | solution.py:281
  187.5 9.8 %collective-permute-start.20 = (bf16[224,256]{1,0:T(8,128)(2,1)S(1)}, bf16[224,256]{1,0:T(8,128)(2,1)S(1)}, u32[]{:S(2)}, u32[]{:S(2)}) collective-permute-start(bf16[224,256]{1,0:T(8,128)(2,1)S(1)} %pad_maximum_fusion.3), channel_id=1, source_target_pairs={{0,96},{32,0},{64,32},{96,64},{1,97},{33,1},{65,33},{97,65},{2,98}... | collective-permute-start | bytes 344072 | tf_op jit(solution)/shard_map/ppermute | solution.py:281
  197.4 3.4 %collective-permute-start.21 = (bf16[112,256]{1,0:T(8,128)(2,1)S(1)}, bf16[112,256]{1,0:T(8,128)(2,1)S(1)}, u32[]{:S(2)}, u32[]{:S(2)}) collective-permute-start(bf16[112,256]{1,0:T(8,128)(2,1)S(1)} %get-tuple-element.50), channel_id=1, source_target_pairs={{0,16},{16,0},{1,17},{17,1},{2,18},{18,2},{3,19},{19,3},{4,20},{20... | collective-permute-start | bytes 172040 | tf_op jit(solution)/shard_map/ppermute | solution.py:281
Sparse Core Ops, SparseCore 0:
  11.1 77.4 all-gather.1

commit v6 on v0

v6 whole, which is shorter than its diff:
```python
import jax
import jax.numpy as jnp
from jax import lax
from jax.experimental import pallas as pl
from jax.experimental.pallas import tpu as pltpu
from jax.sharding import Mesh, PartitionSpec as P

BF = jnp.bfloat16
F32 = jnp.float32
I32 = jnp.int32
AXES = ("x", "zh", "c", "y", "zl")
PEERS = ("x", "y", "zl")
TOK = 128
D = 3584
EXPERTS = 8
CAP = 6
HALF = 512
SHARD = 112
PART = D // 4
SOURCES = 2 * EXPERTS
ROWS = SOURCES * CAP
VMEM_LIMIT = 24 * 1024 * 1024
VMEM = pl.BlockSpec(memory_space=pltpu.VMEM)


def iota(shape, dim):
    return lax.broadcasted_iota(I32, shape, dim)


def onehot(hit):
    return jnp.where(hit, 1.0, 0.0).astype(BF)


def sixth(i):
    return (i * 171) >> 10


def token_ranks(ids):
    member = jnp.where(ids == iota((EXPERTS, TOK), 0), 1.0, 0.0)
    earlier = onehot(iota((TOK, TOK), 0) < iota((TOK, TOK), 1))
    counts = jnp.dot(member.astype(BF), earlier, preferred_element_type=F32)
    return jnp.sum(member * counts, axis=0, keepdims=True).astype(I32)


def to_column(row):
    diagonal = iota((TOK, TOK), 0) == iota((TOK, TOK), 1)
    return jnp.sum(jnp.where(diagonal, row, 0.0), axis=1, keepdims=True)


def call(body, name, out_shape, operands, flops, scratch=(), specs=None):
    return pl.pallas_call(
        body,
        in_specs=specs or [VMEM] * len(operands),
        out_specs=[VMEM] * len(out_shape),
        out_shape=[jax.ShapeDtypeStruct(shape, kind) for shape, kind in out_shape],
        scratch_shapes=list(scratch),
        compiler_params=pltpu.CompilerParams(vmem_limit_bytes=VMEM_LIMIT),
        cost_estimate=pl.CostEstimate(flops=flops, bytes_accessed=4 * 10**6, transcendentals=0),
        name=name,
    )(*operands)


def dispatch_kernel(ids_ref, p_ref, x_ref, g_ref, out_ref):
    ids = ids_ref[...]
    slot = jnp.where(ids < EXPERTS, ids * 16 + token_ranks(ids), -16)
    at = iota((TOK, TOK), 0)
    sel = jnp.concatenate([onehot(slot == at), onehot(slot + 8 == at)], axis=1)
    scaled = (to_column(p_ref[...]) * g_ref[...].astype(F32)).astype(BF)
    for i in range(4):
        columns = slice(i * PART, (i + 1) * PART)
        both = jnp.concatenate([x_ref[:, columns], scaled[:, columns]], axis=0)
        rows = jnp.dot(sel, both, preferred_element_type=F32).astype(BF).reshape(EXPERTS, 16, PART)
        out_ref[i, :, 0] = rows
        out_ref[i, :, 1] = rows


def before_kernel(rows_ref, weight_ref, part_ref, g_ref, x_scr):
    row, at = iota((2 * ROWS, SOURCES * 16), 0), iota((2 * ROWS, SOURCES * 16), 1)
    grad = jnp.where(row >= ROWS, 1, 0)
    slot = row - ROWS * grad
    source = sixth(slot)
    pick = onehot(at == source * 16 + (slot - CAP * source) + 8 * grad)
    for i in range(4):
        moved = jnp.dot(pick, rows_ref[i], preferred_element_type=F32).astype(BF)
        x_scr[i * ROWS:(i + 1) * ROWS] = moved[:ROWS]
        g_ref[i * ROWS:(i + 1) * ROWS] = moved[ROWS:]
    pre = jnp.dot(x_scr[...], weight_ref[:, :2 * HALF], preferred_element_type=F32).astype(BF)
    part_ref[:, :, :2 * HALF] = pre.reshape(4, ROWS, 2 * HALF)
    hid = jnp.dot(g_ref[...], weight_ref[:, 2 * HALF:], preferred_element_type=F32).astype(BF)
    part_ref[:, :, 2 * HALF:] = hid.reshape(4, ROWS, HALF)


def middle_kernel(part_ref, out_ref, line_ref):
    total = part_ref[0].astype(F32) + part_ref[1].astype(F32) + part_ref[2].astype(F32) + part_ref[3].astype(F32)
    gate, up, grad = total[:, :HALF], total[:, HALF:2 * HALF], total[:, 2 * HALF:]
    sig = jax.nn.sigmoid(gate)
    act = gate * sig
    slope = sig * (1.0 + gate * (1.0 - sig))
    hidden = (act * up).astype(BF)
    route = jnp.sum(hidden.astype(F32) * grad, axis=1, keepdims=True)
    d_gate, d_up = (grad * up * slope).astype(BF), (grad * act).astype(BF)
    for i in range(4):
        out_ref[i, :, :HALF] = d_gate
        out_ref[i, :, HALF:2 * HALF] = d_up
        out_ref[i, :, 2 * HALF:] = hidden
    row = iota((ROWS, 128), 0)
    line_ref[...] = jnp.where(iota((ROWS, 128), 1) == row - CAP * sixth(row), route, 0.0).astype(BF)


def after_kernel(mid_ref, line_ref, g_ref, weight_ref, back_ref, far_ref, plus_ref, minus_ref, own_ref, send_ref, down):
    xi, zi, ci = lax.axis_index("x"), lax.axis_index("zh"), lax.axis_index("c")
    mid = mid_ref[...].reshape(4 * ROWS, 3 * HALF)
    down[...] = lax.dot_general(
        g_ref[...], mid[:, 2 * HALF:], (((0,), (0,)), ((), ())), preferred_element_type=F32
    ).astype(BF)

    def shard(shift, core):
        block = 2 * lax.rem(zi + shift, 4) + core
        return down[pl.ds(pl.multiple_of(block * SHARD, 16), SHARD)]

    for i, (ref, shift) in enumerate(((far_ref, 2), (plus_ref, 1), (minus_ref, 3), (own_ref, 0))):
        ref[...] = shard(shift, ci)
        send_ref[i] = shard(shift, 1 - ci)
    grads = lax.dot_general(
        mid[:, :2 * HALF], weight_ref[:, :2 * HALF], (((1,), (1,)), ((), ())), preferred_element_type=F32
    ).astype(BF)
    row, at = iota((SOURCES * 8, ROWS), 0), iota((SOURCES * 8, ROWS), 1)
    source = sixth(at)
    spread = onehot(row == source * 8 + (at - CAP * source))
    gather = onehot(row == source * 8 + CAP)
    extra = jnp.dot(gather, line_ref[...], preferred_element_type=F32)
    for i in range(4):
        rows = jnp.dot(spread, grads[i * ROWS:(i + 1) * ROWS], preferred_element_type=F32)
        first = rows[:, :128] + jnp.where(xi == i, extra, 0.0)
        back_ref[i] = jnp.concatenate([first, rows[:, 128:]], axis=1).astype(BF)


def finish_kernel(ids_ref, p_ref, rows_ref, tok_ref, route_ref):
    ids = ids_ref[...]
    rank = token_ranks(ids)
    valid = ids < EXPERTS
    base = to_column(jnp.where(valid, ids * 16, -64).astype(F32)).astype(I32)
    rank = to_column(rank.astype(F32)).astype(I32)
    at = iota((TOK, TOK), 1)
    sel = onehot((at == base + rank) | (at == base + rank + 8))
    pick = onehot((at == base + CAP) | (at == base + CAP + 8))
    values = jnp.zeros((TOK, TOK), F32)
    for i in range(4):
        got = jnp.dot(sel, rows_ref[i], preferred_element_type=F32)
        tok_ref[:, i * PART:(i + 1) * PART] = got.astype(BF)
        values = values + jnp.dot(pick, rows_ref[i, :, :TOK], preferred_element_type=F32)
    route = jnp.sum(jnp.where(at == rank, values, 0.0), axis=1, keepdims=True)
    diagonal = iota((TOK, TOK), 0) == at
    route_ref[...] = jnp.sum(jnp.where(diagonal, route, 0.0), axis=0, keepdims=True) / p_ref[...]


def hop(a, axis, shift):
    n = lax.axis_size(axis)
    return lax.ppermute(a, axis, [(i, (i + shift) % n) for i in range(n)])


def add(*terms):
    return sum(a.astype(F32) for a in terms).astype(BF)


def exchange(a, axes):
    return lax.all_to_all(a, axes, split_axis=0, concat_axis=0, tiled=True)


def per_device(tokens, grad_out, routing, route_weight, gate_weight, up_weight, down_weight):
    ids, share = routing.reshape(1, TOK), route_weight.reshape(1, TOK)
    weights = jnp.concatenate([gate_weight, up_weight, down_weight], axis=1)
    weights = lax.all_gather(weights, ("zh", "c"), axis=0, tiled=True)

    sent, = call(dispatch_kernel, "dispatch", [((4, EXPERTS, 2, 16, PART), BF)],
                 (ids, share, tokens, grad_out), 3 * 10**8)
    rows = exchange(sent.reshape(64, 16, PART), PEERS).reshape(4, SOURCES * 16, PART)
    part, g_rows = call(before_kernel, "before", [((4, ROWS, 3 * HALF), BF), ((4 * ROWS, PART), BF)],
                        (rows, weights), 14 * 10**8, [pltpu.VMEM((4 * ROWS, PART), BF)])
    mid, line = call(middle_kernel, "middle", [((4, ROWS, 3 * HALF), BF), ((ROWS, 128), BF)],
                     (exchange(part, "x"),), 10**7)
    shard = ((SHARD, HALF), BF)
    back, far, plus, minus, mine, send = call(
        after_kernel, "after",
        [((4, SOURCES * 8, PART), BF), shard, shard, shard, shard, ((4, SHARD, HALF), BF)],
        (exchange(mid, "x"), line, g_rows, weights), 14 * 10**8, [pltpu.VMEM((PART, HALF), BF)],
    )
    back = exchange(back.reshape(64, 8, PART), PEERS).reshape(4, SOURCES * 8, PART)
    token_grad, route_grad = call(finish_kernel, "finish", [((TOK, D), BF), ((1, TOK), F32)],
                                  (ids, share, back), 2 * 10**8)

    got = hop(send, "c", 1)
    far, plus, minus, mine = [add(a, got[i]) for i, a in enumerate((far, plus, minus, mine))]
    cut = SHARD // 2
    low, high = hop(far[:cut], "zh", 1), hop(far[cut:], "zh", -1)
    plus = jnp.concatenate([add(plus[:cut], low), plus[cut:]], axis=0)
    minus = jnp.concatenate([minus[:cut], add(minus[cut:], high)], axis=0)
    down_grad = add(hop(plus, "zh", 1), hop(minus, "zh", -1), mine)
    return token_grad, route_grad.reshape(TOK, 1), down_grad


def solution(mesh):
    inner = Mesh(mesh.devices.reshape(4, 4, 2, 8, 2), AXES)
    rows = P(AXES, None)
    weights = P(("x", "zh", "c"), ("y", "zl"))
    return jax.shard_map(
        per_device,
        mesh=inner,
        in_specs=(rows, rows, rows, rows, weights, weights, weights),
        out_specs=(rows, rows, weights),
        check_vma=False,
    )
```

time: 337 us -> 169 us (0.50)
  waiting for transfers between devices: 258 us -> 19.4 us
  blocking collectives: 0 us -> 94.4 us
  matrix products: 16.2 us -> 0 us
  local copies, waits for them, and re-layouts: 12.9 us -> 4.3 us
  Pallas kernels: 0 us -> 6.97 us
  starting transfers between devices: 29.5 us -> 25.9 us
    all_gather x3 -> x1, waiting for transfers between devices: 122 us -> 7.91 us  [per_device(): weights = lax.all_gather(weights, ('zh', 'c'), axis=0, tiled=True)]
    all_to_all x0 -> x3, blocking collectives: none -> 94.4 us  [exchange(): return lax.all_to_all(a, axes, split_axis=0, concat_axis=0, tiled=True)]
    all_to_all x5 -> x1, waiting for transfers between devices: 80.6 us -> 0.01 us  [exchange(): return lax.all_to_all(a, axes, split_axis=0, concat_axis=0, tiled=True)]
    reduce_scatter x1 -> x0, waiting for transfers between devices: 53.2 us -> none  [per_device(): lax.psum_scatter(lax.dot_general(scaled, hidden, (((0,), (0,)), ((), ()))...]
    all_to_all x5 -> x1, starting transfers between devices: 29.3 us -> 9.71 us  [exchange(): return lax.all_to_all(a, axes, split_axis=0, concat_axis=0, tiled=True)]
    dot_general x6 -> x0, matrix products: 16.2 us -> none  [the longest x1 3.43 us: per_device(): lax.dot_general(d_gate_pre, gate_full, contract, preferred_element_type=j...]
    ppermute x0 -> x5, starting transfers between devices: none -> 16.2 us  [hop(): return lax.ppermute(a, axis, [(i, (i + shift) % n) for i in range(n)])]
    ppermute x0 -> x5, waiting for transfers between devices: none -> 11.5 us  [hop(): return lax.ppermute(a, axis, [(i, (i + shift) % n) for i in range(n)])]
  transfers between devices with their start and end apart: 9 -> 7, of which waited for: 8 -> 4; matrix products, arithmetic and copies ran while one was open for 8% -> 1% of each run, Pallas kernels for 0% -> 0%
where the time goes in v6:
time: 169 us; the launch traced here: 168 us
  blocking collectives  94.4 us (56%)
  starting transfers between devices  25.9 us (15%)
  waiting for transfers between devices  19.4 us (11%)
  between operations  14.2 us (8%)
  Pallas kernels  6.97 us (4%)
  local copies, waits for them, and re-layouts  4.3 us (3%)
  other arithmetic  2.69 us (2%)
    all_to_all x3, blocking collectives, exchange(): return lax.all_to_all(a, axes, split_axis=0, concat_axis=0, tiled=True)  94.4 us
    ppermute x5, starting transfers between devices, hop(): return lax.ppermute(a, axis, [(i, (i + shift) % n) for i in range(n)])  16.2 us
    ppermute x5, waiting for transfers between devices, hop(): return lax.ppermute(a, axis, [(i, (i + shift) % n) for i in range(n)])  11.5 us
    all_to_all x1, starting transfers between devices, exchange(): return lax.all_to_all(a, axes, split_axis=0, concat_axis=0, tiled=True)  9.71 us
    all_gather x1, waiting for transfers between devices, per_device(): weights = lax.all_gather(weights, ('zh', 'c'), axis=0, tiled=True)  7.91 us
    pallas_call x5, Pallas kernels, call(): pl.pallas_call(body, in_specs=specs or [VMEM] * len(operands), out_specs=...  6.97 us
    unnamed x16, local copies, waits for them, and re-layouts  4.28 us
  transfers between devices with their start and end apart: 7, of which 4 were waited for; matrix products, arithmetic and copies ran while one was open for 1% of the time, Pallas kernels for 0%

profile of v6, /device:TPU:6, one launch (start us, length us, event | category | flops | bytes accessed | tf_op | source)
XLA Modules:
  0.0 167.9 jit_solution(9220187639761399596)
XLA Ops:
  7.2 0.0 copy-start
  7.2 0.0 all-gather.2.cloned.1.call-start
  7.2 1.8 %pad_maximum_fusion = bf16[112,1536]{1,0:T(8,128)(2,1)} fusion(bf16[112,512]{1,0:T(8,128)(2,1)} %param.13, bf16[112,512]{1,0:T(8,128)(2,1)} %param.12, bf16[112,512]{1,0:T(8,128)(2,1)} %param.11), kind=kLoop, calls=%fused_computation | loop fusion | flops 1032192 | bytes 688128 | tf_op jit(solution)/shard_map/concatenate | solution.py:172
  9.1 0.0 all-gather.2.cloned.1.call-update
  9.1 0.0 copy-done
  9.1 0.0 copy-start.1
  9.1 1.2 copy-done.1
  10.3 0.0 copy-start.2
  10.3 0.7 copy-done.2
  10.9 0.0 copy-start.4
  10.9 0.7 copy-done.4
  11.6 0.6 dispatch.1
  12.2 56.3 %all_to_all.20 = bf16[64,16,896]{2,1,0:T(8,128)(2,1)S(1)} all-to-all(bf16[64,16,896]{2,1,0:T(8,128)(2,1)S(1)} %bitcast.27), channel_id=1, replica_groups=mesh['x'=4,'zh'=4,'c'=2,'y'=8,'zl'=2] {'x','y','zl'}, dimensions={0} | all-to-all | bytes 3670016 | tf_op jit(solution)/shard_map/all_to_all | solution.py:167
  68.5 7.9 %all-gather.2.cloned.1.call-done.weight_ref = bf16[896,1536]{1,0:T(8,128)(2,1)} async-done(((bf16[112,1536]{1,0:T(8,128)(2,1)}), bf16[896,1536]{1,0:T(8,128)(2,1)}) %all-gather.2.cloned.1.call-update) | async-done | bytes 2752528 | tf_op jit(solution)/shard_map/all_gather | solution.py:173
  76.4 0.0 copy-start.6
  76.4 1.8 %copy-done.6 = bf16[896,1536]{1,0:T(8,128)(2,1)S(1)} copy-done((bf16[896,1536]{1,0:T(8,128)(2,1)S(1)}, bf16[896,1536]{1,0:T(8,128)(2,1)}, u32[]{:S(2)}) %copy-start.6) | copy-done | bytes 2752536
  78.2 1.8 %before.1 = (bf16[4,96,1536]{2,1,0:T(8,128)(2,1)S(1)}, bf16[384,896]{1,0:T(8,128)(2,1)S(1)}) custom-call(bf16[4,256,896]{2,1,0:T(8,128)(2,1)S(1)} %bitcast.29, bf16[896,1536]{1,0:T(8,128)(2,1)S(1)} %copy-done.6), custom_call_target="tpu_custom_call" | custom-call | flops 1400000000 | bytes 4000000 | tf_op jit(solution)/shard_map/before/pallas_call | solution.py:51
  80.0 19.4 %all_to_all.21.part_ref = bf16[4,96,1536]{2,1,0:T(8,128)(2,1)S(1)} all-to-all(bf16[4,96,1536]{2,1,0:T(8,128)(2,1)S(1)} %get-tuple-element.15), channel_id=1, replica_groups=mesh['x'=4,'zh'=4,'c'=2,'y'=8,'zl'=2] {'x'}, dimensions={0} | all-to-all | bytes 2359296 | tf_op jit(solution)/shard_map/all_to_all | solution.py:167
  99.4 0.0 copy-start.7
  99.4 0.4 middle.1
  99.8 18.6 %all_to_all.22.mid_ref = bf16[4,96,1536]{2,1,0:T(8,128)(2,1)S(1)} all-to-all(bf16[4,96,1536]{2,1,0:T(8,128)(2,1)S(1)} %get-tuple-element.16), channel_id=1, replica_groups=mesh['x'=4,'zh'=4,'c'=2,'y'=8,'zl'=2] {'x'}, dimensions={0} | all-to-all | bytes 2359296 | tf_op jit(solution)/shard_map/all_to_all | solution.py:167
  118.4 0.0 copy-done.7
  118.4 2.7 %after.1 = (bf16[4,128,896]{2,1,0:T(8,128)(2,1)}, bf16[112,512]{1,0:T(8,128)(2,1)S(1)}, bf16[112,512]{1,0:T(8,128)(2,1)S(1)}, bf16[112,512]{1,0:T(8,128)(2,1)S(1...) custom-call(bf16[4,96,1536]{2,1,0:T(8,128)(2,1)S(1)} %all_to_all.22.mid_ref, ...), custom_call_target="tpu_custom_call" | custom-call | flops 1400000000 | bytes 4000000 | tf_op jit(solution)/shard_map/after/pallas_call | solution.py:51
  121.1 1.9 %collective-permute-start = (bf16[4,112,512]{2,1,0:T(8,128)(2,1)S(1)}, bf16[4,112,512]{2,1,0:T(8,128)(2,1)S(1)}, u32[]{:S(2)}, u32[]{:S(2)}) collective-permute-start(bf16[4,112,512]{2,1,0:T(8,128)(2,1)S(1)} %get-tuple-element.23), channel_id=1, source_target_pairs={{0,16},{16,0},{1,17},{17,1},{2,18},{18,2},{3,19},{19,3},{4,20},{20... | collective-permute-start | bytes 1376264 | tf_op jit(solution)/shard_map/ppermute | solution.py:159
  123.0 9.7 %all-to-all-start.3 = ((bf16[64,8,896]{2,1,0:T(8,128)(2,1)}), bf16[64,8,896]{2,1,0:T(8,128)(2,1)S(1)}, u32[]{:S(2)}, u32[]{:S(2)}) async-start(bf16[64,8,896]{2,1,0:T(8,128)(2,1)} %bitcast.4), calls=%async_computation.3 | async-start | bytes 1835008 | tf_op jit(solution)/shard_map/all_to_all | solution.py:167
  132.7 0.0 collective-permute-done
  132.7 0.1 fusion.3
  132.8 0.0 copy-start.3
  132.8 0.0 copy-start.5
  132.9 3.5 %collective-permute-start.3 = (bf16[56,512]{1,0:T(8,128)(2,1)S(1)}, bf16[56,512]{1,0:T(8,128)(2,1)S(1)}, u32[]{:S(2)}, u32[]{:S(2)}) collective-permute-start(bf16[56,512]{1,0:T(8,128)(2,1)S(1)} %get-tuple-element.31), channel_id=1, source_target_pairs={{0,96},{32,0},{64,32},{96,64},{1,97},{33,1},{65,33},{97,65},{2,98}... | collective-permute-start | bytes 172040 | tf_op jit(solution)/shard_map/ppermute | solution.py:159
  136.4 3.3 %collective-permute-start.1 = (bf16[56,512]{1,0:T(8,128)(2,1)S(1)}, bf16[56,512]{1,0:T(8,128)(2,1)S(1)}, u32[]{:S(2)}, u32[]{:S(2)}) collective-permute-start(bf16[56,512]{1,0:T(8,128)(2,1)S(1)} %get-tuple-element.30), channel_id=1, source_target_pairs={{0,32},{32,64},{64,96},{96,0},{1,33},{33,65},{65,97},{97,1},{2,34}... | collective-permute-start | bytes 172040 | tf_op jit(solution)/shard_map/ppermute | solution.py:159
  139.6 0.7 collective-permute-done.3
  140.3 4.8 %collective-permute-start.4 = (bf16[112,512]{1,0:T(8,128)(2,1)S(1)}, bf16[112,512]{1,0:T(8,128)(2,1)S(1)}, u32[]{:S(2)}, u32[]{:S(2)}) collective-permute-start(bf16[112,512]{1,0:T(8,128)(2,1)S(1)} %pad_maximum_fusion.2), channel_id=1, source_target_pairs={{0,96},{32,0},{64,32},{96,64},{1,97},{33,1},{65,33},{97,65},{2,98}... | collective-permute-start | bytes 344072 | tf_op jit(solution)/shard_map/ppermute | solution.py:159
  145.2 1.2 collective-permute-done.1
  146.4 2.7 %collective-permute-start.2 = (bf16[112,512]{1,0:T(8,128)(2,1)S(1)}, bf16[112,512]{1,0:T(8,128)(2,1)S(1)}, u32[]{:S(2)}, u32[]{:S(2)}) collective-permute-start(bf16[112,512]{1,0:T(8,128)(2,1)S(1)} %pad_maximum_fusion.1), channel_id=1, source_target_pairs={{0,32},{32,64},{64,96},{96,0},{1,33},{33,65},{65,97},{97,1},{2,34}... | collective-permute-start | bytes 344072 | tf_op jit(solution)/shard_map/ppermute | solution.py:159
  149.1 0.0 collective-permute-done.4
  149.1 9.6 %collective-permute-done.2 = bf16[112,512]{1,0:T(8,128)(2,1)S(1)} collective-permute-done((bf16[112,512]{1,0:T(8,128)(2,1)S(1)}, bf16[112,512]{1,0:T(8,128)(2,1)S(1)}, u32[]{:S(2)}, u32[]{:S(2)}) %collective-permute-start.2) | collective-permute-done | bytes 114720 | tf_op jit(solution)/shard_map/ppermute | solution.py:159
  158.8 0.7 add_convert_fusion
  159.5 0.0 all-to-all-done.3
  159.5 0.0 copy-done.3
  159.5 0.0 copy-done.5
  159.5 1.6 finish.1
  (7 shorter events, 0.1 us)
Async XLA Ops:
  7.2 1.9 %copy-start = (bf16[128,3584]{1,0:T(8,128)(2,1)S(1)}, bf16[128,3584]{1,0:T(8,128)(2,1)}, u32[]{:S(2)}) copy-start(bf16[128,3584]{1,0:T(8,128)(2,1)} %x_ref.1) | copy-start | bytes 2752516
  7.2 69.2 %all-gather.2.cloned.1.call-start = ((), (), s32[]{:S(2)}) async-start(), calls=%async_computation.4 | async-start | bytes 3096576 | tf_op jit(solution)/shard_map/all_gather | solution.py:173
  9.1 1.2 copy-start.1
  10.3 0.7 copy-start.2
  10.9 0.7 copy-start.4
  76.4 1.8 %copy-start.6 = (bf16[896,1536]{1,0:T(8,128)(2,1)S(1)}, bf16[896,1536]{1,0:T(8,128)(2,1)}, u32[]{:S(2)}) copy-start(bf16[896,1536]{1,0:T(8,128)(2,1)} %all-gather.2.cloned.1.call-done.weight_ref) | copy-start | bytes 8257540
  99.4 19.0 %copy-start.7 = (bf16[896,1536]{1,0:T(8,128)(2,1)S(1)}, bf16[896,1536]{1,0:T(8,128)(2,1)}, u32[]{:S(2)}) copy-start(bf16[896,1536]{1,0:T(8,128)(2,1)} %all-gather.2.cloned.1.call-done.weight_ref) | copy-start | bytes 8257540
  121.1 11.6 %collective-permute-start = (bf16[4,112,512]{2,1,0:T(8,128)(2,1)S(1)}, bf16[4,112,512]{2,1,0:T(8,128)(2,1)S(1)}, u32[]{:S(2)}, u32[]{:S(2)}) collective-permute-start(bf16[4,112,512]{2,1,0:T(8,128)(2,1)S(1)} %get-tuple-element.23), channel_id=1, source_target_pairs={{0,16},{16,0},{1,17},{17,1},{2,18},{18,2},{3,19},{19,3},{4,20},{20... | collective-permute-start | bytes 1376264 | tf_op jit(solution)/shard_map/ppermute | solution.py:159
  123.0 36.5 %all-to-all-start.3 = ((bf16[64,8,896]{2,1,0:T(8,128)(2,1)}), bf16[64,8,896]{2,1,0:T(8,128)(2,1)S(1)}, u32[]{:S(2)}, u32[]{:S(2)}) async-start(bf16[64,8,896]{2,1,0:T(8,128)(2,1)} %bitcast.4), calls=%async_computation.3 | async-start | bytes 1835008 | tf_op jit(solution)/shard_map/all_to_all | solution.py:167
  132.8 26.7 %copy-start.3 = (s32[128,1]{0,1:T(1,128)S(1)}, s32[128,1]{0,1:T(1,128)}, u32[]{:S(2)}) copy-start(s32[128,1]{0,1:T(1,128)} %param.9) | copy-start | bytes 1540
  132.8 26.7 %copy-start.5 = (f32[128,1]{0,1:T(1,128)S(1)}, f32[128,1]{0,1:T(1,128)}, u32[]{:S(2)}) copy-start(f32[128,1]{0,1:T(1,128)} %param.10) | copy-start | bytes 1540
  132.9 7.4 %collective-permute-start.3 = (bf16[56,512]{1,0:T(8,128)(2,1)S(1)}, bf16[56,512]{1,0:T(8,128)(2,1)S(1)}, u32[]{:S(2)}, u32[]{:S(2)}) collective-permute-start(bf16[56,512]{1,0:T(8,128)(2,1)S(1)} %get-tuple-element.31), channel_id=1, source_target_pairs={{0,96},{32,0},{64,32},{96,64},{1,97},{33,1},{65,33},{97,65},{2,98}... | collective-permute-start | bytes 172040 | tf_op jit(solution)/shard_map/ppermute | solution.py:159
  136.4 10.0 %collective-permute-start.1 = (bf16[56,512]{1,0:T(8,128)(2,1)S(1)}, bf16[56,512]{1,0:T(8,128)(2,1)S(1)}, u32[]{:S(2)}, u32[]{:S(2)}) collective-permute-start(bf16[56,512]{1,0:T(8,128)(2,1)S(1)} %get-tuple-element.30), channel_id=1, source_target_pairs={{0,32},{32,64},{64,96},{96,0},{1,33},{33,65},{65,97},{97,1},{2,34}... | collective-permute-start | bytes 172040 | tf_op jit(solution)/shard_map/ppermute | solution.py:159
  140.3 8.8 %collective-permute-start.4 = (bf16[112,512]{1,0:T(8,128)(2,1)S(1)}, bf16[112,512]{1,0:T(8,128)(2,1)S(1)}, u32[]{:S(2)}, u32[]{:S(2)}) collective-permute-start(bf16[112,512]{1,0:T(8,128)(2,1)S(1)} %pad_maximum_fusion.2), channel_id=1, source_target_pairs={{0,96},{32,0},{64,32},{96,64},{1,97},{33,1},{65,33},{97,65},{2,98}... | collective-permute-start | bytes 344072 | tf_op jit(solution)/shard_map/ppermute | solution.py:159
  146.4 12.4 %collective-permute-start.2 = (bf16[112,512]{1,0:T(8,128)(2,1)S(1)}, bf16[112,512]{1,0:T(8,128)(2,1)S(1)}, u32[]{:S(2)}, u32[]{:S(2)}) collective-permute-start(bf16[112,512]{1,0:T(8,128)(2,1)S(1)} %pad_maximum_fusion.1), channel_id=1, source_target_pairs={{0,32},{32,64},{64,96},{96,0},{1,33},{33,65},{65,97},{97,1},{2,34}... | collective-permute-start | bytes 344072 | tf_op jit(solution)/shard_map/ppermute | solution.py:159
Sparse Core Ops, SparseCore 0:
  10.7 65.6 all-gather.1

commit v7 on v6

--- a/solution.py
+++ b/solution.py
@@ -19,7 +19,10 @@
 PART = D // 4
 SOURCES = 2 * EXPERTS
 ROWS = SOURCES * CAP
+SLAB = 88
 VMEM_LIMIT = 24 * 1024 * 1024
+MOST_VMEM = 56 * 1024 * 1024
+ANYWHERE = pl.BlockSpec(memory_space=pl.ANY)
 VMEM = pl.BlockSpec(memory_space=pltpu.VMEM)
 
 
@@ -47,47 +50,82 @@
     return jnp.sum(jnp.where(diagonal, row, 0.0), axis=1, keepdims=True)
 
 
-def call(body, name, out_shape, operands, flops, scratch=(), specs=None):
+def call(body, name, out_shape, operands, flops, scratch=(), specs=None, limit=VMEM_LIMIT):
     return pl.pallas_call(
         body,
         in_specs=specs or [VMEM] * len(operands),
         out_specs=[VMEM] * len(out_shape),
         out_shape=[jax.ShapeDtypeStruct(shape, kind) for shape, kind in out_shape],
         scratch_shapes=list(scratch),
-        compiler_params=pltpu.CompilerParams(vmem_limit_bytes=VMEM_LIMIT),
+        compiler_params=pltpu.CompilerParams(vmem_limit_bytes=limit),
         cost_estimate=pl.CostEstimate(flops=flops, bytes_accessed=4 * 10**6, transcendentals=0),
         name=name,
     )(*operands)
 
 
-def dispatch_kernel(ids_ref, p_ref, x_ref, g_ref, out_ref):
+def dispatch_kernel(ids_hbm, p_hbm, x_hbm, g_hbm, out_ref, ids_ref, p_ref, x_ref, g_ref, sems):
+    copies = [
+        pltpu.make_async_copy(source, target, sems.at[i])
+        for i, (source, target) in enumerate(((ids_hbm, ids_ref), (p_hbm, p_ref), (x_hbm, x_ref), (g_hbm, g_ref)))
+    ]
+    for copy in copies:
+        copy.start()
+    k, at = iota((EXPERTS, SLAB, 7 * TOK), 1), iota((EXPERTS, SLAB, 7 * TOK), 2)
+    q = (k * 43) >> 9
+    k = k - 12 * q
+    order = q * TOK + iota((EXPERTS, SLAB, 7 * TOK), 0) * 16 + k + jnp.where(k >= CAP, 2, 0)
+    order = onehot(at == order).reshape(EXPERTS * SLAB, 7 * TOK)
+    for copy in copies:
+        copy.wait()
     ids = ids_ref[...]
     slot = jnp.where(ids < EXPERTS, ids * 16 + token_ranks(ids), -16)
     at = iota((TOK, TOK), 0)
     sel = jnp.concatenate([onehot(slot == at), onehot(slot + 8 == at)], axis=1)
     scaled = (to_column(p_ref[...]) * g_ref[...].astype(F32)).astype(BF)
-    for i in range(4):
-        columns = slice(i * PART, (i + 1) * PART)
-        both = jnp.concatenate([x_ref[:, columns], scaled[:, columns]], axis=0)
-        rows = jnp.dot(sel, both, preferred_element_type=F32).astype(BF).reshape(EXPERTS, 16, PART)
-        out_ref[i, :, 0] = rows
-        out_ref[i, :, 1] = rows
-
-
-def before_kernel(rows_ref, weight_ref, part_ref, g_ref, x_scr):
-    row, at = iota((2 * ROWS, SOURCES * 16), 0), iota((2 * ROWS, SOURCES * 16), 1)
-    grad = jnp.where(row >= ROWS, 1, 0)
-    slot = row - ROWS * grad
-    source = sixth(slot)
-    pick = onehot(at == source * 16 + (slot - CAP * source) + 8 * grad)
-    for i in range(4):
-        moved = jnp.dot(pick, rows_ref[i], preferred_element_type=F32).astype(BF)
-        x_scr[i * ROWS:(i + 1) * ROWS] = moved[:ROWS]
-        g_ref[i * ROWS:(i + 1) * ROWS] = moved[ROWS:]
-    pre = jnp.dot(x_scr[...], weight_ref[:, :2 * HALF], preferred_element_type=F32).astype(BF)
+    both = jnp.concatenate([x_ref[...], scaled], axis=0)
+    rows = jnp.dot(sel, both, preferred_element_type=F32).astype(BF)
+    for i in range(2):
+        stack = []
+        for q in range(7):
+            left = 2 * i * PART + q * TOK
+            stack.append(jnp.concatenate([rows[:, left:left + TOK], rows[:, left + PART:left + PART + TOK]], axis=1))
+        moved = jnp.dot(order, jnp.concatenate(stack, axis=0), preferred_element_type=F32).astype(BF)
+        for j in range(2):
+            one = moved[:, j * TOK:(j + 1) * TOK].reshape(EXPERTS, SLAB, TOK)
+            out_ref[2 * i + j, :, 0] = one
+            out_ref[2 * i + j, :, 1] = one
+
+
+def before_kernel(rows_ref, wide_hbm, line_ref, other_ref, part_ref, g_ref, x_scr, wide, down, sem):
+    zi, ci = lax.axis_index("zh"), lax.axis_index("c")
+    copy = pltpu.make_async_copy(wide_hbm, wide, sem)
+    copy.start()
+    shape = (7, 2, 48, EXPERTS * SLAB)
+    j = iota(shape, 2)
+    source = sixth(j)
+    place = source * SLAB + iota(shape, 0) * 12 + iota(shape, 1) * CAP + (j - CAP * source)
+    pick = onehot(iota(shape, 3) == place).reshape(7 * ROWS, EXPERTS * SLAB)
+    for i in range(2):
+        for h in range(2):
+            half = slice(h * EXPERTS * SLAB, (h + 1) * EXPERTS * SLAB)
+            both = jnp.concatenate([rows_ref[2 * i, half], rows_ref[2 * i + 1, half]], axis=1)
+            moved = jnp.dot(pick, both, preferred_element_type=F32).astype(BF)
+            for k in range(2):
+                at = slice((2 * i + k) * ROWS + h * 48, (2 * i + k) * ROWS + h * 48 + 48)
+                for q in range(7):
+                    columns = slice(q * TOK, (q + 1) * TOK)
+                    x_scr[at, columns] = moved[q * ROWS:q * ROWS + 48, k * TOK:(k + 1) * TOK]
+                    g_ref[at, columns] = moved[q * ROWS + 48:(q + 1) * ROWS, k * TOK:(k + 1) * TOK]
+    for i, shift in enumerate((0, 3, 1, 2)):
+        block = 2 * lax.rem(zi + shift, 4)
+        rows = slice(i * SHARD, (i + 1) * SHARD)
+        down[pl.ds(pl.multiple_of((block + ci) * SHARD, 16), SHARD)] = line_ref[rows]
+        down[pl.ds(pl.multiple_of((block + 1 - ci) * SHARD, 16), SHARD)] = other_ref[rows]
+    hid = jnp.dot(g_ref[...], down[...], preferred_element_type=F32).astype(BF)
+    part_ref[:, :, 2 * HALF:] = hid.reshape(4, ROWS, HALF)
+    copy.wait()
+    pre = jnp.dot(x_scr[...], wide[...], preferred_element_type=F32).astype(BF)
     part_ref[:, :, :2 * HALF] = pre.reshape(4, ROWS, 2 * HALF)
-    hid = jnp.dot(g_ref[...], weight_ref[:, 2 * HALF:], preferred_element_type=F32).astype(BF)
-    part_ref[:, :, 2 * HALF:] = hid.reshape(4, ROWS, HALF)
 
 
 def middle_kernel(part_ref, out_ref, line_ref):
@@ -122,7 +160,7 @@
         ref[...] = shard(shift, ci)
         send_ref[i] = shard(shift, 1 - ci)
     grads = lax.dot_general(
-        mid[:, :2 * HALF], weight_ref[:, :2 * HALF], (((1,), (1,)), ((), ())), preferred_element_type=F32
+        mid[:, :2 * HALF], weight_ref[...], (((1,), (1,)), ((), ())), preferred_element_type=F32
     ).astype(BF)
     row, at = iota((SOURCES * 8, ROWS), 0), iota((SOURCES * 8, ROWS), 1)
     source = sixth(at)
@@ -169,21 +207,32 @@
 
 def per_device(tokens, grad_out, routing, route_weight, gate_weight, up_weight, down_weight):
     ids, share = routing.reshape(1, TOK), route_weight.reshape(1, TOK)
-    weights = jnp.concatenate([gate_weight, up_weight, down_weight], axis=1)
-    weights = lax.all_gather(weights, ("zh", "c"), axis=0, tiled=True)
-
-    sent, = call(dispatch_kernel, "dispatch", [((4, EXPERTS, 2, 16, PART), BF)],
-                 (ids, share, tokens, grad_out), 3 * 10**8)
-    rows = exchange(sent.reshape(64, 16, PART), PEERS).reshape(4, SOURCES * 16, PART)
-    part, g_rows = call(before_kernel, "before", [((4, ROWS, 3 * HALF), BF), ((4 * ROWS, PART), BF)],
-                        (rows, weights), 14 * 10**8, [pltpu.VMEM((4 * ROWS, PART), BF)])
+    wide = lax.all_gather(jnp.concatenate([gate_weight, up_weight], axis=1), ("zh", "c"), axis=0, tiled=True)
+
+    sent, = call(
+        dispatch_kernel, "dispatch", [((4, EXPERTS, 2, SLAB, TOK), BF)], (ids, share, tokens, grad_out), 10**9,
+        [pltpu.VMEM((1, TOK), I32), pltpu.VMEM((1, TOK), F32), pltpu.VMEM((TOK, D), BF), pltpu.VMEM((TOK, D), BF),
+         pltpu.SemaphoreType.DMA((4,))], [ANYWHERE] * 4, MOST_VMEM,
+    )
+    rows = exchange(sent.reshape(64, SLAB, TOK), PEERS).reshape(4, SOURCES * SLAB, TOK)
+
+    cut = SHARD // 2
+    z_before, z_after = hop(down_weight, "zh", 1), hop(down_weight, "zh", -1)
+    z_low, z_high = hop(z_before[:cut], "zh", 1), hop(z_after[cut:], "zh", -1)
+    shards = jnp.concatenate([down_weight, z_before, z_after, z_low, z_high], axis=0)
+    part, g_rows = call(
+        before_kernel, "before", [((4, ROWS, 3 * HALF), BF), ((4 * ROWS, PART), BF)],
+        (rows, wide, shards, hop(shards, "c", 1)), 2 * 10**9,
+        [pltpu.VMEM((4 * ROWS, PART), BF), pltpu.VMEM((PART, 2 * HALF), BF), pltpu.VMEM((PART, HALF), BF),
+         pltpu.SemaphoreType.DMA(())], [VMEM, ANYWHERE, VMEM, VMEM],
+    )
     mid, line = call(middle_kernel, "middle", [((4, ROWS, 3 * HALF), BF), ((ROWS, 128), BF)],
                      (exchange(part, "x"),), 10**7)
     shard = ((SHARD, HALF), BF)
     back, far, plus, minus, mine, send = call(
         after_kernel, "after",
         [((4, SOURCES * 8, PART), BF), shard, shard, shard, shard, ((4, SHARD, HALF), BF)],
-        (exchange(mid, "x"), line, g_rows, weights), 14 * 10**8, [pltpu.VMEM((PART, HALF), BF)],
+        (exchange(mid, "x"), line, g_rows, wide), 14 * 10**8, [pltpu.VMEM((PART, HALF), BF)],
     )
     back = exchange(back.reshape(64, 8, PART), PEERS).reshape(4, SOURCES * 8, PART)
     token_grad, route_grad = call(finish_kernel, "finish", [((TOK, D), BF), ((1, TOK), F32)],
@@ -191,11 +240,7 @@
 
     got = hop(send, "c", 1)
     far, plus, minus, mine = [add(a, got[i]) for i, a in enumerate((far, plus, minus, mine))]
-    cut = SHARD // 2
-    low, high = hop(far[:cut], "zh", 1), hop(far[cut:], "zh", -1)
-    plus = jnp.concatenate([add(plus[:cut], low), plus[cut:]], axis=0)
-    minus = jnp.concatenate([minus[:cut], add(minus[cut:], high)], axis=0)
-    down_grad = add(hop(plus, "zh", 1), hop(minus, "zh", -1), mine)
+    down_grad = add(hop(plus, "zh", 1), hop(minus, "zh", -1), hop(far, "zh", 2), mine)
     return token_grad, route_grad.reshape(TOK, 1), down_grad
 
 

time: 169 us -> 173 us (1.024)
  blocking collectives: 94.4 us -> 37.3 us
  starting transfers between devices: 25.9 us -> 59.7 us
  waiting for transfers between devices: 19.4 us -> 45.5 us
  Pallas kernels: 6.97 us -> 11.3 us
  local copies, waits for them, and re-layouts: 4.3 us -> 1.57 us
    all_to_all x3 -> x2, blocking collectives: 94.4 us -> 37.3 us  [exchange(): return lax.all_to_all(a, axes, split_axis=0, concat_axis=0, tiled=True)]
    ppermute x5 -> x9, waiting for transfers between devices: 11.5 us -> 45.5 us  [hop(): return lax.ppermute(a, axis, [(i, (i + shift) % n) for i in range(n)])]
    ppermute x5 -> x9, starting transfers between devices: 16.2 us -> 36.3 us  [hop(): return lax.ppermute(a, axis, [(i, (i + shift) % n) for i in range(n)])]
    all_to_all x1 -> x2, starting transfers between devices: 9.71 us -> 23.3 us  [exchange(): return lax.all_to_all(a, axes, split_axis=0, concat_axis=0, tiled=True)]
    all_gather x1, waiting for transfers between devices: 7.91 us -> 0.01 us  [per_device(): lax.all_gather(jnp.concatenate([gate_weight, up_weight], axis=1), ('zh',...]
    pallas_call x5, Pallas kernels: 6.97 us -> 11.3 us  [call(): pl.pallas_call(body, in_specs=specs or [VMEM] * len(operands), out_specs=...]
    unnamed x16 -> x14, local copies, waits for them, and re-layouts: 4.28 us -> 1.56 us
  transfers between devices with their start and end apart: 7 -> 12, of which waited for: 4 -> 8; matrix products, arithmetic and copies ran while one was open for 1% -> 0% of each run, Pallas kernels for 0% -> 2%
where the time goes in v7:
time: 173 us; the launch traced here: 172 us
  starting transfers between devices  59.7 us (35%)
  waiting for transfers between devices  45.5 us (26%)
  blocking collectives  37.3 us (22%)
  between operations  14.2 us (8%)
  Pallas kernels  11.3 us (7%)
  other arithmetic  2.47 us (1%)
    ppermute x9, waiting for transfers between devices, hop(): return lax.ppermute(a, axis, [(i, (i + shift) % n) for i in range(n)])  45.5 us
    all_to_all x2, blocking collectives, exchange(): return lax.all_to_all(a, axes, split_axis=0, concat_axis=0, tiled=True)  37.3 us
    ppermute x9, starting transfers between devices, hop(): return lax.ppermute(a, axis, [(i, (i + shift) % n) for i in range(n)])  36.3 us
    all_to_all x2, starting transfers between devices, exchange(): return lax.all_to_all(a, axes, split_axis=0, concat_axis=0, tiled=True)  23.3 us
    pallas_call x5, Pallas kernels, call(): pl.pallas_call(body, in_specs=specs or [VMEM] * len(operands), out_specs=...  11.3 us
  transfers between devices with their start and end apart: 12, of which 8 were waited for; matrix products, arithmetic and copies ran while one was open for 0% of the time, Pallas kernels for 2%

profile of v7, /device:TPU:6, one launch (start us, length us, event | category | flops | bytes accessed | tf_op | source)
XLA Modules:
  0.0 172.0 jit_solution(12792671812722831247)
XLA Ops:
  7.2 0.0 all-gather.2.cloned.1.call-start
  7.2 1.7 pad_maximum_fusion
  8.9 0.0 all-gather.2.cloned.1.call-update
  8.9 4.0 %dispatch.1 = bf16[4,8,2,88,128]{4,3,2,1,0:T(8,128)(2,1)} custom-call(s32[1,128]{1,0:T(1,128)} %bitcast.29, f32[1,128]{1,0:T(1,128)} %bitcast.31, bf16[128,3584]{1,0:T(8,128)(2,1)} %x_hbm.1, bf16[128,3584]{1,0:T(8,128)(2,1)} %g_hbm.1), custom_call_target="tpu_custom_call" | custom-call | flops 1000000000 | bytes 4000000 | tf_op jit(solution)/shard_map/dispatch/pallas_call | solution.py:54
  12.9 0.0 copy-start.4
  12.9 12.8 %all-to-all-start = ((bf16[64,88,128]{2,1,0:T(8,128)(2,1)}), bf16[64,88,128]{2,1,0:T(8,128)(2,1)S(1)}, u32[]{:S(2)}, u32[]{:S(2)}) async-start(bf16[64,88,128]{2,1,0:T(8,128)(2,1)} %bitcast.33), calls=%async_computation | async-start | bytes 2883584 | tf_op jit(solution)/shard_map/all_to_all | solution.py:205
  25.7 0.0 copy-done.4
  25.7 6.1 %collective-permute-start = (bf16[112,512]{1,0:T(8,128)(2,1)S(1)}, bf16[112,512]{1,0:T(8,128)(2,1)S(1)}, u32[]{:S(2)}, u32[]{:S(2)}) collective-permute-start(bf16[112,512]{1,0:T(8,128)(2,1)S(1)} %copy-done.4), channel_id=1, source_target_pairs={{0,32},{32,64},{64,96},{96,0},{1,33},{33,65},{65,97},{97,1},{2,34}... | collective-permute-start | bytes 344072 | tf_op jit(solution)/shard_map/ppermute | solution.py:197
  31.8 5.9 %collective-permute-start.1 = (bf16[112,512]{1,0:T(8,128)(2,1)S(1)}, bf16[112,512]{1,0:T(8,128)(2,1)S(1)}, u32[]{:S(2)}, u32[]{:S(2)}) collective-permute-start(bf16[112,512]{1,0:T(8,128)(2,1)S(1)} %copy-done.4), channel_id=1, source_target_pairs={{0,96},{32,0},{64,32},{96,64},{1,97},{33,1},{65,33},{97,65},{2,98}... | collective-permute-start | bytes 344072 | tf_op jit(solution)/shard_map/ppermute | solution.py:197
  37.7 28.4 %collective-permute-done = bf16[112,512]{1,0:T(8,128)(2,1)S(1)} collective-permute-done((bf16[112,512]{1,0:T(8,128)(2,1)S(1)}, bf16[112,512]{1,0:T(8,128)(2,1)S(1)}, u32[]{:S(2)}, u32[]{:S(2)}) %collective-permute-start) | collective-permute-done | bytes 114720 | tf_op jit(solution)/shard_map/ppermute | solution.py:197
  66.1 1.9 %collective-permute-start.2 = (bf16[56,512]{1,0:T(8,128)(2,1)S(1)}, bf16[56,512]{1,0:T(8,128)(2,1)S(1)}, u32[]{:S(2)}, u32[]{:S(2)}) collective-permute-start(bf16[56,512]{1,0:T(8,128)(2,1)S(1)} %slice.24), channel_id=1, source_target_pairs={{0,32},{32,64},{64,96},{96,0},{1,33},{33,65},{65,97},{97,1},{2,34}... | collective-permute-start | bytes 172040 | tf_op jit(solution)/shard_map/ppermute | solution.py:197
  68.0 0.0 collective-permute-done.1
  68.0 6.0 %collective-permute-start.3 = (bf16[56,512]{1,0:T(8,128)(2,1)S(1)}, bf16[56,512]{1,0:T(8,128)(2,1)S(1)}, u32[]{:S(2)}, u32[]{:S(2)}) collective-permute-start(bf16[56,512]{1,0:T(8,128)(2,1)S(1)} %slice.25), channel_id=1, source_target_pairs={{0,96},{32,0},{64,32},{96,64},{1,97},{33,1},{65,33},{97,65},{2,98}... | collective-permute-start | bytes 172040 | tf_op jit(solution)/shard_map/ppermute | solution.py:197
  74.1 0.2 collective-permute-done.2
  74.3 1.6 collective-permute-done.3
  75.9 1.9 %collective-permute-start.4 = (bf16[448,512]{1,0:T(8,128)(2,1)S(1)}, bf16[448,512]{1,0:T(8,128)(2,1)S(1)}, u32[]{:S(2)}, u32[]{:S(2)}) collective-permute-start(bf16[448,512]{1,0:T(8,128)(2,1)S(1)} %constant_dynamic-update-slice_fusion.line_ref), channel_id=1, source_target_pairs={{0,16},{16,0},{1,17},{17,1},{2,18},{18,2},{3,19},{19,3},{4,20},{20... | collective-permute-start | bytes 1376264 | tf_op jit(solution)/shard_map/ppermute | solution.py:197
  77.8 1.8 %collective-permute-done.4.other_ref = bf16[448,512]{1,0:T(8,128)(2,1)S(1)} collective-permute-done((bf16[448,512]{1,0:T(8,128)(2,1)S(1)}, bf16[448,512]{1,0:T(8,128)(2,1)S(1)}, u32[]{:S(2)}, u32[]{:S(2)}) %collective-permute-start.4) | collective-permute-done | bytes 458784 | tf_op jit(solution)/shard_map/ppermute | solution.py:197
  79.6 0.0 all-to-all-done
  79.6 0.0 all-gather.2.cloned.1.call-done.wide_hbm.weight_ref
  79.6 0.0 copy-start.2
  79.6 1.5 copy-done.2
  81.1 2.8 %before.1 = (bf16[4,96,1536]{2,1,0:T(8,128)(2,1)S(1)}, bf16[384,896]{1,0:T(8,128)(2,1)S(1)}) custom-call(bf16[4,1408,128]{2,1,0:T(8,128)(2,1)S(1)} %bitcast.28, bf16[896,1024]{1,0:T(8,128)(2,1)S(1)} %copy-done.2, bf16[448,512]{1,0:T(8,128)(2,1)S(1)} %constant_dynamic-update-slice_fusion.line_ref, bf16[448,512]{1,0:T(8,128)(2,1)S(1)} %collective-permute-done.4.other_ref), custom_call_target="tpu_custom_call" | custom-call | flops 2000000000 | bytes 4000000 | tf_op jit(solution)/shard_map/before/pallas_call | solution.py:54
  83.9 19.1 %all_to_all.20.part_ref = bf16[4,96,1536]{2,1,0:T(8,128)(2,1)S(1)} all-to-all(bf16[4,96,1536]{2,1,0:T(8,128)(2,1)S(1)} %get-tuple-element.15), channel_id=1, replica_groups=mesh['x'=4,'zh'=4,'c'=2,'y'=8,'zl'=2] {'x'}, dimensions={0} | all-to-all | bytes 2359296 | tf_op jit(solution)/shard_map/all_to_all | solution.py:205
  103.0 0.4 middle.1
  103.3 0.0 copy-start.3
  103.3 18.2 %all_to_all.21.mid_ref = bf16[4,96,1536]{2,1,0:T(8,128)(2,1)S(1)} all-to-all(bf16[4,96,1536]{2,1,0:T(8,128)(2,1)S(1)} %get-tuple-element.16), channel_id=1, replica_groups=mesh['x'=4,'zh'=4,'c'=2,'y'=8,'zl'=2] {'x'}, dimensions={0} | all-to-all | bytes 2359296 | tf_op jit(solution)/shard_map/all_to_all | solution.py:205
  121.5 0.0 copy-done.3
  121.5 2.7 %after.1 = (bf16[4,128,896]{2,1,0:T(8,128)(2,1)}, bf16[112,512]{1,0:T(8,128)(2,1)S(1)}, bf16[112,512]{1,0:T(8,128)(2,1)S(1)}, bf16[112,512]{1,0:T(8,128)(2,1)S(1...) custom-call(bf16[4,96,1536]{2,1,0:T(8,128)(2,1)S(1)} %all_to_all.21.mid_ref, ...), custom_call_target="tpu_custom_call" | custom-call | flops 1400000000 | bytes 4000000 | tf_op jit(solution)/shard_map/after/pallas_call | solution.py:54
  124.2 10.6 %all-to-all-start.3 = ((bf16[64,8,896]{2,1,0:T(8,128)(2,1)}), bf16[64,8,896]{2,1,0:T(8,128)(2,1)S(1)}, u32[]{:S(2)}, u32[]{:S(2)}) async-start(bf16[64,8,896]{2,1,0:T(8,128)(2,1)} %bitcast.4), calls=%async_computation.3 | async-start | bytes 1835008 | tf_op jit(solution)/shard_map/all_to_all | solution.py:205
  134.8 0.0 copy-start
  134.8 0.0 copy-start.1
  134.8 1.9 %collective-permute-start.5 = (bf16[4,112,512]{2,1,0:T(8,128)(2,1)S(1)}, bf16[4,112,512]{2,1,0:T(8,128)(2,1)S(1)}, u32[]{:S(2)}, u32[]{:S(2)}) collective-permute-start(bf16[4,112,512]{2,1,0:T(8,128)(2,1)S(1)} %get-tuple-element.23), channel_id=1, source_target_pairs={{0,16},{16,0},{1,17},{17,1},{2,18},{18,2},{3,19},{19,3},{4,20},{20... | collective-permute-start | bytes 1376264 | tf_op jit(solution)/shard_map/ppermute | solution.py:197
  136.8 1.8 %collective-permute-done.5 = bf16[4,112,512]{2,1,0:T(8,128)(2,1)S(1)} collective-permute-done((bf16[4,112,512]{2,1,0:T(8,128)(2,1)S(1)}, bf16[4,112,512]{2,1,0:T(8,128)(2,1)S(1)}, u32[]{:S(2)}, u32[]{:S(2)}) %collective-permute-start.5) | collective-permute-done | bytes 458784 | tf_op jit(solution)/shard_map/ppermute | solution.py:197
  138.5 0.1 fusion.3
  138.6 2.2 %collective-permute-start.6 = (bf16[112,512]{1,0:T(8,128)(2,1)S(1)}, bf16[112,512]{1,0:T(8,128)(2,1)S(1)}, u32[]{:S(2)}, u32[]{:S(2)}) collective-permute-start(bf16[112,512]{1,0:T(8,128)(2,1)S(1)} %get-tuple-element.27), channel_id=1, source_target_pairs={{0,32},{32,64},{64,96},{96,0},{1,33},{33,65},{65,97},{97,1},{2,34}... | collective-permute-start | bytes 344072 | tf_op jit(solution)/shard_map/ppermute | solution.py:197
  140.9 8.4 %collective-permute-start.8 = (bf16[112,512]{1,0:T(8,128)(2,1)S(1)}, bf16[112,512]{1,0:T(8,128)(2,1)S(1)}, u32[]{:S(2)}, u32[]{:S(2)}) collective-permute-start(bf16[112,512]{1,0:T(8,128)(2,1)S(1)} %get-tuple-element.28), channel_id=1, source_target_pairs={{0,64},{32,96},{64,0},{96,32},{1,65},{33,97},{65,1},{97,33},{2,66}... | collective-permute-start | bytes 344072 | tf_op jit(solution)/shard_map/ppermute | solution.py:197
  149.3 1.9 %collective-permute-start.7 = (bf16[112,512]{1,0:T(8,128)(2,1)S(1)}, bf16[112,512]{1,0:T(8,128)(2,1)S(1)}, u32[]{:S(2)}, u32[]{:S(2)}) collective-permute-start(bf16[112,512]{1,0:T(8,128)(2,1)S(1)} %get-tuple-element.29), channel_id=1, source_target_pairs={{0,96},{32,0},{64,32},{96,64},{1,97},{33,1},{65,33},{97,65},{2,98}... | collective-permute-start | bytes 344072 | tf_op jit(solution)/shard_map/ppermute | solution.py:197
  151.2 4.3 %collective-permute-done.6 = bf16[112,512]{1,0:T(8,128)(2,1)S(1)} collective-permute-done((bf16[112,512]{1,0:T(8,128)(2,1)S(1)}, bf16[112,512]{1,0:T(8,128)(2,1)S(1)}, u32[]{:S(2)}, u32[]{:S(2)}) %collective-permute-start.6) | collective-permute-done | bytes 114720 | tf_op jit(solution)/shard_map/ppermute | solution.py:197
  155.5 4.4 %collective-permute-done.8 = bf16[112,512]{1,0:T(8,128)(2,1)S(1)} collective-permute-done((bf16[112,512]{1,0:T(8,128)(2,1)S(1)}, bf16[112,512]{1,0:T(8,128)(2,1)S(1)}, u32[]{:S(2)}, u32[]{:S(2)}) %collective-permute-start.8) | collective-permute-done | bytes 114720 | tf_op jit(solution)/shard_map/ppermute | solution.py:197
  159.9 3.0 %collective-permute-done.7 = bf16[112,512]{1,0:T(8,128)(2,1)S(1)} collective-permute-done((bf16[112,512]{1,0:T(8,128)(2,1)S(1)}, bf16[112,512]{1,0:T(8,128)(2,1)S(1)}, u32[]{:S(2)}, u32[]{:S(2)}) %collective-permute-start.7) | collective-permute-done | bytes 114720 | tf_op jit(solution)/shard_map/ppermute | solution.py:197
  162.9 0.7 add_convert_fusion
  163.6 0.0 all-to-all-done.3
  163.6 0.0 copy-done
  163.6 0.0 copy-done.1
  163.6 1.6 finish.1
  (7 shorter events, 0.0 us)
Async XLA Ops:
  7.2 72.4 %all-gather.2.cloned.1.call-start = ((), (), s32[]{:S(2)}) async-start(), calls=%async_computation.4 | async-start | bytes 2064384 | tf_op jit(solution)/shard_map/all_gather | solution.py:210
  12.9 12.8 %copy-start.4 = (bf16[112,512]{1,0:T(8,128)(2,1)S(1)}, bf16[112,512]{1,0:T(8,128)(2,1)}, u32[]{:S(2)}) copy-start(bf16[112,512]{1,0:T(8,128)(2,1)} %param.13) | copy-start | bytes 344068
  12.9 66.7 %all-to-all-start = ((bf16[64,88,128]{2,1,0:T(8,128)(2,1)}), bf16[64,88,128]{2,1,0:T(8,128)(2,1)S(1)}, u32[]{:S(2)}, u32[]{:S(2)}) async-start(bf16[64,88,128]{2,1,0:T(8,128)(2,1)} %bitcast.33), calls=%async_computation | async-start | bytes 2883584 | tf_op jit(solution)/shard_map/all_to_all | solution.py:205
  25.7 40.4 %collective-permute-start = (bf16[112,512]{1,0:T(8,128)(2,1)S(1)}, bf16[112,512]{1,0:T(8,128)(2,1)S(1)}, u32[]{:S(2)}, u32[]{:S(2)}) collective-permute-start(bf16[112,512]{1,0:T(8,128)(2,1)S(1)} %copy-done.4), channel_id=1, source_target_pairs={{0,32},{32,64},{64,96},{96,0},{1,33},{33,65},{65,97},{97,1},{2,34}... | collective-permute-start | bytes 344072 | tf_op jit(solution)/shard_map/ppermute | solution.py:197
  31.8 36.2 %collective-permute-start.1 = (bf16[112,512]{1,0:T(8,128)(2,1)S(1)}, bf16[112,512]{1,0:T(8,128)(2,1)S(1)}, u32[]{:S(2)}, u32[]{:S(2)}) collective-permute-start(bf16[112,512]{1,0:T(8,128)(2,1)S(1)} %copy-done.4), channel_id=1, source_target_pairs={{0,96},{32,0},{64,32},{96,64},{1,97},{33,1},{65,33},{97,65},{2,98}... | collective-permute-start | bytes 344072 | tf_op jit(solution)/shard_map/ppermute | solution.py:197
  66.1 8.2 %collective-permute-start.2 = (bf16[56,512]{1,0:T(8,128)(2,1)S(1)}, bf16[56,512]{1,0:T(8,128)(2,1)S(1)}, u32[]{:S(2)}, u32[]{:S(2)}) collective-permute-start(bf16[56,512]{1,0:T(8,128)(2,1)S(1)} %slice.24), channel_id=1, source_target_pairs={{0,32},{32,64},{64,96},{96,0},{1,33},{33,65},{65,97},{97,1},{2,34}... | collective-permute-start | bytes 172040 | tf_op jit(solution)/shard_map/ppermute | solution.py:197
  68.0 7.8 %collective-permute-start.3 = (bf16[56,512]{1,0:T(8,128)(2,1)S(1)}, bf16[56,512]{1,0:T(8,128)(2,1)S(1)}, u32[]{:S(2)}, u32[]{:S(2)}) collective-permute-start(bf16[56,512]{1,0:T(8,128)(2,1)S(1)} %slice.25), channel_id=1, source_target_pairs={{0,96},{32,0},{64,32},{96,64},{1,97},{33,1},{65,33},{97,65},{2,98}... | collective-permute-start | bytes 172040 | tf_op jit(solution)/shard_map/ppermute | solution.py:197
  75.9 3.7 %collective-permute-start.4 = (bf16[448,512]{1,0:T(8,128)(2,1)S(1)}, bf16[448,512]{1,0:T(8,128)(2,1)S(1)}, u32[]{:S(2)}, u32[]{:S(2)}) collective-permute-start(bf16[448,512]{1,0:T(8,128)(2,1)S(1)} %constant_dynamic-update-slice_fusion.line_ref), channel_id=1, source_target_pairs={{0,16},{16,0},{1,17},{17,1},{2,18},{18,2},{3,19},{19,3},{4,20},{20... | collective-permute-start | bytes 1376264 | tf_op jit(solution)/shard_map/ppermute | solution.py:197
  79.6 1.5 copy-start.2
  103.3 18.2 %copy-start.3 = (bf16[896,1024]{1,0:T(8,128)(2,1)S(1)}, bf16[896,1024]{1,0:T(8,128)(2,1)}, u32[]{:S(2)}) copy-start(bf16[896,1024]{1,0:T(8,128)(2,1)} %all-gather.2.cloned.1.call-done.wide_hbm.weight_ref) | copy-start | bytes 5505028
  124.2 39.4 %all-to-all-start.3 = ((bf16[64,8,896]{2,1,0:T(8,128)(2,1)}), bf16[64,8,896]{2,1,0:T(8,128)(2,1)S(1)}, u32[]{:S(2)}, u32[]{:S(2)}) async-start(bf16[64,8,896]{2,1,0:T(8,128)(2,1)} %bitcast.4), calls=%async_computation.3 | async-start | bytes 1835008 | tf_op jit(solution)/shard_map/all_to_all | solution.py:205
  134.8 28.8 %copy-start = (s32[128,1]{0,1:T(1,128)S(1)}, s32[128,1]{0,1:T(1,128)}, u32[]{:S(2)}) copy-start(s32[128,1]{0,1:T(1,128)} %param.9) | copy-start | bytes 1540
  134.8 28.8 %copy-start.1 = (f32[128,1]{0,1:T(1,128)S(1)}, f32[128,1]{0,1:T(1,128)}, u32[]{:S(2)}) copy-start(f32[128,1]{0,1:T(1,128)} %param.10) | copy-start | bytes 1540
  134.8 3.7 %collective-permute-start.5 = (bf16[4,112,512]{2,1,0:T(8,128)(2,1)S(1)}, bf16[4,112,512]{2,1,0:T(8,128)(2,1)S(1)}, u32[]{:S(2)}, u32[]{:S(2)}) collective-permute-start(bf16[4,112,512]{2,1,0:T(8,128)(2,1)S(1)} %get-tuple-element.23), channel_id=1, source_target_pairs={{0,16},{16,0},{1,17},{17,1},{2,18},{18,2},{3,19},{19,3},{4,20},{20... | collective-permute-start | bytes 1376264 | tf_op jit(solution)/shard_map/ppermute | solution.py:197
  138.6 16.9 %collective-permute-start.6 = (bf16[112,512]{1,0:T(8,128)(2,1)S(1)}, bf16[112,512]{1,0:T(8,128)(2,1)S(1)}, u32[]{:S(2)}, u32[]{:S(2)}) collective-permute-start(bf16[112,512]{1,0:T(8,128)(2,1)S(1)} %get-tuple-element.27), channel_id=1, source_target_pairs={{0,32},{32,64},{64,96},{96,0},{1,33},{33,65},{65,97},{97,1},{2,34}... | collective-permute-start | bytes 344072 | tf_op jit(solution)/shard_map/ppermute | solution.py:197
  140.9 19.0 %collective-permute-start.8 = (bf16[112,512]{1,0:T(8,128)(2,1)S(1)}, bf16[112,512]{1,0:T(8,128)(2,1)S(1)}, u32[]{:S(2)}, u32[]{:S(2)}) collective-permute-start(bf16[112,512]{1,0:T(8,128)(2,1)S(1)} %get-tuple-element.28), channel_id=1, source_target_pairs={{0,64},{32,96},{64,0},{96,32},{1,65},{33,97},{65,1},{97,33},{2,66}... | collective-permute-start | bytes 344072 | tf_op jit(solution)/shard_map/ppermute | solution.py:197
  149.3 13.6 %collective-permute-start.7 = (bf16[112,512]{1,0:T(8,128)(2,1)S(1)}, bf16[112,512]{1,0:T(8,128)(2,1)S(1)}, u32[]{:S(2)}, u32[]{:S(2)}) collective-permute-start(bf16[112,512]{1,0:T(8,128)(2,1)S(1)} %get-tuple-element.29), channel_id=1, source_target_pairs={{0,96},{32,0},{64,32},{96,64},{1,97},{33,1},{65,33},{97,65},{2,98}... | collective-permute-start | bytes 344072 | tf_op jit(solution)/shard_map/ppermute | solution.py:197
Sparse Core Ops, SparseCore 0:
  10.7 62.8 all-gather.1

commit v8 on v7

v8 whole, which is shorter than its diff:
```python
import jax
import jax.numpy as jnp
from jax import lax
from jax.experimental import pallas as pl
from jax.experimental.pallas import tpu as pltpu
from jax.sharding import Mesh, PartitionSpec as P

BF = jnp.bfloat16
F32 = jnp.float32
I32 = jnp.int32
AXES = ("x", "zh", "c", "y", "zl")
PEERS = ("x", "y")
TOK = 128
D = 3584
EXPERTS = 8
CAP = 6
HALF = 512
SHARD = 112
PART = D // 4
ROWS = 2 * EXPERTS * CAP
SLAB = 48
GROUP = 8 * SLAB
VMEM_LIMIT = 56 * 1024 * 1024
MOST_VMEM = 56 * 1024 * 1024
ANYWHERE = pl.BlockSpec(memory_space=pl.ANY)
VMEM = pl.BlockSpec(memory_space=pltpu.VMEM)


def iota(shape, dim):
    return lax.broadcasted_iota(I32, shape, dim)


def onehot(hit):
    return jnp.where(hit, 1.0, 0.0).astype(BF)


def sixth(i):
    return (i * 43) >> 8


def regroup():
    a, i = iota((8, SLAB, GROUP), 0), iota((8, SLAB, GROUP), 1)
    b = sixth(i)
    return onehot(iota((8, SLAB, GROUP), 2) == b * SLAB + a * CAP + (i - CAP * b)).reshape(GROUP, GROUP)


def token_ranks(ids):
    member = jnp.where(ids == iota((EXPERTS, TOK), 0), 1.0, 0.0)
    earlier = onehot(iota((TOK, TOK), 0) < iota((TOK, TOK), 1))
    counts = jnp.dot(member.astype(BF), earlier, preferred_element_type=F32)
    return jnp.sum(member * counts, axis=0, keepdims=True).astype(I32)


def to_column(row):
    diagonal = iota((TOK, TOK), 0) == iota((TOK, TOK), 1)
    return jnp.sum(jnp.where(diagonal, row, 0.0), axis=1, keepdims=True)


def call(body, name, out_shape, operands, flops, scratch=(), specs=None, limit=VMEM_LIMIT):
    return pl.pallas_call(
        body,
        in_specs=specs or [VMEM] * len(operands),
        out_specs=[VMEM] * len(out_shape),
        out_shape=[jax.ShapeDtypeStruct(shape, kind) for shape, kind in out_shape],
        scratch_shapes=list(scratch),
        compiler_params=pltpu.CompilerParams(vmem_limit_bytes=limit),
        cost_estimate=pl.CostEstimate(flops=flops, bytes_accessed=4 * 10**6, transcendentals=0),
        name=name,
    )(*operands)


def dispatch_kernel(ids_hbm, p_hbm, rows_hbm, out_ref, ids_ref, p_ref, rows_ref, sems, scale):
    copies = [
        pltpu.make_async_copy(source, target, sems.at[i])
        for i, (source, target) in enumerate(((ids_hbm, ids_ref), (p_hbm, p_ref), (rows_hbm, rows_ref)))
    ]
    for copy in copies:
        copy.start()
    k, at = iota((EXPERTS, SLAB, 7 * 64), 1), iota((EXPERTS, SLAB, 7 * 64), 2)
    q = sixth(k)
    order = onehot((at == q * 64 + iota((EXPERTS, SLAB, 7 * 64), 0) * 8 + (k - CAP * q)) & (q < 7))
    order = order.reshape(GROUP, 7 * 64)
    for copy in copies:
        copy.wait()
    ids = ids_ref[...]
    slot = jnp.where(ids < EXPERTS, ids * 8 + token_ranks(ids), -16)
    sel = onehot(slot == iota((64, TOK), 0))
    rows = rows_ref[...]
    if scale:
        rows = (to_column(p_ref[...]) * rows.astype(F32)).astype(BF)
    rows = jnp.dot(sel, rows, preferred_element_type=F32).astype(BF)
    for i in range(2):
        stack = []
        for q in range(7):
            left = 2 * i * PART + q * TOK
            stack.append(jnp.concatenate([rows[:, left:left + TOK], rows[:, left + PART:left + PART + TOK]], axis=1))
        moved = jnp.dot(order, jnp.concatenate(stack, axis=0), preferred_element_type=F32).astype(BF)
        for j in range(2):
            out_ref[2 * i + j] = moved[:, j * TOK:(j + 1) * TOK].reshape(EXPERTS, SLAB, TOK)


def dispatch(ids, share, rows, scale, name):
    return call(
        lambda *refs: dispatch_kernel(*refs, scale), name, [((4, EXPERTS, SLAB, TOK), BF)], (ids, share, rows),
        3 * 10**8,
        [pltpu.VMEM((1, TOK), I32), pltpu.VMEM((1, TOK), F32), pltpu.VMEM((TOK, D), BF), pltpu.SemaphoreType.DMA((3,))],
        [ANYWHERE] * 3, MOST_VMEM,
    )[0]


def unpack(mine_ref, other_ref, out_ref):
    zl = lax.axis_index("zl")
    order = regroup()
    for ref, z in ((mine_ref, zl), (other_ref, 1 - zl)):
        for i in range(2):
            both = jnp.concatenate([ref[2 * i], ref[2 * i + 1]], axis=1)
            moved = jnp.dot(order, both, preferred_element_type=F32).astype(BF)
            for j in range(2):
                rows = pl.ds(pl.multiple_of((2 * (2 * i + j) + z) * SLAB, 16), SLAB)
                for q in range(7):
                    part = moved[q * SLAB:(q + 1) * SLAB, j * TOK:(j + 1) * TOK]
                    out_ref[rows, q * TOK:(q + 1) * TOK] = part


def gate_up_kernel(mine_ref, other_ref, weights_hbm, part_ref, x_scr, wide, sem):
    copy = pltpu.make_async_copy(weights_hbm.at[:, pl.ds(0, 2 * HALF)], wide, sem)
    copy.start()
    unpack(mine_ref, other_ref, x_scr)
    copy.wait()
    pre = jnp.dot(x_scr[...], wide[...], preferred_element_type=F32).astype(BF)
    part_ref[...] = pre.reshape(4, ROWS, 2 * HALF)


def hidden_grad_kernel(mine_ref, other_ref, weights_hbm, g_ref, own_ref, plus_ref, minus_ref, far_ref, part, down, sem):
    xi = lax.axis_index("x")
    copy = pltpu.make_async_copy(weights_hbm.at[:, pl.ds(2 * HALF, HALF)], down, sem)
    copy.start()
    unpack(mine_ref, other_ref, g_ref)
    copy.wait()
    part[...] = jnp.dot(g_ref[...], down[...], preferred_element_type=F32).astype(BF)
    for ref, shift in ((own_ref, 0), (plus_ref, 1), (minus_ref, 3), (far_ref, 2)):
        ref[...] = part[pl.ds(pl.multiple_of(lax.rem(xi + shift, 4) * ROWS, 16), ROWS)]


def middle_kernel(part_ref, a_ref, b_ref, c_ref, d_ref, out_ref, line_ref):
    total = part_ref[0].astype(F32) + part_ref[1].astype(F32) + part_ref[2].astype(F32) + part_ref[3].astype(F32)
    grad = a_ref[...].astype(F32) + b_ref[...].astype(F32) + c_ref[...].astype(F32) + d_ref[...].astype(F32)
    gate, up = total[:, :HALF], total[:, HALF:]
    sig = jax.nn.sigmoid(gate)
    act = gate * sig
    slope = sig * (1.0 + gate * (1.0 - sig))
    hidden = (act * up).astype(BF)
    route = jnp.sum(hidden.astype(F32) * grad, axis=1, keepdims=True)
    d_gate, d_up = (grad * up * slope).astype(BF), (grad * act).astype(BF)
    for i in range(4):
        out_ref[i, :, :HALF] = d_gate
        out_ref[i, :, HALF:2 * HALF] = d_up
        out_ref[i, :, 2 * HALF:] = hidden
    line_ref[...] = jnp.where(iota((ROWS, TOK), 1) == 0, route, 0.0).astype(BF)


def after_kernel(mid_ref, line_ref, g_ref, weights_hbm, keep_ref, give_ref,
                 far_ref, plus_ref, minus_ref, own_ref, send_ref, down, wide, grads, line, sem):
    xi, zi, ci, zl = [lax.axis_index(a) for a in ("x", "zh", "c", "zl")]
    copy = pltpu.make_async_copy(weights_hbm.at[:, pl.ds(0, 2 * HALF)], wide, sem)
    copy.start()
    mid = mid_ref[...].reshape(4 * ROWS, 3 * HALF)
    copy.wait()
    grads[...] = lax.dot_general(
        mid[:, :2 * HALF], wide[...], (((1,), (1,)), ((), ())), preferred_element_type=F32
    ).astype(BF)
    line[...] = line_ref[...]
    for ref, z in ((keep_ref, zl), (give_ref, 1 - zl)):
        own = line[pl.ds(pl.multiple_of(z * SLAB, 16), SLAB)]
        for i in range(4):
            ref[i, :, :PART] = grads[pl.ds(pl.multiple_of((2 * i + z) * SLAB, 16), SLAB)]
            ref[i, :, PART:] = jnp.where(xi == i, own, jnp.zeros_like(own))
    down[...] = lax.dot_general(
        g_ref[...], mid[:, 2 * HALF:], (((0,), (0,)), ((), ())), preferred_element_type=F32
    ).astype(BF)

    def shard(shift, core):
        block = 2 * lax.rem(zi + shift, 4) + core
        return down[pl.ds(pl.multiple_of(block * SHARD, 16), SHARD)]

    for i, (ref, shift) in enumerate(((far_ref, 2), (plus_ref, 1), (minus_ref, 3), (own_ref, 0))):
        ref[...] = shard(shift, ci)
        send_ref[i] = shard(shift, 1 - ci)


def combine_kernel(keep_ref, got_ref, out_ref):
    order = regroup()
    for i in range(2):
        left, right = add(keep_ref[2 * i], got_ref[2 * i]), add(keep_ref[2 * i + 1], got_ref[2 * i + 1])
        stack = []
        for q in range(8):
            columns = slice(q * TOK, (q + 1) * TOK)
            stack.append(jnp.concatenate([left[:, columns], right[:, columns]], axis=1))
        moved = jnp.dot(order, jnp.concatenate(stack, axis=0), preferred_element_type=F32).astype(BF)
        for j in range(2):
            out_ref[2 * i + j] = moved[:, j * TOK:(j + 1) * TOK].reshape(EXPERTS, SLAB, TOK)


def finish_kernel(ids_ref, p_ref, rows_ref, tok_ref, route_ref):
    ids = ids_ref[...]
    base = jnp.where(ids < EXPERTS, ids * SLAB + token_ranks(ids), -GROUP)
    offset = iota((TOK, GROUP), 1) - to_column(base.astype(F32)).astype(I32)
    pairs = [jnp.concatenate([rows_ref[2 * i], rows_ref[2 * i + 1]], axis=1) for i in range(2)]
    route = jnp.zeros((TOK, 1), F32)
    for q in range(8):
        sel = onehot(offset == q * CAP)
        for i in range(2):
            got = jnp.dot(sel, pairs[i], preferred_element_type=F32)
            if q == 7:
                route = route + got[:, :1] + got[:, TOK:TOK + 1]
                continue
            for j in range(2):
                left = (2 * i + j) * PART + q * TOK
                tok_ref[:, left:left + TOK] = got[:, j * TOK:(j + 1) * TOK].astype(BF)
    diagonal = iota((TOK, TOK), 0) == iota((TOK, TOK), 1)
    route_ref[...] = jnp.sum(jnp.where(diagonal, route, 0.0), axis=0, keepdims=True) / p_ref[...]


def hop(a, axis, shift):
    n = lax.axis_size(axis)
    return lax.ppermute(a, axis, [(i, (i + shift) % n) for i in range(n)])


def add(*terms):
    return sum(a.astype(F32) for a in terms).astype(BF)


def exchange(a, axes):
    return lax.all_to_all(a, axes, split_axis=0, concat_axis=0, tiled=True)


def per_device(tokens, grad_out, routing, route_weight, gate_weight, up_weight, down_weight):
    ids, share = routing.reshape(1, TOK), route_weight.reshape(1, TOK)
    weights = jnp.concatenate([gate_weight, up_weight, down_weight], axis=1)
    weights = lax.all_gather(weights, ("zh", "c"), axis=0, tiled=True)

    def send_rows(a):
        return exchange(a.reshape(32, SLAB, TOK), PEERS).reshape(4, GROUP, TOK)

    x_own = send_rows(dispatch(ids, share, tokens, False, "pack_tokens"))
    g_own = send_rows(dispatch(ids, share, grad_out, True, "pack_grads"))
    x_own, x_other, g_other = lax.optimization_barrier((x_own, hop(x_own, "zl", 1), hop(g_own, "zl", 1)))
    x_rows, g_rows = (x_own, x_other), (g_own, g_other)

    semaphore = pltpu.SemaphoreType.DMA(())
    dense = pltpu.VMEM((4 * ROWS, PART), BF)
    part, = call(
        gate_up_kernel, "gate_up", [((4, ROWS, 2 * HALF), BF)], (*x_rows, weights), 10**9,
        [dense, pltpu.VMEM((PART, 2 * HALF), BF), semaphore], [VMEM, VMEM, ANYWHERE],
    )
    block = ((ROWS, HALF), BF)
    g_dense, own, plus, minus, far = call(
        hidden_grad_kernel, "hidden_grad", [((4 * ROWS, PART), BF), block, block, block, block], (*g_rows, weights),
        6 * 10**8, [pltpu.VMEM((4 * ROWS, HALF), BF), pltpu.VMEM((PART, HALF), BF), semaphore], [VMEM, VMEM, ANYWHERE],
    )
    mid, line = call(
        middle_kernel, "middle", [((4, ROWS, 3 * HALF), BF), ((ROWS, TOK), BF)],
        (exchange(part, "x"), own, hop(plus, "x", 1), hop(minus, "x", -1), hop(far, "x", 2)), 10**7,
    )
    shard, wide = ((SHARD, HALF), BF), ((4, SLAB, PART + TOK), BF)
    keep, give, far, plus, minus, mine, send = call(
        after_kernel, "after", [wide, wide, shard, shard, shard, shard, ((4, SHARD, HALF), BF)],
        (exchange(mid, "x"), line, g_dense, weights), 14 * 10**8,
        [pltpu.VMEM((PART, HALF), BF), pltpu.VMEM((PART, 2 * HALF), BF), dense, pltpu.VMEM((ROWS, TOK), BF), semaphore],
        [VMEM, VMEM, VMEM, ANYWHERE],
    )
    back, = call(combine_kernel, "combine", [((4, EXPERTS, SLAB, TOK), BF)], (keep, hop(give, "zl", 1)), 2 * 10**8)
    back = exchange(back.reshape(32, SLAB, TOK), PEERS).reshape(4, GROUP, TOK)
    token_grad, route_grad = call(finish_kernel, "finish", [((TOK, D), BF), ((1, TOK), F32)],
                                  (ids, share, back), 4 * 10**8)

    got = hop(send, "c", 1)
    far, plus, minus, mine = [add(a, got[i]) for i, a in enumerate((far, plus, minus, mine))]
    down_grad = add(hop(plus, "zh", 1), hop(minus, "zh", -1), hop(far, "zh", 2), mine)
    return token_grad, route_grad.reshape(TOK, 1), down_grad


def solution(mesh):
    inner = Mesh(mesh.devices.reshape(4, 4, 2, 8, 2), AXES)
    rows = P(AXES, None)
    weights = P(("x", "zh", "c"), ("y", "zl"))
    return jax.shard_map(
        per_device,
        mesh=inner,
        in_specs=(rows, rows, rows, rows, weights, weights, weights),
        out_specs=(rows, rows, weights),
        check_vma=False,
    )
```

time: 173 us -> 182 us (1.052)
  blocking collectives: 37.3 us -> 18.2 us
  Pallas kernels: 11.3 us -> 27.3 us
  starting transfers between devices: 59.7 us -> 69.4 us
    all_to_all x2 -> x1, blocking collectives: 37.3 us -> 18.2 us  [exchange(): return lax.all_to_all(a, axes, split_axis=0, concat_axis=0, tiled=True)]
    all_to_all x2 -> x4, waiting for transfers between devices: 0.01 us -> 18 us  [exchange(): return lax.all_to_all(a, axes, split_axis=0, concat_axis=0, tiled=True)]
    ppermute x9 -> x10, waiting for transfers between devices: 45.5 us -> 28 us  [hop(): return lax.ppermute(a, axis, [(i, (i + shift) % n) for i in range(n)])]
    pallas_call x5 -> x8, Pallas kernels: 11.3 us -> 27.3 us  [call(): pl.pallas_call(body, in_specs=specs or [VMEM] * len(operands), out_specs=...]
    all_to_all x2 -> x4, starting transfers between devices: 23.3 us -> 31.7 us  [exchange(): return lax.all_to_all(a, axes, split_axis=0, concat_axis=0, tiled=True)]
    ppermute x9 -> x10, starting transfers between devices: 36.3 us -> 37.7 us  [hop(): return lax.ppermute(a, axis, [(i, (i + shift) % n) for i in range(n)])]
  transfers between devices with their start and end apart: 12 -> 15, of which waited for: 8 -> 9; matrix products, arithmetic and copies ran while one was open for 0% -> 0% of each run, Pallas kernels for 2% -> 6%
where the time goes in v8:
time: 182 us; the launch traced here: 181 us
  starting transfers between devices  69.4 us (38%)
  waiting for transfers between devices  46 us (25%)
  Pallas kernels  27.3 us (15%)
  blocking collectives  18.2 us (10%)
  between operations  14.3 us (8%)
  local copies, waits for them, and re-layouts  3.17 us (2%)
  other arithmetic  2.59 us (1%)
    ppermute x10, starting transfers between devices, hop(): return lax.ppermute(a, axis, [(i, (i + shift) % n) for i in range(n)])  37.7 us
    all_to_all x4, starting transfers between devices, exchange(): return lax.all_to_all(a, axes, split_axis=0, concat_axis=0, tiled=True)  31.7 us
    ppermute x10, waiting for transfers between devices, hop(): return lax.ppermute(a, axis, [(i, (i + shift) % n) for i in range(n)])  28 us
    pallas_call x8, Pallas kernels, call(): pl.pallas_call(body, in_specs=specs or [VMEM] * len(operands), out_specs=...  27.3 us
    all_to_all x1, blocking collectives, exchange(): return lax.all_to_all(a, axes, split_axis=0, concat_axis=0, tiled=True)  18.2 us
    all_to_all x4, waiting for transfers between devices, exchange(): return lax.all_to_all(a, axes, split_axis=0, concat_axis=0, tiled=True)  18 us
  transfers between devices with their start and end apart: 15, of which 9 were waited for; matrix products, arithmetic and copies ran while one was open for 0% of the time, Pallas kernels for 6%

profile of v8, /device:TPU:6, one launch (start us, length us, event | category | flops | bytes accessed | tf_op | source)
XLA Modules:
  0.0 181.1 jit_solution(2007276802818071179)
XLA Ops:
  7.2 0.0 all-gather.2.cloned.1.call-start
  7.2 1.8 pad_maximum_fusion
  9.0 0.0 all-gather.2.cloned.1.call-update
  9.0 2.7 %pack_grads.1 = bf16[4,8,48,128]{3,2,1,0:T(8,128)(2,1)} custom-call(s32[1,128]{1,0:T(1,128)} %bitcast.37, f32[1,128]{1,0:T(1,128)} %bitcast.40, bf16[128,3584]{1,0:T(8,128)(2,1)} %refs_2_.3), custom_call_target="tpu_custom_call" | custom-call | flops 300000000 | bytes 4000000 | tf_op jit(solution)/shard_map/pack_grads/pallas_call | solution.py:60
  11.8 10.2 %all-to-all-start.1 = ((bf16[32,48,128]{2,1,0:T(8,128)(2,1)}), bf16[32,48,128]{2,1,0:T(8,128)(2,1)S(1)}, u32[]{:S(2)}, u32[]{:S(2)}) async-start(bf16[32,48,128]{2,1,0:T(8,128)(2,1)} %bitcast.35), calls=%async_computation.1 | async-start | bytes 786432 | tf_op jit(solution)/shard_map/all_to_all | solution.py:234
  22.0 2.7 %pack_tokens.1 = bf16[4,8,48,128]{3,2,1,0:T(8,128)(2,1)} custom-call(s32[1,128]{1,0:T(1,128)} %bitcast.38, f32[1,128]{1,0:T(1,128)} %bitcast.41, bf16[128,3584]{1,0:T(8,128)(2,1)} %refs_2_.2), custom_call_target="tpu_custom_call" | custom-call | flops 300000000 | bytes 4000000 | tf_op jit(solution)/shard_map/pack_tokens/pallas_call | solution.py:60
  24.7 10.1 %all-to-all-done.1 = bf16[32,48,128]{2,1,0:T(8,128)(2,1)S(1)} async-done(((bf16[32,48,128]{2,1,0:T(8,128)(2,1)}), bf16[32,48,128]{2,1,0:T(8,128)(2,1)S(1)}, u32[]{:S(2)}, u32[]{:S(2)}) %all-to-all-start.1) | async-done | bytes 393248 | tf_op jit(solution)/shard_map/all_to_all | solution.py:234
  34.8 0.0 copy-start.1
  34.8 6.9 %all-to-all-start = ((bf16[32,48,128]{2,1,0:T(8,128)(2,1)}), bf16[32,48,128]{2,1,0:T(8,128)(2,1)S(1)}, u32[]{:S(2)}, u32[]{:S(2)}) async-start(bf16[32,48,128]{2,1,0:T(8,128)(2,1)} %bitcast.34), calls=%async_computation | async-start | bytes 786432 | tf_op jit(solution)/shard_map/all_to_all | solution.py:234
  41.7 4.3 %collective-permute-start.1 = (bf16[4,384,128]{2,1,0:T(8,128)(2,1)S(1)}, bf16[4,384,128]{2,1,0:T(8,128)(2,1)S(1)}, u32[]{:S(2)}, u32[]{:S(2)}) collective-permute-start(bf16[4,384,128]{2,1,0:T(8,128)(2,1)S(1)} %bitcast.29), channel_id=1, source_target_pairs={{0,1},{1,0},{2,3},{3,2},{4,5},{5,4},{6,7},{7,6},{8,9},{9,8},{10,11... | collective-permute-start | bytes 1179656 | tf_op jit(solution)/shard_map/ppermute | solution.py:226
  46.0 7.9 %all-to-all-done = bf16[32,48,128]{2,1,0:T(8,128)(2,1)S(1)} async-done(((bf16[32,48,128]{2,1,0:T(8,128)(2,1)}), bf16[32,48,128]{2,1,0:T(8,128)(2,1)S(1)}, u32[]{:S(2)}, u32[]{:S(2)}) %all-to-all-start) | async-done | bytes 393248 | tf_op jit(solution)/shard_map/all_to_all | solution.py:234
  53.9 0.0 copy-start.2
  53.9 4.3 %collective-permute-start = (bf16[4,384,128]{2,1,0:T(8,128)(2,1)S(1)}, bf16[4,384,128]{2,1,0:T(8,128)(2,1)S(1)}, u32[]{:S(2)}, u32[]{:S(2)}) collective-permute-start(bf16[4,384,128]{2,1,0:T(8,128)(2,1)S(1)} %bitcast.31), channel_id=1, source_target_pairs={{0,1},{1,0},{2,3},{3,2},{4,5},{5,4},{6,7},{7,6},{8,9},{9,8},{10,11... | collective-permute-start | bytes 1179656 | tf_op jit(solution)/shard_map/ppermute | solution.py:226
  58.2 6.8 %collective-permute-done.1.other_ref = bf16[4,384,128]{2,1,0:T(8,128)(2,1)S(1)} collective-permute-done((bf16[4,384,128]{2,1,0:T(8,128)(2,1)S(1)}, bf16[4,384,128]{2,1,0:T(8,128)(2,1)S(1)}, u32[]{:S(2)}, u32[]{:S(2)}) %collective-permute-start.1) | collective-permute-done | bytes 393248 | tf_op jit(solution)/shard_map/ppermute | solution.py:226
  65.0 0.0 copy-start.3
  65.0 8.1 %collective-permute-done.other_ref = bf16[4,384,128]{2,1,0:T(8,128)(2,1)S(1)} collective-permute-done((bf16[4,384,128]{2,1,0:T(8,128)(2,1)S(1)}, bf16[4,384,128]{2,1,0:T(8,128)(2,1)S(1)}, u32[]{:S(2)}, u32[]{:S(2)}) %collective-permute-start) | collective-permute-done | bytes 393248 | tf_op jit(solution)/shard_map/ppermute | solution.py:226
  73.0 0.0 copy-start.4
  73.1 0.0 copy-done.2
  73.1 0.7 copy-done.4
  73.8 4.5 %gate_up.1 = bf16[4,96,1024]{2,1,0:T(8,128)(2,1)} custom-call(bf16[4,384,128]{2,1,0:T(8,128)(2,1)} %bitcast.32, bf16[4,384,128]{2,1,0:T(8,128)(2,1)} %copy-done.4, bf16[896,1536]{1,0:T(8,128)(2,1)} %all-gather.2.cloned.1.call-done.weights_hbm), custom_call_target="tpu_custom_call" | custom-call | flops 1000000000 | bytes 4000000 | tf_op jit(solution)/shard_map/gate_up/pallas_call | solution.py:60
  78.3 0.0 copy-done.1
  78.3 0.0 copy-done.3
  78.3 4.8 %all-to-all-start.2 = ((bf16[4,96,1024]{2,1,0:T(8,128)(2,1)}), bf16[4,96,1024]{2,1,0:T(8,128)(2,1)S(1)}, u32[]{:S(2)}, u32[]{:S(2)}) async-start(bf16[4,96,1024]{2,1,0:T(8,128)(2,1)} %gate_up.1), calls=%async_computation.2 | async-start | bytes 1572864 | tf_op jit(solution)/shard_map/all_to_all | solution.py:234
  83.1 4.0 %hidden_grad.1 = (bf16[384,896]{1,0:T(8,128)(2,1)}, bf16[96,512]{1,0:T(8,128)(2,1)}, bf16[96,512]{1,0:T(8,128)(2,1)}, bf16[96,512]{1,0:T(8,128)(2,1)}, bf16[96,512]{1,0:T(8,128)(2,1)}) custom-call(bf16[4,384,128]{2,1,0:T(8,128)(2,1)} %bitcast.30, bf16[4,384,128]{2,1,0:T(8,128)(2,1)} %copy-done.3, bf16[896,1536]{1,0:T(8,128)(2,1)} %all-gather.2.cloned.1.call-done.weights_hbm), custom_call_target="tpu_custom_call" | custom-call | flops 600000000 | bytes 4000000 | tf_op jit(solution)/shard_map/hidden_grad/pallas_call | solution.py:60
  87.1 1.9 %collective-permute-start.2 = (bf16[96,512]{1,0:T(8,128)(2,1)}, bf16[96,512]{1,0:T(8,128)(2,1)S(1)}, u32[]{:S(2)}, u32[]{:S(2)}) collective-permute-start(bf16[96,512]{1,0:T(8,128)(2,1)} %get-tuple-element.26), channel_id=1, source_target_pairs={{0,128},{128,256},{256,384},{384,0},{1,129},{129,257},{257,385},{3... | collective-permute-start | bytes 294920 | tf_op jit(solution)/shard_map/ppermute | solution.py:226
  89.1 3.9 %collective-permute-start.3 = (bf16[96,512]{1,0:T(8,128)(2,1)}, bf16[96,512]{1,0:T(8,128)(2,1)S(1)}, u32[]{:S(2)}, u32[]{:S(2)}) collective-permute-start(bf16[96,512]{1,0:T(8,128)(2,1)} %get-tuple-element.27), channel_id=1, source_target_pairs={{0,384},{128,0},{256,128},{384,256},{1,385},{129,1},{257,129},{385... | collective-permute-start | bytes 294920 | tf_op jit(solution)/shard_map/ppermute | solution.py:226
  93.0 3.4 %collective-permute-start.4 = (bf16[96,512]{1,0:T(8,128)(2,1)}, bf16[96,512]{1,0:T(8,128)(2,1)S(1)}, u32[]{:S(2)}, u32[]{:S(2)}) collective-permute-start(bf16[96,512]{1,0:T(8,128)(2,1)} %get-tuple-element.28), channel_id=1, source_target_pairs={{0,256},{128,384},{256,0},{384,128},{1,257},{129,385},{257,1},{385... | collective-permute-start | bytes 294920 | tf_op jit(solution)/shard_map/ppermute | solution.py:226
  96.4 0.0 collective-permute-done.2.b_ref
  96.4 0.0 copy-start.11
  96.4 0.6 collective-permute-done.3.c_ref
  97.0 4.2 %collective-permute-done.4.d_ref = bf16[96,512]{1,0:T(8,128)(2,1)S(1)} collective-permute-done((bf16[96,512]{1,0:T(8,128)(2,1)}, bf16[96,512]{1,0:T(8,128)(2,1)S(1)}, u32[]{:S(2)}, u32[]{:S(2)}) %collective-permute-start.4) | collective-permute-done | bytes 98336 | tf_op jit(solution)/shard_map/ppermute | solution.py:226
  101.2 0.0 all-to-all-done.2.part_ref
  101.2 0.0 copy-done.11
  101.2 0.0 copy-done.12
  101.2 0.6 copy-done.13
  101.9 0.3 copy-done
  102.1 2.7 %middle.1 = (bf16[4,96,1536]{2,1,0:T(8,128)(2,1)}, bf16[96,128]{1,0:T(8,128)(2,1)}) custom-call(bf16[4,96,1024]{2,1,0:T(8,128)(2,1)} %copy-done, bf16[96,512]{1,0:T(8,128)(2,1)} %get-tuple-element.25.a_ref, bf16[96,512]{1,0:T(8,128)(2,1)} %copy-done.11, bf16[96,512]{1,0:T(8,128)(2,1)} %copy-done.12, bf16[96,512]{1,0:T(8,128)(2,1)} %copy-done.13), custom_call_target="tpu_custom_call" | custom-call | flops 10000000 | bytes 4000000 | tf_op jit(solution)/shard_map/middle/pallas_call | solution.py:60
  104.8 18.2 %all_to_all.25.mid_ref = bf16[4,96,1536]{2,1,0:T(8,128)(2,1)} all-to-all(bf16[4,96,1536]{2,1,0:T(8,128)(2,1)} %get-tuple-element.29), channel_id=1, replica_groups=mesh['x'=4,'zh'=4,'c'=2,'y'=8,'zl'=2] {'x'}, dimensions={0} | all-to-all | bytes 2359296 | tf_op jit(solution)/shard_map/all_to_all | solution.py:234
  123.0 5.6 %after.1 = (bf16[4,48,1024]{2,1,0:T(8,128)(2,1)}, bf16[4,48,1024]{2,1,0:T(8,128)(2,1)}, bf16[112,512]{1,0:T(8,128)(2,1)}, bf16[112,512]{1,0:T(8,128)(2,1)}, bf16...) custom-call(bf16[4,96,1536]{2,1,0:T(8,128)(2,1)} %all_to_all.25.mid_ref, ...), custom_call_target="tpu_custom_call" | custom-call | flops 1400000000 | bytes 4000000 | tf_op jit(solution)/shard_map/after/pallas_call | solution.py:60
  128.6 0.0 copy-start.8
  128.6 0.0 copy-start.9
  128.6 0.0 copy-start.10
  128.6 3.5 %collective-permute-start.5 = (bf16[4,48,1024]{2,1,0:T(8,128)(2,1)}, bf16[4,48,1024]{2,1,0:T(8,128)(2,1)S(1)}, u32[]{:S(2)}, u32[]{:S(2)}) collective-permute-start(bf16[4,48,1024]{2,1,0:T(8,128)(2,1)} %get-tuple-element.33), channel_id=1, source_target_pairs={{0,1},{1,0},{2,3},{3,2},{4,5},{5,4},{6,7},{7,6},{8,9},{9,8},{10,11... | collective-permute-start | bytes 1179656 | tf_op jit(solution)/shard_map/ppermute | solution.py:226
  132.1 1.9 %collective-permute-start.6 = (bf16[4,112,512]{2,1,0:T(8,128)(2,1)}, bf16[4,112,512]{2,1,0:T(8,128)(2,1)S(1)}, u32[]{:S(2)}, u32[]{:S(2)}) collective-permute-start(bf16[4,112,512]{2,1,0:T(8,128)(2,1)} %get-tuple-element.37), channel_id=1, source_target_pairs={{0,16},{16,0},{1,17},{17,1},{2,18},{18,2},{3,19},{19,3},{4,20},{20... | collective-permute-start | bytes 1376264 | tf_op jit(solution)/shard_map/ppermute | solution.py:226
  134.0 4.6 %collective-permute-done.5.got_ref = bf16[4,48,1024]{2,1,0:T(8,128)(2,1)S(1)} collective-permute-done((bf16[4,48,1024]{2,1,0:T(8,128)(2,1)}, bf16[4,48,1024]{2,1,0:T(8,128)(2,1)S(1)}, u32[]{:S(2)}, u32[]{:S(2)}) %collective-permute-start.5) | collective-permute-done | bytes 393248 | tf_op jit(solution)/shard_map/ppermute | solution.py:226
  138.6 0.7 copy-done.6
  139.4 2.3 %combine.1 = bf16[4,8,48,128]{3,2,1,0:T(8,128)(2,1)} custom-call(bf16[4,48,1024]{2,1,0:T(8,128)(2,1)} %get-tuple-element.32.keep_ref, bf16[4,48,1024]{2,1,0:T(8,128)(2,1)} %copy-done.6), custom_call_target="tpu_custom_call" | custom-call | flops 200000000 | bytes 4000000 | tf_op jit(solution)/shard_map/combine/pallas_call | solution.py:60
  141.7 9.7 %all-to-all-start.4 = ((bf16[32,48,128]{2,1,0:T(8,128)(2,1)}), bf16[32,48,128]{2,1,0:T(8,128)(2,1)S(1)}, u32[]{:S(2)}, u32[]{:S(2)}) async-start(bf16[32,48,128]{2,1,0:T(8,128)(2,1)} %bitcast.33), calls=%async_computation.4 | async-start | bytes 786432 | tf_op jit(solution)/shard_map/all_to_all | solution.py:234
  151.4 0.0 collective-permute-done.6
  151.4 0.0 copy-done.8
  151.5 0.0 copy-done.9
  151.5 0.0 copy-done.10
  151.5 0.1 fusion.3
  151.6 4.3 %collective-permute-start.7 = (bf16[112,512]{1,0:T(8,128)(2,1)S(1)}, bf16[112,512]{1,0:T(8,128)(2,1)S(1)}, u32[]{:S(2)}, u32[]{:S(2)}) collective-permute-start(bf16[112,512]{1,0:T(8,128)(2,1)S(1)} %get-tuple-element.41), channel_id=1, source_target_pairs={{0,32},{32,64},{64,96},{96,0},{1,33},{33,65},{65,97},{97,1},{2,34}... | collective-permute-start | bytes 344072 | tf_op jit(solution)/shard_map/ppermute | solution.py:226
  155.9 4.2 %collective-permute-start.9 = (bf16[112,512]{1,0:T(8,128)(2,1)S(1)}, bf16[112,512]{1,0:T(8,128)(2,1)S(1)}, u32[]{:S(2)}, u32[]{:S(2)}) collective-permute-start(bf16[112,512]{1,0:T(8,128)(2,1)S(1)} %get-tuple-element.42), channel_id=1, source_target_pairs={{0,64},{32,96},{64,0},{96,32},{1,65},{33,97},{65,1},{97,33},{2,66}... | collective-permute-start | bytes 344072 | tf_op jit(solution)/shard_map/ppermute | solution.py:226
  160.1 6.0 %collective-permute-start.8 = (bf16[112,512]{1,0:T(8,128)(2,1)S(1)}, bf16[112,512]{1,0:T(8,128)(2,1)S(1)}, u32[]{:S(2)}, u32[]{:S(2)}) collective-permute-start(bf16[112,512]{1,0:T(8,128)(2,1)S(1)} %get-tuple-element.43), channel_id=1, source_target_pairs={{0,96},{32,0},{64,32},{96,64},{1,97},{33,1},{65,33},{97,65},{2,98}... | collective-permute-start | bytes 344072 | tf_op jit(solution)/shard_map/ppermute | solution.py:226
  166.2 0.0 collective-permute-done.7
  166.2 1.2 collective-permute-done.9
  167.4 2.6 %collective-permute-done.8 = bf16[112,512]{1,0:T(8,128)(2,1)S(1)} collective-permute-done((bf16[112,512]{1,0:T(8,128)(2,1)S(1)}, bf16[112,512]{1,0:T(8,128)(2,1)S(1)}, u32[]{:S(2)}, u32[]{:S(2)}) %collective-permute-start.8) | collective-permute-done | bytes 114720 | tf_op jit(solution)/shard_map/ppermute | solution.py:226
  169.9 0.0 copy-done.7
  169.9 0.7 add_convert_fusion
  170.6 0.0 all-to-all-done.4
  170.7 0.8 copy-done.5
  171.4 2.8 %finish.1 = (bf16[128,3584]{1,0:T(8,128)(2,1)}, f32[1,128]{1,0:T(1,128)}) custom-call(s32[1,128]{1,0:T(1,128)} %bitcast.39, f32[1,128]{1,0:T(1,128)} %bitcast.42, bf16[4,384,128]{2,1,0:T(8,128)(2,1)} %bitcast.36), custom_call_target="tpu_custom_call" | custom-call | flops 400000000 | bytes 4000000 | tf_op jit(solution)/shard_map/finish/pallas_call | solution.py:60
  (7 shorter events, 0.0 us)
Async XLA Ops:
  7.2 65.9 %all-gather.2.cloned.1.call-start = ((), (), s32[]{:S(2)}) async-start(), calls=%async_computation.5 | async-start | bytes 3096576 | tf_op jit(solution)/shard_map/all_gather | solution.py:240
  11.8 23.0 %all-to-all-start.1 = ((bf16[32,48,128]{2,1,0:T(8,128)(2,1)}), bf16[32,48,128]{2,1,0:T(8,128)(2,1)S(1)}, u32[]{:S(2)}, u32[]{:S(2)}) async-start(bf16[32,48,128]{2,1,0:T(8,128)(2,1)} %bitcast.35), calls=%async_computation.1 | async-start | bytes 786432 | tf_op jit(solution)/shard_map/all_to_all | solution.py:234
  34.8 43.5 %copy-start.1 = (bf16[32,48,128]{2,1,0:T(8,128)(2,1)}, bf16[32,48,128]{2,1,0:T(8,128)(2,1)S(1)}, u32[]{:S(2)}) copy-start(bf16[32,48,128]{2,1,0:T(8,128)(2,1)S(1)} %all-to-all-done.1) | copy-start | bytes 1179652
  34.8 19.1 %all-to-all-start = ((bf16[32,48,128]{2,1,0:T(8,128)(2,1)}), bf16[32,48,128]{2,1,0:T(8,128)(2,1)S(1)}, u32[]{:S(2)}, u32[]{:S(2)}) async-start(bf16[32,48,128]{2,1,0:T(8,128)(2,1)} %bitcast.34), calls=%async_computation | async-start | bytes 786432 | tf_op jit(solution)/shard_map/all_to_all | solution.py:234
  41.7 23.3 %collective-permute-start.1 = (bf16[4,384,128]{2,1,0:T(8,128)(2,1)S(1)}, bf16[4,384,128]{2,1,0:T(8,128)(2,1)S(1)}, u32[]{:S(2)}, u32[]{:S(2)}) collective-permute-start(bf16[4,384,128]{2,1,0:T(8,128)(2,1)S(1)} %bitcast.29), channel_id=1, source_target_pairs={{0,1},{1,0},{2,3},{3,2},{4,5},{5,4},{6,7},{7,6},{8,9},{9,8},{10,11... | collective-permute-start | bytes 1179656 | tf_op jit(solution)/shard_map/ppermute | solution.py:226
  53.9 19.1 %copy-start.2 = (bf16[32,48,128]{2,1,0:T(8,128)(2,1)}, bf16[32,48,128]{2,1,0:T(8,128)(2,1)S(1)}, u32[]{:S(2)}) copy-start(bf16[32,48,128]{2,1,0:T(8,128)(2,1)S(1)} %all-to-all-done) | copy-start | bytes 1179652
  53.9 19.1 %collective-permute-start = (bf16[4,384,128]{2,1,0:T(8,128)(2,1)S(1)}, bf16[4,384,128]{2,1,0:T(8,128)(2,1)S(1)}, u32[]{:S(2)}, u32[]{:S(2)}) collective-permute-start(bf16[4,384,128]{2,1,0:T(8,128)(2,1)S(1)} %bitcast.31), channel_id=1, source_target_pairs={{0,1},{1,0},{2,3},{3,2},{4,5},{5,4},{6,7},{7,6},{8,9},{9,8},{10,11... | collective-permute-start | bytes 1179656 | tf_op jit(solution)/shard_map/ppermute | solution.py:226
  65.0 13.4 %copy-start.3 = (bf16[4,384,128]{2,1,0:T(8,128)(2,1)}, bf16[4,384,128]{2,1,0:T(8,128)(2,1)S(1)}, u32[]{:S(2)}) copy-start(bf16[4,384,128]{2,1,0:T(8,128)(2,1)S(1)} %collective-permute-done.1.other_ref) | copy-start | bytes 1179652
  73.0 0.7 copy-start.4
  78.3 22.9 %all-to-all-start.2 = ((bf16[4,96,1024]{2,1,0:T(8,128)(2,1)}), bf16[4,96,1024]{2,1,0:T(8,128)(2,1)S(1)}, u32[]{:S(2)}, u32[]{:S(2)}) async-start(bf16[4,96,1024]{2,1,0:T(8,128)(2,1)} %gate_up.1), calls=%async_computation.2 | async-start | bytes 1572864 | tf_op jit(solution)/shard_map/all_to_all | solution.py:234
  87.1 9.2 %collective-permute-start.2 = (bf16[96,512]{1,0:T(8,128)(2,1)}, bf16[96,512]{1,0:T(8,128)(2,1)S(1)}, u32[]{:S(2)}, u32[]{:S(2)}) collective-permute-start(bf16[96,512]{1,0:T(8,128)(2,1)} %get-tuple-element.26), channel_id=1, source_target_pairs={{0,128},{128,256},{256,384},{384,0},{1,129},{129,257},{257,385},{3... | collective-permute-start | bytes 294920 | tf_op jit(solution)/shard_map/ppermute | solution.py:226
  89.1 7.9 %collective-permute-start.3 = (bf16[96,512]{1,0:T(8,128)(2,1)}, bf16[96,512]{1,0:T(8,128)(2,1)S(1)}, u32[]{:S(2)}, u32[]{:S(2)}) collective-permute-start(bf16[96,512]{1,0:T(8,128)(2,1)} %get-tuple-element.27), channel_id=1, source_target_pairs={{0,384},{128,0},{256,128},{384,256},{1,385},{129,1},{257,129},{385... | collective-permute-start | bytes 294920 | tf_op jit(solution)/shard_map/ppermute | solution.py:226
  93.0 8.2 %collective-permute-start.4 = (bf16[96,512]{1,0:T(8,128)(2,1)}, bf16[96,512]{1,0:T(8,128)(2,1)S(1)}, u32[]{:S(2)}, u32[]{:S(2)}) collective-permute-start(bf16[96,512]{1,0:T(8,128)(2,1)} %get-tuple-element.28), channel_id=1, source_target_pairs={{0,256},{128,384},{256,0},{384,128},{1,257},{129,385},{257,1},{385... | collective-permute-start | bytes 294920 | tf_op jit(solution)/shard_map/ppermute | solution.py:226
  96.4 4.9 %copy-start.11 = (bf16[96,512]{1,0:T(8,128)(2,1)}, bf16[96,512]{1,0:T(8,128)(2,1)S(1)}, u32[]{:S(2)}) copy-start(bf16[96,512]{1,0:T(8,128)(2,1)S(1)} %collective-permute-done.2.b_ref) | copy-start | bytes 294916
  97.0 4.2 %copy-start.12 = (bf16[96,512]{1,0:T(8,128)(2,1)}, bf16[96,512]{1,0:T(8,128)(2,1)S(1)}, u32[]{:S(2)}) copy-start(bf16[96,512]{1,0:T(8,128)(2,1)S(1)} %collective-permute-done.3.c_ref) | copy-start | bytes 294916
  101.2 0.6 copy-start.13
  101.2 0.9 copy-start
  128.6 22.8 %copy-start.8 = (bf16[112,512]{1,0:T(8,128)(2,1)S(1)}, bf16[112,512]{1,0:T(8,128)(2,1)}, u32[]{:S(2)}) copy-start(bf16[112,512]{1,0:T(8,128)(2,1)} %get-tuple-element.39) | copy-start | bytes 344068
  128.6 22.8 %copy-start.9 = (bf16[112,512]{1,0:T(8,128)(2,1)S(1)}, bf16[112,512]{1,0:T(8,128)(2,1)}, u32[]{:S(2)}) copy-start(bf16[112,512]{1,0:T(8,128)(2,1)} %get-tuple-element.36) | copy-start | bytes 344068
  128.6 22.8 %copy-start.10 = (bf16[112,512]{1,0:T(8,128)(2,1)S(1)}, bf16[112,512]{1,0:T(8,128)(2,1)}, u32[]{:S(2)}) copy-start(bf16[112,512]{1,0:T(8,128)(2,1)} %get-tuple-element.38) | copy-start | bytes 344068
  128.6 10.0 %collective-permute-start.5 = (bf16[4,48,1024]{2,1,0:T(8,128)(2,1)}, bf16[4,48,1024]{2,1,0:T(8,128)(2,1)S(1)}, u32[]{:S(2)}, u32[]{:S(2)}) collective-permute-start(bf16[4,48,1024]{2,1,0:T(8,128)(2,1)} %get-tuple-element.33), channel_id=1, source_target_pairs={{0,1},{1,0},{2,3},{3,2},{4,5},{5,4},{6,7},{7,6},{8,9},{9,8},{10,11... | collective-permute-start | bytes 1179656 | tf_op jit(solution)/shard_map/ppermute | solution.py:226
  132.1 19.3 %collective-permute-start.6 = (bf16[4,112,512]{2,1,0:T(8,128)(2,1)}, bf16[4,112,512]{2,1,0:T(8,128)(2,1)S(1)}, u32[]{:S(2)}, u32[]{:S(2)}) collective-permute-start(bf16[4,112,512]{2,1,0:T(8,128)(2,1)} %get-tuple-element.37), channel_id=1, source_target_pairs={{0,16},{16,0},{1,17},{17,1},{2,18},{18,2},{3,19},{19,3},{4,20},{20... | collective-permute-start | bytes 1376264 | tf_op jit(solution)/shard_map/ppermute | solution.py:226
  138.6 0.7 copy-start.6
  141.7 28.2 %copy-start.7 = (bf16[112,512]{1,0:T(8,128)(2,1)S(1)}, bf16[112,512]{1,0:T(8,128)(2,1)}, u32[]{:S(2)}) copy-start(bf16[112,512]{1,0:T(8,128)(2,1)} %get-tuple-element.40) | copy-start | bytes 344068
  141.7 29.0 %all-to-all-start.4 = ((bf16[32,48,128]{2,1,0:T(8,128)(2,1)}), bf16[32,48,128]{2,1,0:T(8,128)(2,1)S(1)}, u32[]{:S(2)}, u32[]{:S(2)}) async-start(bf16[32,48,128]{2,1,0:T(8,128)(2,1)} %bitcast.33), calls=%async_computation.4 | async-start | bytes 786432 | tf_op jit(solution)/shard_map/all_to_all | solution.py:234
  151.6 14.6 %collective-permute-start.7 = (bf16[112,512]{1,0:T(8,128)(2,1)S(1)}, bf16[112,512]{1,0:T(8,128)(2,1)S(1)}, u32[]{:S(2)}, u32[]{:S(2)}) collective-permute-start(bf16[112,512]{1,0:T(8,128)(2,1)S(1)} %get-tuple-element.41), channel_id=1, source_target_pairs={{0,32},{32,64},{64,96},{96,0},{1,33},{33,65},{65,97},{97,1},{2,34}... | collective-permute-start | bytes 344072 | tf_op jit(solution)/shard_map/ppermute | solution.py:226
  155.9 11.5 %collective-permute-start.9 = (bf16[112,512]{1,0:T(8,128)(2,1)S(1)}, bf16[112,512]{1,0:T(8,128)(2,1)S(1)}, u32[]{:S(2)}, u32[]{:S(2)}) collective-permute-start(bf16[112,512]{1,0:T(8,128)(2,1)S(1)} %get-tuple-element.42), channel_id=1, source_target_pairs={{0,64},{32,96},{64,0},{96,32},{1,65},{33,97},{65,1},{97,33},{2,66}... | collective-permute-start | bytes 344072 | tf_op jit(solution)/shard_map/ppermute | solution.py:226
  160.1 9.8 %collective-permute-start.8 = (bf16[112,512]{1,0:T(8,128)(2,1)S(1)}, bf16[112,512]{1,0:T(8,128)(2,1)S(1)}, u32[]{:S(2)}, u32[]{:S(2)}) collective-permute-start(bf16[112,512]{1,0:T(8,128)(2,1)S(1)} %get-tuple-element.43), channel_id=1, source_target_pairs={{0,96},{32,0},{64,32},{96,64},{1,97},{33,1},{65,33},{97,65},{2,98}... | collective-permute-start | bytes 344072 | tf_op jit(solution)/shard_map/ppermute | solution.py:226
  170.7 0.8 copy-start.5
Sparse Core Ops, SparseCore 0:
  10.1 51.8 all-gather.1

commit v9 on v8

--- a/solution.py
+++ b/solution.py
@@ -20,7 +20,9 @@
 ROWS = 2 * EXPERTS * CAP
 SLAB = 48
 GROUP = 8 * SLAB
-VMEM_LIMIT = 56 * 1024 * 1024
+WIDE = 88
+WIDER = 8 * WIDE
+VMEM_LIMIT = 24 * 1024 * 1024
 MOST_VMEM = 56 * 1024 * 1024
 ANYWHERE = pl.BlockSpec(memory_space=pl.ANY)
 VMEM = pl.BlockSpec(memory_space=pltpu.VMEM)
@@ -69,26 +71,27 @@
     )(*operands)
 
 
-def dispatch_kernel(ids_hbm, p_hbm, rows_hbm, out_ref, ids_ref, p_ref, rows_ref, sems, scale):
+def dispatch_kernel(ids_hbm, p_hbm, x_hbm, g_hbm, out_ref, ids_ref, p_ref, x_ref, g_ref, sems):
     copies = [
         pltpu.make_async_copy(source, target, sems.at[i])
-        for i, (source, target) in enumerate(((ids_hbm, ids_ref), (p_hbm, p_ref), (rows_hbm, rows_ref)))
+        for i, (source, target) in enumerate(((ids_hbm, ids_ref), (p_hbm, p_ref), (x_hbm, x_ref), (g_hbm, g_ref)))
     ]
     for copy in copies:
         copy.start()
-    k, at = iota((EXPERTS, SLAB, 7 * 64), 1), iota((EXPERTS, SLAB, 7 * 64), 2)
-    q = sixth(k)
-    order = onehot((at == q * 64 + iota((EXPERTS, SLAB, 7 * 64), 0) * 8 + (k - CAP * q)) & (q < 7))
-    order = order.reshape(GROUP, 7 * 64)
+    k, at = iota((EXPERTS, WIDE, 7 * TOK), 1), iota((EXPERTS, WIDE, 7 * TOK), 2)
+    q = (k * 43) >> 9
+    k = k - 12 * q
+    order = q * TOK + iota((EXPERTS, WIDE, 7 * TOK), 0) * 16 + k + jnp.where(k >= CAP, 2, 0)
+    order = onehot(at == order).reshape(EXPERTS * WIDE, 7 * TOK)
     for copy in copies:
         copy.wait()
     ids = ids_ref[...]
-    slot = jnp.where(ids < EXPERTS, ids * 8 + token_ranks(ids), -16)
-    sel = onehot(slot == iota((64, TOK), 0))
-    rows = rows_ref[...]
-    if scale:
-        rows = (to_column(p_ref[...]) * rows.astype(F32)).astype(BF)
-    rows = jnp.dot(sel, rows, preferred_element_type=F32).astype(BF)
+    slot = jnp.where(ids < EXPERTS, ids * 16 + token_ranks(ids), -16)
+    at = iota((TOK, TOK), 0)
+    sel = jnp.concatenate([onehot(slot == at), onehot(slot + 8 == at)], axis=1)
+    scaled = (to_column(p_ref[...]) * g_ref[...].astype(F32)).astype(BF)
+    both = jnp.concatenate([x_ref[...], scaled], axis=0)
+    rows = jnp.dot(sel, both, preferred_element_type=F32).astype(BF)
     for i in range(2):
         stack = []
         for q in range(7):
@@ -96,56 +99,36 @@
             stack.append(jnp.concatenate([rows[:, left:left + TOK], rows[:, left + PART:left + PART + TOK]], axis=1))
         moved = jnp.dot(order, jnp.concatenate(stack, axis=0), preferred_element_type=F32).astype(BF)
         for j in range(2):
-            out_ref[2 * i + j] = moved[:, j * TOK:(j + 1) * TOK].reshape(EXPERTS, SLAB, TOK)
-
-
-def dispatch(ids, share, rows, scale, name):
-    return call(
-        lambda *refs: dispatch_kernel(*refs, scale), name, [((4, EXPERTS, SLAB, TOK), BF)], (ids, share, rows),
-        3 * 10**8,
-        [pltpu.VMEM((1, TOK), I32), pltpu.VMEM((1, TOK), F32), pltpu.VMEM((TOK, D), BF), pltpu.SemaphoreType.DMA((3,))],
-        [ANYWHERE] * 3, MOST_VMEM,
-    )[0]
-
-
-def unpack(mine_ref, other_ref, out_ref):
+            one = moved[:, j * TOK:(j + 1) * TOK].reshape(EXPERTS, WIDE, TOK)
+            out_ref[2 * i + j] = one
+
+
+def before_kernel(mine_ref, other_ref, weight_ref, part_ref, g_ref, x_scr):
     zl = lax.axis_index("zl")
-    order = regroup()
+    shape = (7, 2, SLAB, WIDER)
+    j = iota(shape, 2)
+    source = sixth(j)
+    place = source * WIDE + iota(shape, 0) * 12 + iota(shape, 1) * CAP + (j - CAP * source)
+    pick = onehot(iota(shape, 3) == place).reshape(14 * SLAB, WIDER)
     for ref, z in ((mine_ref, zl), (other_ref, 1 - zl)):
         for i in range(2):
             both = jnp.concatenate([ref[2 * i], ref[2 * i + 1]], axis=1)
-            moved = jnp.dot(order, both, preferred_element_type=F32).astype(BF)
-            for j in range(2):
-                rows = pl.ds(pl.multiple_of((2 * (2 * i + j) + z) * SLAB, 16), SLAB)
+            moved = jnp.dot(pick, both, preferred_element_type=F32).astype(BF)
+            for k in range(2):
+                rows = pl.ds(pl.multiple_of((2 * (2 * i + k) + z) * SLAB, 16), SLAB)
                 for q in range(7):
-                    part = moved[q * SLAB:(q + 1) * SLAB, j * TOK:(j + 1) * TOK]
-                    out_ref[rows, q * TOK:(q + 1) * TOK] = part
-
-
-def gate_up_kernel(mine_ref, other_ref, weights_hbm, part_ref, x_scr, wide, sem):
-    copy = pltpu.make_async_copy(weights_hbm.at[:, pl.ds(0, 2 * HALF)], wide, sem)
-    copy.start()
-    unpack(mine_ref, other_ref, x_scr)
-    copy.wait()
-    pre = jnp.dot(x_scr[...], wide[...], preferred_element_type=F32).astype(BF)
-    part_ref[...] = pre.reshape(4, ROWS, 2 * HALF)
-
-
-def hidden_grad_kernel(mine_ref, other_ref, weights_hbm, g_ref, own_ref, plus_ref, minus_ref, far_ref, part, down, sem):
-    xi = lax.axis_index("x")
-    copy = pltpu.make_async_copy(weights_hbm.at[:, pl.ds(2 * HALF, HALF)], down, sem)
-    copy.start()
-    unpack(mine_ref, other_ref, g_ref)
-    copy.wait()
-    part[...] = jnp.dot(g_ref[...], down[...], preferred_element_type=F32).astype(BF)
-    for ref, shift in ((own_ref, 0), (plus_ref, 1), (minus_ref, 3), (far_ref, 2)):
-        ref[...] = part[pl.ds(pl.multiple_of(lax.rem(xi + shift, 4) * ROWS, 16), ROWS)]
-
-
-def middle_kernel(part_ref, a_ref, b_ref, c_ref, d_ref, out_ref, line_ref):
+                    columns, lanes = slice(q * TOK, (q + 1) * TOK), slice(k * TOK, (k + 1) * TOK)
+                    x_scr[rows, columns] = moved[2 * q * SLAB:(2 * q + 1) * SLAB, lanes]
+                    g_ref[rows, columns] = moved[(2 * q + 1) * SLAB:(2 * q + 2) * SLAB, lanes]
+    pre = jnp.dot(x_scr[...], weight_ref[:, :2 * HALF], preferred_element_type=F32).astype(BF)
+    part_ref[:, :, :2 * HALF] = pre.reshape(4, ROWS, 2 * HALF)
+    hid = jnp.dot(g_ref[...], weight_ref[:, 2 * HALF:], preferred_element_type=F32).astype(BF)
+    part_ref[:, :, 2 * HALF:] = hid.reshape(4, ROWS, HALF)
+
+
+def middle_kernel(part_ref, out_ref, line_ref):
     total = part_ref[0].astype(F32) + part_ref[1].astype(F32) + part_ref[2].astype(F32) + part_ref[3].astype(F32)
-    grad = a_ref[...].astype(F32) + b_ref[...].astype(F32) + c_ref[...].astype(F32) + d_ref[...].astype(F32)
-    gate, up = total[:, :HALF], total[:, HALF:]
+    gate, up, grad = total[:, :HALF], total[:, HALF:2 * HALF], total[:, 2 * HALF:]
     sig = jax.nn.sigmoid(gate)
     act = gate * sig
     slope = sig * (1.0 + gate * (1.0 - sig))
@@ -159,19 +142,15 @@
     line_ref[...] = jnp.where(iota((ROWS, TOK), 1) == 0, route, 0.0).astype(BF)
 
 
-def after_kernel(mid_ref, line_ref, g_ref, weights_hbm, keep_ref, give_ref,
-                 far_ref, plus_ref, minus_ref, own_ref, send_ref, down, wide, grads, line, sem):
+def after_kernel(mid_ref, line_ref, g_ref, weight_ref, keep_ref, give_ref,
+                 far_ref, plus_ref, minus_ref, own_ref, send_ref, down, grads):
     xi, zi, ci, zl = [lax.axis_index(a) for a in ("x", "zh", "c", "zl")]
-    copy = pltpu.make_async_copy(weights_hbm.at[:, pl.ds(0, 2 * HALF)], wide, sem)
-    copy.start()
     mid = mid_ref[...].reshape(4 * ROWS, 3 * HALF)
-    copy.wait()
     grads[...] = lax.dot_general(
-        mid[:, :2 * HALF], wide[...], (((1,), (1,)), ((), ())), preferred_element_type=F32
+        mid[:, :2 * HALF], weight_ref[:, :2 * HALF], (((1,), (1,)), ((), ())), preferred_element_type=F32
     ).astype(BF)
-    line[...] = line_ref[...]
     for ref, z in ((keep_ref, zl), (give_ref, 1 - zl)):
-        own = line[pl.ds(pl.multiple_of(z * SLAB, 16), SLAB)]
+        own = line_ref[pl.ds(pl.multiple_of(z * SLAB, 16), SLAB)]
         for i in range(4):
             ref[i, :, :PART] = grads[pl.ds(pl.multiple_of((2 * i + z) * SLAB, 16), SLAB)]
             ref[i, :, PART:] = jnp.where(xi == i, own, jnp.zeros_like(own))
@@ -239,35 +218,23 @@
     weights = jnp.concatenate([gate_weight, up_weight, down_weight], axis=1)
     weights = lax.all_gather(weights, ("zh", "c"), axis=0, tiled=True)
 
-    def send_rows(a):
-        return exchange(a.reshape(32, SLAB, TOK), PEERS).reshape(4, GROUP, TOK)
-
-    x_own = send_rows(dispatch(ids, share, tokens, False, "pack_tokens"))
-    g_own = send_rows(dispatch(ids, share, grad_out, True, "pack_grads"))
-    x_own, x_other, g_other = lax.optimization_barrier((x_own, hop(x_own, "zl", 1), hop(g_own, "zl", 1)))
-    x_rows, g_rows = (x_own, x_other), (g_own, g_other)
-
-    semaphore = pltpu.SemaphoreType.DMA(())
+    sent, = call(
+        dispatch_kernel, "dispatch", [((4, EXPERTS, WIDE, TOK), BF)], (ids, share, tokens, grad_out), 10**9,
+        [pltpu.VMEM((1, TOK), I32), pltpu.VMEM((1, TOK), F32), pltpu.VMEM((TOK, D), BF), pltpu.VMEM((TOK, D), BF),
+         pltpu.SemaphoreType.DMA((4,))], [ANYWHERE] * 4, MOST_VMEM,
+    )
+    rows = exchange(sent.reshape(32, WIDE, TOK), PEERS).reshape(4, WIDER, TOK)
     dense = pltpu.VMEM((4 * ROWS, PART), BF)
-    part, = call(
-        gate_up_kernel, "gate_up", [((4, ROWS, 2 * HALF), BF)], (*x_rows, weights), 10**9,
-        [dense, pltpu.VMEM((PART, 2 * HALF), BF), semaphore], [VMEM, VMEM, ANYWHERE],
-    )
-    block = ((ROWS, HALF), BF)
-    g_dense, own, plus, minus, far = call(
-        hidden_grad_kernel, "hidden_grad", [((4 * ROWS, PART), BF), block, block, block, block], (*g_rows, weights),
-        6 * 10**8, [pltpu.VMEM((4 * ROWS, HALF), BF), pltpu.VMEM((PART, HALF), BF), semaphore], [VMEM, VMEM, ANYWHERE],
-    )
-    mid, line = call(
-        middle_kernel, "middle", [((4, ROWS, 3 * HALF), BF), ((ROWS, TOK), BF)],
-        (exchange(part, "x"), own, hop(plus, "x", 1), hop(minus, "x", -1), hop(far, "x", 2)), 10**7,
-    )
+    part, g_rows = call(
+        before_kernel, "before", [((4, ROWS, 3 * HALF), BF), ((4 * ROWS, PART), BF)],
+        (rows, hop(rows, "zl", 1), weights), 2 * 10**9, [dense],
+    )
+    mid, line = call(middle_kernel, "middle", [((4, ROWS, 3 * HALF), BF), ((ROWS, TOK), BF)],
+                     (exchange(part, "x"),), 10**7)
     shard, wide = ((SHARD, HALF), BF), ((4, SLAB, PART + TOK), BF)
     keep, give, far, plus, minus, mine, send = call(
         after_kernel, "after", [wide, wide, shard, shard, shard, shard, ((4, SHARD, HALF), BF)],
-        (exchange(mid, "x"), line, g_dense, weights), 14 * 10**8,
-        [pltpu.VMEM((PART, HALF), BF), pltpu.VMEM((PART, 2 * HALF), BF), dense, pltpu.VMEM((ROWS, TOK), BF), semaphore],
-        [VMEM, VMEM, VMEM, ANYWHERE],
+        (exchange(mid, "x"), line, g_rows, weights), 14 * 10**8, [pltpu.VMEM((PART, HALF), BF), dense],
     )
     back, = call(combine_kernel, "combine", [((4, EXPERTS, SLAB, TOK), BF)], (keep, hop(give, "zl", 1)), 2 * 10**8)
     back = exchange(back.reshape(32, SLAB, TOK), PEERS).reshape(4, GROUP, TOK)

time: 182 us -> 166 us (0.912)
  blocking collectives: 18.2 us -> 65.8 us
  starting transfers between devices: 69.4 us -> 35 us
  Pallas kernels: 27.3 us -> 11.3 us
  waiting for transfers between devices: 46 us -> 34.2 us
    all_to_all x1 -> x3, blocking collectives: 18.2 us -> 65.8 us  [exchange(): return lax.all_to_all(a, axes, split_axis=0, concat_axis=0, tiled=True)]
    all_to_all x4 -> x1, starting transfers between devices: 31.7 us -> 11.3 us  [exchange(): return lax.all_to_all(a, axes, split_axis=0, concat_axis=0, tiled=True)]
    all_to_all x4 -> x1, waiting for transfers between devices: 18 us -> 0.01 us  [exchange(): return lax.all_to_all(a, axes, split_axis=0, concat_axis=0, tiled=True)]
    pallas_call x8 -> x6, Pallas kernels: 27.3 us -> 11.3 us  [call(): pl.pallas_call(body, in_specs=specs or [VMEM] * len(operands), out_specs=...]
    ppermute x10 -> x6, starting transfers between devices: 37.7 us -> 23.7 us  [hop(): return lax.ppermute(a, axis, [(i, (i + shift) % n) for i in range(n)])]
    ppermute x10 -> x6, waiting for transfers between devices: 28 us -> 34.2 us  [hop(): return lax.ppermute(a, axis, [(i, (i + shift) % n) for i in range(n)])]
  transfers between devices with their start and end apart: 15 -> 8, of which waited for: 9 -> 4; matrix products, arithmetic and copies ran while one was open for 0% -> 0% of each run, Pallas kernels for 6% -> 3%
where the time goes in v9:
time: 166 us; the launch traced here: 165 us
  blocking collectives  65.8 us (40%)
  starting transfers between devices  35 us (21%)
  waiting for transfers between devices  34.2 us (21%)
  between operations  14.1 us (8%)
  Pallas kernels  11.3 us (7%)
  other arithmetic  2.61 us (2%)
  local copies, waits for them, and re-layouts  1.79 us (1%)
    all_to_all x3, blocking collectives, exchange(): return lax.all_to_all(a, axes, split_axis=0, concat_axis=0, tiled=True)  65.8 us
    ppermute x6, waiting for transfers between devices, hop(): return lax.ppermute(a, axis, [(i, (i + shift) % n) for i in range(n)])  34.2 us
    ppermute x6, starting transfers between devices, hop(): return lax.ppermute(a, axis, [(i, (i + shift) % n) for i in range(n)])  23.7 us
    pallas_call x6, Pallas kernels, call(): pl.pallas_call(body, in_specs=specs or [VMEM] * len(operands), out_specs=...  11.3 us
    all_to_all x1, starting transfers between devices, exchange(): return lax.all_to_all(a, axes, split_axis=0, concat_axis=0, tiled=True)  11.3 us
  transfers between devices with their start and end apart: 8, of which 4 were waited for; matrix products, arithmetic and copies ran while one was open for 0% of the time, Pallas kernels for 3%

profile of v9, /device:TPU:6, one launch (start us, length us, event | category | flops | bytes accessed | tf_op | source)
XLA Modules:
  0.0 165.0 jit_solution(15966878404371065709)
XLA Ops:
  7.2 0.0 all-gather.2.cloned.1.call-start
  7.2 1.8 %pad_maximum_fusion = bf16[112,1536]{1,0:T(8,128)(2,1)} fusion(bf16[112,512]{1,0:T(8,128)(2,1)} %param.13, bf16[112,512]{1,0:T(8,128)(2,1)} %param.12, bf16[112,512]{1,0:T(8,128)(2,1)} %param.11), kind=kLoop, calls=%fused_computation | loop fusion | flops 1032192 | bytes 688128 | tf_op jit(solution)/shard_map/concatenate | solution.py:218
  9.0 0.0 all-gather.2.cloned.1.call-update
  9.0 3.7 %dispatch.1 = bf16[4,8,88,128]{3,2,1,0:T(8,128)(2,1)} custom-call(s32[1,128]{1,0:T(1,128)} %bitcast.30, f32[1,128]{1,0:T(1,128)} %bitcast.32, bf16[128,3584]{1,0:T(8,128)(2,1)} %x_hbm.1, bf16[128,3584]{1,0:T(8,128)(2,1)} %g_hbm.1), custom_call_target="tpu_custom_call" | custom-call | flops 1000000000 | bytes 4000000 | tf_op jit(solution)/shard_map/dispatch/pallas_call | solution.py:62
  12.8 29.6 %all_to_all.20 = bf16[32,88,128]{2,1,0:T(8,128)(2,1)S(1)} all-to-all(bf16[32,88,128]{2,1,0:T(8,128)(2,1)} %bitcast.34), channel_id=1, replica_groups=mesh['x'=4,'zh'=4,'c'=2,'y'=8,'zl'=2] {'x','y'}, dimensions={0} | all-to-all | bytes 1441792 | tf_op jit(solution)/shard_map/all_to_all | solution.py:213
  42.3 4.3 %collective-permute-start = (bf16[4,704,128]{2,1,0:T(8,128)(2,1)S(1)}, bf16[4,704,128]{2,1,0:T(8,128)(2,1)S(1)}, u32[]{:S(2)}, u32[]{:S(2)}) collective-permute-start(bf16[4,704,128]{2,1,0:T(8,128)(2,1)S(1)} %bitcast.27), channel_id=1, source_target_pairs={{0,1},{1,0},{2,3},{3,2},{4,5},{5,4},{6,7},{7,6},{8,9},{9,8},{10,11... | collective-permute-start | bytes 2162696 | tf_op jit(solution)/shard_map/ppermute | solution.py:205
  46.6 25.0 %collective-permute-done.other_ref = bf16[4,704,128]{2,1,0:T(8,128)(2,1)S(1)} collective-permute-done((bf16[4,704,128]{2,1,0:T(8,128)(2,1)S(1)}, bf16[4,704,128]{2,1,0:T(8,128)(2,1)S(1)}, u32[]{:S(2)}, u32[]{:S(2)}) %collective-permute-start) | collective-permute-done | bytes 720928 | tf_op jit(solution)/shard_map/ppermute | solution.py:205
  71.6 0.0 all-gather.2.cloned.1.call-done.weight_ref
  71.6 0.0 copy-start
  71.6 1.8 %copy-done = bf16[896,1536]{1,0:T(8,128)(2,1)S(1)} copy-done((bf16[896,1536]{1,0:T(8,128)(2,1)S(1)}, bf16[896,1536]{1,0:T(8,128)(2,1)}, u32[]{:S(2)}) %copy-start) | copy-done | bytes 2752536
  73.4 2.5 %before.1 = (bf16[4,96,1536]{2,1,0:T(8,128)(2,1)S(1)}, bf16[384,896]{1,0:T(8,128)(2,1)S(1)}) custom-call(bf16[4,704,128]{2,1,0:T(8,128)(2,1)S(1)} %bitcast.28, bf16[4,704,128]{2,1,0:T(8,128)(2,1)S(1)} %collective-permute-done.other_ref, bf16[896,1536]{1,0:T(8,128)(2,1)S(1)} %copy-done), custom_call_target="tpu_custom_call" | custom-call | flops 2000000000 | bytes 4000000 | tf_op jit(solution)/shard_map/before/pallas_call | solution.py:62
  75.9 18.7 %all_to_all.21.part_ref = bf16[4,96,1536]{2,1,0:T(8,128)(2,1)S(1)} all-to-all(bf16[4,96,1536]{2,1,0:T(8,128)(2,1)S(1)} %get-tuple-element.16), channel_id=1, replica_groups=mesh['x'=4,'zh'=4,'c'=2,'y'=8,'zl'=2] {'x'}, dimensions={0} | all-to-all | bytes 2359296 | tf_op jit(solution)/shard_map/all_to_all | solution.py:213
  94.6 0.0 copy-start.1
  94.6 0.3 middle.1
  95.0 17.5 %all_to_all.22.mid_ref = bf16[4,96,1536]{2,1,0:T(8,128)(2,1)S(1)} all-to-all(bf16[4,96,1536]{2,1,0:T(8,128)(2,1)S(1)} %get-tuple-element.17), channel_id=1, replica_groups=mesh['x'=4,'zh'=4,'c'=2,'y'=8,'zl'=2] {'x'}, dimensions={0} | all-to-all | bytes 2359296 | tf_op jit(solution)/shard_map/all_to_all | solution.py:213
  112.5 0.0 copy-done.1
  112.5 1.7 %after.1 = (bf16[4,48,1024]{2,1,0:T(8,128)(2,1)S(1)}, bf16[4,48,1024]{2,1,0:T(8,128)(2,1)S(1)}, bf16[112,512]{1,0:T(8,128)(2,1)S(1)}, bf16[112,512]{1,0:T(8,128)...) custom-call(bf16[4,96,1536]{2,1,0:T(8,128)(2,1)S(1)} %all_to_all.22.mid_ref,, ...), custom_call_target="tpu_custom_call" | custom-call | flops 1400000000 | bytes 4000000 | tf_op jit(solution)/shard_map/after/pallas_call | solution.py:62
  114.3 3.4 %collective-permute-start.1 = (bf16[4,48,1024]{2,1,0:T(8,128)(2,1)S(1)}, bf16[4,48,1024]{2,1,0:T(8,128)(2,1)S(1)}, u32[]{:S(2)}, u32[]{:S(2)}) collective-permute-start(bf16[4,48,1024]{2,1,0:T(8,128)(2,1)S(1)} %get-tuple-element.21), channel_id=1, source_target_pairs={{0,1},{1,0},{2,3},{3,2},{4,5},{5,4},{6,7},{7,6},{8,9},{9,8},{10,11... | collective-permute-start | bytes 1179656 | tf_op jit(solution)/shard_map/ppermute | solution.py:205
  117.6 1.9 %collective-permute-start.2 = (bf16[4,112,512]{2,1,0:T(8,128)(2,1)S(1)}, bf16[4,112,512]{2,1,0:T(8,128)(2,1)S(1)}, u32[]{:S(2)}, u32[]{:S(2)}) collective-permute-start(bf16[4,112,512]{2,1,0:T(8,128)(2,1)S(1)} %get-tuple-element.25), channel_id=1, source_target_pairs={{0,16},{16,0},{1,17},{17,1},{2,18},{18,2},{3,19},{19,3},{4,20},{20... | collective-permute-start | bytes 1376264 | tf_op jit(solution)/shard_map/ppermute | solution.py:205
  119.6 4.7 %collective-permute-done.1.got_ref = bf16[4,48,1024]{2,1,0:T(8,128)(2,1)S(1)} collective-permute-done((bf16[4,48,1024]{2,1,0:T(8,128)(2,1)S(1)}, bf16[4,48,1024]{2,1,0:T(8,128)(2,1)S(1)}, u32[]{:S(2)}, u32[]{:S(2)}) %collective-permute-start.1) | collective-permute-done | bytes 393248 | tf_op jit(solution)/shard_map/ppermute | solution.py:205
  124.3 1.2 combine.1
  125.5 0.0 copy-start.2
  125.5 0.0 copy-start.3
  125.5 11.3 %all-to-all-start.3 = ((bf16[32,48,128]{2,1,0:T(8,128)(2,1)}), bf16[32,48,128]{2,1,0:T(8,128)(2,1)S(1)}, u32[]{:S(2)}, u32[]{:S(2)}) async-start(bf16[32,48,128]{2,1,0:T(8,128)(2,1)} %bitcast.4), calls=%async_computation.3 | async-start | bytes 786432 | tf_op jit(solution)/shard_map/all_to_all | solution.py:213
  136.8 0.0 collective-permute-done.2
  136.8 0.1 fusion.3
  136.9 4.6 %collective-permute-start.3 = (bf16[112,512]{1,0:T(8,128)(2,1)S(1)}, bf16[112,512]{1,0:T(8,128)(2,1)S(1)}, u32[]{:S(2)}, u32[]{:S(2)}) collective-permute-start(bf16[112,512]{1,0:T(8,128)(2,1)S(1)} %get-tuple-element.29), channel_id=1, source_target_pairs={{0,32},{32,64},{64,96},{96,0},{1,33},{33,65},{65,97},{97,1},{2,34}... | collective-permute-start | bytes 344072 | tf_op jit(solution)/shard_map/ppermute | solution.py:205
  141.5 3.7 %collective-permute-start.5 = (bf16[112,512]{1,0:T(8,128)(2,1)S(1)}, bf16[112,512]{1,0:T(8,128)(2,1)S(1)}, u32[]{:S(2)}, u32[]{:S(2)}) collective-permute-start(bf16[112,512]{1,0:T(8,128)(2,1)S(1)} %get-tuple-element.30), channel_id=1, source_target_pairs={{0,64},{32,96},{64,0},{96,32},{1,65},{33,97},{65,1},{97,33},{2,66}... | collective-permute-start | bytes 344072 | tf_op jit(solution)/shard_map/ppermute | solution.py:205
  145.1 5.9 %collective-permute-start.4 = (bf16[112,512]{1,0:T(8,128)(2,1)S(1)}, bf16[112,512]{1,0:T(8,128)(2,1)S(1)}, u32[]{:S(2)}, u32[]{:S(2)}) collective-permute-start(bf16[112,512]{1,0:T(8,128)(2,1)S(1)} %get-tuple-element.31), channel_id=1, source_target_pairs={{0,96},{32,0},{64,32},{96,64},{1,97},{33,1},{65,33},{97,65},{2,98}... | collective-permute-start | bytes 344072 | tf_op jit(solution)/shard_map/ppermute | solution.py:205
  151.1 0.0 collective-permute-done.3
  151.1 2.8 %collective-permute-done.5 = bf16[112,512]{1,0:T(8,128)(2,1)S(1)} collective-permute-done((bf16[112,512]{1,0:T(8,128)(2,1)S(1)}, bf16[112,512]{1,0:T(8,128)(2,1)S(1)}, u32[]{:S(2)}, u32[]{:S(2)}) %collective-permute-start.5) | collective-permute-done | bytes 114720 | tf_op jit(solution)/shard_map/ppermute | solution.py:205
  153.8 1.8 %collective-permute-done.4 = bf16[112,512]{1,0:T(8,128)(2,1)S(1)} collective-permute-done((bf16[112,512]{1,0:T(8,128)(2,1)S(1)}, bf16[112,512]{1,0:T(8,128)(2,1)S(1)}, u32[]{:S(2)}, u32[]{:S(2)}) %collective-permute-start.4) | collective-permute-done | bytes 114720 | tf_op jit(solution)/shard_map/ppermute | solution.py:205
  155.6 0.7 add_convert_fusion
  156.3 0.0 all-to-all-done.3
  156.3 0.0 copy-done.2
  156.3 0.0 copy-done.3
  156.3 1.8 %finish.1 = (bf16[128,3584]{1,0:T(8,128)(2,1)}, f32[1,128]{1,0:T(1,128)}) custom-call(s32[1,128]{1,0:T(1,128)S(1)} %bitcast.31, f32[1,128]{1,0:T(1,128)S(1)} %bitcast.33, bf16[4,384,128]{2,1,0:T(8,128)(2,1)S(1)} %bitcast.29), custom_call_target="tpu_custom_call" | custom-call | flops 400000000 | bytes 4000000 | tf_op jit(solution)/shard_map/finish/pallas_call | solution.py:62
Async XLA Ops:
  7.2 64.4 %all-gather.2.cloned.1.call-start = ((), (), s32[]{:S(2)}) async-start(), calls=%async_computation.4 | async-start | bytes 3096576 | tf_op jit(solution)/shard_map/all_gather | solution.py:219
  42.3 29.3 %collective-permute-start = (bf16[4,704,128]{2,1,0:T(8,128)(2,1)S(1)}, bf16[4,704,128]{2,1,0:T(8,128)(2,1)S(1)}, u32[]{:S(2)}, u32[]{:S(2)}) collective-permute-start(bf16[4,704,128]{2,1,0:T(8,128)(2,1)S(1)} %bitcast.27), channel_id=1, source_target_pairs={{0,1},{1,0},{2,3},{3,2},{4,5},{5,4},{6,7},{7,6},{8,9},{9,8},{10,11... | collective-permute-start | bytes 2162696 | tf_op jit(solution)/shard_map/ppermute | solution.py:205
  71.6 1.8 %copy-start = (bf16[896,1536]{1,0:T(8,128)(2,1)S(1)}, bf16[896,1536]{1,0:T(8,128)(2,1)}, u32[]{:S(2)}) copy-start(bf16[896,1536]{1,0:T(8,128)(2,1)} %all-gather.2.cloned.1.call-done.weight_ref) | copy-start | bytes 8257540
  94.6 17.9 %copy-start.1 = (bf16[896,1536]{1,0:T(8,128)(2,1)S(1)}, bf16[896,1536]{1,0:T(8,128)(2,1)}, u32[]{:S(2)}) copy-start(bf16[896,1536]{1,0:T(8,128)(2,1)} %all-gather.2.cloned.1.call-done.weight_ref) | copy-start | bytes 8257540
  114.3 10.0 %collective-permute-start.1 = (bf16[4,48,1024]{2,1,0:T(8,128)(2,1)S(1)}, bf16[4,48,1024]{2,1,0:T(8,128)(2,1)S(1)}, u32[]{:S(2)}, u32[]{:S(2)}) collective-permute-start(bf16[4,48,1024]{2,1,0:T(8,128)(2,1)S(1)} %get-tuple-element.21), channel_id=1, source_target_pairs={{0,1},{1,0},{2,3},{3,2},{4,5},{5,4},{6,7},{7,6},{8,9},{9,8},{10,11... | collective-permute-start | bytes 1179656 | tf_op jit(solution)/shard_map/ppermute | solution.py:205
  117.6 19.1 %collective-permute-start.2 = (bf16[4,112,512]{2,1,0:T(8,128)(2,1)S(1)}, bf16[4,112,512]{2,1,0:T(8,128)(2,1)S(1)}, u32[]{:S(2)}, u32[]{:S(2)}) collective-permute-start(bf16[4,112,512]{2,1,0:T(8,128)(2,1)S(1)} %get-tuple-element.25), channel_id=1, source_target_pairs={{0,16},{16,0},{1,17},{17,1},{2,18},{18,2},{3,19},{19,3},{4,20},{20... | collective-permute-start | bytes 1376264 | tf_op jit(solution)/shard_map/ppermute | solution.py:205
  125.5 30.9 %copy-start.2 = (s32[128,1]{0,1:T(1,128)S(1)}, s32[128,1]{0,1:T(1,128)}, u32[]{:S(2)}) copy-start(s32[128,1]{0,1:T(1,128)} %param.9) | copy-start | bytes 1540
  125.5 30.9 %copy-start.3 = (f32[128,1]{0,1:T(1,128)S(1)}, f32[128,1]{0,1:T(1,128)}, u32[]{:S(2)}) copy-start(f32[128,1]{0,1:T(1,128)} %param.10) | copy-start | bytes 1540
  125.5 30.8 %all-to-all-start.3 = ((bf16[32,48,128]{2,1,0:T(8,128)(2,1)}), bf16[32,48,128]{2,1,0:T(8,128)(2,1)S(1)}, u32[]{:S(2)}, u32[]{:S(2)}) async-start(bf16[32,48,128]{2,1,0:T(8,128)(2,1)} %bitcast.4), calls=%async_computation.3 | async-start | bytes 786432 | tf_op jit(solution)/shard_map/all_to_all | solution.py:213
  136.9 14.2 %collective-permute-start.3 = (bf16[112,512]{1,0:T(8,128)(2,1)S(1)}, bf16[112,512]{1,0:T(8,128)(2,1)S(1)}, u32[]{:S(2)}, u32[]{:S(2)}) collective-permute-start(bf16[112,512]{1,0:T(8,128)(2,1)S(1)} %get-tuple-element.29), channel_id=1, source_target_pairs={{0,32},{32,64},{64,96},{96,0},{1,33},{33,65},{65,97},{97,1},{2,34}... | collective-permute-start | bytes 344072 | tf_op jit(solution)/shard_map/ppermute | solution.py:205
  141.5 12.4 %collective-permute-start.5 = (bf16[112,512]{1,0:T(8,128)(2,1)S(1)}, bf16[112,512]{1,0:T(8,128)(2,1)S(1)}, u32[]{:S(2)}, u32[]{:S(2)}) collective-permute-start(bf16[112,512]{1,0:T(8,128)(2,1)S(1)} %get-tuple-element.30), channel_id=1, source_target_pairs={{0,64},{32,96},{64,0},{96,32},{1,65},{33,97},{65,1},{97,33},{2,66}... | collective-permute-start | bytes 344072 | tf_op jit(solution)/shard_map/ppermute | solution.py:205
  145.1 10.5 %collective-permute-start.4 = (bf16[112,512]{1,0:T(8,128)(2,1)S(1)}, bf16[112,512]{1,0:T(8,128)(2,1)S(1)}, u32[]{:S(2)}, u32[]{:S(2)}) collective-permute-start(bf16[112,512]{1,0:T(8,128)(2,1)S(1)} %get-tuple-element.31), channel_id=1, source_target_pairs={{0,96},{32,0},{64,32},{96,64},{1,97},{33,1},{65,33},{97,65},{2,98}... | collective-permute-start | bytes 344072 | tf_op jit(solution)/shard_map/ppermute | solution.py:205
Sparse Core Ops, SparseCore 0:
  10.1 51.8 all-gather.1

commit v10 on v9

--- a/solution.py
+++ b/solution.py
@@ -103,6 +103,14 @@
             out_ref[2 * i + j] = one
 
 
+def assemble_kernel(near_ref, near_other_ref, far_ref, far_other_ref, out_ref):
+    zi, ci = lax.axis_index("zh"), lax.axis_index("c")
+    for core, near, far in ((ci, near_ref, far_ref), (1 - ci, near_other_ref, far_other_ref)):
+        for i, shift in enumerate((0, 3, 1, 2)):
+            at = pl.multiple_of((2 * lax.rem(zi + shift, 4) + core) * SHARD, 16)
+            out_ref[pl.ds(at, SHARD)] = far[...] if shift == 2 else near[i * SHARD:(i + 1) * SHARD]
+
+
 def before_kernel(mine_ref, other_ref, weight_ref, part_ref, g_ref, x_scr):
     zl = lax.axis_index("zl")
     shape = (7, 2, SLAB, WIDER)
@@ -215,15 +223,23 @@
 
 def per_device(tokens, grad_out, routing, route_weight, gate_weight, up_weight, down_weight):
     ids, share = routing.reshape(1, TOK), route_weight.reshape(1, TOK)
-    weights = jnp.concatenate([gate_weight, up_weight, down_weight], axis=1)
-    weights = lax.all_gather(weights, ("zh", "c"), axis=0, tiled=True)
-
     sent, = call(
         dispatch_kernel, "dispatch", [((4, EXPERTS, WIDE, TOK), BF)], (ids, share, tokens, grad_out), 10**9,
         [pltpu.VMEM((1, TOK), I32), pltpu.VMEM((1, TOK), F32), pltpu.VMEM((TOK, D), BF), pltpu.VMEM((TOK, D), BF),
          pltpu.SemaphoreType.DMA((4,))], [ANYWHERE] * 4, MOST_VMEM,
     )
+    gate_weight, sent = lax.optimization_barrier((gate_weight, sent))
     rows = exchange(sent.reshape(32, WIDE, TOK), PEERS).reshape(4, WIDER, TOK)
+
+    cut = SHARD // 2
+    weights = jnp.concatenate([gate_weight, up_weight, down_weight], axis=1)
+    z_before, z_after = hop(weights, "zh", 1), hop(weights, "zh", -1)
+    z_low, z_high = hop(z_before[:cut], "zh", 1), hop(z_after[cut:], "zh", -1)
+    near = jnp.concatenate([weights, z_before, z_after], axis=0)
+    far = jnp.concatenate([z_low, z_high], axis=0)
+    weights, = call(assemble_kernel, "assemble", [((PART, 3 * HALF), BF)],
+                    (near, hop(near, "c", 1), far, hop(far, "c", 1)), 10**6)
+
     dense = pltpu.VMEM((4 * ROWS, PART), BF)
     part, g_rows = call(
         before_kernel, "before", [((4, ROWS, 3 * HALF), BF), ((4 * ROWS, PART), BF)],

time: 166 us -> 162 us (0.976)
  blocking collectives: 65.8 us -> 37.1 us
  starting transfers between devices: 35 us -> 61.6 us
  waiting for transfers between devices: 34.2 us -> 48.8 us
  between operations: 14.1 us -> 0.93 us
  other arithmetic: 2.61 us -> 0.88 us
  local copies, waits for them, and re-layouts: 1.79 us -> 0.11 us
    all_to_all x3 -> x2, blocking collectives: 65.8 us -> 37.1 us  [exchange(): return lax.all_to_all(a, axes, split_axis=0, concat_axis=0, tiled=True)]
    ppermute x6 -> x12, starting transfers between devices: 23.7 us -> 41.9 us  [hop(): return lax.ppermute(a, axis, [(i, (i + shift) % n) for i in range(n)])]
    ppermute x6 -> x12, waiting for transfers between devices: 34.2 us -> 48.8 us  [hop(): return lax.ppermute(a, axis, [(i, (i + shift) % n) for i in range(n)])]
    all_to_all x1 -> x2, starting transfers between devices: 11.3 us -> 19.8 us  [exchange(): return lax.all_to_all(a, axes, split_axis=0, concat_axis=0, tiled=True)]
    unnamed x8 -> x13, local copies, waits for them, and re-layouts: 1.79 us -> 0.06 us
    concatenate x1, other arithmetic: 1.79 us -> 0.07 us  [per_device(): near = jnp.concatenate([weights, z_before, z_after], axis=0)]
    pallas_call x6 -> x7, Pallas kernels: 11.3 us -> 11.5 us  [call(): pl.pallas_call(body, in_specs=specs or [VMEM] * len(operands), out_specs=...]
  transfers between devices with their start and end apart: 8 -> 14, of which waited for: 4 -> 9; matrix products, arithmetic and copies ran while one was open for 0% -> 1% of each run, Pallas kernels for 3% -> 1%
where the time goes in v10:
time: 162 us; the launch traced here: 161 us
  starting transfers between devices  61.6 us (38%)
  waiting for transfers between devices  48.8 us (30%)
  blocking collectives  37.1 us (23%)
  Pallas kernels  11.5 us (7%)
    ppermute x12, waiting for transfers between devices, hop(): return lax.ppermute(a, axis, [(i, (i + shift) % n) for i in range(n)])  48.8 us
    ppermute x12, starting transfers between devices, hop(): return lax.ppermute(a, axis, [(i, (i + shift) % n) for i in range(n)])  41.9 us
    all_to_all x2, blocking collectives, exchange(): return lax.all_to_all(a, axes, split_axis=0, concat_axis=0, tiled=True)  37.1 us
    all_to_all x2, starting transfers between devices, exchange(): return lax.all_to_all(a, axes, split_axis=0, concat_axis=0, tiled=True)  19.8 us
    pallas_call x7, Pallas kernels, call(): pl.pallas_call(body, in_specs=specs or [VMEM] * len(operands), out_specs=...  11.5 us
  transfers between devices with their start and end apart: 14, of which 9 were waited for; matrix products, arithmetic and copies ran while one was open for 1% of the time, Pallas kernels for 1%

profile of v10, /device:TPU:6, one launch (start us, length us, event | category | flops | bytes accessed | tf_op | source)
XLA Modules:
  0.0 161.0 jit_solution(15650704808353687060)
XLA Ops:
  0.6 0.0 copy-start.2
  0.6 0.0 copy-start.3
  0.7 0.0 copy-start.4
  0.7 3.8 %dispatch.1 = bf16[4,8,88,128]{3,2,1,0:T(8,128)(2,1)} custom-call(s32[1,128]{1,0:T(1,128)} %bitcast.30, f32[1,128]{1,0:T(1,128)} %bitcast.32, bf16[128,3584]{1,0:T(8,128)(2,1)} %x_hbm.1, bf16[128,3584]{1,0:T(8,128)(2,1)} %g_hbm.1), custom_call_target="tpu_custom_call" | custom-call | flops 1000000000 | bytes 4000000 | tf_op jit(solution)/shard_map/dispatch/pallas_call | solution.py:62
  4.5 10.2 %all-to-all-start = ((bf16[32,88,128]{2,1,0:T(8,128)(2,1)}), bf16[32,88,128]{2,1,0:T(8,128)(2,1)S(1)}, u32[]{:S(2)}, u32[]{:S(2)}) async-start(bf16[32,88,128]{2,1,0:T(8,128)(2,1)} %bitcast.34), calls=%async_computation | async-start | bytes 1441792 | tf_op jit(solution)/shard_map/all_to_all | solution.py:221
  14.7 0.0 copy-done.2
  14.8 0.0 copy-done.3
  14.8 0.0 copy-done.4
  14.8 6.1 %collective-permute-start.1 = (bf16[112,1536]{1,0:T(8,128)(2,1)S(1)}, bf16[112,1536]{1,0:T(8,128)(2,1)S(1)}, u32[]{:S(2)}, u32[]{:S(2)}) collective-permute-start(bf16[112,1536]{1,0:T(8,128)(2,1)S(1)} %constant_dynamic-update-slice_fusion), channel_id=1, source_target_pairs={{0,32},{32,64},{64,96},{96,0},{1,33},{33,65},{65,97},{97,1},{2,34}... | collective-permute-start | bytes 1032200 | tf_op jit(solution)/shard_map/ppermute | solution.py:213
  20.9 6.8 %collective-permute-start.2 = (bf16[112,1536]{1,0:T(8,128)(2,1)S(1)}, bf16[112,1536]{1,0:T(8,128)(2,1)S(1)}, u32[]{:S(2)}, u32[]{:S(2)}) collective-permute-start(bf16[112,1536]{1,0:T(8,128)(2,1)S(1)} %constant_dynamic-update-slice_fusion), channel_id=1, source_target_pairs={{0,96},{32,0},{64,32},{96,64},{1,97},{33,1},{65,33},{97,65},{2,98}... | collective-permute-start | bytes 1032200 | tf_op jit(solution)/shard_map/ppermute | solution.py:213
  27.7 5.7 %collective-permute-done.1 = bf16[112,1536]{1,0:T(8,128)(2,1)S(1)} collective-permute-done((bf16[112,1536]{1,0:T(8,128)(2,1)S(1)}, bf16[112,1536]{1,0:T(8,128)(2,1)S(1)}, u32[]{:S(2)}, u32[]{:S(2)}) %collective-permute-start.1) | collective-permute-done | bytes 344096 | tf_op jit(solution)/shard_map/ppermute | solution.py:213
  33.4 9.5 %collective-permute-done.2 = bf16[112,1536]{1,0:T(8,128)(2,1)S(1)} collective-permute-done((bf16[112,1536]{1,0:T(8,128)(2,1)S(1)}, bf16[112,1536]{1,0:T(8,128)(2,1)S(1)}, u32[]{:S(2)}, u32[]{:S(2)}) %collective-permute-start.2) | collective-permute-done | bytes 344096 | tf_op jit(solution)/shard_map/ppermute | solution.py:213
  42.9 0.1 pad_maximum_fusion.near_ref
  43.0 1.9 %collective-permute-start.3 = (bf16[336,1536]{1,0:T(8,128)(2,1)S(1)}, bf16[336,1536]{1,0:T(8,128)(2,1)S(1)}, u32[]{:S(2)}, u32[]{:S(2)}) collective-permute-start(bf16[336,1536]{1,0:T(8,128)(2,1)S(1)} %pad_maximum_fusion.near_ref), channel_id=1, source_target_pairs={{0,16},{16,0},{1,17},{17,1},{2,18},{18,2},{3,19},{19,3},{4,20},{20... | collective-permute-start | bytes 3096584 | tf_op jit(solution)/shard_map/ppermute | solution.py:213
  44.9 3.4 %collective-permute-start.4 = (bf16[56,1536]{1,0:T(8,128)(2,1)S(1)}, bf16[56,1536]{1,0:T(8,128)(2,1)S(1)}, u32[]{:S(2)}, u32[]{:S(2)}) collective-permute-start(bf16[56,1536]{1,0:T(8,128)(2,1)S(1)} %slice.24), channel_id=1, source_target_pairs={{0,32},{32,64},{64,96},{96,0},{1,33},{33,65},{65,97},{97,1},{2,34}... | collective-permute-start | bytes 516104 | tf_op jit(solution)/shard_map/ppermute | solution.py:213
  48.3 4.6 %collective-permute-start.5 = (bf16[56,1536]{1,0:T(8,128)(2,1)S(1)}, bf16[56,1536]{1,0:T(8,128)(2,1)S(1)}, u32[]{:S(2)}, u32[]{:S(2)}) collective-permute-start(bf16[56,1536]{1,0:T(8,128)(2,1)S(1)} %slice.25), channel_id=1, source_target_pairs={{0,96},{32,0},{64,32},{96,64},{1,97},{33,1},{65,33},{97,65},{2,98}... | collective-permute-start | bytes 516104 | tf_op jit(solution)/shard_map/ppermute | solution.py:213
  52.9 0.0 all-to-all-done
  52.9 2.7 %collective-permute-start = (bf16[4,704,128]{2,1,0:T(8,128)(2,1)S(1)}, bf16[4,704,128]{2,1,0:T(8,128)(2,1)S(1)}, u32[]{:S(2)}, u32[]{:S(2)}) collective-permute-start(bf16[4,704,128]{2,1,0:T(8,128)(2,1)S(1)} %bitcast.27), channel_id=1, source_target_pairs={{0,1},{1,0},{2,3},{3,2},{4,5},{5,4},{6,7},{7,6},{8,9},{9,8},{10,11... | collective-permute-start | bytes 2162696 | tf_op jit(solution)/shard_map/ppermute | solution.py:213
  55.6 3.7 %collective-permute-done.4 = bf16[56,1536]{1,0:T(8,128)(2,1)S(1)} collective-permute-done((bf16[56,1536]{1,0:T(8,128)(2,1)S(1)}, bf16[56,1536]{1,0:T(8,128)(2,1)S(1)}, u32[]{:S(2)}, u32[]{:S(2)}) %collective-permute-start.4) | collective-permute-done | bytes 172064 | tf_op jit(solution)/shard_map/ppermute | solution.py:213
  59.3 1.7 %collective-permute-done.5 = bf16[56,1536]{1,0:T(8,128)(2,1)S(1)} collective-permute-done((bf16[56,1536]{1,0:T(8,128)(2,1)S(1)}, bf16[56,1536]{1,0:T(8,128)(2,1)S(1)}, u32[]{:S(2)}, u32[]{:S(2)}) %collective-permute-start.5) | collective-permute-done | bytes 172064 | tf_op jit(solution)/shard_map/ppermute | solution.py:213
  61.1 1.9 %collective-permute-start.6 = (bf16[112,1536]{1,0:T(8,128)(2,1)S(1)}, bf16[112,1536]{1,0:T(8,128)(2,1)S(1)}, u32[]{:S(2)}, u32[]{:S(2)}) collective-permute-start(bf16[112,1536]{1,0:T(8,128)(2,1)S(1)} %constant_dynamic-update-slice_fusion.3.far_ref), channel_id=1, source_target_pairs={{0,16},{16,0},{1,17},{17,1},{2,18},{18,2},{3,19},{19,3},{4,20},{20... | collective-permute-start | bytes 1032200 | tf_op jit(solution)/shard_map/ppermute | solution.py:213
  63.0 1.6 %collective-permute-done.6.far_other_ref = bf16[112,1536]{1,0:T(8,128)(2,1)S(1)} collective-permute-done((bf16[112,1536]{1,0:T(8,128)(2,1)S(1)}, bf16[112,1536]{1,0:T(8,128)(2,1)S(1)}, u32[]{:S(2)}, u32[]{:S(2)}) %collective-permute-start.6) | collective-permute-done | bytes 344096 | tf_op jit(solution)/shard_map/ppermute | solution.py:213
  64.6 0.0 collective-permute-done.3.near_other_ref
  64.6 0.2 assemble.1.weight_ref
  64.8 12.8 %collective-permute-done.other_ref = bf16[4,704,128]{2,1,0:T(8,128)(2,1)S(1)} collective-permute-done((bf16[4,704,128]{2,1,0:T(8,128)(2,1)S(1)}, bf16[4,704,128]{2,1,0:T(8,128)(2,1)S(1)}, u32[]{:S(2)}, u32[]{:S(2)}) %collective-permute-start) | collective-permute-done | bytes 720928 | tf_op jit(solution)/shard_map/ppermute | solution.py:213
  77.6 2.5 %before.1 = (bf16[4,96,1536]{2,1,0:T(8,128)(2,1)S(1)}, bf16[384,896]{1,0:T(8,128)(2,1)S(1)}) custom-call(bf16[4,704,128]{2,1,0:T(8,128)(2,1)S(1)} %bitcast.28, bf16[4,704,128]{2,1,0:T(8,128)(2,1)S(1)} %collective-permute-done.other_ref, bf16[896,1536]{1,0:T(8,128)(2,1)S(1)} %assemble.1.weight_ref), custom_call_target="tpu_custom_call" | custom-call | flops 2000000000 | bytes 4000000 | tf_op jit(solution)/shard_map/before/pallas_call | solution.py:62
  80.2 19.1 %all_to_all.20.part_ref = bf16[4,96,1536]{2,1,0:T(8,128)(2,1)S(1)} all-to-all(bf16[4,96,1536]{2,1,0:T(8,128)(2,1)S(1)} %get-tuple-element.20), channel_id=1, replica_groups=mesh['x'=4,'zh'=4,'c'=2,'y'=8,'zl'=2] {'x'}, dimensions={0} | all-to-all | bytes 2359296 | tf_op jit(solution)/shard_map/all_to_all | solution.py:221
  99.3 0.3 middle.1
  99.6 18.0 %all_to_all.21.mid_ref = bf16[4,96,1536]{2,1,0:T(8,128)(2,1)S(1)} all-to-all(bf16[4,96,1536]{2,1,0:T(8,128)(2,1)S(1)} %get-tuple-element.21), channel_id=1, replica_groups=mesh['x'=4,'zh'=4,'c'=2,'y'=8,'zl'=2] {'x'}, dimensions={0} | all-to-all | bytes 2359296 | tf_op jit(solution)/shard_map/all_to_all | solution.py:221
  117.6 1.7 %after.1 = (bf16[4,48,1024]{2,1,0:T(8,128)(2,1)S(1)}, bf16[4,48,1024]{2,1,0:T(8,128)(2,1)S(1)}, bf16[112,512]{1,0:T(8,128)(2,1)S(1)}, bf16[112,512]{1,0:T(8,128)...) custom-call(bf16[4,96,1536]{2,1,0:T(8,128)(2,1)S(1)} %all_to_all.21.mid_ref,, ...), custom_call_target="tpu_custom_call" | custom-call | flops 1400000000 | bytes 4000000 | tf_op jit(solution)/shard_map/after/pallas_call | solution.py:62
  119.3 0.0 copy-start
  119.4 0.0 copy-start.1
  119.4 1.9 %collective-permute-start.7 = (bf16[4,48,1024]{2,1,0:T(8,128)(2,1)S(1)}, bf16[4,48,1024]{2,1,0:T(8,128)(2,1)S(1)}, u32[]{:S(2)}, u32[]{:S(2)}) collective-permute-start(bf16[4,48,1024]{2,1,0:T(8,128)(2,1)S(1)} %get-tuple-element.25), channel_id=1, source_target_pairs={{0,1},{1,0},{2,3},{3,2},{4,5},{5,4},{6,7},{7,6},{8,9},{9,8},{10,11... | collective-permute-start | bytes 1179656 | tf_op jit(solution)/shard_map/ppermute | solution.py:213
  121.3 1.9 %collective-permute-start.8 = (bf16[4,112,512]{2,1,0:T(8,128)(2,1)S(1)}, bf16[4,112,512]{2,1,0:T(8,128)(2,1)S(1)}, u32[]{:S(2)}, u32[]{:S(2)}) collective-permute-start(bf16[4,112,512]{2,1,0:T(8,128)(2,1)S(1)} %get-tuple-element.29), channel_id=1, source_target_pairs={{0,16},{16,0},{1,17},{17,1},{2,18},{18,2},{3,19},{19,3},{4,20},{20... | collective-permute-start | bytes 1376264 | tf_op jit(solution)/shard_map/ppermute | solution.py:213
  123.2 6.8 %collective-permute-done.7.got_ref = bf16[4,48,1024]{2,1,0:T(8,128)(2,1)S(1)} collective-permute-done((bf16[4,48,1024]{2,1,0:T(8,128)(2,1)S(1)}, bf16[4,48,1024]{2,1,0:T(8,128)(2,1)S(1)}, u32[]{:S(2)}, u32[]{:S(2)}) %collective-permute-start.7) | collective-permute-done | bytes 393248 | tf_op jit(solution)/shard_map/ppermute | solution.py:213
  130.0 1.2 combine.1
  131.2 9.5 %all-to-all-start.3 = ((bf16[32,48,128]{2,1,0:T(8,128)(2,1)}), bf16[32,48,128]{2,1,0:T(8,128)(2,1)S(1)}, u32[]{:S(2)}, u32[]{:S(2)}) async-start(bf16[32,48,128]{2,1,0:T(8,128)(2,1)} %bitcast.4), calls=%async_computation.3 | async-start | bytes 786432 | tf_op jit(solution)/shard_map/all_to_all | solution.py:221
  140.7 0.0 collective-permute-done.8
  140.7 0.1 fusion.3
  140.8 1.9 %collective-permute-start.10 = (bf16[112,512]{1,0:T(8,128)(2,1)S(1)}, bf16[112,512]{1,0:T(8,128)(2,1)S(1)}, u32[]{:S(2)}, u32[]{:S(2)}) collective-permute-start(bf16[112,512]{1,0:T(8,128)(2,1)S(1)} %get-tuple-element.35), channel_id=1, source_target_pairs={{0,96},{32,0},{64,32},{96,64},{1,97},{33,1},{65,33},{97,65},{2,98}... | collective-permute-start | bytes 344072 | tf_op jit(solution)/shard_map/ppermute | solution.py:213
  142.8 6.0 %collective-permute-start.11 = (bf16[112,512]{1,0:T(8,128)(2,1)S(1)}, bf16[112,512]{1,0:T(8,128)(2,1)S(1)}, u32[]{:S(2)}, u32[]{:S(2)}) collective-permute-start(bf16[112,512]{1,0:T(8,128)(2,1)S(1)} %get-tuple-element.34), channel_id=1, source_target_pairs={{0,64},{32,96},{64,0},{96,32},{1,65},{33,97},{65,1},{97,33},{2,66}... | collective-permute-start | bytes 344072 | tf_op jit(solution)/shard_map/ppermute | solution.py:213
  148.8 2.7 %collective-permute-start.9 = (bf16[112,512]{1,0:T(8,128)(2,1)S(1)}, bf16[112,512]{1,0:T(8,128)(2,1)S(1)}, u32[]{:S(2)}, u32[]{:S(2)}) collective-permute-start(bf16[112,512]{1,0:T(8,128)(2,1)S(1)} %get-tuple-element.33), channel_id=1, source_target_pairs={{0,32},{32,64},{64,96},{96,0},{1,33},{33,65},{65,97},{97,1},{2,34}... | collective-permute-start | bytes 344072 | tf_op jit(solution)/shard_map/ppermute | solution.py:213
  151.5 0.0 collective-permute-done.10
  151.5 5.2 %collective-permute-done.11 = bf16[112,512]{1,0:T(8,128)(2,1)S(1)} collective-permute-done((bf16[112,512]{1,0:T(8,128)(2,1)S(1)}, bf16[112,512]{1,0:T(8,128)(2,1)S(1)}, u32[]{:S(2)}, u32[]{:S(2)}) %collective-permute-start.11) | collective-permute-done | bytes 114720 | tf_op jit(solution)/shard_map/ppermute | solution.py:213
  156.7 1.8 %collective-permute-done.9 = bf16[112,512]{1,0:T(8,128)(2,1)S(1)} collective-permute-done((bf16[112,512]{1,0:T(8,128)(2,1)S(1)}, bf16[112,512]{1,0:T(8,128)(2,1)S(1)}, u32[]{:S(2)}, u32[]{:S(2)}) %collective-permute-start.9) | collective-permute-done | bytes 114720 | tf_op jit(solution)/shard_map/ppermute | solution.py:213
  158.5 0.7 add_convert_fusion
  159.2 0.0 all-to-all-done.3
  159.2 0.0 copy-done
  159.2 0.0 copy-done.1
  159.2 1.8 %finish.1 = (bf16[128,3584]{1,0:T(8,128)(2,1)}, f32[1,128]{1,0:T(1,128)}) custom-call(s32[1,128]{1,0:T(1,128)S(1)} %bitcast.31, f32[1,128]{1,0:T(1,128)S(1)} %bitcast.33, bf16[4,384,128]{2,1,0:T(8,128)(2,1)S(1)} %bitcast.29), custom_call_target="tpu_custom_call" | custom-call | flops 400000000 | bytes 4000000 | tf_op jit(solution)/shard_map/finish/pallas_call | solution.py:62
  (7 shorter events, 0.1 us)
Async XLA Ops:
  0.6 14.1 %copy-start.2 = (bf16[112,512]{1,0:T(8,128)(2,1)S(1)}, bf16[112,512]{1,0:T(8,128)(2,1)}, u32[]{:S(2)}) copy-start(bf16[112,512]{1,0:T(8,128)(2,1)} %param.11) | copy-start | bytes 344068
  0.6 14.1 %copy-start.3 = (bf16[112,512]{1,0:T(8,128)(2,1)S(1)}, bf16[112,512]{1,0:T(8,128)(2,1)}, u32[]{:S(2)}) copy-start(bf16[112,512]{1,0:T(8,128)(2,1)} %param.12) | copy-start | bytes 344068
  0.7 14.1 %copy-start.4 = (bf16[112,512]{1,0:T(8,128)(2,1)S(1)}, bf16[112,512]{1,0:T(8,128)(2,1)}, u32[]{:S(2)}) copy-start(bf16[112,512]{1,0:T(8,128)(2,1)} %param.13) | copy-start | bytes 344068
  4.5 48.4 %all-to-all-start = ((bf16[32,88,128]{2,1,0:T(8,128)(2,1)}), bf16[32,88,128]{2,1,0:T(8,128)(2,1)S(1)}, u32[]{:S(2)}, u32[]{:S(2)}) async-start(bf16[32,88,128]{2,1,0:T(8,128)(2,1)} %bitcast.34), calls=%async_computation | async-start | bytes 1441792 | tf_op jit(solution)/shard_map/all_to_all | solution.py:221
  14.8 18.6 %collective-permute-start.1 = (bf16[112,1536]{1,0:T(8,128)(2,1)S(1)}, bf16[112,1536]{1,0:T(8,128)(2,1)S(1)}, u32[]{:S(2)}, u32[]{:S(2)}) collective-permute-start(bf16[112,1536]{1,0:T(8,128)(2,1)S(1)} %constant_dynamic-update-slice_fusion), channel_id=1, source_target_pairs={{0,32},{32,64},{64,96},{96,0},{1,33},{33,65},{65,97},{97,1},{2,34}... | collective-permute-start | bytes 1032200 | tf_op jit(solution)/shard_map/ppermute | solution.py:213
  20.9 22.0 %collective-permute-start.2 = (bf16[112,1536]{1,0:T(8,128)(2,1)S(1)}, bf16[112,1536]{1,0:T(8,128)(2,1)S(1)}, u32[]{:S(2)}, u32[]{:S(2)}) collective-permute-start(bf16[112,1536]{1,0:T(8,128)(2,1)S(1)} %constant_dynamic-update-slice_fusion), channel_id=1, source_target_pairs={{0,96},{32,0},{64,32},{96,64},{1,97},{33,1},{65,33},{97,65},{2,98}... | collective-permute-start | bytes 1032200 | tf_op jit(solution)/shard_map/ppermute | solution.py:213
  43.0 21.6 %collective-permute-start.3 = (bf16[336,1536]{1,0:T(8,128)(2,1)S(1)}, bf16[336,1536]{1,0:T(8,128)(2,1)S(1)}, u32[]{:S(2)}, u32[]{:S(2)}) collective-permute-start(bf16[336,1536]{1,0:T(8,128)(2,1)S(1)} %pad_maximum_fusion.near_ref), channel_id=1, source_target_pairs={{0,16},{16,0},{1,17},{17,1},{2,18},{18,2},{3,19},{19,3},{4,20},{20... | collective-permute-start | bytes 3096584 | tf_op jit(solution)/shard_map/ppermute | solution.py:213
  44.9 14.4 %collective-permute-start.4 = (bf16[56,1536]{1,0:T(8,128)(2,1)S(1)}, bf16[56,1536]{1,0:T(8,128)(2,1)S(1)}, u32[]{:S(2)}, u32[]{:S(2)}) collective-permute-start(bf16[56,1536]{1,0:T(8,128)(2,1)S(1)} %slice.24), channel_id=1, source_target_pairs={{0,32},{32,64},{64,96},{96,0},{1,33},{33,65},{65,97},{97,1},{2,34}... | collective-permute-start | bytes 516104 | tf_op jit(solution)/shard_map/ppermute | solution.py:213
  48.3 12.7 %collective-permute-start.5 = (bf16[56,1536]{1,0:T(8,128)(2,1)S(1)}, bf16[56,1536]{1,0:T(8,128)(2,1)S(1)}, u32[]{:S(2)}, u32[]{:S(2)}) collective-permute-start(bf16[56,1536]{1,0:T(8,128)(2,1)S(1)} %slice.25), channel_id=1, source_target_pairs={{0,96},{32,0},{64,32},{96,64},{1,97},{33,1},{65,33},{97,65},{2,98}... | collective-permute-start | bytes 516104 | tf_op jit(solution)/shard_map/ppermute | solution.py:213
  52.9 24.7 %collective-permute-start = (bf16[4,704,128]{2,1,0:T(8,128)(2,1)S(1)}, bf16[4,704,128]{2,1,0:T(8,128)(2,1)S(1)}, u32[]{:S(2)}, u32[]{:S(2)}) collective-permute-start(bf16[4,704,128]{2,1,0:T(8,128)(2,1)S(1)} %bitcast.27), channel_id=1, source_target_pairs={{0,1},{1,0},{2,3},{3,2},{4,5},{5,4},{6,7},{7,6},{8,9},{9,8},{10,11... | collective-permute-start | bytes 2162696 | tf_op jit(solution)/shard_map/ppermute | solution.py:213
  61.1 3.5 %collective-permute-start.6 = (bf16[112,1536]{1,0:T(8,128)(2,1)S(1)}, bf16[112,1536]{1,0:T(8,128)(2,1)S(1)}, u32[]{:S(2)}, u32[]{:S(2)}) collective-permute-start(bf16[112,1536]{1,0:T(8,128)(2,1)S(1)} %constant_dynamic-update-slice_fusion.3.far_ref), channel_id=1, source_target_pairs={{0,16},{16,0},{1,17},{17,1},{2,18},{18,2},{3,19},{19,3},{4,20},{20... | collective-permute-start | bytes 1032200 | tf_op jit(solution)/shard_map/ppermute | solution.py:213
  119.3 39.9 %copy-start = (s32[128,1]{0,1:T(1,128)S(1)}, s32[128,1]{0,1:T(1,128)}, u32[]{:S(2)}) copy-start(s32[128,1]{0,1:T(1,128)} %param.9) | copy-start | bytes 1540
  119.4 39.9 %copy-start.1 = (f32[128,1]{0,1:T(1,128)S(1)}, f32[128,1]{0,1:T(1,128)}, u32[]{:S(2)}) copy-start(f32[128,1]{0,1:T(1,128)} %param.10) | copy-start | bytes 1540
  119.4 10.6 %collective-permute-start.7 = (bf16[4,48,1024]{2,1,0:T(8,128)(2,1)S(1)}, bf16[4,48,1024]{2,1,0:T(8,128)(2,1)S(1)}, u32[]{:S(2)}, u32[]{:S(2)}) collective-permute-start(bf16[4,48,1024]{2,1,0:T(8,128)(2,1)S(1)} %get-tuple-element.25), channel_id=1, source_target_pairs={{0,1},{1,0},{2,3},{3,2},{4,5},{5,4},{6,7},{7,6},{8,9},{9,8},{10,11... | collective-permute-start | bytes 1179656 | tf_op jit(solution)/shard_map/ppermute | solution.py:213
  121.3 19.4 %collective-permute-start.8 = (bf16[4,112,512]{2,1,0:T(8,128)(2,1)S(1)}, bf16[4,112,512]{2,1,0:T(8,128)(2,1)S(1)}, u32[]{:S(2)}, u32[]{:S(2)}) collective-permute-start(bf16[4,112,512]{2,1,0:T(8,128)(2,1)S(1)} %get-tuple-element.29), channel_id=1, source_target_pairs={{0,16},{16,0},{1,17},{17,1},{2,18},{18,2},{3,19},{19,3},{4,20},{20... | collective-permute-start | bytes 1376264 | tf_op jit(solution)/shard_map/ppermute | solution.py:213
  131.2 28.0 %all-to-all-start.3 = ((bf16[32,48,128]{2,1,0:T(8,128)(2,1)}), bf16[32,48,128]{2,1,0:T(8,128)(2,1)S(1)}, u32[]{:S(2)}, u32[]{:S(2)}) async-start(bf16[32,48,128]{2,1,0:T(8,128)(2,1)} %bitcast.4), calls=%async_computation.3 | async-start | bytes 786432 | tf_op jit(solution)/shard_map/all_to_all | solution.py:221
  140.8 10.7 %collective-permute-start.10 = (bf16[112,512]{1,0:T(8,128)(2,1)S(1)}, bf16[112,512]{1,0:T(8,128)(2,1)S(1)}, u32[]{:S(2)}, u32[]{:S(2)}) collective-permute-start(bf16[112,512]{1,0:T(8,128)(2,1)S(1)} %get-tuple-element.35), channel_id=1, source_target_pairs={{0,96},{32,0},{64,32},{96,64},{1,97},{33,1},{65,33},{97,65},{2,98}... | collective-permute-start | bytes 344072 | tf_op jit(solution)/shard_map/ppermute | solution.py:213
  142.8 14.0 %collective-permute-start.11 = (bf16[112,512]{1,0:T(8,128)(2,1)S(1)}, bf16[112,512]{1,0:T(8,128)(2,1)S(1)}, u32[]{:S(2)}, u32[]{:S(2)}) collective-permute-start(bf16[112,512]{1,0:T(8,128)(2,1)S(1)} %get-tuple-element.34), channel_id=1, source_target_pairs={{0,64},{32,96},{64,0},{96,32},{1,65},{33,97},{65,1},{97,33},{2,66}... | collective-permute-start | bytes 344072 | tf_op jit(solution)/shard_map/ppermute | solution.py:213
  148.8 9.7 %collective-permute-start.9 = (bf16[112,512]{1,0:T(8,128)(2,1)S(1)}, bf16[112,512]{1,0:T(8,128)(2,1)S(1)}, u32[]{:S(2)}, u32[]{:S(2)}) collective-permute-start(bf16[112,512]{1,0:T(8,128)(2,1)S(1)} %get-tuple-element.33), channel_id=1, source_target_pairs={{0,32},{32,64},{64,96},{96,0},{1,33},{33,65},{65,97},{97,1},{2,34}... | collective-permute-start | bytes 344072 | tf_op jit(solution)/shard_map/ppermute | solution.py:213

commit v11 on v10

--- a/solution.py
+++ b/solution.py
@@ -228,7 +228,6 @@
         [pltpu.VMEM((1, TOK), I32), pltpu.VMEM((1, TOK), F32), pltpu.VMEM((TOK, D), BF), pltpu.VMEM((TOK, D), BF),
          pltpu.SemaphoreType.DMA((4,))], [ANYWHERE] * 4, MOST_VMEM,
     )
-    gate_weight, sent = lax.optimization_barrier((gate_weight, sent))
     rows = exchange(sent.reshape(32, WIDE, TOK), PEERS).reshape(4, WIDER, TOK)
 
     cut = SHARD // 2
@@ -238,7 +237,7 @@
     near = jnp.concatenate([weights, z_before, z_after], axis=0)
     far = jnp.concatenate([z_low, z_high], axis=0)
     weights, = call(assemble_kernel, "assemble", [((PART, 3 * HALF), BF)],
-                    (near, hop(near, "c", 1), far, hop(far, "c", 1)), 10**6)
+                    (near, hop(near, "c", 1), far, hop(far, "c", 1)), 2 * 10**10)
 
     dense = pltpu.VMEM((4 * ROWS, PART), BF)
     part, g_rows = call(

time: 162 us -> 160 us (0.988)
  waiting for transfers between devices: 48.8 us -> 38.8 us
  starting transfers between devices: 61.6 us -> 67.2 us
  local copies, waits for them, and re-layouts: 0.11 us -> 2.78 us
    ppermute x12, waiting for transfers between devices: 48.8 us -> 38.8 us  [hop(): return lax.ppermute(a, axis, [(i, (i + shift) % n) for i in range(n)])]
    ppermute x12, starting transfers between devices: 41.9 us -> 47 us  [hop(): return lax.ppermute(a, axis, [(i, (i + shift) % n) for i in range(n)])]
    unnamed x13 -> x7, local copies, waits for them, and re-layouts: 0.06 us -> 1.84 us
  transfers between devices with their start and end apart: 14 -> 14, of which waited for: 9 -> 7; matrix products, arithmetic and copies ran while one was open for 1% -> 1% of each run, Pallas kernels for 1% -> 3%
where the time goes in v11:
time: 160 us; the launch traced here: 159 us
  starting transfers between devices  67.2 us (42%)
  waiting for transfers between devices  38.8 us (24%)
  blocking collectives  37.1 us (23%)
  Pallas kernels  11.5 us (7%)
  local copies, waits for them, and re-layouts  2.78 us (2%)
    ppermute x12, starting transfers between devices, hop(): return lax.ppermute(a, axis, [(i, (i + shift) % n) for i in range(n)])  47 us
    ppermute x12, waiting for transfers between devices, hop(): return lax.ppermute(a, axis, [(i, (i + shift) % n) for i in range(n)])  38.8 us
    all_to_all x2, blocking collectives, exchange(): return lax.all_to_all(a, axes, split_axis=0, concat_axis=0, tiled=True)  37.1 us
    all_to_all x2, starting transfers between devices, exchange(): return lax.all_to_all(a, axes, split_axis=0, concat_axis=0, tiled=True)  20.2 us
    pallas_call x7, Pallas kernels, call(): pl.pallas_call(body, in_specs=specs or [VMEM] * len(operands), out_specs=...  11.5 us
  transfers between devices with their start and end apart: 14, of which 7 were waited for; matrix products, arithmetic and copies ran while one was open for 1% of the time, Pallas kernels for 3%

profile of v11, /device:TPU:6, one launch (start us, length us, event | category | flops | bytes accessed | tf_op | source)
XLA Modules:
  0.0 159.2 jit_solution(7522288257525763838)
XLA Ops:
  0.6 0.9 constant_dynamic-update-slice_fusion.2
  1.5 0.9 constant_dynamic-update-slice_fusion.1
  2.4 0.9 constant_dynamic-update-slice_fusion
  3.4 6.1 %collective-permute-start.1 = (bf16[112,1536]{1,0:T(8,128)(2,1)S(1)}, bf16[112,1536]{1,0:T(8,128)(2,1)S(1)}, u32[]{:S(2)}, u32[]{:S(2)}) collective-permute-start(bf16[112,1536]{1,0:T(8,128)(2,1)S(1)} %constant_dynamic-update-slice_fusion), channel_id=1, source_target_pairs={{0,32},{32,64},{64,96},{96,0},{1,33},{33,65},{65,97},{97,1},{2,34}... | collective-permute-start | bytes 1032200 | tf_op jit(solution)/shard_map/ppermute | solution.py:213
  9.4 6.8 %collective-permute-start.2 = (bf16[112,1536]{1,0:T(8,128)(2,1)S(1)}, bf16[112,1536]{1,0:T(8,128)(2,1)S(1)}, u32[]{:S(2)}, u32[]{:S(2)}) collective-permute-start(bf16[112,1536]{1,0:T(8,128)(2,1)S(1)} %constant_dynamic-update-slice_fusion), channel_id=1, source_target_pairs={{0,96},{32,0},{64,32},{96,64},{1,97},{33,1},{65,33},{97,65},{2,98}... | collective-permute-start | bytes 1032200 | tf_op jit(solution)/shard_map/ppermute | solution.py:213
  16.2 3.7 %dispatch.1 = bf16[4,8,88,128]{3,2,1,0:T(8,128)(2,1)} custom-call(s32[1,128]{1,0:T(1,128)} %bitcast.30, f32[1,128]{1,0:T(1,128)} %bitcast.32, bf16[128,3584]{1,0:T(8,128)(2,1)} %x_hbm.1, bf16[128,3584]{1,0:T(8,128)(2,1)} %g_hbm.1), custom_call_target="tpu_custom_call" | custom-call | flops 1000000000 | bytes 4000000 | tf_op jit(solution)/shard_map/dispatch/pallas_call | solution.py:62
  20.0 10.2 %all-to-all-start = ((bf16[32,88,128]{2,1,0:T(8,128)(2,1)}), bf16[32,88,128]{2,1,0:T(8,128)(2,1)S(1)}, u32[]{:S(2)}, u32[]{:S(2)}) async-start(bf16[32,88,128]{2,1,0:T(8,128)(2,1)} %bitcast.34), calls=%async_computation | async-start | bytes 1441792 | tf_op jit(solution)/shard_map/all_to_all | solution.py:221
  30.2 0.0 collective-permute-done.1
  30.2 1.7 %collective-permute-done.2 = bf16[112,1536]{1,0:T(8,128)(2,1)S(1)} collective-permute-done((bf16[112,1536]{1,0:T(8,128)(2,1)S(1)}, bf16[112,1536]{1,0:T(8,128)(2,1)S(1)}, u32[]{:S(2)}, u32[]{:S(2)}) %collective-permute-start.2) | collective-permute-done | bytes 344096 | tf_op jit(solution)/shard_map/ppermute | solution.py:213
  32.0 0.1 pad_maximum_fusion.near_ref
  32.1 1.9 %collective-permute-start.3 = (bf16[336,1536]{1,0:T(8,128)(2,1)S(1)}, bf16[336,1536]{1,0:T(8,128)(2,1)S(1)}, u32[]{:S(2)}, u32[]{:S(2)}) collective-permute-start(bf16[336,1536]{1,0:T(8,128)(2,1)S(1)} %pad_maximum_fusion.near_ref), channel_id=1, source_target_pairs={{0,16},{16,0},{1,17},{17,1},{2,18},{18,2},{3,19},{19,3},{4,20},{20... | collective-permute-start | bytes 3096584 | tf_op jit(solution)/shard_map/ppermute | solution.py:213
  34.0 3.4 %collective-permute-start.4 = (bf16[56,1536]{1,0:T(8,128)(2,1)S(1)}, bf16[56,1536]{1,0:T(8,128)(2,1)S(1)}, u32[]{:S(2)}, u32[]{:S(2)}) collective-permute-start(bf16[56,1536]{1,0:T(8,128)(2,1)S(1)} %slice.24), channel_id=1, source_target_pairs={{0,32},{32,64},{64,96},{96,0},{1,33},{33,65},{65,97},{97,1},{2,34}... | collective-permute-start | bytes 516104 | tf_op jit(solution)/shard_map/ppermute | solution.py:213
  37.4 4.6 %collective-permute-start.5 = (bf16[56,1536]{1,0:T(8,128)(2,1)S(1)}, bf16[56,1536]{1,0:T(8,128)(2,1)S(1)}, u32[]{:S(2)}, u32[]{:S(2)}) collective-permute-start(bf16[56,1536]{1,0:T(8,128)(2,1)S(1)} %slice.25), channel_id=1, source_target_pairs={{0,96},{32,0},{64,32},{96,64},{1,97},{33,1},{65,33},{97,65},{2,98}... | collective-permute-start | bytes 516104 | tf_op jit(solution)/shard_map/ppermute | solution.py:213
  42.0 6.4 %collective-permute-done.4 = bf16[56,1536]{1,0:T(8,128)(2,1)S(1)} collective-permute-done((bf16[56,1536]{1,0:T(8,128)(2,1)S(1)}, bf16[56,1536]{1,0:T(8,128)(2,1)S(1)}, u32[]{:S(2)}, u32[]{:S(2)}) %collective-permute-start.4) | collective-permute-done | bytes 172064 | tf_op jit(solution)/shard_map/ppermute | solution.py:213
  48.4 1.7 %collective-permute-done.5 = bf16[56,1536]{1,0:T(8,128)(2,1)S(1)} collective-permute-done((bf16[56,1536]{1,0:T(8,128)(2,1)S(1)}, bf16[56,1536]{1,0:T(8,128)(2,1)S(1)}, u32[]{:S(2)}, u32[]{:S(2)}) %collective-permute-start.5) | collective-permute-done | bytes 172064 | tf_op jit(solution)/shard_map/ppermute | solution.py:213
  50.1 1.9 %collective-permute-start.6 = (bf16[112,1536]{1,0:T(8,128)(2,1)S(1)}, bf16[112,1536]{1,0:T(8,128)(2,1)S(1)}, u32[]{:S(2)}, u32[]{:S(2)}) collective-permute-start(bf16[112,1536]{1,0:T(8,128)(2,1)S(1)} %constant_dynamic-update-slice_fusion.3.far_ref), channel_id=1, source_target_pairs={{0,16},{16,0},{1,17},{17,1},{2,18},{18,2},{3,19},{19,3},{4,20},{20... | collective-permute-start | bytes 1032200 | tf_op jit(solution)/shard_map/ppermute | solution.py:213
  52.1 0.0 all-to-all-done
  52.1 4.7 %collective-permute-start = (bf16[4,704,128]{2,1,0:T(8,128)(2,1)S(1)}, bf16[4,704,128]{2,1,0:T(8,128)(2,1)S(1)}, u32[]{:S(2)}, u32[]{:S(2)}) collective-permute-start(bf16[4,704,128]{2,1,0:T(8,128)(2,1)S(1)} %bitcast.27), channel_id=1, source_target_pairs={{0,1},{1,0},{2,3},{3,2},{4,5},{5,4},{6,7},{7,6},{8,9},{9,8},{10,11... | collective-permute-start | bytes 2162696 | tf_op jit(solution)/shard_map/ppermute | solution.py:213
  56.8 0.0 collective-permute-done.6.far_other_ref
  56.8 0.0 collective-permute-done.3.near_other_ref
  56.8 0.2 assemble.1.weight_ref
  57.1 16.6 %collective-permute-done.other_ref = bf16[4,704,128]{2,1,0:T(8,128)(2,1)S(1)} collective-permute-done((bf16[4,704,128]{2,1,0:T(8,128)(2,1)S(1)}, bf16[4,704,128]{2,1,0:T(8,128)(2,1)S(1)}, u32[]{:S(2)}, u32[]{:S(2)}) %collective-permute-start) | collective-permute-done | bytes 720928 | tf_op jit(solution)/shard_map/ppermute | solution.py:213
  73.6 2.5 %before.1 = (bf16[4,96,1536]{2,1,0:T(8,128)(2,1)S(1)}, bf16[384,896]{1,0:T(8,128)(2,1)S(1)}) custom-call(bf16[4,704,128]{2,1,0:T(8,128)(2,1)S(1)} %bitcast.28, bf16[4,704,128]{2,1,0:T(8,128)(2,1)S(1)} %collective-permute-done.other_ref, bf16[896,1536]{1,0:T(8,128)(2,1)S(1)} %assemble.1.weight_ref), custom_call_target="tpu_custom_call" | custom-call | flops 2000000000 | bytes 4000000 | tf_op jit(solution)/shard_map/before/pallas_call | solution.py:62
  76.1 19.1 %all_to_all.20.part_ref = bf16[4,96,1536]{2,1,0:T(8,128)(2,1)S(1)} all-to-all(bf16[4,96,1536]{2,1,0:T(8,128)(2,1)S(1)} %get-tuple-element.16), channel_id=1, replica_groups=mesh['x'=4,'zh'=4,'c'=2,'y'=8,'zl'=2] {'x'}, dimensions={0} | all-to-all | bytes 2359296 | tf_op jit(solution)/shard_map/all_to_all | solution.py:221
  95.2 0.3 middle.1
  95.6 18.0 %all_to_all.21.mid_ref = bf16[4,96,1536]{2,1,0:T(8,128)(2,1)S(1)} all-to-all(bf16[4,96,1536]{2,1,0:T(8,128)(2,1)S(1)} %get-tuple-element.17), channel_id=1, replica_groups=mesh['x'=4,'zh'=4,'c'=2,'y'=8,'zl'=2] {'x'}, dimensions={0} | all-to-all | bytes 2359296 | tf_op jit(solution)/shard_map/all_to_all | solution.py:221
  113.6 1.7 %after.1 = (bf16[4,48,1024]{2,1,0:T(8,128)(2,1)S(1)}, bf16[4,48,1024]{2,1,0:T(8,128)(2,1)S(1)}, bf16[112,512]{1,0:T(8,128)(2,1)S(1)}, bf16[112,512]{1,0:T(8,128)...) custom-call(bf16[4,96,1536]{2,1,0:T(8,128)(2,1)S(1)} %all_to_all.21.mid_ref,, ...), custom_call_target="tpu_custom_call" | custom-call | flops 1400000000 | bytes 4000000 | tf_op jit(solution)/shard_map/after/pallas_call | solution.py:62
  115.3 0.0 copy-start
  115.4 0.0 copy-start.1
  115.4 3.3 %collective-permute-start.7 = (bf16[4,48,1024]{2,1,0:T(8,128)(2,1)S(1)}, bf16[4,48,1024]{2,1,0:T(8,128)(2,1)S(1)}, u32[]{:S(2)}, u32[]{:S(2)}) collective-permute-start(bf16[4,48,1024]{2,1,0:T(8,128)(2,1)S(1)} %get-tuple-element.21), channel_id=1, source_target_pairs={{0,1},{1,0},{2,3},{3,2},{4,5},{5,4},{6,7},{7,6},{8,9},{9,8},{10,11... | collective-permute-start | bytes 1179656 | tf_op jit(solution)/shard_map/ppermute | solution.py:213
  118.7 1.9 %collective-permute-start.8 = (bf16[4,112,512]{2,1,0:T(8,128)(2,1)S(1)}, bf16[4,112,512]{2,1,0:T(8,128)(2,1)S(1)}, u32[]{:S(2)}, u32[]{:S(2)}) collective-permute-start(bf16[4,112,512]{2,1,0:T(8,128)(2,1)S(1)} %get-tuple-element.25), channel_id=1, source_target_pairs={{0,16},{16,0},{1,17},{17,1},{2,18},{18,2},{3,19},{19,3},{4,20},{20... | collective-permute-start | bytes 1376264 | tf_op jit(solution)/shard_map/ppermute | solution.py:213
  120.6 5.4 %collective-permute-done.7.got_ref = bf16[4,48,1024]{2,1,0:T(8,128)(2,1)S(1)} collective-permute-done((bf16[4,48,1024]{2,1,0:T(8,128)(2,1)S(1)}, bf16[4,48,1024]{2,1,0:T(8,128)(2,1)S(1)}, u32[]{:S(2)}, u32[]{:S(2)}) %collective-permute-start.7) | collective-permute-done | bytes 393248 | tf_op jit(solution)/shard_map/ppermute | solution.py:213
  126.0 1.2 combine.1
  127.2 10.0 %all-to-all-start.3 = ((bf16[32,48,128]{2,1,0:T(8,128)(2,1)}), bf16[32,48,128]{2,1,0:T(8,128)(2,1)S(1)}, u32[]{:S(2)}, u32[]{:S(2)}) async-start(bf16[32,48,128]{2,1,0:T(8,128)(2,1)} %bitcast.4), calls=%async_computation.3 | async-start | bytes 786432 | tf_op jit(solution)/shard_map/all_to_all | solution.py:221
  137.2 0.0 collective-permute-done.8
  137.2 0.1 fusion.3
  137.3 4.4 %collective-permute-start.10 = (bf16[112,512]{1,0:T(8,128)(2,1)S(1)}, bf16[112,512]{1,0:T(8,128)(2,1)S(1)}, u32[]{:S(2)}, u32[]{:S(2)}) collective-permute-start(bf16[112,512]{1,0:T(8,128)(2,1)S(1)} %get-tuple-element.31), channel_id=1, source_target_pairs={{0,96},{32,0},{64,32},{96,64},{1,97},{33,1},{65,33},{97,65},{2,98}... | collective-permute-start | bytes 344072 | tf_op jit(solution)/shard_map/ppermute | solution.py:213
  141.7 6.1 %collective-permute-start.11 = (bf16[112,512]{1,0:T(8,128)(2,1)S(1)}, bf16[112,512]{1,0:T(8,128)(2,1)S(1)}, u32[]{:S(2)}, u32[]{:S(2)}) collective-permute-start(bf16[112,512]{1,0:T(8,128)(2,1)S(1)} %get-tuple-element.30), channel_id=1, source_target_pairs={{0,64},{32,96},{64,0},{96,32},{1,65},{33,97},{65,1},{97,33},{2,66}... | collective-permute-start | bytes 344072 | tf_op jit(solution)/shard_map/ppermute | solution.py:213
  147.8 1.9 %collective-permute-start.9 = (bf16[112,512]{1,0:T(8,128)(2,1)S(1)}, bf16[112,512]{1,0:T(8,128)(2,1)S(1)}, u32[]{:S(2)}, u32[]{:S(2)}) collective-permute-start(bf16[112,512]{1,0:T(8,128)(2,1)S(1)} %get-tuple-element.29), channel_id=1, source_target_pairs={{0,32},{32,64},{64,96},{96,0},{1,33},{33,65},{65,97},{97,1},{2,34}... | collective-permute-start | bytes 344072 | tf_op jit(solution)/shard_map/ppermute | solution.py:213
  149.7 0.0 collective-permute-done.10
  149.7 3.1 %collective-permute-done.11 = bf16[112,512]{1,0:T(8,128)(2,1)S(1)} collective-permute-done((bf16[112,512]{1,0:T(8,128)(2,1)S(1)}, bf16[112,512]{1,0:T(8,128)(2,1)S(1)}, u32[]{:S(2)}, u32[]{:S(2)}) %collective-permute-start.11) | collective-permute-done | bytes 114720 | tf_op jit(solution)/shard_map/ppermute | solution.py:213
  152.9 3.8 %collective-permute-done.9 = bf16[112,512]{1,0:T(8,128)(2,1)S(1)} collective-permute-done((bf16[112,512]{1,0:T(8,128)(2,1)S(1)}, bf16[112,512]{1,0:T(8,128)(2,1)S(1)}, u32[]{:S(2)}, u32[]{:S(2)}) %collective-permute-start.9) | collective-permute-done | bytes 114720 | tf_op jit(solution)/shard_map/ppermute | solution.py:213
  156.7 0.7 add_convert_fusion
  157.4 0.0 all-to-all-done.3
  157.4 0.0 copy-done
  157.4 0.0 copy-done.1
  157.4 1.8 %finish.1 = (bf16[128,3584]{1,0:T(8,128)(2,1)}, f32[1,128]{1,0:T(1,128)}) custom-call(s32[1,128]{1,0:T(1,128)S(1)} %bitcast.31, f32[1,128]{1,0:T(1,128)S(1)} %bitcast.33, bf16[4,384,128]{2,1,0:T(8,128)(2,1)S(1)} %bitcast.29), custom_call_target="tpu_custom_call" | custom-call | flops 400000000 | bytes 4000000 | tf_op jit(solution)/shard_map/finish/pallas_call | solution.py:62
  (4 shorter events, 0.1 us)
Async XLA Ops:
  3.4 26.9 %collective-permute-start.1 = (bf16[112,1536]{1,0:T(8,128)(2,1)S(1)}, bf16[112,1536]{1,0:T(8,128)(2,1)S(1)}, u32[]{:S(2)}, u32[]{:S(2)}) collective-permute-start(bf16[112,1536]{1,0:T(8,128)(2,1)S(1)} %constant_dynamic-update-slice_fusion), channel_id=1, source_target_pairs={{0,32},{32,64},{64,96},{96,0},{1,33},{33,65},{65,97},{97,1},{2,34}... | collective-permute-start | bytes 1032200 | tf_op jit(solution)/shard_map/ppermute | solution.py:213
  9.4 22.5 %collective-permute-start.2 = (bf16[112,1536]{1,0:T(8,128)(2,1)S(1)}, bf16[112,1536]{1,0:T(8,128)(2,1)S(1)}, u32[]{:S(2)}, u32[]{:S(2)}) collective-permute-start(bf16[112,1536]{1,0:T(8,128)(2,1)S(1)} %constant_dynamic-update-slice_fusion), channel_id=1, source_target_pairs={{0,96},{32,0},{64,32},{96,64},{1,97},{33,1},{65,33},{97,65},{2,98}... | collective-permute-start | bytes 1032200 | tf_op jit(solution)/shard_map/ppermute | solution.py:213
  20.0 32.1 %all-to-all-start = ((bf16[32,88,128]{2,1,0:T(8,128)(2,1)}), bf16[32,88,128]{2,1,0:T(8,128)(2,1)S(1)}, u32[]{:S(2)}, u32[]{:S(2)}) async-start(bf16[32,88,128]{2,1,0:T(8,128)(2,1)} %bitcast.34), calls=%async_computation | async-start | bytes 1441792 | tf_op jit(solution)/shard_map/all_to_all | solution.py:221
  32.1 24.8 %collective-permute-start.3 = (bf16[336,1536]{1,0:T(8,128)(2,1)S(1)}, bf16[336,1536]{1,0:T(8,128)(2,1)S(1)}, u32[]{:S(2)}, u32[]{:S(2)}) collective-permute-start(bf16[336,1536]{1,0:T(8,128)(2,1)S(1)} %pad_maximum_fusion.near_ref), channel_id=1, source_target_pairs={{0,16},{16,0},{1,17},{17,1},{2,18},{18,2},{3,19},{19,3},{4,20},{20... | collective-permute-start | bytes 3096584 | tf_op jit(solution)/shard_map/ppermute | solution.py:213
  34.0 14.4 %collective-permute-start.4 = (bf16[56,1536]{1,0:T(8,128)(2,1)S(1)}, bf16[56,1536]{1,0:T(8,128)(2,1)S(1)}, u32[]{:S(2)}, u32[]{:S(2)}) collective-permute-start(bf16[56,1536]{1,0:T(8,128)(2,1)S(1)} %slice.24), channel_id=1, source_target_pairs={{0,32},{32,64},{64,96},{96,0},{1,33},{33,65},{65,97},{97,1},{2,34}... | collective-permute-start | bytes 516104 | tf_op jit(solution)/shard_map/ppermute | solution.py:213
  37.4 12.7 %collective-permute-start.5 = (bf16[56,1536]{1,0:T(8,128)(2,1)S(1)}, bf16[56,1536]{1,0:T(8,128)(2,1)S(1)}, u32[]{:S(2)}, u32[]{:S(2)}) collective-permute-start(bf16[56,1536]{1,0:T(8,128)(2,1)S(1)} %slice.25), channel_id=1, source_target_pairs={{0,96},{32,0},{64,32},{96,64},{1,97},{33,1},{65,33},{97,65},{2,98}... | collective-permute-start | bytes 516104 | tf_op jit(solution)/shard_map/ppermute | solution.py:213
  50.1 6.7 %collective-permute-start.6 = (bf16[112,1536]{1,0:T(8,128)(2,1)S(1)}, bf16[112,1536]{1,0:T(8,128)(2,1)S(1)}, u32[]{:S(2)}, u32[]{:S(2)}) collective-permute-start(bf16[112,1536]{1,0:T(8,128)(2,1)S(1)} %constant_dynamic-update-slice_fusion.3.far_ref), channel_id=1, source_target_pairs={{0,16},{16,0},{1,17},{17,1},{2,18},{18,2},{3,19},{19,3},{4,20},{20... | collective-permute-start | bytes 1032200 | tf_op jit(solution)/shard_map/ppermute | solution.py:213
  52.1 21.5 %collective-permute-start = (bf16[4,704,128]{2,1,0:T(8,128)(2,1)S(1)}, bf16[4,704,128]{2,1,0:T(8,128)(2,1)S(1)}, u32[]{:S(2)}, u32[]{:S(2)}) collective-permute-start(bf16[4,704,128]{2,1,0:T(8,128)(2,1)S(1)} %bitcast.27), channel_id=1, source_target_pairs={{0,1},{1,0},{2,3},{3,2},{4,5},{5,4},{6,7},{7,6},{8,9},{9,8},{10,11... | collective-permute-start | bytes 2162696 | tf_op jit(solution)/shard_map/ppermute | solution.py:213
  115.3 42.1 %copy-start = (s32[128,1]{0,1:T(1,128)S(1)}, s32[128,1]{0,1:T(1,128)}, u32[]{:S(2)}) copy-start(s32[128,1]{0,1:T(1,128)} %param.9) | copy-start | bytes 1540
  115.4 42.1 %copy-start.1 = (f32[128,1]{0,1:T(1,128)S(1)}, f32[128,1]{0,1:T(1,128)}, u32[]{:S(2)}) copy-start(f32[128,1]{0,1:T(1,128)} %param.10) | copy-start | bytes 1540
  115.4 10.7 %collective-permute-start.7 = (bf16[4,48,1024]{2,1,0:T(8,128)(2,1)S(1)}, bf16[4,48,1024]{2,1,0:T(8,128)(2,1)S(1)}, u32[]{:S(2)}, u32[]{:S(2)}) collective-permute-start(bf16[4,48,1024]{2,1,0:T(8,128)(2,1)S(1)} %get-tuple-element.21), channel_id=1, source_target_pairs={{0,1},{1,0},{2,3},{3,2},{4,5},{5,4},{6,7},{7,6},{8,9},{9,8},{10,11... | collective-permute-start | bytes 1179656 | tf_op jit(solution)/shard_map/ppermute | solution.py:213
  118.7 18.5 %collective-permute-start.8 = (bf16[4,112,512]{2,1,0:T(8,128)(2,1)S(1)}, bf16[4,112,512]{2,1,0:T(8,128)(2,1)S(1)}, u32[]{:S(2)}, u32[]{:S(2)}) collective-permute-start(bf16[4,112,512]{2,1,0:T(8,128)(2,1)S(1)} %get-tuple-element.25), channel_id=1, source_target_pairs={{0,16},{16,0},{1,17},{17,1},{2,18},{18,2},{3,19},{19,3},{4,20},{20... | collective-permute-start | bytes 1376264 | tf_op jit(solution)/shard_map/ppermute | solution.py:213
  127.2 30.2 %all-to-all-start.3 = ((bf16[32,48,128]{2,1,0:T(8,128)(2,1)}), bf16[32,48,128]{2,1,0:T(8,128)(2,1)S(1)}, u32[]{:S(2)}, u32[]{:S(2)}) async-start(bf16[32,48,128]{2,1,0:T(8,128)(2,1)} %bitcast.4), calls=%async_computation.3 | async-start | bytes 786432 | tf_op jit(solution)/shard_map/all_to_all | solution.py:221
  137.3 12.4 %collective-permute-start.10 = (bf16[112,512]{1,0:T(8,128)(2,1)S(1)}, bf16[112,512]{1,0:T(8,128)(2,1)S(1)}, u32[]{:S(2)}, u32[]{:S(2)}) collective-permute-start(bf16[112,512]{1,0:T(8,128)(2,1)S(1)} %get-tuple-element.31), channel_id=1, source_target_pairs={{0,96},{32,0},{64,32},{96,64},{1,97},{33,1},{65,33},{97,65},{2,98}... | collective-permute-start | bytes 344072 | tf_op jit(solution)/shard_map/ppermute | solution.py:213
  141.7 11.2 %collective-permute-start.11 = (bf16[112,512]{1,0:T(8,128)(2,1)S(1)}, bf16[112,512]{1,0:T(8,128)(2,1)S(1)}, u32[]{:S(2)}, u32[]{:S(2)}) collective-permute-start(bf16[112,512]{1,0:T(8,128)(2,1)S(1)} %get-tuple-element.30), channel_id=1, source_target_pairs={{0,64},{32,96},{64,0},{96,32},{1,65},{33,97},{65,1},{97,33},{2,66}... | collective-permute-start | bytes 344072 | tf_op jit(solution)/shard_map/ppermute | solution.py:213
  147.8 8.9 %collective-permute-start.9 = (bf16[112,512]{1,0:T(8,128)(2,1)S(1)}, bf16[112,512]{1,0:T(8,128)(2,1)S(1)}, u32[]{:S(2)}, u32[]{:S(2)}) collective-permute-start(bf16[112,512]{1,0:T(8,128)(2,1)S(1)} %get-tuple-element.29), channel_id=1, source_target_pairs={{0,32},{32,64},{64,96},{96,0},{1,33},{33,65},{65,97},{97,1},{2,34}... | collective-permute-start | bytes 344072 | tf_op jit(solution)/shard_map/ppermute | solution.py:213

commit v12 on v9

--- a/solution.py
+++ b/solution.py
@@ -103,17 +103,37 @@
             out_ref[2 * i + j] = one
 
 
-def before_kernel(mine_ref, other_ref, weight_ref, part_ref, g_ref, x_scr):
-    zl = lax.axis_index("zl")
+def stack_kernel(a_ref, b_ref, c_ref, out_ref):
+    for i, ref in enumerate((a_ref, b_ref, c_ref)):
+        out_ref[:, i * HALF:(i + 1) * HALF] = ref[...]
+
+
+def near_kernel(own_ref, before_ref, after_ref, out_ref, before_out):
+    for i, ref in enumerate((own_ref, before_ref, after_ref)):
+        out_ref[i * SHARD:(i + 1) * SHARD] = ref[...]
+    before_out[...] = before_ref[...]
+
+
+def assemble_kernel(near_ref, near_other_ref, far_ref, far_other_ref, out_ref, pick_ref):
     shape = (7, 2, SLAB, WIDER)
     j = iota(shape, 2)
     source = sixth(j)
     place = source * WIDE + iota(shape, 0) * 12 + iota(shape, 1) * CAP + (j - CAP * source)
-    pick = onehot(iota(shape, 3) == place).reshape(14 * SLAB, WIDER)
+    pick_ref[...] = onehot(iota(shape, 3) == place).reshape(14 * SLAB, WIDER)
+    zi, ci = lax.axis_index("zh"), lax.axis_index("c")
+    for core, near, far in ((ci, near_ref, far_ref), (1 - ci, near_other_ref, far_other_ref)):
+        for i, shift in enumerate((0, 3, 1, 2)):
+            block = lax.rem(zi + jnp.where(core == 0, shift, 4 - shift), 4)
+            at = pl.multiple_of((2 * block + core) * SHARD, 16)
+            out_ref[pl.ds(at, SHARD)] = far[...] if shift == 2 else near[i * SHARD:(i + 1) * SHARD]
+
+
+def before_kernel(mine_ref, other_ref, weight_ref, pick_ref, part_ref, g_ref, x_scr):
+    zl = lax.axis_index("zl")
     for ref, z in ((mine_ref, zl), (other_ref, 1 - zl)):
         for i in range(2):
             both = jnp.concatenate([ref[2 * i], ref[2 * i + 1]], axis=1)
-            moved = jnp.dot(pick, both, preferred_element_type=F32).astype(BF)
+            moved = jnp.dot(pick_ref[...], both, preferred_element_type=F32).astype(BF)
             for k in range(2):
                 rows = pl.ds(pl.multiple_of((2 * (2 * i + k) + z) * SLAB, 16), SLAB)
                 for q in range(7):
@@ -205,6 +225,14 @@
     return lax.ppermute(a, axis, [(i, (i + shift) % n) for i in range(n)])
 
 
+def turn(a, axis, shift):
+    n = lax.axis_size(axis)
+    pairs = []
+    for i in range(n):
+        pairs += [(2 * i, 2 * ((i + shift) % n)), (2 * i + 1, 2 * ((i - shift) % n) + 1)]
+    return lax.ppermute(a, (axis, "c"), pairs)
+
+
 def add(*terms):
     return sum(a.astype(F32) for a in terms).astype(BF)
 
@@ -215,19 +243,26 @@
 
 def per_device(tokens, grad_out, routing, route_weight, gate_weight, up_weight, down_weight):
     ids, share = routing.reshape(1, TOK), route_weight.reshape(1, TOK)
-    weights = jnp.concatenate([gate_weight, up_weight, down_weight], axis=1)
-    weights = lax.all_gather(weights, ("zh", "c"), axis=0, tiled=True)
-
+    weights, = call(stack_kernel, "stack", [((SHARD, 3 * HALF), BF)], (gate_weight, up_weight, down_weight), 10**6)
     sent, = call(
         dispatch_kernel, "dispatch", [((4, EXPERTS, WIDE, TOK), BF)], (ids, share, tokens, grad_out), 10**9,
         [pltpu.VMEM((1, TOK), I32), pltpu.VMEM((1, TOK), F32), pltpu.VMEM((TOK, D), BF), pltpu.VMEM((TOK, D), BF),
          pltpu.SemaphoreType.DMA((4,))], [ANYWHERE] * 4, MOST_VMEM,
     )
     rows = exchange(sent.reshape(32, WIDE, TOK), PEERS).reshape(4, WIDER, TOK)
+
+    z_before, z_after = turn(weights, "zh", 1), turn(weights, "zh", -1)
+    near, passed = call(near_kernel, "near", [((3 * SHARD, 3 * HALF), BF), ((SHARD, 3 * HALF), BF)],
+                        (weights, z_before, z_after), 4 * 10**9)
+    far = turn(passed, "zh", 1)
+    rows_other = hop(rows, "zl", 1)
+    weights, pick = call(assemble_kernel, "assemble", [((PART, 3 * HALF), BF), ((14 * SLAB, WIDER), BF)],
+                    (near, hop(near, "c", 1), far, hop(far, "c", 1)), 4 * 10**9)
+
     dense = pltpu.VMEM((4 * ROWS, PART), BF)
     part, g_rows = call(
         before_kernel, "before", [((4, ROWS, 3 * HALF), BF), ((4 * ROWS, PART), BF)],
-        (rows, hop(rows, "zl", 1), weights), 2 * 10**9, [dense],
+        (rows, rows_other, weights, pick), 2 * 10**9, [dense],
     )
     mid, line = call(middle_kernel, "middle", [((4, ROWS, 3 * HALF), BF), ((ROWS, TOK), BF)],
                      (exchange(part, "x"),), 10**7)

time: 166 us -> 148 us (0.89)
  blocking collectives: 65.8 us -> 28.6 us
  starting transfers between devices: 35 us -> 67.7 us
  between operations: 14.1 us -> 0.85 us
  other arithmetic: 2.61 us -> 0.82 us
    all_to_all x3 -> x2, blocking collectives: 65.8 us -> 28.6 us  [exchange(): return lax.all_to_all(a, axes, split_axis=0, concat_axis=0, tiled=True)]
    ppermute x0 -> x3, starting transfers between devices: none -> 15.3 us  [turn(): return lax.ppermute(a, (axis, 'c'), pairs)]
    all_to_all x1 -> x2, waiting for transfers between devices: 0.01 us -> 14.9 us  [exchange(): return lax.all_to_all(a, axes, split_axis=0, concat_axis=0, tiled=True)]
    all_to_all x1 -> x2, starting transfers between devices: 11.3 us -> 26 us  [exchange(): return lax.all_to_all(a, axes, split_axis=0, concat_axis=0, tiled=True)]
    ppermute x6 -> x8, waiting for transfers between devices: 34.2 us -> 20.3 us  [hop(): return lax.ppermute(a, axis, [(i, (i + shift) % n) for i in range(n)])]
    ppermute x6 -> x8, starting transfers between devices: 23.7 us -> 26.4 us  [hop(): return lax.ppermute(a, axis, [(i, (i + shift) % n) for i in range(n)])]
    concatenate x1 -> x0, other arithmetic: 1.79 us -> none  [per_device(): weights = jnp.concatenate([gate_weight, up_weight, down_weight], axis=1)]
    pallas_call x6 -> x9, Pallas kernels: 11.3 us -> 11.8 us  [call(): pl.pallas_call(body, in_specs=specs or [VMEM] * len(operands), out_specs=...]
  transfers between devices with their start and end apart: 8 -> 13, of which waited for: 4 -> 6; matrix products, arithmetic and copies ran while one was open for 0% -> 1% of each run, Pallas kernels for 3% -> 4%
where the time goes in v12:
time: 148 us
  starting transfers between devices  67.7 us (46%)
  waiting for transfers between devices  35.2 us (24%)
  blocking collectives  28.6 us (19%)
  Pallas kernels  11.8 us (8%)
  local copies, waits for them, and re-layouts  2.69 us (2%)
    all_to_all x2, blocking collectives, exchange(): return lax.all_to_all(a, axes, split_axis=0, concat_axis=0, tiled=True)  28.6 us
    ppermute x8, starting transfers between devices, hop(): return lax.ppermute(a, axis, [(i, (i + shift) % n) for i in range(n)])  26.4 us
    all_to_all x2, starting transfers between devices, exchange(): return lax.all_to_all(a, axes, split_axis=0, concat_axis=0, tiled=True)  26 us
    ppermute x8, waiting for transfers between devices, hop(): return lax.ppermute(a, axis, [(i, (i + shift) % n) for i in range(n)])  20.3 us
    ppermute x3, starting transfers between devices, turn(): return lax.ppermute(a, (axis, 'c'), pairs)  15.3 us
    all_to_all x2, waiting for transfers between devices, exchange(): return lax.all_to_all(a, axes, split_axis=0, concat_axis=0, tiled=True)  14.9 us
    pallas_call x9, Pallas kernels, call(): pl.pallas_call(body, in_specs=specs or [VMEM] * len(operands), out_specs=...  11.8 us
  transfers between devices with their start and end apart: 13, of which 6 were waited for; matrix products, arithmetic and copies ran while one was open for 1% of the time, Pallas kernels for 4%

profile of v12, /device:TPU:6, one launch (start us, length us, event | category | flops | bytes accessed | tf_op | source)
XLA Modules:
  0.0 147.7 jit_solution(4697445935920947922)
XLA Ops:
  0.6 0.0 copy-start
  0.6 0.9 copy-done
  1.5 0.0 copy-start.1
  1.5 0.9 copy-done.1
  2.4 0.0 copy-start.2
  2.4 0.9 copy-done.2
  3.4 6.1 %collective-permute-start.1 = (bf16[112,1536]{1,0:T(8,128)(2,1)S(1)}, bf16[112,1536]{1,0:T(8,128)(2,1)S(1)}, u32[]{:S(2)}, u32[]{:S(2)}) collective-permute-start(bf16[112,1536]{1,0:T(8,128)(2,1)S(1)} %stack.1.own_ref), channel_id=1, source_target_pairs={{0,32},{16,112},{32,64},{48,16},{64,96},{80,48},{96,0},{112,80},{1... | collective-permute-start | bytes 1032200 | tf_op jit(solution)/shard_map/ppermute | solution.py:233
  9.5 6.8 %collective-permute-start.2 = (bf16[112,1536]{1,0:T(8,128)(2,1)S(1)}, bf16[112,1536]{1,0:T(8,128)(2,1)S(1)}, u32[]{:S(2)}, u32[]{:S(2)}) collective-permute-start(bf16[112,1536]{1,0:T(8,128)(2,1)S(1)} %stack.1.own_ref), channel_id=1, source_target_pairs={{0,96},{16,48},{32,0},{48,80},{64,32},{80,112},{96,64},{112,16},{1... | collective-permute-start | bytes 1032200 | tf_op jit(solution)/shard_map/ppermute | solution.py:233
  16.2 3.7 %dispatch.1 = bf16[4,8,88,128]{3,2,1,0:T(8,128)(2,1)} custom-call(s32[1,128]{1,0:T(1,128)} %bitcast.30, f32[1,128]{1,0:T(1,128)} %bitcast.32, bf16[128,3584]{1,0:T(8,128)(2,1)} %x_hbm.1, bf16[128,3584]{1,0:T(8,128)(2,1)} %g_hbm.1), custom_call_target="tpu_custom_call" | custom-call | flops 1000000000 | bytes 4000000 | tf_op jit(solution)/shard_map/dispatch/pallas_call | solution.py:62
  20.0 10.2 %all-to-all-start = ((bf16[32,88,128]{2,1,0:T(8,128)(2,1)}), bf16[32,88,128]{2,1,0:T(8,128)(2,1)S(1)}, u32[]{:S(2)}, u32[]{:S(2)}) async-start(bf16[32,88,128]{2,1,0:T(8,128)(2,1)} %bitcast.34), calls=%async_computation | async-start | bytes 1441792 | tf_op jit(solution)/shard_map/all_to_all | solution.py:241
  30.2 0.0 collective-permute-done.1.before_ref
  30.3 0.0 collective-permute-done.2.after_ref
  30.3 0.1 near.1
  30.4 1.9 %collective-permute-start.3 = (bf16[336,1536]{1,0:T(8,128)(2,1)S(1)}, bf16[336,1536]{1,0:T(8,128)(2,1)S(1)}, u32[]{:S(2)}, u32[]{:S(2)}) collective-permute-start(bf16[336,1536]{1,0:T(8,128)(2,1)S(1)} %get-tuple-element.20.near_ref), channel_id=1, source_target_pairs={{0,16},{16,0},{1,17},{17,1},{2,18},{18,2},{3,19},{19,3},{4,20},{20... | collective-permute-start | bytes 3096584 | tf_op jit(solution)/shard_map/ppermute | solution.py:225
  32.3 2.5 %collective-permute-start.4 = (bf16[112,1536]{1,0:T(8,128)(2,1)S(1)}, bf16[112,1536]{1,0:T(8,128)(2,1)S(1)}, u32[]{:S(2)}, u32[]{:S(2)}) collective-permute-start(bf16[112,1536]{1,0:T(8,128)(2,1)S(1)} %get-tuple-element.21), channel_id=1, source_target_pairs={{0,32},{16,112},{32,64},{48,16},{64,96},{80,48},{96,0},{112,80},{1... | collective-permute-start | bytes 1032200 | tf_op jit(solution)/shard_map/ppermute | solution.py:233
  34.8 14.9 %all-to-all-done = bf16[32,88,128]{2,1,0:T(8,128)(2,1)S(1)} async-done(((bf16[32,88,128]{2,1,0:T(8,128)(2,1)}), bf16[32,88,128]{2,1,0:T(8,128)(2,1)S(1)}, u32[]{:S(2)}, u32[]{:S(2)}) %all-to-all-start) | async-done | bytes 720928 | tf_op jit(solution)/shard_map/all_to_all | solution.py:241
  49.7 3.4 %collective-permute-start = (bf16[4,704,128]{2,1,0:T(8,128)(2,1)S(1)}, bf16[4,704,128]{2,1,0:T(8,128)(2,1)S(1)}, u32[]{:S(2)}, u32[]{:S(2)}) collective-permute-start(bf16[4,704,128]{2,1,0:T(8,128)(2,1)S(1)} %bitcast.27), channel_id=1, source_target_pairs={{0,1},{1,0},{2,3},{3,2},{4,5},{5,4},{6,7},{7,6},{8,9},{9,8},{10,11... | collective-permute-start | bytes 2162696 | tf_op jit(solution)/shard_map/ppermute | solution.py:225
  53.0 0.0 collective-permute-done.4.far_ref
  53.1 1.9 %collective-permute-start.5 = (bf16[112,1536]{1,0:T(8,128)(2,1)S(1)}, bf16[112,1536]{1,0:T(8,128)(2,1)S(1)}, u32[]{:S(2)}, u32[]{:S(2)}) collective-permute-start(bf16[112,1536]{1,0:T(8,128)(2,1)S(1)} %collective-permute-done.4.far_ref), channel_id=1, source_target_pairs={{0,16},{16,0},{1,17},{17,1},{2,18},{18,2},{3,19},{19,3},{4,20},{20... | collective-permute-start | bytes 1032200 | tf_op jit(solution)/shard_map/ppermute | solution.py:225
  55.0 1.6 %collective-permute-done.5.far_other_ref = bf16[112,1536]{1,0:T(8,128)(2,1)S(1)} collective-permute-done((bf16[112,1536]{1,0:T(8,128)(2,1)S(1)}, bf16[112,1536]{1,0:T(8,128)(2,1)S(1)}, u32[]{:S(2)}, u32[]{:S(2)}) %collective-permute-start.5) | collective-permute-done | bytes 344096 | tf_op jit(solution)/shard_map/ppermute | solution.py:225
  56.6 0.0 collective-permute-done.3.near_other_ref
  56.6 0.4 assemble.1
  57.0 8.7 %collective-permute-done.other_ref = bf16[4,704,128]{2,1,0:T(8,128)(2,1)S(1)} collective-permute-done((bf16[4,704,128]{2,1,0:T(8,128)(2,1)S(1)}, bf16[4,704,128]{2,1,0:T(8,128)(2,1)S(1)}, u32[]{:S(2)}, u32[]{:S(2)}) %collective-permute-start) | collective-permute-done | bytes 720928 | tf_op jit(solution)/shard_map/ppermute | solution.py:225
  65.7 2.5 %before.1 = (bf16[4,96,1536]{2,1,0:T(8,128)(2,1)S(1)}, bf16[384,896]{1,0:T(8,128)(2,1)S(1)}) custom-call(bf16[4,704,128]{2,1,0:T(8,128)(2,1)S(1)} %bitcast.28, bf16[4,704,128]{2,1,0:T(8,128)(2,1)S(1)} %collective-permute-done.other_ref, bf16[896,1536]{1,0:T(8,128)(2,1)S(1)} %get-tuple-element.22.weight_ref, bf16[672,704]{1,0:T(8,128)(2,1)S(1)} %get-tuple-element.23.pick_ref), custom_call_target="tpu_custom_call" | custom-call | flops 2000000000 | bytes 4000000 | tf_op jit(solution)/shard_map/before/pallas_call | solution.py:62
  68.2 14.6 %all_to_all.20.part_ref = bf16[4,96,1536]{2,1,0:T(8,128)(2,1)S(1)} all-to-all(bf16[4,96,1536]{2,1,0:T(8,128)(2,1)S(1)} %get-tuple-element.24), channel_id=1, replica_groups=mesh['x'=4,'zh'=4,'c'=2,'y'=8,'zl'=2] {'x'}, dimensions={0} | all-to-all | bytes 2359296 | tf_op jit(solution)/shard_map/all_to_all | solution.py:241
  82.8 0.3 middle.1
  83.1 14.0 %all_to_all.21.mid_ref = bf16[4,96,1536]{2,1,0:T(8,128)(2,1)S(1)} all-to-all(bf16[4,96,1536]{2,1,0:T(8,128)(2,1)S(1)} %get-tuple-element.25), channel_id=1, replica_groups=mesh['x'=4,'zh'=4,'c'=2,'y'=8,'zl'=2] {'x'}, dimensions={0} | all-to-all | bytes 2359296 | tf_op jit(solution)/shard_map/all_to_all | solution.py:241
  97.1 1.7 %after.1 = (bf16[4,48,1024]{2,1,0:T(8,128)(2,1)S(1)}, bf16[4,48,1024]{2,1,0:T(8,128)(2,1)S(1)}, bf16[112,512]{1,0:T(8,128)(2,1)S(1)}, bf16[112,512]{1,0:T(8,128)...) custom-call(bf16[4,96,1536]{2,1,0:T(8,128)(2,1)S(1)} %all_to_all.21.mid_ref,, ...), custom_call_target="tpu_custom_call" | custom-call | flops 1400000000 | bytes 4000000 | tf_op jit(solution)/shard_map/after/pallas_call | solution.py:62
  98.9 3.4 %collective-permute-start.6 = (bf16[4,48,1024]{2,1,0:T(8,128)(2,1)S(1)}, bf16[4,48,1024]{2,1,0:T(8,128)(2,1)S(1)}, u32[]{:S(2)}, u32[]{:S(2)}) collective-permute-start(bf16[4,48,1024]{2,1,0:T(8,128)(2,1)S(1)} %get-tuple-element.29), channel_id=1, source_target_pairs={{0,1},{1,0},{2,3},{3,2},{4,5},{5,4},{6,7},{7,6},{8,9},{9,8},{10,11... | collective-permute-start | bytes 1179656 | tf_op jit(solution)/shard_map/ppermute | solution.py:225
  102.3 1.9 %collective-permute-start.7 = (bf16[4,112,512]{2,1,0:T(8,128)(2,1)S(1)}, bf16[4,112,512]{2,1,0:T(8,128)(2,1)S(1)}, u32[]{:S(2)}, u32[]{:S(2)}) collective-permute-start(bf16[4,112,512]{2,1,0:T(8,128)(2,1)S(1)} %get-tuple-element.33), channel_id=1, source_target_pairs={{0,16},{16,0},{1,17},{17,1},{2,18},{18,2},{3,19},{19,3},{4,20},{20... | collective-permute-start | bytes 1376264 | tf_op jit(solution)/shard_map/ppermute | solution.py:225
  104.2 4.3 %collective-permute-done.6.got_ref = bf16[4,48,1024]{2,1,0:T(8,128)(2,1)S(1)} collective-permute-done((bf16[4,48,1024]{2,1,0:T(8,128)(2,1)S(1)}, bf16[4,48,1024]{2,1,0:T(8,128)(2,1)S(1)}, u32[]{:S(2)}, u32[]{:S(2)}) %collective-permute-start.6) | collective-permute-done | bytes 393248 | tf_op jit(solution)/shard_map/ppermute | solution.py:225
  108.5 1.2 combine.1
  109.7 0.0 copy-start.3
  109.7 0.0 copy-start.4
  109.7 15.8 %all-to-all-start.3 = ((bf16[32,48,128]{2,1,0:T(8,128)(2,1)}), bf16[32,48,128]{2,1,0:T(8,128)(2,1)S(1)}, u32[]{:S(2)}, u32[]{:S(2)}) async-start(bf16[32,48,128]{2,1,0:T(8,128)(2,1)} %bitcast.4), calls=%async_computation.3 | async-start | bytes 786432 | tf_op jit(solution)/shard_map/all_to_all | solution.py:241
  125.5 0.0 collective-permute-done.7
  125.5 0.1 fusion.3
  125.6 1.9 %collective-permute-start.10 = (bf16[112,512]{1,0:T(8,128)(2,1)S(1)}, bf16[112,512]{1,0:T(8,128)(2,1)S(1)}, u32[]{:S(2)}, u32[]{:S(2)}) collective-permute-start(bf16[112,512]{1,0:T(8,128)(2,1)S(1)} %get-tuple-element.38), channel_id=1, source_target_pairs={{0,64},{32,96},{64,0},{96,32},{1,65},{33,97},{65,1},{97,33},{2,66}... | collective-permute-start | bytes 344072 | tf_op jit(solution)/shard_map/ppermute | solution.py:225
  127.6 10.0 %collective-permute-start.8 = (bf16[112,512]{1,0:T(8,128)(2,1)S(1)}, bf16[112,512]{1,0:T(8,128)(2,1)S(1)}, u32[]{:S(2)}, u32[]{:S(2)}) collective-permute-start(bf16[112,512]{1,0:T(8,128)(2,1)S(1)} %get-tuple-element.37), channel_id=1, source_target_pairs={{0,32},{32,64},{64,96},{96,0},{1,33},{33,65},{65,97},{97,1},{2,34}... | collective-permute-start | bytes 344072 | tf_op jit(solution)/shard_map/ppermute | solution.py:225
  137.5 1.9 %collective-permute-start.9 = (bf16[112,512]{1,0:T(8,128)(2,1)S(1)}, bf16[112,512]{1,0:T(8,128)(2,1)S(1)}, u32[]{:S(2)}, u32[]{:S(2)}) collective-permute-start(bf16[112,512]{1,0:T(8,128)(2,1)S(1)} %get-tuple-element.39), channel_id=1, source_target_pairs={{0,96},{32,0},{64,32},{96,64},{1,97},{33,1},{65,33},{97,65},{2,98}... | collective-permute-start | bytes 344072 | tf_op jit(solution)/shard_map/ppermute | solution.py:225
  139.5 0.0 collective-permute-done.10
  139.5 0.5 collective-permute-done.8
  140.0 5.2 %collective-permute-done.9 = bf16[112,512]{1,0:T(8,128)(2,1)S(1)} collective-permute-done((bf16[112,512]{1,0:T(8,128)(2,1)S(1)}, bf16[112,512]{1,0:T(8,128)(2,1)S(1)}, u32[]{:S(2)}, u32[]{:S(2)}) %collective-permute-start.9) | collective-permute-done | bytes 114720 | tf_op jit(solution)/shard_map/ppermute | solution.py:225
  145.2 0.7 add_convert_fusion
  145.9 0.0 all-to-all-done.3
  145.9 0.0 copy-done.3
  145.9 0.0 copy-done.4
  145.9 1.8 %finish.1 = (bf16[128,3584]{1,0:T(8,128)(2,1)}, f32[1,128]{1,0:T(1,128)}) custom-call(s32[1,128]{1,0:T(1,128)S(1)} %bitcast.31, f32[1,128]{1,0:T(1,128)S(1)} %bitcast.33, bf16[4,384,128]{2,1,0:T(8,128)(2,1)S(1)} %bitcast.29), custom_call_target="tpu_custom_call" | custom-call | flops 400000000 | bytes 4000000 | tf_op jit(solution)/shard_map/finish/pallas_call | solution.py:62
  (1 shorter events, 0.0 us)
Async XLA Ops:
  0.6 0.9 copy-start
  1.5 0.9 copy-start.1
  2.4 0.9 copy-start.2
  3.4 26.9 %collective-permute-start.1 = (bf16[112,1536]{1,0:T(8,128)(2,1)S(1)}, bf16[112,1536]{1,0:T(8,128)(2,1)S(1)}, u32[]{:S(2)}, u32[]{:S(2)}) collective-permute-start(bf16[112,1536]{1,0:T(8,128)(2,1)S(1)} %stack.1.own_ref), channel_id=1, source_target_pairs={{0,32},{16,112},{32,64},{48,16},{64,96},{80,48},{96,0},{112,80},{1... | collective-permute-start | bytes 1032200 | tf_op jit(solution)/shard_map/ppermute | solution.py:233
  9.5 20.8 %collective-permute-start.2 = (bf16[112,1536]{1,0:T(8,128)(2,1)S(1)}, bf16[112,1536]{1,0:T(8,128)(2,1)S(1)}, u32[]{:S(2)}, u32[]{:S(2)}) collective-permute-start(bf16[112,1536]{1,0:T(8,128)(2,1)S(1)} %stack.1.own_ref), channel_id=1, source_target_pairs={{0,96},{16,48},{32,0},{48,80},{64,32},{80,112},{96,64},{112,16},{1... | collective-permute-start | bytes 1032200 | tf_op jit(solution)/shard_map/ppermute | solution.py:233
  20.0 29.7 %all-to-all-start = ((bf16[32,88,128]{2,1,0:T(8,128)(2,1)}), bf16[32,88,128]{2,1,0:T(8,128)(2,1)S(1)}, u32[]{:S(2)}, u32[]{:S(2)}) async-start(bf16[32,88,128]{2,1,0:T(8,128)(2,1)} %bitcast.34), calls=%async_computation | async-start | bytes 1441792 | tf_op jit(solution)/shard_map/all_to_all | solution.py:241
  30.4 26.2 %collective-permute-start.3 = (bf16[336,1536]{1,0:T(8,128)(2,1)S(1)}, bf16[336,1536]{1,0:T(8,128)(2,1)S(1)}, u32[]{:S(2)}, u32[]{:S(2)}) collective-permute-start(bf16[336,1536]{1,0:T(8,128)(2,1)S(1)} %get-tuple-element.20.near_ref), channel_id=1, source_target_pairs={{0,16},{16,0},{1,17},{17,1},{2,18},{18,2},{3,19},{19,3},{4,20},{20... | collective-permute-start | bytes 3096584 | tf_op jit(solution)/shard_map/ppermute | solution.py:225
  32.3 20.8 %collective-permute-start.4 = (bf16[112,1536]{1,0:T(8,128)(2,1)S(1)}, bf16[112,1536]{1,0:T(8,128)(2,1)S(1)}, u32[]{:S(2)}, u32[]{:S(2)}) collective-permute-start(bf16[112,1536]{1,0:T(8,128)(2,1)S(1)} %get-tuple-element.21), channel_id=1, source_target_pairs={{0,32},{16,112},{32,64},{48,16},{64,96},{80,48},{96,0},{112,80},{1... | collective-permute-start | bytes 1032200 | tf_op jit(solution)/shard_map/ppermute | solution.py:233
  49.7 16.0 %collective-permute-start = (bf16[4,704,128]{2,1,0:T(8,128)(2,1)S(1)}, bf16[4,704,128]{2,1,0:T(8,128)(2,1)S(1)}, u32[]{:S(2)}, u32[]{:S(2)}) collective-permute-start(bf16[4,704,128]{2,1,0:T(8,128)(2,1)S(1)} %bitcast.27), channel_id=1, source_target_pairs={{0,1},{1,0},{2,3},{3,2},{4,5},{5,4},{6,7},{7,6},{8,9},{9,8},{10,11... | collective-permute-start | bytes 2162696 | tf_op jit(solution)/shard_map/ppermute | solution.py:225
  53.1 3.5 %collective-permute-start.5 = (bf16[112,1536]{1,0:T(8,128)(2,1)S(1)}, bf16[112,1536]{1,0:T(8,128)(2,1)S(1)}, u32[]{:S(2)}, u32[]{:S(2)}) collective-permute-start(bf16[112,1536]{1,0:T(8,128)(2,1)S(1)} %collective-permute-done.4.far_ref), channel_id=1, source_target_pairs={{0,16},{16,0},{1,17},{17,1},{2,18},{18,2},{3,19},{19,3},{4,20},{20... | collective-permute-start | bytes 1032200 | tf_op jit(solution)/shard_map/ppermute | solution.py:225
  98.9 9.7 %collective-permute-start.6 = (bf16[4,48,1024]{2,1,0:T(8,128)(2,1)S(1)}, bf16[4,48,1024]{2,1,0:T(8,128)(2,1)S(1)}, u32[]{:S(2)}, u32[]{:S(2)}) collective-permute-start(bf16[4,48,1024]{2,1,0:T(8,128)(2,1)S(1)} %get-tuple-element.29), channel_id=1, source_target_pairs={{0,1},{1,0},{2,3},{3,2},{4,5},{5,4},{6,7},{7,6},{8,9},{9,8},{10,11... | collective-permute-start | bytes 1179656 | tf_op jit(solution)/shard_map/ppermute | solution.py:225
  102.3 23.2 %collective-permute-start.7 = (bf16[4,112,512]{2,1,0:T(8,128)(2,1)S(1)}, bf16[4,112,512]{2,1,0:T(8,128)(2,1)S(1)}, u32[]{:S(2)}, u32[]{:S(2)}) collective-permute-start(bf16[4,112,512]{2,1,0:T(8,128)(2,1)S(1)} %get-tuple-element.33), channel_id=1, source_target_pairs={{0,16},{16,0},{1,17},{17,1},{2,18},{18,2},{3,19},{19,3},{4,20},{20... | collective-permute-start | bytes 1376264 | tf_op jit(solution)/shard_map/ppermute | solution.py:225
  109.7 36.2 %copy-start.3 = (s32[128,1]{0,1:T(1,128)S(1)}, s32[128,1]{0,1:T(1,128)}, u32[]{:S(2)}) copy-start(s32[128,1]{0,1:T(1,128)} %param.9) | copy-start | bytes 1540
  109.7 36.2 %copy-start.4 = (f32[128,1]{0,1:T(1,128)S(1)}, f32[128,1]{0,1:T(1,128)}, u32[]{:S(2)}) copy-start(f32[128,1]{0,1:T(1,128)} %param.10) | copy-start | bytes 1540
  109.7 36.2 %all-to-all-start.3 = ((bf16[32,48,128]{2,1,0:T(8,128)(2,1)}), bf16[32,48,128]{2,1,0:T(8,128)(2,1)S(1)}, u32[]{:S(2)}, u32[]{:S(2)}) async-start(bf16[32,48,128]{2,1,0:T(8,128)(2,1)} %bitcast.4), calls=%async_computation.3 | async-start | bytes 786432 | tf_op jit(solution)/shard_map/all_to_all | solution.py:241
  125.6 13.9 %collective-permute-start.10 = (bf16[112,512]{1,0:T(8,128)(2,1)S(1)}, bf16[112,512]{1,0:T(8,128)(2,1)S(1)}, u32[]{:S(2)}, u32[]{:S(2)}) collective-permute-start(bf16[112,512]{1,0:T(8,128)(2,1)S(1)} %get-tuple-element.38), channel_id=1, source_target_pairs={{0,64},{32,96},{64,0},{96,32},{1,65},{33,97},{65,1},{97,33},{2,66}... | collective-permute-start | bytes 344072 | tf_op jit(solution)/shard_map/ppermute | solution.py:225
  127.6 12.4 %collective-permute-start.8 = (bf16[112,512]{1,0:T(8,128)(2,1)S(1)}, bf16[112,512]{1,0:T(8,128)(2,1)S(1)}, u32[]{:S(2)}, u32[]{:S(2)}) collective-permute-start(bf16[112,512]{1,0:T(8,128)(2,1)S(1)} %get-tuple-element.37), channel_id=1, source_target_pairs={{0,32},{32,64},{64,96},{96,0},{1,33},{33,65},{65,97},{97,1},{2,34}... | collective-permute-start | bytes 344072 | tf_op jit(solution)/shard_map/ppermute | solution.py:225
  137.5 7.6 %collective-permute-start.9 = (bf16[112,512]{1,0:T(8,128)(2,1)S(1)}, bf16[112,512]{1,0:T(8,128)(2,1)S(1)}, u32[]{:S(2)}, u32[]{:S(2)}) collective-permute-start(bf16[112,512]{1,0:T(8,128)(2,1)S(1)} %get-tuple-element.39), channel_id=1, source_target_pairs={{0,96},{32,0},{64,32},{96,64},{1,97},{33,1},{65,33},{97,65},{2,98}... | collective-permute-start | bytes 344072 | tf_op jit(solution)/shard_map/ppermute | solution.py:225

commit v13 on v12

--- a/solution.py
+++ b/solution.py
@@ -103,9 +103,15 @@
             out_ref[2 * i + j] = one
 
 
-def stack_kernel(a_ref, b_ref, c_ref, out_ref):
-    for i, ref in enumerate((a_ref, b_ref, c_ref)):
-        out_ref[:, i * HALF:(i + 1) * HALF] = ref[...]
+def stack_kernel(a_hbm, b_hbm, c_hbm, out_ref, sems):
+    copies = [
+        pltpu.make_async_copy(source, out_ref.at[:, pl.ds(i * HALF, HALF)], sems.at[i])
+        for i, source in enumerate((a_hbm, b_hbm, c_hbm))
+    ]
+    for copy in copies:
+        copy.start()
+    for copy in copies:
+        copy.wait()
 
 
 def near_kernel(own_ref, before_ref, after_ref, out_ref, before_out):
@@ -243,7 +249,8 @@
 
 def per_device(tokens, grad_out, routing, route_weight, gate_weight, up_weight, down_weight):
     ids, share = routing.reshape(1, TOK), route_weight.reshape(1, TOK)
-    weights, = call(stack_kernel, "stack", [((SHARD, 3 * HALF), BF)], (gate_weight, up_weight, down_weight), 10**6)
+    weights, = call(stack_kernel, "stack", [((SHARD, 3 * HALF), BF)], (gate_weight, up_weight, down_weight), 10**6,
+                    [pltpu.SemaphoreType.DMA((3,))], [ANYWHERE] * 3, MOST_VMEM)
     sent, = call(
         dispatch_kernel, "dispatch", [((4, EXPERTS, WIDE, TOK), BF)], (ids, share, tokens, grad_out), 10**9,
         [pltpu.VMEM((1, TOK), I32), pltpu.VMEM((1, TOK), F32), pltpu.VMEM((TOK, D), BF), pltpu.VMEM((TOK, D), BF),

time: 148 us -> 148 us (level)
  local copies, waits for them, and re-layouts: 2.69 us -> 0.01 us
  Pallas kernels: 11.8 us -> 13.5 us
    unnamed x10 -> x6, local copies, waits for them, and re-layouts: 2.69 us -> 0.01 us
    pallas_call x9, Pallas kernels: 11.8 us -> 13.5 us  [call(): pl.pallas_call(body, in_specs=specs or [VMEM] * len(operands), out_specs=...]
where the time goes in v13:
time: 148 us; the launch traced here: 147 us
  starting transfers between devices  68 us (46%)
  waiting for transfers between devices  35.1 us (24%)
  blocking collectives  28.6 us (19%)
  Pallas kernels  13.5 us (9%)
    all_to_all x2, blocking collectives, exchange(): return lax.all_to_all(a, axes, split_axis=0, concat_axis=0, tiled=True)  28.6 us
    ppermute x8, starting transfers between devices, hop(): return lax.ppermute(a, axis, [(i, (i + shift) % n) for i in range(n)])  26.4 us
    all_to_all x2, starting transfers between devices, exchange(): return lax.all_to_all(a, axes, split_axis=0, concat_axis=0, tiled=True)  26.2 us
    ppermute x8, waiting for transfers between devices, hop(): return lax.ppermute(a, axis, [(i, (i + shift) % n) for i in range(n)])  20.3 us
    ppermute x3, starting transfers between devices, turn(): return lax.ppermute(a, (axis, 'c'), pairs)  15.4 us
    all_to_all x2, waiting for transfers between devices, exchange(): return lax.all_to_all(a, axes, split_axis=0, concat_axis=0, tiled=True)  14.8 us
    pallas_call x9, Pallas kernels, call(): pl.pallas_call(body, in_specs=specs or [VMEM] * len(operands), out_specs=...  13.5 us
  transfers between devices with their start and end apart: 13, of which 6 were waited for; matrix products, arithmetic and copies ran while one was open for 1% of the time, Pallas kernels for 4%

profile of v13, /device:TPU:6, one launch (start us, length us, event | category | flops | bytes accessed | tf_op | source)
XLA Modules:
  0.0 146.9 jit_solution(16533498704319836978)
XLA Ops:
  0.6 1.8 %stack.1.own_ref = bf16[112,1536]{1,0:T(8,128)(2,1)} custom-call(bf16[112,512]{1,0:T(8,128)(2,1)} %a_hbm.1, bf16[112,512]{1,0:T(8,128)(2,1)} %b_hbm.1, bf16[112,512]{1,0:T(8,128)(2,1)} %c_hbm.1), custom_call_target="tpu_custom_call" | custom-call | flops 1000000 | bytes 4000000 | tf_op jit(solution)/shard_map/stack/pallas_call | solution.py:62
  2.4 6.1 %collective-permute-start.1 = (bf16[112,1536]{1,0:T(8,128)(2,1)}, bf16[112,1536]{1,0:T(8,128)(2,1)S(1)}, u32[]{:S(2)}, u32[]{:S(2)}) collective-permute-start(bf16[112,1536]{1,0:T(8,128)(2,1)} %stack.1.own_ref), channel_id=1, source_target_pairs={{0,32},{16,112},{32,64},{48,16},{64,96},{80,48},{96,0},{112,80},{1... | collective-permute-start | bytes 1032200 | tf_op jit(solution)/shard_map/ppermute | solution.py:239
  8.5 6.8 %collective-permute-start.2 = (bf16[112,1536]{1,0:T(8,128)(2,1)}, bf16[112,1536]{1,0:T(8,128)(2,1)S(1)}, u32[]{:S(2)}, u32[]{:S(2)}) collective-permute-start(bf16[112,1536]{1,0:T(8,128)(2,1)} %stack.1.own_ref), channel_id=1, source_target_pairs={{0,96},{16,48},{32,0},{48,80},{64,32},{80,112},{96,64},{112,16},{1... | collective-permute-start | bytes 1032200 | tf_op jit(solution)/shard_map/ppermute | solution.py:239
  15.3 3.7 %dispatch.1 = bf16[4,8,88,128]{3,2,1,0:T(8,128)(2,1)} custom-call(s32[1,128]{1,0:T(1,128)} %bitcast.30, f32[1,128]{1,0:T(1,128)} %bitcast.32, bf16[128,3584]{1,0:T(8,128)(2,1)} %x_hbm.1, bf16[128,3584]{1,0:T(8,128)(2,1)} %g_hbm.1), custom_call_target="tpu_custom_call" | custom-call | flops 1000000000 | bytes 4000000 | tf_op jit(solution)/shard_map/dispatch/pallas_call | solution.py:62
  19.0 0.0 copy-start
  19.0 10.4 %all-to-all-start = ((bf16[32,88,128]{2,1,0:T(8,128)(2,1)}), bf16[32,88,128]{2,1,0:T(8,128)(2,1)S(1)}, u32[]{:S(2)}, u32[]{:S(2)}) async-start(bf16[32,88,128]{2,1,0:T(8,128)(2,1)} %bitcast.34), calls=%async_computation | async-start | bytes 1441792 | tf_op jit(solution)/shard_map/all_to_all | solution.py:247
  29.4 0.0 collective-permute-done.1.before_ref
  29.4 0.0 collective-permute-done.2.after_ref
  29.5 0.0 copy-done
  29.5 0.1 near.1
  29.6 1.9 %collective-permute-start.3 = (bf16[336,1536]{1,0:T(8,128)(2,1)S(1)}, bf16[336,1536]{1,0:T(8,128)(2,1)S(1)}, u32[]{:S(2)}, u32[]{:S(2)}) collective-permute-start(bf16[336,1536]{1,0:T(8,128)(2,1)S(1)} %get-tuple-element.20.near_ref), channel_id=1, source_target_pairs={{0,16},{16,0},{1,17},{17,1},{2,18},{18,2},{3,19},{19,3},{4,20},{20... | collective-permute-start | bytes 3096584 | tf_op jit(solution)/shard_map/ppermute | solution.py:231
  31.5 2.6 %collective-permute-start.4 = (bf16[112,1536]{1,0:T(8,128)(2,1)S(1)}, bf16[112,1536]{1,0:T(8,128)(2,1)S(1)}, u32[]{:S(2)}, u32[]{:S(2)}) collective-permute-start(bf16[112,1536]{1,0:T(8,128)(2,1)S(1)} %get-tuple-element.21), channel_id=1, source_target_pairs={{0,32},{16,112},{32,64},{48,16},{64,96},{80,48},{96,0},{112,80},{1... | collective-permute-start | bytes 1032200 | tf_op jit(solution)/shard_map/ppermute | solution.py:239
  34.1 14.8 %all-to-all-done = bf16[32,88,128]{2,1,0:T(8,128)(2,1)S(1)} async-done(((bf16[32,88,128]{2,1,0:T(8,128)(2,1)}), bf16[32,88,128]{2,1,0:T(8,128)(2,1)S(1)}, u32[]{:S(2)}, u32[]{:S(2)}) %all-to-all-start) | async-done | bytes 720928 | tf_op jit(solution)/shard_map/all_to_all | solution.py:247
  48.9 3.4 %collective-permute-start = (bf16[4,704,128]{2,1,0:T(8,128)(2,1)S(1)}, bf16[4,704,128]{2,1,0:T(8,128)(2,1)S(1)}, u32[]{:S(2)}, u32[]{:S(2)}) collective-permute-start(bf16[4,704,128]{2,1,0:T(8,128)(2,1)S(1)} %bitcast.27), channel_id=1, source_target_pairs={{0,1},{1,0},{2,3},{3,2},{4,5},{5,4},{6,7},{7,6},{8,9},{9,8},{10,11... | collective-permute-start | bytes 2162696 | tf_op jit(solution)/shard_map/ppermute | solution.py:231
  52.2 0.0 collective-permute-done.4.far_ref
  52.2 1.9 %collective-permute-start.5 = (bf16[112,1536]{1,0:T(8,128)(2,1)S(1)}, bf16[112,1536]{1,0:T(8,128)(2,1)S(1)}, u32[]{:S(2)}, u32[]{:S(2)}) collective-permute-start(bf16[112,1536]{1,0:T(8,128)(2,1)S(1)} %collective-permute-done.4.far_ref), channel_id=1, source_target_pairs={{0,16},{16,0},{1,17},{17,1},{2,18},{18,2},{3,19},{19,3},{4,20},{20... | collective-permute-start | bytes 1032200 | tf_op jit(solution)/shard_map/ppermute | solution.py:231
  54.2 1.6 %collective-permute-done.5.far_other_ref = bf16[112,1536]{1,0:T(8,128)(2,1)S(1)} collective-permute-done((bf16[112,1536]{1,0:T(8,128)(2,1)S(1)}, bf16[112,1536]{1,0:T(8,128)(2,1)S(1)}, u32[]{:S(2)}, u32[]{:S(2)}) %collective-permute-start.5) | collective-permute-done | bytes 344096 | tf_op jit(solution)/shard_map/ppermute | solution.py:231
  55.8 0.0 collective-permute-done.3.near_other_ref
  55.8 0.4 assemble.1
  56.2 8.7 %collective-permute-done.other_ref = bf16[4,704,128]{2,1,0:T(8,128)(2,1)S(1)} collective-permute-done((bf16[4,704,128]{2,1,0:T(8,128)(2,1)S(1)}, bf16[4,704,128]{2,1,0:T(8,128)(2,1)S(1)}, u32[]{:S(2)}, u32[]{:S(2)}) %collective-permute-start) | collective-permute-done | bytes 720928 | tf_op jit(solution)/shard_map/ppermute | solution.py:231
  64.9 2.5 %before.1 = (bf16[4,96,1536]{2,1,0:T(8,128)(2,1)S(1)}, bf16[384,896]{1,0:T(8,128)(2,1)S(1)}) custom-call(bf16[4,704,128]{2,1,0:T(8,128)(2,1)S(1)} %bitcast.28, bf16[4,704,128]{2,1,0:T(8,128)(2,1)S(1)} %collective-permute-done.other_ref, bf16[896,1536]{1,0:T(8,128)(2,1)S(1)} %get-tuple-element.22.weight_ref, bf16[672,704]{1,0:T(8,128)(2,1)S(1)} %get-tuple-element.23.pick_ref), custom_call_target="tpu_custom_call" | custom-call | flops 2000000000 | bytes 4000000 | tf_op jit(solution)/shard_map/before/pallas_call | solution.py:62
  67.4 14.6 %all_to_all.20.part_ref = bf16[4,96,1536]{2,1,0:T(8,128)(2,1)S(1)} all-to-all(bf16[4,96,1536]{2,1,0:T(8,128)(2,1)S(1)} %get-tuple-element.24), channel_id=1, replica_groups=mesh['x'=4,'zh'=4,'c'=2,'y'=8,'zl'=2] {'x'}, dimensions={0} | all-to-all | bytes 2359296 | tf_op jit(solution)/shard_map/all_to_all | solution.py:247
  82.0 0.3 middle.1
  82.3 14.0 %all_to_all.21.mid_ref = bf16[4,96,1536]{2,1,0:T(8,128)(2,1)S(1)} all-to-all(bf16[4,96,1536]{2,1,0:T(8,128)(2,1)S(1)} %get-tuple-element.25), channel_id=1, replica_groups=mesh['x'=4,'zh'=4,'c'=2,'y'=8,'zl'=2] {'x'}, dimensions={0} | all-to-all | bytes 2359296 | tf_op jit(solution)/shard_map/all_to_all | solution.py:247
  96.3 1.7 %after.1 = (bf16[4,48,1024]{2,1,0:T(8,128)(2,1)S(1)}, bf16[4,48,1024]{2,1,0:T(8,128)(2,1)S(1)}, bf16[112,512]{1,0:T(8,128)(2,1)S(1)}, bf16[112,512]{1,0:T(8,128)...) custom-call(bf16[4,96,1536]{2,1,0:T(8,128)(2,1)S(1)} %all_to_all.21.mid_ref,, ...), custom_call_target="tpu_custom_call" | custom-call | flops 1400000000 | bytes 4000000 | tf_op jit(solution)/shard_map/after/pallas_call | solution.py:62
  98.1 3.4 %collective-permute-start.6 = (bf16[4,48,1024]{2,1,0:T(8,128)(2,1)S(1)}, bf16[4,48,1024]{2,1,0:T(8,128)(2,1)S(1)}, u32[]{:S(2)}, u32[]{:S(2)}) collective-permute-start(bf16[4,48,1024]{2,1,0:T(8,128)(2,1)S(1)} %get-tuple-element.29), channel_id=1, source_target_pairs={{0,1},{1,0},{2,3},{3,2},{4,5},{5,4},{6,7},{7,6},{8,9},{9,8},{10,11... | collective-permute-start | bytes 1179656 | tf_op jit(solution)/shard_map/ppermute | solution.py:231
  101.5 1.9 %collective-permute-start.7 = (bf16[4,112,512]{2,1,0:T(8,128)(2,1)S(1)}, bf16[4,112,512]{2,1,0:T(8,128)(2,1)S(1)}, u32[]{:S(2)}, u32[]{:S(2)}) collective-permute-start(bf16[4,112,512]{2,1,0:T(8,128)(2,1)S(1)} %get-tuple-element.33), channel_id=1, source_target_pairs={{0,16},{16,0},{1,17},{17,1},{2,18},{18,2},{3,19},{19,3},{4,20},{20... | collective-permute-start | bytes 1376264 | tf_op jit(solution)/shard_map/ppermute | solution.py:231
  103.4 4.3 %collective-permute-done.6.got_ref = bf16[4,48,1024]{2,1,0:T(8,128)(2,1)S(1)} collective-permute-done((bf16[4,48,1024]{2,1,0:T(8,128)(2,1)S(1)}, bf16[4,48,1024]{2,1,0:T(8,128)(2,1)S(1)}, u32[]{:S(2)}, u32[]{:S(2)}) %collective-permute-start.6) | collective-permute-done | bytes 393248 | tf_op jit(solution)/shard_map/ppermute | solution.py:231
  107.7 1.2 combine.1
  108.9 0.0 copy-start.1
  108.9 0.0 copy-start.2
  108.9 15.8 %all-to-all-start.3 = ((bf16[32,48,128]{2,1,0:T(8,128)(2,1)}), bf16[32,48,128]{2,1,0:T(8,128)(2,1)S(1)}, u32[]{:S(2)}, u32[]{:S(2)}) async-start(bf16[32,48,128]{2,1,0:T(8,128)(2,1)} %bitcast.4), calls=%async_computation.3 | async-start | bytes 786432 | tf_op jit(solution)/shard_map/all_to_all | solution.py:247
  124.7 0.0 collective-permute-done.7
  124.7 0.1 fusion.3
  124.8 1.9 %collective-permute-start.10 = (bf16[112,512]{1,0:T(8,128)(2,1)S(1)}, bf16[112,512]{1,0:T(8,128)(2,1)S(1)}, u32[]{:S(2)}, u32[]{:S(2)}) collective-permute-start(bf16[112,512]{1,0:T(8,128)(2,1)S(1)} %get-tuple-element.38), channel_id=1, source_target_pairs={{0,64},{32,96},{64,0},{96,32},{1,65},{33,97},{65,1},{97,33},{2,66}... | collective-permute-start | bytes 344072 | tf_op jit(solution)/shard_map/ppermute | solution.py:231
  126.7 10.0 %collective-permute-start.8 = (bf16[112,512]{1,0:T(8,128)(2,1)S(1)}, bf16[112,512]{1,0:T(8,128)(2,1)S(1)}, u32[]{:S(2)}, u32[]{:S(2)}) collective-permute-start(bf16[112,512]{1,0:T(8,128)(2,1)S(1)} %get-tuple-element.37), channel_id=1, source_target_pairs={{0,32},{32,64},{64,96},{96,0},{1,33},{33,65},{65,97},{97,1},{2,34}... | collective-permute-start | bytes 344072 | tf_op jit(solution)/shard_map/ppermute | solution.py:231
  136.7 1.9 %collective-permute-start.9 = (bf16[112,512]{1,0:T(8,128)(2,1)S(1)}, bf16[112,512]{1,0:T(8,128)(2,1)S(1)}, u32[]{:S(2)}, u32[]{:S(2)}) collective-permute-start(bf16[112,512]{1,0:T(8,128)(2,1)S(1)} %get-tuple-element.39), channel_id=1, source_target_pairs={{0,96},{32,0},{64,32},{96,64},{1,97},{33,1},{65,33},{97,65},{2,98}... | collective-permute-start | bytes 344072 | tf_op jit(solution)/shard_map/ppermute | solution.py:231
  138.7 0.0 collective-permute-done.10
  138.7 0.5 collective-permute-done.8
  139.1 5.2 %collective-permute-done.9 = bf16[112,512]{1,0:T(8,128)(2,1)S(1)} collective-permute-done((bf16[112,512]{1,0:T(8,128)(2,1)S(1)}, bf16[112,512]{1,0:T(8,128)(2,1)S(1)}, u32[]{:S(2)}, u32[]{:S(2)}) %collective-permute-start.9) | collective-permute-done | bytes 114720 | tf_op jit(solution)/shard_map/ppermute | solution.py:231
  144.3 0.7 add_convert_fusion
  145.1 0.0 all-to-all-done.3
  145.1 0.0 copy-done.1
  145.1 0.0 copy-done.2
  145.1 1.8 %finish.1 = (bf16[128,3584]{1,0:T(8,128)(2,1)}, f32[1,128]{1,0:T(1,128)}) custom-call(s32[1,128]{1,0:T(1,128)S(1)} %bitcast.31, f32[1,128]{1,0:T(1,128)S(1)} %bitcast.33, bf16[4,384,128]{2,1,0:T(8,128)(2,1)S(1)} %bitcast.29), custom_call_target="tpu_custom_call" | custom-call | flops 400000000 | bytes 4000000 | tf_op jit(solution)/shard_map/finish/pallas_call | solution.py:62
Async XLA Ops:
  2.4 27.0 %collective-permute-start.1 = (bf16[112,1536]{1,0:T(8,128)(2,1)}, bf16[112,1536]{1,0:T(8,128)(2,1)S(1)}, u32[]{:S(2)}, u32[]{:S(2)}) collective-permute-start(bf16[112,1536]{1,0:T(8,128)(2,1)} %stack.1.own_ref), channel_id=1, source_target_pairs={{0,32},{16,112},{32,64},{48,16},{64,96},{80,48},{96,0},{112,80},{1... | collective-permute-start | bytes 1032200 | tf_op jit(solution)/shard_map/ppermute | solution.py:239
  8.5 20.9 %collective-permute-start.2 = (bf16[112,1536]{1,0:T(8,128)(2,1)}, bf16[112,1536]{1,0:T(8,128)(2,1)S(1)}, u32[]{:S(2)}, u32[]{:S(2)}) collective-permute-start(bf16[112,1536]{1,0:T(8,128)(2,1)} %stack.1.own_ref), channel_id=1, source_target_pairs={{0,96},{16,48},{32,0},{48,80},{64,32},{80,112},{96,64},{112,16},{1... | collective-permute-start | bytes 1032200 | tf_op jit(solution)/shard_map/ppermute | solution.py:239
  19.0 10.4 %copy-start = (bf16[112,1536]{1,0:T(8,128)(2,1)S(1)}, bf16[112,1536]{1,0:T(8,128)(2,1)}, u32[]{:S(2)}) copy-start(bf16[112,1536]{1,0:T(8,128)(2,1)} %stack.1.own_ref) | copy-start | bytes 1032196
  19.0 29.8 %all-to-all-start = ((bf16[32,88,128]{2,1,0:T(8,128)(2,1)}), bf16[32,88,128]{2,1,0:T(8,128)(2,1)S(1)}, u32[]{:S(2)}, u32[]{:S(2)}) async-start(bf16[32,88,128]{2,1,0:T(8,128)(2,1)} %bitcast.34), calls=%async_computation | async-start | bytes 1441792 | tf_op jit(solution)/shard_map/all_to_all | solution.py:247
  29.6 26.2 %collective-permute-start.3 = (bf16[336,1536]{1,0:T(8,128)(2,1)S(1)}, bf16[336,1536]{1,0:T(8,128)(2,1)S(1)}, u32[]{:S(2)}, u32[]{:S(2)}) collective-permute-start(bf16[336,1536]{1,0:T(8,128)(2,1)S(1)} %get-tuple-element.20.near_ref), channel_id=1, source_target_pairs={{0,16},{16,0},{1,17},{17,1},{2,18},{18,2},{3,19},{19,3},{4,20},{20... | collective-permute-start | bytes 3096584 | tf_op jit(solution)/shard_map/ppermute | solution.py:231
  31.5 20.7 %collective-permute-start.4 = (bf16[112,1536]{1,0:T(8,128)(2,1)S(1)}, bf16[112,1536]{1,0:T(8,128)(2,1)S(1)}, u32[]{:S(2)}, u32[]{:S(2)}) collective-permute-start(bf16[112,1536]{1,0:T(8,128)(2,1)S(1)} %get-tuple-element.21), channel_id=1, source_target_pairs={{0,32},{16,112},{32,64},{48,16},{64,96},{80,48},{96,0},{112,80},{1... | collective-permute-start | bytes 1032200 | tf_op jit(solution)/shard_map/ppermute | solution.py:239
  48.9 16.0 %collective-permute-start = (bf16[4,704,128]{2,1,0:T(8,128)(2,1)S(1)}, bf16[4,704,128]{2,1,0:T(8,128)(2,1)S(1)}, u32[]{:S(2)}, u32[]{:S(2)}) collective-permute-start(bf16[4,704,128]{2,1,0:T(8,128)(2,1)S(1)} %bitcast.27), channel_id=1, source_target_pairs={{0,1},{1,0},{2,3},{3,2},{4,5},{5,4},{6,7},{7,6},{8,9},{9,8},{10,11... | collective-permute-start | bytes 2162696 | tf_op jit(solution)/shard_map/ppermute | solution.py:231
  52.2 3.5 %collective-permute-start.5 = (bf16[112,1536]{1,0:T(8,128)(2,1)S(1)}, bf16[112,1536]{1,0:T(8,128)(2,1)S(1)}, u32[]{:S(2)}, u32[]{:S(2)}) collective-permute-start(bf16[112,1536]{1,0:T(8,128)(2,1)S(1)} %collective-permute-done.4.far_ref), channel_id=1, source_target_pairs={{0,16},{16,0},{1,17},{17,1},{2,18},{18,2},{3,19},{19,3},{4,20},{20... | collective-permute-start | bytes 1032200 | tf_op jit(solution)/shard_map/ppermute | solution.py:231
  98.1 9.7 %collective-permute-start.6 = (bf16[4,48,1024]{2,1,0:T(8,128)(2,1)S(1)}, bf16[4,48,1024]{2,1,0:T(8,128)(2,1)S(1)}, u32[]{:S(2)}, u32[]{:S(2)}) collective-permute-start(bf16[4,48,1024]{2,1,0:T(8,128)(2,1)S(1)} %get-tuple-element.29), channel_id=1, source_target_pairs={{0,1},{1,0},{2,3},{3,2},{4,5},{5,4},{6,7},{7,6},{8,9},{9,8},{10,11... | collective-permute-start | bytes 1179656 | tf_op jit(solution)/shard_map/ppermute | solution.py:231
  101.5 23.2 %collective-permute-start.7 = (bf16[4,112,512]{2,1,0:T(8,128)(2,1)S(1)}, bf16[4,112,512]{2,1,0:T(8,128)(2,1)S(1)}, u32[]{:S(2)}, u32[]{:S(2)}) collective-permute-start(bf16[4,112,512]{2,1,0:T(8,128)(2,1)S(1)} %get-tuple-element.33), channel_id=1, source_target_pairs={{0,16},{16,0},{1,17},{17,1},{2,18},{18,2},{3,19},{19,3},{4,20},{20... | collective-permute-start | bytes 1376264 | tf_op jit(solution)/shard_map/ppermute | solution.py:231
  108.9 36.2 %copy-start.1 = (s32[128,1]{0,1:T(1,128)S(1)}, s32[128,1]{0,1:T(1,128)}, u32[]{:S(2)}) copy-start(s32[128,1]{0,1:T(1,128)} %param.9) | copy-start | bytes 1540
  108.9 36.2 %copy-start.2 = (f32[128,1]{0,1:T(1,128)S(1)}, f32[128,1]{0,1:T(1,128)}, u32[]{:S(2)}) copy-start(f32[128,1]{0,1:T(1,128)} %param.10) | copy-start | bytes 1540
  108.9 36.2 %all-to-all-start.3 = ((bf16[32,48,128]{2,1,0:T(8,128)(2,1)}), bf16[32,48,128]{2,1,0:T(8,128)(2,1)S(1)}, u32[]{:S(2)}, u32[]{:S(2)}) async-start(bf16[32,48,128]{2,1,0:T(8,128)(2,1)} %bitcast.4), calls=%async_computation.3 | async-start | bytes 786432 | tf_op jit(solution)/shard_map/all_to_all | solution.py:247
  124.8 13.8 %collective-permute-start.10 = (bf16[112,512]{1,0:T(8,128)(2,1)S(1)}, bf16[112,512]{1,0:T(8,128)(2,1)S(1)}, u32[]{:S(2)}, u32[]{:S(2)}) collective-permute-start(bf16[112,512]{1,0:T(8,128)(2,1)S(1)} %get-tuple-element.38), channel_id=1, source_target_pairs={{0,64},{32,96},{64,0},{96,32},{1,65},{33,97},{65,1},{97,33},{2,66}... | collective-permute-start | bytes 344072 | tf_op jit(solution)/shard_map/ppermute | solution.py:231
  126.7 12.4 %collective-permute-start.8 = (bf16[112,512]{1,0:T(8,128)(2,1)S(1)}, bf16[112,512]{1,0:T(8,128)(2,1)S(1)}, u32[]{:S(2)}, u32[]{:S(2)}) collective-permute-start(bf16[112,512]{1,0:T(8,128)(2,1)S(1)} %get-tuple-element.37), channel_id=1, source_target_pairs={{0,32},{32,64},{64,96},{96,0},{1,33},{33,65},{65,97},{97,1},{2,34}... | collective-permute-start | bytes 344072 | tf_op jit(solution)/shard_map/ppermute | solution.py:231
  136.7 7.6 %collective-permute-start.9 = (bf16[112,512]{1,0:T(8,128)(2,1)S(1)}, bf16[112,512]{1,0:T(8,128)(2,1)S(1)}, u32[]{:S(2)}, u32[]{:S(2)}) collective-permute-start(bf16[112,512]{1,0:T(8,128)(2,1)S(1)} %get-tuple-element.39), channel_id=1, source_target_pairs={{0,96},{32,0},{64,32},{96,64},{1,97},{33,1},{65,33},{97,65},{2,98}... | collective-permute-start | bytes 344072 | tf_op jit(solution)/shard_map/ppermute | solution.py:231

commit v14 on v13

--- a/solution.py
+++ b/solution.py
@@ -78,20 +78,22 @@
     ]
     for copy in copies:
         copy.start()
-    k, at = iota((EXPERTS, WIDE, 7 * TOK), 1), iota((EXPERTS, WIDE, 7 * TOK), 2)
+    shape = (EXPERTS, WIDE, 14 * SLAB)
+    k = iota(shape, 1)
     q = (k * 43) >> 9
     k = k - 12 * q
-    order = q * TOK + iota((EXPERTS, WIDE, 7 * TOK), 0) * 16 + k + jnp.where(k >= CAP, 2, 0)
-    order = onehot(at == order).reshape(EXPERTS * WIDE, 7 * TOK)
+    order = q * (2 * SLAB) + iota(shape, 0) * CAP + k + jnp.where(k >= CAP, SLAB - CAP, 0)
+    order = onehot(iota(shape, 2) == order).reshape(EXPERTS * WIDE, 14 * SLAB)
     for copy in copies:
         copy.wait()
     ids = ids_ref[...]
-    slot = jnp.where(ids < EXPERTS, ids * 16 + token_ranks(ids), -16)
-    at = iota((TOK, TOK), 0)
-    sel = jnp.concatenate([onehot(slot == at), onehot(slot + 8 == at)], axis=1)
+    slot = jnp.where(ids < EXPERTS, ids * CAP + token_ranks(ids), -1)
+    sel = onehot(slot == iota((SLAB, TOK), 0))
     scaled = (to_column(p_ref[...]) * g_ref[...].astype(F32)).astype(BF)
-    both = jnp.concatenate([x_ref[...], scaled], axis=0)
-    rows = jnp.dot(sel, both, preferred_element_type=F32).astype(BF)
+    rows = jnp.concatenate([
+        jnp.dot(sel, x_ref[...], preferred_element_type=F32).astype(BF),
+        jnp.dot(sel, scaled, preferred_element_type=F32).astype(BF),
+    ], axis=0)
     for i in range(2):
         stack = []
         for q in range(7):

time: 148 us -> 147 us (level)
  no operation moved by 1% of the time
where the time goes in v14:
time: 147 us
  starting transfers between devices  68.2 us (46%)
  waiting for transfers between devices  34.9 us (24%)
  blocking collectives  28.6 us (19%)
  Pallas kernels  13.3 us (9%)
    all_to_all x2, blocking collectives, exchange(): return lax.all_to_all(a, axes, split_axis=0, concat_axis=0, tiled=True)  28.6 us
    ppermute x8, starting transfers between devices, hop(): return lax.ppermute(a, axis, [(i, (i + shift) % n) for i in range(n)])  26.4 us
    all_to_all x2, starting transfers between devices, exchange(): return lax.all_to_all(a, axes, split_axis=0, concat_axis=0, tiled=True)  26.2 us
    ppermute x8, waiting for transfers between devices, hop(): return lax.ppermute(a, axis, [(i, (i + shift) % n) for i in range(n)])  20.3 us
    ppermute x3, starting transfers between devices, turn(): return lax.ppermute(a, (axis, 'c'), pairs)  15.6 us
    all_to_all x2, waiting for transfers between devices, exchange(): return lax.all_to_all(a, axes, split_axis=0, concat_axis=0, tiled=True)  14.6 us
    pallas_call x9, Pallas kernels, call(): pl.pallas_call(body, in_specs=specs or [VMEM] * len(operands), out_specs=...  13.3 us
  transfers between devices with their start and end apart: 13, of which 6 were waited for; matrix products, arithmetic and copies ran while one was open for 1% of the time, Pallas kernels for 4%

profile of v14, /device:TPU:6, one launch (start us, length us, event | category | flops | bytes accessed | tf_op | source)
XLA Modules:
  0.0 146.7 jit_solution(17622758171498281359)
XLA Ops:
  0.6 1.8 %stack.1.own_ref = bf16[112,1536]{1,0:T(8,128)(2,1)} custom-call(bf16[112,512]{1,0:T(8,128)(2,1)} %a_hbm.1, bf16[112,512]{1,0:T(8,128)(2,1)} %b_hbm.1, bf16[112,512]{1,0:T(8,128)(2,1)} %c_hbm.1), custom_call_target="tpu_custom_call" | custom-call | flops 1000000 | bytes 4000000 | tf_op jit(solution)/shard_map/stack/pallas_call | solution.py:62
  2.4 6.1 %collective-permute-start.1 = (bf16[112,1536]{1,0:T(8,128)(2,1)}, bf16[112,1536]{1,0:T(8,128)(2,1)S(1)}, u32[]{:S(2)}, u32[]{:S(2)}) collective-permute-start(bf16[112,1536]{1,0:T(8,128)(2,1)} %stack.1.own_ref), channel_id=1, source_target_pairs={{0,32},{16,112},{32,64},{48,16},{64,96},{80,48},{96,0},{112,80},{1... | collective-permute-start | bytes 1032200 | tf_op jit(solution)/shard_map/ppermute | solution.py:241
  8.5 6.8 %collective-permute-start.2 = (bf16[112,1536]{1,0:T(8,128)(2,1)}, bf16[112,1536]{1,0:T(8,128)(2,1)S(1)}, u32[]{:S(2)}, u32[]{:S(2)}) collective-permute-start(bf16[112,1536]{1,0:T(8,128)(2,1)} %stack.1.own_ref), channel_id=1, source_target_pairs={{0,96},{16,48},{32,0},{48,80},{64,32},{80,112},{96,64},{112,16},{1... | collective-permute-start | bytes 1032200 | tf_op jit(solution)/shard_map/ppermute | solution.py:241
  15.3 3.6 %dispatch.1 = bf16[4,8,88,128]{3,2,1,0:T(8,128)(2,1)} custom-call(s32[1,128]{1,0:T(1,128)} %bitcast.30, f32[1,128]{1,0:T(1,128)} %bitcast.32, bf16[128,3584]{1,0:T(8,128)(2,1)} %x_hbm.1, bf16[128,3584]{1,0:T(8,128)(2,1)} %g_hbm.1), custom_call_target="tpu_custom_call" | custom-call | flops 1000000000 | bytes 4000000 | tf_op jit(solution)/shard_map/dispatch/pallas_call | solution.py:62
  18.9 0.0 copy-start
  18.9 10.4 %all-to-all-start = ((bf16[32,88,128]{2,1,0:T(8,128)(2,1)}), bf16[32,88,128]{2,1,0:T(8,128)(2,1)S(1)}, u32[]{:S(2)}, u32[]{:S(2)}) async-start(bf16[32,88,128]{2,1,0:T(8,128)(2,1)} %bitcast.34), calls=%async_computation | async-start | bytes 1441792 | tf_op jit(solution)/shard_map/all_to_all | solution.py:249
  29.3 0.0 collective-permute-done.1.before_ref
  29.3 0.0 collective-permute-done.2.after_ref
  29.3 0.0 copy-done
  29.3 0.1 near.1
  29.4 1.9 %collective-permute-start.3 = (bf16[336,1536]{1,0:T(8,128)(2,1)S(1)}, bf16[336,1536]{1,0:T(8,128)(2,1)S(1)}, u32[]{:S(2)}, u32[]{:S(2)}) collective-permute-start(bf16[336,1536]{1,0:T(8,128)(2,1)S(1)} %get-tuple-element.20.near_ref), channel_id=1, source_target_pairs={{0,16},{16,0},{1,17},{17,1},{2,18},{18,2},{3,19},{19,3},{4,20},{20... | collective-permute-start | bytes 3096584 | tf_op jit(solution)/shard_map/ppermute | solution.py:233
  31.3 2.8 %collective-permute-start.4 = (bf16[112,1536]{1,0:T(8,128)(2,1)S(1)}, bf16[112,1536]{1,0:T(8,128)(2,1)S(1)}, u32[]{:S(2)}, u32[]{:S(2)}) collective-permute-start(bf16[112,1536]{1,0:T(8,128)(2,1)S(1)} %get-tuple-element.21), channel_id=1, source_target_pairs={{0,32},{16,112},{32,64},{48,16},{64,96},{80,48},{96,0},{112,80},{1... | collective-permute-start | bytes 1032200 | tf_op jit(solution)/shard_map/ppermute | solution.py:241
  34.1 14.6 %all-to-all-done = bf16[32,88,128]{2,1,0:T(8,128)(2,1)S(1)} async-done(((bf16[32,88,128]{2,1,0:T(8,128)(2,1)}), bf16[32,88,128]{2,1,0:T(8,128)(2,1)S(1)}, u32[]{:S(2)}, u32[]{:S(2)}) %all-to-all-start) | async-done | bytes 720928 | tf_op jit(solution)/shard_map/all_to_all | solution.py:249
  48.7 3.4 %collective-permute-start = (bf16[4,704,128]{2,1,0:T(8,128)(2,1)S(1)}, bf16[4,704,128]{2,1,0:T(8,128)(2,1)S(1)}, u32[]{:S(2)}, u32[]{:S(2)}) collective-permute-start(bf16[4,704,128]{2,1,0:T(8,128)(2,1)S(1)} %bitcast.27), channel_id=1, source_target_pairs={{0,1},{1,0},{2,3},{3,2},{4,5},{5,4},{6,7},{7,6},{8,9},{9,8},{10,11... | collective-permute-start | bytes 2162696 | tf_op jit(solution)/shard_map/ppermute | solution.py:233
  52.1 0.0 collective-permute-done.4.far_ref
  52.1 1.9 %collective-permute-start.5 = (bf16[112,1536]{1,0:T(8,128)(2,1)S(1)}, bf16[112,1536]{1,0:T(8,128)(2,1)S(1)}, u32[]{:S(2)}, u32[]{:S(2)}) collective-permute-start(bf16[112,1536]{1,0:T(8,128)(2,1)S(1)} %collective-permute-done.4.far_ref), channel_id=1, source_target_pairs={{0,16},{16,0},{1,17},{17,1},{2,18},{18,2},{3,19},{19,3},{4,20},{20... | collective-permute-start | bytes 1032200 | tf_op jit(solution)/shard_map/ppermute | solution.py:233
  54.0 1.6 %collective-permute-done.5.far_other_ref = bf16[112,1536]{1,0:T(8,128)(2,1)S(1)} collective-permute-done((bf16[112,1536]{1,0:T(8,128)(2,1)S(1)}, bf16[112,1536]{1,0:T(8,128)(2,1)S(1)}, u32[]{:S(2)}, u32[]{:S(2)}) %collective-permute-start.5) | collective-permute-done | bytes 344096 | tf_op jit(solution)/shard_map/ppermute | solution.py:233
  55.6 0.0 collective-permute-done.3.near_other_ref
  55.6 0.4 assemble.1
  56.0 8.7 %collective-permute-done.other_ref = bf16[4,704,128]{2,1,0:T(8,128)(2,1)S(1)} collective-permute-done((bf16[4,704,128]{2,1,0:T(8,128)(2,1)S(1)}, bf16[4,704,128]{2,1,0:T(8,128)(2,1)S(1)}, u32[]{:S(2)}, u32[]{:S(2)}) %collective-permute-start) | collective-permute-done | bytes 720928 | tf_op jit(solution)/shard_map/ppermute | solution.py:233
  64.7 2.5 %before.1 = (bf16[4,96,1536]{2,1,0:T(8,128)(2,1)S(1)}, bf16[384,896]{1,0:T(8,128)(2,1)S(1)}) custom-call(bf16[4,704,128]{2,1,0:T(8,128)(2,1)S(1)} %bitcast.28, bf16[4,704,128]{2,1,0:T(8,128)(2,1)S(1)} %collective-permute-done.other_ref, bf16[896,1536]{1,0:T(8,128)(2,1)S(1)} %get-tuple-element.22.weight_ref, bf16[672,704]{1,0:T(8,128)(2,1)S(1)} %get-tuple-element.23.pick_ref), custom_call_target="tpu_custom_call" | custom-call | flops 2000000000 | bytes 4000000 | tf_op jit(solution)/shard_map/before/pallas_call | solution.py:62
  67.2 14.6 %all_to_all.20.part_ref = bf16[4,96,1536]{2,1,0:T(8,128)(2,1)S(1)} all-to-all(bf16[4,96,1536]{2,1,0:T(8,128)(2,1)S(1)} %get-tuple-element.24), channel_id=1, replica_groups=mesh['x'=4,'zh'=4,'c'=2,'y'=8,'zl'=2] {'x'}, dimensions={0} | all-to-all | bytes 2359296 | tf_op jit(solution)/shard_map/all_to_all | solution.py:249
  81.8 0.3 middle.1
  82.2 14.0 %all_to_all.21.mid_ref = bf16[4,96,1536]{2,1,0:T(8,128)(2,1)S(1)} all-to-all(bf16[4,96,1536]{2,1,0:T(8,128)(2,1)S(1)} %get-tuple-element.25), channel_id=1, replica_groups=mesh['x'=4,'zh'=4,'c'=2,'y'=8,'zl'=2] {'x'}, dimensions={0} | all-to-all | bytes 2359296 | tf_op jit(solution)/shard_map/all_to_all | solution.py:249
  96.2 1.7 %after.1 = (bf16[4,48,1024]{2,1,0:T(8,128)(2,1)S(1)}, bf16[4,48,1024]{2,1,0:T(8,128)(2,1)S(1)}, bf16[112,512]{1,0:T(8,128)(2,1)S(1)}, bf16[112,512]{1,0:T(8,128)...) custom-call(bf16[4,96,1536]{2,1,0:T(8,128)(2,1)S(1)} %all_to_all.21.mid_ref,, ...), custom_call_target="tpu_custom_call" | custom-call | flops 1400000000 | bytes 4000000 | tf_op jit(solution)/shard_map/after/pallas_call | solution.py:62
  97.9 3.4 %collective-permute-start.6 = (bf16[4,48,1024]{2,1,0:T(8,128)(2,1)S(1)}, bf16[4,48,1024]{2,1,0:T(8,128)(2,1)S(1)}, u32[]{:S(2)}, u32[]{:S(2)}) collective-permute-start(bf16[4,48,1024]{2,1,0:T(8,128)(2,1)S(1)} %get-tuple-element.29), channel_id=1, source_target_pairs={{0,1},{1,0},{2,3},{3,2},{4,5},{5,4},{6,7},{7,6},{8,9},{9,8},{10,11... | collective-permute-start | bytes 1179656 | tf_op jit(solution)/shard_map/ppermute | solution.py:233
  101.3 1.9 %collective-permute-start.7 = (bf16[4,112,512]{2,1,0:T(8,128)(2,1)S(1)}, bf16[4,112,512]{2,1,0:T(8,128)(2,1)S(1)}, u32[]{:S(2)}, u32[]{:S(2)}) collective-permute-start(bf16[4,112,512]{2,1,0:T(8,128)(2,1)S(1)} %get-tuple-element.33), channel_id=1, source_target_pairs={{0,16},{16,0},{1,17},{17,1},{2,18},{18,2},{3,19},{19,3},{4,20},{20... | collective-permute-start | bytes 1376264 | tf_op jit(solution)/shard_map/ppermute | solution.py:233
  103.2 4.3 %collective-permute-done.6.got_ref = bf16[4,48,1024]{2,1,0:T(8,128)(2,1)S(1)} collective-permute-done((bf16[4,48,1024]{2,1,0:T(8,128)(2,1)S(1)}, bf16[4,48,1024]{2,1,0:T(8,128)(2,1)S(1)}, u32[]{:S(2)}, u32[]{:S(2)}) %collective-permute-start.6) | collective-permute-done | bytes 393248 | tf_op jit(solution)/shard_map/ppermute | solution.py:233
  107.6 1.2 combine.1
  108.7 0.0 copy-start.1
  108.7 0.0 copy-start.2
  108.7 15.8 %all-to-all-start.3 = ((bf16[32,48,128]{2,1,0:T(8,128)(2,1)}), bf16[32,48,128]{2,1,0:T(8,128)(2,1)S(1)}, u32[]{:S(2)}, u32[]{:S(2)}) async-start(bf16[32,48,128]{2,1,0:T(8,128)(2,1)} %bitcast.4), calls=%async_computation.3 | async-start | bytes 786432 | tf_op jit(solution)/shard_map/all_to_all | solution.py:249
  124.6 0.0 collective-permute-done.7
  124.6 0.1 fusion.3
  124.7 1.9 %collective-permute-start.10 = (bf16[112,512]{1,0:T(8,128)(2,1)S(1)}, bf16[112,512]{1,0:T(8,128)(2,1)S(1)}, u32[]{:S(2)}, u32[]{:S(2)}) collective-permute-start(bf16[112,512]{1,0:T(8,128)(2,1)S(1)} %get-tuple-element.38), channel_id=1, source_target_pairs={{0,64},{32,96},{64,0},{96,32},{1,65},{33,97},{65,1},{97,33},{2,66}... | collective-permute-start | bytes 344072 | tf_op jit(solution)/shard_map/ppermute | solution.py:233
  126.6 10.0 %collective-permute-start.8 = (bf16[112,512]{1,0:T(8,128)(2,1)S(1)}, bf16[112,512]{1,0:T(8,128)(2,1)S(1)}, u32[]{:S(2)}, u32[]{:S(2)}) collective-permute-start(bf16[112,512]{1,0:T(8,128)(2,1)S(1)} %get-tuple-element.37), channel_id=1, source_target_pairs={{0,32},{32,64},{64,96},{96,0},{1,33},{33,65},{65,97},{97,1},{2,34}... | collective-permute-start | bytes 344072 | tf_op jit(solution)/shard_map/ppermute | solution.py:233
  136.6 1.9 %collective-permute-start.9 = (bf16[112,512]{1,0:T(8,128)(2,1)S(1)}, bf16[112,512]{1,0:T(8,128)(2,1)S(1)}, u32[]{:S(2)}, u32[]{:S(2)}) collective-permute-start(bf16[112,512]{1,0:T(8,128)(2,1)S(1)} %get-tuple-element.39), channel_id=1, source_target_pairs={{0,96},{32,0},{64,32},{96,64},{1,97},{33,1},{65,33},{97,65},{2,98}... | collective-permute-start | bytes 344072 | tf_op jit(solution)/shard_map/ppermute | solution.py:233
  138.5 0.0 collective-permute-done.10
  138.5 0.5 collective-permute-done.8
  139.0 5.2 %collective-permute-done.9 = bf16[112,512]{1,0:T(8,128)(2,1)S(1)} collective-permute-done((bf16[112,512]{1,0:T(8,128)(2,1)S(1)}, bf16[112,512]{1,0:T(8,128)(2,1)S(1)}, u32[]{:S(2)}, u32[]{:S(2)}) %collective-permute-start.9) | collective-permute-done | bytes 114720 | tf_op jit(solution)/shard_map/ppermute | solution.py:233
  144.2 0.7 add_convert_fusion
  144.9 0.0 all-to-all-done.3
  144.9 0.0 copy-done.1
  144.9 0.0 copy-done.2
  144.9 1.8 %finish.1 = (bf16[128,3584]{1,0:T(8,128)(2,1)}, f32[1,128]{1,0:T(1,128)}) custom-call(s32[1,128]{1,0:T(1,128)S(1)} %bitcast.31, f32[1,128]{1,0:T(1,128)S(1)} %bitcast.33, bf16[4,384,128]{2,1,0:T(8,128)(2,1)S(1)} %bitcast.29), custom_call_target="tpu_custom_call" | custom-call | flops 400000000 | bytes 4000000 | tf_op jit(solution)/shard_map/finish/pallas_call | solution.py:62
Async XLA Ops:
  2.4 26.9 %collective-permute-start.1 = (bf16[112,1536]{1,0:T(8,128)(2,1)}, bf16[112,1536]{1,0:T(8,128)(2,1)S(1)}, u32[]{:S(2)}, u32[]{:S(2)}) collective-permute-start(bf16[112,1536]{1,0:T(8,128)(2,1)} %stack.1.own_ref), channel_id=1, source_target_pairs={{0,32},{16,112},{32,64},{48,16},{64,96},{80,48},{96,0},{112,80},{1... | collective-permute-start | bytes 1032200 | tf_op jit(solution)/shard_map/ppermute | solution.py:241
  8.5 20.8 %collective-permute-start.2 = (bf16[112,1536]{1,0:T(8,128)(2,1)}, bf16[112,1536]{1,0:T(8,128)(2,1)S(1)}, u32[]{:S(2)}, u32[]{:S(2)}) collective-permute-start(bf16[112,1536]{1,0:T(8,128)(2,1)} %stack.1.own_ref), channel_id=1, source_target_pairs={{0,96},{16,48},{32,0},{48,80},{64,32},{80,112},{96,64},{112,16},{1... | collective-permute-start | bytes 1032200 | tf_op jit(solution)/shard_map/ppermute | solution.py:241
  18.9 10.4 %copy-start = (bf16[112,1536]{1,0:T(8,128)(2,1)S(1)}, bf16[112,1536]{1,0:T(8,128)(2,1)}, u32[]{:S(2)}) copy-start(bf16[112,1536]{1,0:T(8,128)(2,1)} %stack.1.own_ref) | copy-start | bytes 1032196
  18.9 29.8 %all-to-all-start = ((bf16[32,88,128]{2,1,0:T(8,128)(2,1)}), bf16[32,88,128]{2,1,0:T(8,128)(2,1)S(1)}, u32[]{:S(2)}, u32[]{:S(2)}) async-start(bf16[32,88,128]{2,1,0:T(8,128)(2,1)} %bitcast.34), calls=%async_computation | async-start | bytes 1441792 | tf_op jit(solution)/shard_map/all_to_all | solution.py:249
  29.4 26.2 %collective-permute-start.3 = (bf16[336,1536]{1,0:T(8,128)(2,1)S(1)}, bf16[336,1536]{1,0:T(8,128)(2,1)S(1)}, u32[]{:S(2)}, u32[]{:S(2)}) collective-permute-start(bf16[336,1536]{1,0:T(8,128)(2,1)S(1)} %get-tuple-element.20.near_ref), channel_id=1, source_target_pairs={{0,16},{16,0},{1,17},{17,1},{2,18},{18,2},{3,19},{19,3},{4,20},{20... | collective-permute-start | bytes 3096584 | tf_op jit(solution)/shard_map/ppermute | solution.py:233
  31.3 20.8 %collective-permute-start.4 = (bf16[112,1536]{1,0:T(8,128)(2,1)S(1)}, bf16[112,1536]{1,0:T(8,128)(2,1)S(1)}, u32[]{:S(2)}, u32[]{:S(2)}) collective-permute-start(bf16[112,1536]{1,0:T(8,128)(2,1)S(1)} %get-tuple-element.21), channel_id=1, source_target_pairs={{0,32},{16,112},{32,64},{48,16},{64,96},{80,48},{96,0},{112,80},{1... | collective-permute-start | bytes 1032200 | tf_op jit(solution)/shard_map/ppermute | solution.py:241
  48.7 16.0 %collective-permute-start = (bf16[4,704,128]{2,1,0:T(8,128)(2,1)S(1)}, bf16[4,704,128]{2,1,0:T(8,128)(2,1)S(1)}, u32[]{:S(2)}, u32[]{:S(2)}) collective-permute-start(bf16[4,704,128]{2,1,0:T(8,128)(2,1)S(1)} %bitcast.27), channel_id=1, source_target_pairs={{0,1},{1,0},{2,3},{3,2},{4,5},{5,4},{6,7},{7,6},{8,9},{9,8},{10,11... | collective-permute-start | bytes 2162696 | tf_op jit(solution)/shard_map/ppermute | solution.py:233
  52.1 3.5 %collective-permute-start.5 = (bf16[112,1536]{1,0:T(8,128)(2,1)S(1)}, bf16[112,1536]{1,0:T(8,128)(2,1)S(1)}, u32[]{:S(2)}, u32[]{:S(2)}) collective-permute-start(bf16[112,1536]{1,0:T(8,128)(2,1)S(1)} %collective-permute-done.4.far_ref), channel_id=1, source_target_pairs={{0,16},{16,0},{1,17},{17,1},{2,18},{18,2},{3,19},{19,3},{4,20},{20... | collective-permute-start | bytes 1032200 | tf_op jit(solution)/shard_map/ppermute | solution.py:233
  97.9 9.7 %collective-permute-start.6 = (bf16[4,48,1024]{2,1,0:T(8,128)(2,1)S(1)}, bf16[4,48,1024]{2,1,0:T(8,128)(2,1)S(1)}, u32[]{:S(2)}, u32[]{:S(2)}) collective-permute-start(bf16[4,48,1024]{2,1,0:T(8,128)(2,1)S(1)} %get-tuple-element.29), channel_id=1, source_target_pairs={{0,1},{1,0},{2,3},{3,2},{4,5},{5,4},{6,7},{7,6},{8,9},{9,8},{10,11... | collective-permute-start | bytes 1179656 | tf_op jit(solution)/shard_map/ppermute | solution.py:233
  101.3 23.2 %collective-permute-start.7 = (bf16[4,112,512]{2,1,0:T(8,128)(2,1)S(1)}, bf16[4,112,512]{2,1,0:T(8,128)(2,1)S(1)}, u32[]{:S(2)}, u32[]{:S(2)}) collective-permute-start(bf16[4,112,512]{2,1,0:T(8,128)(2,1)S(1)} %get-tuple-element.33), channel_id=1, source_target_pairs={{0,16},{16,0},{1,17},{17,1},{2,18},{18,2},{3,19},{19,3},{4,20},{20... | collective-permute-start | bytes 1376264 | tf_op jit(solution)/shard_map/ppermute | solution.py:233
  108.7 36.2 %copy-start.1 = (s32[128,1]{0,1:T(1,128)S(1)}, s32[128,1]{0,1:T(1,128)}, u32[]{:S(2)}) copy-start(s32[128,1]{0,1:T(1,128)} %param.9) | copy-start | bytes 1540
  108.7 36.2 %copy-start.2 = (f32[128,1]{0,1:T(1,128)S(1)}, f32[128,1]{0,1:T(1,128)}, u32[]{:S(2)}) copy-start(f32[128,1]{0,1:T(1,128)} %param.10) | copy-start | bytes 1540
  108.7 36.2 %all-to-all-start.3 = ((bf16[32,48,128]{2,1,0:T(8,128)(2,1)}), bf16[32,48,128]{2,1,0:T(8,128)(2,1)S(1)}, u32[]{:S(2)}, u32[]{:S(2)}) async-start(bf16[32,48,128]{2,1,0:T(8,128)(2,1)} %bitcast.4), calls=%async_computation.3 | async-start | bytes 786432 | tf_op jit(solution)/shard_map/all_to_all | solution.py:249
  124.7 13.8 %collective-permute-start.10 = (bf16[112,512]{1,0:T(8,128)(2,1)S(1)}, bf16[112,512]{1,0:T(8,128)(2,1)S(1)}, u32[]{:S(2)}, u32[]{:S(2)}) collective-permute-start(bf16[112,512]{1,0:T(8,128)(2,1)S(1)} %get-tuple-element.38), channel_id=1, source_target_pairs={{0,64},{32,96},{64,0},{96,32},{1,65},{33,97},{65,1},{97,33},{2,66}... | collective-permute-start | bytes 344072 | tf_op jit(solution)/shard_map/ppermute | solution.py:233
  126.6 12.4 %collective-permute-start.8 = (bf16[112,512]{1,0:T(8,128)(2,1)S(1)}, bf16[112,512]{1,0:T(8,128)(2,1)S(1)}, u32[]{:S(2)}, u32[]{:S(2)}) collective-permute-start(bf16[112,512]{1,0:T(8,128)(2,1)S(1)} %get-tuple-element.37), channel_id=1, source_target_pairs={{0,32},{32,64},{64,96},{96,0},{1,33},{33,65},{65,97},{97,1},{2,34}... | collective-permute-start | bytes 344072 | tf_op jit(solution)/shard_map/ppermute | solution.py:233
  136.6 7.6 %collective-permute-start.9 = (bf16[112,512]{1,0:T(8,128)(2,1)S(1)}, bf16[112,512]{1,0:T(8,128)(2,1)S(1)}, u32[]{:S(2)}, u32[]{:S(2)}) collective-permute-start(bf16[112,512]{1,0:T(8,128)(2,1)S(1)} %get-tuple-element.39), channel_id=1, source_target_pairs={{0,96},{32,0},{64,32},{96,64},{1,97},{33,1},{65,33},{97,65},{2,98}... | collective-permute-start | bytes 344072 | tf_op jit(solution)/shard_map/ppermute | solution.py:233

commit v15 on v14

--- a/solution.py
+++ b/solution.py
@@ -116,10 +116,10 @@
         copy.wait()
 
 
-def near_kernel(own_ref, before_ref, after_ref, out_ref, before_out):
+def near_kernel(own_ref, before_ref, after_ref, out_ref, after_out):
     for i, ref in enumerate((own_ref, before_ref, after_ref)):
         out_ref[i * SHARD:(i + 1) * SHARD] = ref[...]
-    before_out[...] = before_ref[...]
+    after_out[...] = after_ref[...]
 
 
 def assemble_kernel(near_ref, near_other_ref, far_ref, far_other_ref, out_ref, pick_ref):
@@ -130,10 +130,10 @@
     pick_ref[...] = onehot(iota(shape, 3) == place).reshape(14 * SLAB, WIDER)
     zi, ci = lax.axis_index("zh"), lax.axis_index("c")
     for core, near, far in ((ci, near_ref, far_ref), (1 - ci, near_other_ref, far_other_ref)):
-        for i, shift in enumerate((0, 3, 1, 2)):
+        for i, shift in enumerate((0, 3, 2, 1)):
             block = lax.rem(zi + jnp.where(core == 0, shift, 4 - shift), 4)
             at = pl.multiple_of((2 * block + core) * SHARD, 16)
-            out_ref[pl.ds(at, SHARD)] = far[...] if shift == 2 else near[i * SHARD:(i + 1) * SHARD]
+            out_ref[pl.ds(at, SHARD)] = far[...] if i == 3 else near[i * SHARD:(i + 1) * SHARD]
 
 
 def before_kernel(mine_ref, other_ref, weight_ref, pick_ref, part_ref, g_ref, x_scr):
@@ -260,13 +260,14 @@
     )
     rows = exchange(sent.reshape(32, WIDE, TOK), PEERS).reshape(4, WIDER, TOK)
 
-    z_before, z_after = turn(weights, "zh", 1), turn(weights, "zh", -1)
+    first = turn(weights, "zh", 1)
+    second = turn(first, "zh", 1)
     near, passed = call(near_kernel, "near", [((3 * SHARD, 3 * HALF), BF), ((SHARD, 3 * HALF), BF)],
-                        (weights, z_before, z_after), 4 * 10**9)
+                        (weights, first, second), 4 * 10**9)
     far = turn(passed, "zh", 1)
     rows_other = hop(rows, "zl", 1)
     weights, pick = call(assemble_kernel, "assemble", [((PART, 3 * HALF), BF), ((14 * SLAB, WIDER), BF)],
-                    (near, hop(near, "c", 1), far, hop(far, "c", 1)), 4 * 10**9)
+                    (near, hop(near, "c", 1), far, hop(far, "c", 1)), 2 * 10**9)
 
     dense = pltpu.VMEM((4 * ROWS, PART), BF)
     part, g_rows = call(

time: 147 us -> 156 us (1.061)
  blocking collectives: 28.6 us -> 37.4 us
  starting transfers between devices: 68.2 us -> 63.7 us
  waiting for transfers between devices: 34.9 us -> 38.7 us
    ppermute x3, waiting for transfers between devices: 0.01 us -> 16.8 us  [turn(): return lax.ppermute(a, (axis, 'c'), pairs)]
    all_to_all x2, waiting for transfers between devices: 14.6 us -> 0.01 us  [exchange(): return lax.all_to_all(a, axes, split_axis=0, concat_axis=0, tiled=True)]
    all_to_all x2, blocking collectives: 28.6 us -> 37.4 us  [exchange(): return lax.all_to_all(a, axes, split_axis=0, concat_axis=0, tiled=True)]
    all_to_all x2, starting transfers between devices: 26.2 us -> 20 us  [exchange(): return lax.all_to_all(a, axes, split_axis=0, concat_axis=0, tiled=True)]
    ppermute x3, starting transfers between devices: 15.6 us -> 18 us  [turn(): return lax.ppermute(a, (axis, 'c'), pairs)]
    ppermute x8, waiting for transfers between devices: 20.3 us -> 21.9 us  [hop(): return lax.ppermute(a, axis, [(i, (i + shift) % n) for i in range(n)])]
  transfers between devices with their start and end apart: 13 -> 13, of which waited for: 6 -> 7; matrix products, arithmetic and copies ran while one was open for 1% -> 1% of each run, Pallas kernels for 4% -> 3%
where the time goes in v15:
time: 156 us; the launch traced here: 155 us
  starting transfers between devices  63.7 us (41%)
  waiting for transfers between devices  38.7 us (25%)
  blocking collectives  37.4 us (24%)
  Pallas kernels  13.4 us (9%)
    all_to_all x2, blocking collectives, exchange(): return lax.all_to_all(a, axes, split_axis=0, concat_axis=0, tiled=True)  37.4 us
    ppermute x8, starting transfers between devices, hop(): return lax.ppermute(a, axis, [(i, (i + shift) % n) for i in range(n)])  25.7 us
    ppermute x8, waiting for transfers between devices, hop(): return lax.ppermute(a, axis, [(i, (i + shift) % n) for i in range(n)])  21.9 us
    all_to_all x2, starting transfers between devices, exchange(): return lax.all_to_all(a, axes, split_axis=0, concat_axis=0, tiled=True)  20 us
    ppermute x3, starting transfers between devices, turn(): return lax.ppermute(a, (axis, 'c'), pairs)  18 us
    ppermute x3, waiting for transfers between devices, turn(): return lax.ppermute(a, (axis, 'c'), pairs)  16.8 us
    pallas_call x9, Pallas kernels, call(): pl.pallas_call(body, in_specs=specs or [VMEM] * len(operands), out_specs=...  13.4 us
  transfers between devices with their start and end apart: 13, of which 7 were waited for; matrix products, arithmetic and copies ran while one was open for 1% of the time, Pallas kernels for 3%

profile of v15, /device:TPU:6, one launch (start us, length us, event | category | flops | bytes accessed | tf_op | source)
XLA Modules:
  0.0 154.9 jit_solution(6732538248805839577)
XLA Ops:
  0.6 1.8 %stack.1.own_ref = bf16[112,1536]{1,0:T(8,128)(2,1)} custom-call(bf16[112,512]{1,0:T(8,128)(2,1)} %a_hbm.1, bf16[112,512]{1,0:T(8,128)(2,1)} %b_hbm.1, bf16[112,512]{1,0:T(8,128)(2,1)} %c_hbm.1), custom_call_target="tpu_custom_call" | custom-call | flops 1000000 | bytes 4000000 | tf_op jit(solution)/shard_map/stack/pallas_call | solution.py:62
  2.4 6.1 %collective-permute-start.1 = (bf16[112,1536]{1,0:T(8,128)(2,1)}, bf16[112,1536]{1,0:T(8,128)(2,1)S(1)}, u32[]{:S(2)}, u32[]{:S(2)}) collective-permute-start(bf16[112,1536]{1,0:T(8,128)(2,1)} %stack.1.own_ref), channel_id=1, source_target_pairs={{0,32},{16,112},{32,64},{48,16},{64,96},{80,48},{96,0},{112,80},{1... | collective-permute-start | bytes 1032200 | tf_op jit(solution)/shard_map/ppermute | solution.py:241
  8.5 3.6 %dispatch.1 = bf16[4,8,88,128]{3,2,1,0:T(8,128)(2,1)} custom-call(s32[1,128]{1,0:T(1,128)} %bitcast.30, f32[1,128]{1,0:T(1,128)} %bitcast.32, bf16[128,3584]{1,0:T(8,128)(2,1)} %x_hbm.1, bf16[128,3584]{1,0:T(8,128)(2,1)} %g_hbm.1), custom_call_target="tpu_custom_call" | custom-call | flops 1000000000 | bytes 4000000 | tf_op jit(solution)/shard_map/dispatch/pallas_call | solution.py:62
  12.1 0.0 copy-start
  12.1 10.4 %all-to-all-start = ((bf16[32,88,128]{2,1,0:T(8,128)(2,1)}), bf16[32,88,128]{2,1,0:T(8,128)(2,1)S(1)}, u32[]{:S(2)}, u32[]{:S(2)}) async-start(bf16[32,88,128]{2,1,0:T(8,128)(2,1)} %bitcast.34), calls=%async_computation | async-start | bytes 1441792 | tf_op jit(solution)/shard_map/all_to_all | solution.py:249
  22.5 0.0 collective-permute-done.1.before_ref
  22.5 7.3 %collective-permute-start.2 = (bf16[112,1536]{1,0:T(8,128)(2,1)S(1)}, bf16[112,1536]{1,0:T(8,128)(2,1)S(1)}, u32[]{:S(2)}, u32[]{:S(2)}) collective-permute-start(bf16[112,1536]{1,0:T(8,128)(2,1)S(1)} %collective-permute-done.1.before_ref), channel_id=1, source_target_pairs={{0,32},{16,112},{32,64},{48,16},{64,96},{80,48},{96,0},{112,80},{1... | collective-permute-start | bytes 1032200 | tf_op jit(solution)/shard_map/ppermute | solution.py:241
  29.8 8.4 %collective-permute-done.2.after_ref = bf16[112,1536]{1,0:T(8,128)(2,1)S(1)} collective-permute-done((bf16[112,1536]{1,0:T(8,128)(2,1)S(1)}, bf16[112,1536]{1,0:T(8,128)(2,1)S(1)}, u32[]{:S(2)}, u32[]{:S(2)}) %collective-permute-start.2) | collective-permute-done | bytes 344096 | tf_op jit(solution)/shard_map/ppermute | solution.py:241
  38.2 0.0 copy-done
  38.2 0.1 near.1
  38.3 2.7 %collective-permute-start.3 = (bf16[336,1536]{1,0:T(8,128)(2,1)S(1)}, bf16[336,1536]{1,0:T(8,128)(2,1)S(1)}, u32[]{:S(2)}, u32[]{:S(2)}) collective-permute-start(bf16[336,1536]{1,0:T(8,128)(2,1)S(1)} %get-tuple-element.20.near_ref), channel_id=1, source_target_pairs={{0,16},{16,0},{1,17},{17,1},{2,18},{18,2},{3,19},{19,3},{4,20},{20... | collective-permute-start | bytes 3096584 | tf_op jit(solution)/shard_map/ppermute | solution.py:233
  41.0 4.6 %collective-permute-start.4 = (bf16[112,1536]{1,0:T(8,128)(2,1)S(1)}, bf16[112,1536]{1,0:T(8,128)(2,1)S(1)}, u32[]{:S(2)}, u32[]{:S(2)}) collective-permute-start(bf16[112,1536]{1,0:T(8,128)(2,1)S(1)} %get-tuple-element.21), channel_id=1, source_target_pairs={{0,32},{16,112},{32,64},{48,16},{64,96},{80,48},{96,0},{112,80},{1... | collective-permute-start | bytes 1032200 | tf_op jit(solution)/shard_map/ppermute | solution.py:241
  45.6 0.0 all-to-all-done
  45.6 2.5 %collective-permute-start = (bf16[4,704,128]{2,1,0:T(8,128)(2,1)S(1)}, bf16[4,704,128]{2,1,0:T(8,128)(2,1)S(1)}, u32[]{:S(2)}, u32[]{:S(2)}) collective-permute-start(bf16[4,704,128]{2,1,0:T(8,128)(2,1)S(1)} %bitcast.27), channel_id=1, source_target_pairs={{0,1},{1,0},{2,3},{3,2},{4,5},{5,4},{6,7},{7,6},{8,9},{9,8},{10,11... | collective-permute-start | bytes 2162696 | tf_op jit(solution)/shard_map/ppermute | solution.py:233
  48.1 8.4 %collective-permute-done.4.far_ref = bf16[112,1536]{1,0:T(8,128)(2,1)S(1)} collective-permute-done((bf16[112,1536]{1,0:T(8,128)(2,1)S(1)}, bf16[112,1536]{1,0:T(8,128)(2,1)S(1)}, u32[]{:S(2)}, u32[]{:S(2)}) %collective-permute-start.4) | collective-permute-done | bytes 344096 | tf_op jit(solution)/shard_map/ppermute | solution.py:241
  56.6 1.9 %collective-permute-start.5 = (bf16[112,1536]{1,0:T(8,128)(2,1)S(1)}, bf16[112,1536]{1,0:T(8,128)(2,1)S(1)}, u32[]{:S(2)}, u32[]{:S(2)}) collective-permute-start(bf16[112,1536]{1,0:T(8,128)(2,1)S(1)} %collective-permute-done.4.far_ref), channel_id=1, source_target_pairs={{0,16},{16,0},{1,17},{17,1},{2,18},{18,2},{3,19},{19,3},{4,20},{20... | collective-permute-start | bytes 1032200 | tf_op jit(solution)/shard_map/ppermute | solution.py:233
  58.5 1.6 %collective-permute-done.5.far_other_ref = bf16[112,1536]{1,0:T(8,128)(2,1)S(1)} collective-permute-done((bf16[112,1536]{1,0:T(8,128)(2,1)S(1)}, bf16[112,1536]{1,0:T(8,128)(2,1)S(1)}, u32[]{:S(2)}, u32[]{:S(2)}) %collective-permute-start.5) | collective-permute-done | bytes 344096 | tf_op jit(solution)/shard_map/ppermute | solution.py:233
  60.1 0.0 collective-permute-done.3.near_other_ref
  60.1 0.4 assemble.1
  60.5 9.4 %collective-permute-done.other_ref = bf16[4,704,128]{2,1,0:T(8,128)(2,1)S(1)} collective-permute-done((bf16[4,704,128]{2,1,0:T(8,128)(2,1)S(1)}, bf16[4,704,128]{2,1,0:T(8,128)(2,1)S(1)}, u32[]{:S(2)}, u32[]{:S(2)}) %collective-permute-start) | collective-permute-done | bytes 720928 | tf_op jit(solution)/shard_map/ppermute | solution.py:233
  69.8 2.5 %before.1 = (bf16[4,96,1536]{2,1,0:T(8,128)(2,1)S(1)}, bf16[384,896]{1,0:T(8,128)(2,1)S(1)}) custom-call(bf16[4,704,128]{2,1,0:T(8,128)(2,1)S(1)} %bitcast.28, bf16[4,704,128]{2,1,0:T(8,128)(2,1)S(1)} %collective-permute-done.other_ref, bf16[896,1536]{1,0:T(8,128)(2,1)S(1)} %get-tuple-element.22.weight_ref, bf16[672,704]{1,0:T(8,128)(2,1)S(1)} %get-tuple-element.23.pick_ref), custom_call_target="tpu_custom_call" | custom-call | flops 2000000000 | bytes 4000000 | tf_op jit(solution)/shard_map/before/pallas_call | solution.py:62
  72.4 19.3 %all_to_all.20.part_ref = bf16[4,96,1536]{2,1,0:T(8,128)(2,1)S(1)} all-to-all(bf16[4,96,1536]{2,1,0:T(8,128)(2,1)S(1)} %get-tuple-element.24), channel_id=1, replica_groups=mesh['x'=4,'zh'=4,'c'=2,'y'=8,'zl'=2] {'x'}, dimensions={0} | all-to-all | bytes 2359296 | tf_op jit(solution)/shard_map/all_to_all | solution.py:249
  91.7 0.3 middle.1
  92.0 18.1 %all_to_all.21.mid_ref = bf16[4,96,1536]{2,1,0:T(8,128)(2,1)S(1)} all-to-all(bf16[4,96,1536]{2,1,0:T(8,128)(2,1)S(1)} %get-tuple-element.25), channel_id=1, replica_groups=mesh['x'=4,'zh'=4,'c'=2,'y'=8,'zl'=2] {'x'}, dimensions={0} | all-to-all | bytes 2359296 | tf_op jit(solution)/shard_map/all_to_all | solution.py:249
  110.1 1.7 %after.1 = (bf16[4,48,1024]{2,1,0:T(8,128)(2,1)S(1)}, bf16[4,48,1024]{2,1,0:T(8,128)(2,1)S(1)}, bf16[112,512]{1,0:T(8,128)(2,1)S(1)}, bf16[112,512]{1,0:T(8,128)...) custom-call(bf16[4,96,1536]{2,1,0:T(8,128)(2,1)S(1)} %all_to_all.21.mid_ref,, ...), custom_call_target="tpu_custom_call" | custom-call | flops 1400000000 | bytes 4000000 | tf_op jit(solution)/shard_map/after/pallas_call | solution.py:62
  111.8 1.9 %collective-permute-start.6 = (bf16[4,48,1024]{2,1,0:T(8,128)(2,1)S(1)}, bf16[4,48,1024]{2,1,0:T(8,128)(2,1)S(1)}, u32[]{:S(2)}, u32[]{:S(2)}) collective-permute-start(bf16[4,48,1024]{2,1,0:T(8,128)(2,1)S(1)} %get-tuple-element.29), channel_id=1, source_target_pairs={{0,1},{1,0},{2,3},{3,2},{4,5},{5,4},{6,7},{7,6},{8,9},{9,8},{10,11... | collective-permute-start | bytes 1179656 | tf_op jit(solution)/shard_map/ppermute | solution.py:233
  113.8 1.9 %collective-permute-start.7 = (bf16[4,112,512]{2,1,0:T(8,128)(2,1)S(1)}, bf16[4,112,512]{2,1,0:T(8,128)(2,1)S(1)}, u32[]{:S(2)}, u32[]{:S(2)}) collective-permute-start(bf16[4,112,512]{2,1,0:T(8,128)(2,1)S(1)} %get-tuple-element.33), channel_id=1, source_target_pairs={{0,16},{16,0},{1,17},{17,1},{2,18},{18,2},{3,19},{19,3},{4,20},{20... | collective-permute-start | bytes 1376264 | tf_op jit(solution)/shard_map/ppermute | solution.py:233
  115.7 6.9 %collective-permute-done.6.got_ref = bf16[4,48,1024]{2,1,0:T(8,128)(2,1)S(1)} collective-permute-done((bf16[4,48,1024]{2,1,0:T(8,128)(2,1)S(1)}, bf16[4,48,1024]{2,1,0:T(8,128)(2,1)S(1)}, u32[]{:S(2)}, u32[]{:S(2)}) %collective-permute-start.6) | collective-permute-done | bytes 393248 | tf_op jit(solution)/shard_map/ppermute | solution.py:233
  122.6 1.2 combine.1
  123.7 0.0 copy-start.1
  123.7 0.0 copy-start.2
  123.7 9.7 %all-to-all-start.3 = ((bf16[32,48,128]{2,1,0:T(8,128)(2,1)}), bf16[32,48,128]{2,1,0:T(8,128)(2,1)S(1)}, u32[]{:S(2)}, u32[]{:S(2)}) async-start(bf16[32,48,128]{2,1,0:T(8,128)(2,1)} %bitcast.4), calls=%async_computation.3 | async-start | bytes 786432 | tf_op jit(solution)/shard_map/all_to_all | solution.py:249
  133.4 0.0 collective-permute-done.7
  133.4 0.1 fusion.3
  133.5 6.8 %collective-permute-start.10 = (bf16[112,512]{1,0:T(8,128)(2,1)S(1)}, bf16[112,512]{1,0:T(8,128)(2,1)S(1)}, u32[]{:S(2)}, u32[]{:S(2)}) collective-permute-start(bf16[112,512]{1,0:T(8,128)(2,1)S(1)} %get-tuple-element.38), channel_id=1, source_target_pairs={{0,64},{32,96},{64,0},{96,32},{1,65},{33,97},{65,1},{97,33},{2,66}... | collective-permute-start | bytes 344072 | tf_op jit(solution)/shard_map/ppermute | solution.py:233
  140.3 3.4 %collective-permute-start.8 = (bf16[112,512]{1,0:T(8,128)(2,1)S(1)}, bf16[112,512]{1,0:T(8,128)(2,1)S(1)}, u32[]{:S(2)}, u32[]{:S(2)}) collective-permute-start(bf16[112,512]{1,0:T(8,128)(2,1)S(1)} %get-tuple-element.37), channel_id=1, source_target_pairs={{0,32},{32,64},{64,96},{96,0},{1,33},{33,65},{65,97},{97,1},{2,34}... | collective-permute-start | bytes 344072 | tf_op jit(solution)/shard_map/ppermute | solution.py:233
  143.7 4.6 %collective-permute-start.9 = (bf16[112,512]{1,0:T(8,128)(2,1)S(1)}, bf16[112,512]{1,0:T(8,128)(2,1)S(1)}, u32[]{:S(2)}, u32[]{:S(2)}) collective-permute-start(bf16[112,512]{1,0:T(8,128)(2,1)S(1)} %get-tuple-element.39), channel_id=1, source_target_pairs={{0,96},{32,0},{64,32},{96,64},{1,97},{33,1},{65,33},{97,65},{2,98}... | collective-permute-start | bytes 344072 | tf_op jit(solution)/shard_map/ppermute | solution.py:233
  148.3 0.0 collective-permute-done.10
  148.3 1.4 collective-permute-done.8
  149.7 2.7 %collective-permute-done.9 = bf16[112,512]{1,0:T(8,128)(2,1)S(1)} collective-permute-done((bf16[112,512]{1,0:T(8,128)(2,1)S(1)}, bf16[112,512]{1,0:T(8,128)(2,1)S(1)}, u32[]{:S(2)}, u32[]{:S(2)}) %collective-permute-start.9) | collective-permute-done | bytes 114720 | tf_op jit(solution)/shard_map/ppermute | solution.py:233
  152.4 0.7 add_convert_fusion
  153.1 0.0 all-to-all-done.3
  153.1 0.0 copy-done.1
  153.1 0.0 copy-done.2
  153.1 1.8 %finish.1 = (bf16[128,3584]{1,0:T(8,128)(2,1)}, f32[1,128]{1,0:T(1,128)}) custom-call(s32[1,128]{1,0:T(1,128)S(1)} %bitcast.31, f32[1,128]{1,0:T(1,128)S(1)} %bitcast.33, bf16[4,384,128]{2,1,0:T(8,128)(2,1)S(1)} %bitcast.29), custom_call_target="tpu_custom_call" | custom-call | flops 400000000 | bytes 4000000 | tf_op jit(solution)/shard_map/finish/pallas_call | solution.py:62
Async XLA Ops:
  2.4 20.1 %collective-permute-start.1 = (bf16[112,1536]{1,0:T(8,128)(2,1)}, bf16[112,1536]{1,0:T(8,128)(2,1)S(1)}, u32[]{:S(2)}, u32[]{:S(2)}) collective-permute-start(bf16[112,1536]{1,0:T(8,128)(2,1)} %stack.1.own_ref), channel_id=1, source_target_pairs={{0,32},{16,112},{32,64},{48,16},{64,96},{80,48},{96,0},{112,80},{1... | collective-permute-start | bytes 1032200 | tf_op jit(solution)/shard_map/ppermute | solution.py:241
  12.1 26.1 %copy-start = (bf16[112,1536]{1,0:T(8,128)(2,1)S(1)}, bf16[112,1536]{1,0:T(8,128)(2,1)}, u32[]{:S(2)}) copy-start(bf16[112,1536]{1,0:T(8,128)(2,1)} %stack.1.own_ref) | copy-start | bytes 1032196
  12.1 33.5 %all-to-all-start = ((bf16[32,88,128]{2,1,0:T(8,128)(2,1)}), bf16[32,88,128]{2,1,0:T(8,128)(2,1)S(1)}, u32[]{:S(2)}, u32[]{:S(2)}) async-start(bf16[32,88,128]{2,1,0:T(8,128)(2,1)} %bitcast.34), calls=%async_computation | async-start | bytes 1441792 | tf_op jit(solution)/shard_map/all_to_all | solution.py:249
  22.5 15.7 %collective-permute-start.2 = (bf16[112,1536]{1,0:T(8,128)(2,1)S(1)}, bf16[112,1536]{1,0:T(8,128)(2,1)S(1)}, u32[]{:S(2)}, u32[]{:S(2)}) collective-permute-start(bf16[112,1536]{1,0:T(8,128)(2,1)S(1)} %collective-permute-done.1.before_ref), channel_id=1, source_target_pairs={{0,32},{16,112},{32,64},{48,16},{64,96},{80,48},{96,0},{112,80},{1... | collective-permute-start | bytes 1032200 | tf_op jit(solution)/shard_map/ppermute | solution.py:241
  38.3 21.8 %collective-permute-start.3 = (bf16[336,1536]{1,0:T(8,128)(2,1)S(1)}, bf16[336,1536]{1,0:T(8,128)(2,1)S(1)}, u32[]{:S(2)}, u32[]{:S(2)}) collective-permute-start(bf16[336,1536]{1,0:T(8,128)(2,1)S(1)} %get-tuple-element.20.near_ref), channel_id=1, source_target_pairs={{0,16},{16,0},{1,17},{17,1},{2,18},{18,2},{3,19},{19,3},{4,20},{20... | collective-permute-start | bytes 3096584 | tf_op jit(solution)/shard_map/ppermute | solution.py:233
  41.0 15.6 %collective-permute-start.4 = (bf16[112,1536]{1,0:T(8,128)(2,1)S(1)}, bf16[112,1536]{1,0:T(8,128)(2,1)S(1)}, u32[]{:S(2)}, u32[]{:S(2)}) collective-permute-start(bf16[112,1536]{1,0:T(8,128)(2,1)S(1)} %get-tuple-element.21), channel_id=1, source_target_pairs={{0,32},{16,112},{32,64},{48,16},{64,96},{80,48},{96,0},{112,80},{1... | collective-permute-start | bytes 1032200 | tf_op jit(solution)/shard_map/ppermute | solution.py:241
  45.6 24.2 %collective-permute-start = (bf16[4,704,128]{2,1,0:T(8,128)(2,1)S(1)}, bf16[4,704,128]{2,1,0:T(8,128)(2,1)S(1)}, u32[]{:S(2)}, u32[]{:S(2)}) collective-permute-start(bf16[4,704,128]{2,1,0:T(8,128)(2,1)S(1)} %bitcast.27), channel_id=1, source_target_pairs={{0,1},{1,0},{2,3},{3,2},{4,5},{5,4},{6,7},{7,6},{8,9},{9,8},{10,11... | collective-permute-start | bytes 2162696 | tf_op jit(solution)/shard_map/ppermute | solution.py:233
  56.6 3.5 %collective-permute-start.5 = (bf16[112,1536]{1,0:T(8,128)(2,1)S(1)}, bf16[112,1536]{1,0:T(8,128)(2,1)S(1)}, u32[]{:S(2)}, u32[]{:S(2)}) collective-permute-start(bf16[112,1536]{1,0:T(8,128)(2,1)S(1)} %collective-permute-done.4.far_ref), channel_id=1, source_target_pairs={{0,16},{16,0},{1,17},{17,1},{2,18},{18,2},{3,19},{19,3},{4,20},{20... | collective-permute-start | bytes 1032200 | tf_op jit(solution)/shard_map/ppermute | solution.py:233
  111.8 10.7 %collective-permute-start.6 = (bf16[4,48,1024]{2,1,0:T(8,128)(2,1)S(1)}, bf16[4,48,1024]{2,1,0:T(8,128)(2,1)S(1)}, u32[]{:S(2)}, u32[]{:S(2)}) collective-permute-start(bf16[4,48,1024]{2,1,0:T(8,128)(2,1)S(1)} %get-tuple-element.29), channel_id=1, source_target_pairs={{0,1},{1,0},{2,3},{3,2},{4,5},{5,4},{6,7},{7,6},{8,9},{9,8},{10,11... | collective-permute-start | bytes 1179656 | tf_op jit(solution)/shard_map/ppermute | solution.py:233
  113.8 19.6 %collective-permute-start.7 = (bf16[4,112,512]{2,1,0:T(8,128)(2,1)S(1)}, bf16[4,112,512]{2,1,0:T(8,128)(2,1)S(1)}, u32[]{:S(2)}, u32[]{:S(2)}) collective-permute-start(bf16[4,112,512]{2,1,0:T(8,128)(2,1)S(1)} %get-tuple-element.33), channel_id=1, source_target_pairs={{0,16},{16,0},{1,17},{17,1},{2,18},{18,2},{3,19},{19,3},{4,20},{20... | collective-permute-start | bytes 1376264 | tf_op jit(solution)/shard_map/ppermute | solution.py:233
  123.7 29.4 %copy-start.1 = (s32[128,1]{0,1:T(1,128)S(1)}, s32[128,1]{0,1:T(1,128)}, u32[]{:S(2)}) copy-start(s32[128,1]{0,1:T(1,128)} %param.9) | copy-start | bytes 1540
  123.7 29.4 %copy-start.2 = (f32[128,1]{0,1:T(1,128)S(1)}, f32[128,1]{0,1:T(1,128)}, u32[]{:S(2)}) copy-start(f32[128,1]{0,1:T(1,128)} %param.10) | copy-start | bytes 1540
  123.7 29.3 %all-to-all-start.3 = ((bf16[32,48,128]{2,1,0:T(8,128)(2,1)}), bf16[32,48,128]{2,1,0:T(8,128)(2,1)S(1)}, u32[]{:S(2)}, u32[]{:S(2)}) async-start(bf16[32,48,128]{2,1,0:T(8,128)(2,1)} %bitcast.4), calls=%async_computation.3 | async-start | bytes 786432 | tf_op jit(solution)/shard_map/all_to_all | solution.py:249
  133.5 14.8 %collective-permute-start.10 = (bf16[112,512]{1,0:T(8,128)(2,1)S(1)}, bf16[112,512]{1,0:T(8,128)(2,1)S(1)}, u32[]{:S(2)}, u32[]{:S(2)}) collective-permute-start(bf16[112,512]{1,0:T(8,128)(2,1)S(1)} %get-tuple-element.38), channel_id=1, source_target_pairs={{0,64},{32,96},{64,0},{96,32},{1,65},{33,97},{65,1},{97,33},{2,66}... | collective-permute-start | bytes 344072 | tf_op jit(solution)/shard_map/ppermute | solution.py:233
  140.3 9.3 %collective-permute-start.8 = (bf16[112,512]{1,0:T(8,128)(2,1)S(1)}, bf16[112,512]{1,0:T(8,128)(2,1)S(1)}, u32[]{:S(2)}, u32[]{:S(2)}) collective-permute-start(bf16[112,512]{1,0:T(8,128)(2,1)S(1)} %get-tuple-element.37), channel_id=1, source_target_pairs={{0,32},{32,64},{64,96},{96,0},{1,33},{33,65},{65,97},{97,1},{2,34}... | collective-permute-start | bytes 344072 | tf_op jit(solution)/shard_map/ppermute | solution.py:233
  143.7 8.6 %collective-permute-start.9 = (bf16[112,512]{1,0:T(8,128)(2,1)S(1)}, bf16[112,512]{1,0:T(8,128)(2,1)S(1)}, u32[]{:S(2)}, u32[]{:S(2)}) collective-permute-start(bf16[112,512]{1,0:T(8,128)(2,1)S(1)} %get-tuple-element.39), channel_id=1, source_target_pairs={{0,96},{32,0},{64,32},{96,64},{1,97},{33,1},{65,33},{97,65},{2,98}... | collective-permute-start | bytes 344072 | tf_op jit(solution)/shard_map/ppermute | solution.py:233
